TPU v7x, 32 devices: a whole 2x2x4 slice. The times are simulated.
32 devices in a mesh: ctx: 4 (over x, core), fsdp: 8 (over z, y).
Axes of the slice: x: 2, y: 2, z: 4, core: 2. Of those that a mesh axis runs over, the one named last changes fastest.
Arguments:
- hidden_in: bfloat16 [8, 512, 1536], P('fsdp', 'ctx'), may hold values from -6 to 6
- w_query: bfloat16 [2, 1536, 1536], P(None, ('ctx', 'fsdp')), may hold values from -0.15625 to 0.15625
- w_key_value: bfloat16 [2, 1536, 1024], P(None, ('ctx', 'fsdp')), may hold values from -0.15625 to 0.15625
- w_output: bfloat16 [2, 1536, 1536], P(None, ('ctx', 'fsdp')), may hold values from -1.25 to 1.25
- w_router: bfloat16 [2, 1536, 16], P(None, ('ctx', 'fsdp')), may hold values from -0.078125 to 0.078125
- norm_gains: bfloat16 [2, 1536, 2], P(None, ('ctx', 'fsdp')), may hold values from 0.5 to 1.5
- w_gate_up: bfloat16 [2, 16, 1536, 1024], P(None, 'fsdp', 'ctx'), may hold values from -0.15625 to 0.15625
- w_down: bfloat16 [2, 16, 512, 1536], P(None, 'fsdp', 'ctx'), may hold values from -1 to 1
- expert_ids: int32 [2, 8, 512, 8], P(None, 'fsdp', 'ctx'), may hold values from 0 to 15, all different within a row; in each aligned block of 128 rows (0 to 127, 128 to 255, ..., all dimensions but the last counted through in order) at most 96 rows name the same one
- out_grad: bfloat16 [8, 512, 1536], P('fsdp', 'ctx'), may hold values from -6 to 6
Outputs:
- hidden_out: bfloat16 [8, 512, 1536], P('fsdp', 'ctx')
- grad_hidden: float32 [8, 512, 1536], P('fsdp', 'ctx')
- grad_query: float32 [2, 1536, 1536], P(None, ('ctx', 'fsdp'))
- grad_key_value: float32 [2, 1536, 1024], P(None, ('ctx', 'fsdp'))
- grad_output: float32 [2, 1536, 1536], P(None, ('ctx', 'fsdp'))
- grad_router: float32 [2, 1536, 16], P(None, ('ctx', 'fsdp'))
- grad_gains: float32 [2, 1536, 2], P(None, ('ctx', 'fsdp'))
- grad_gate_up: float32 [2, 16, 1536, 1024], P(None, 'fsdp', 'ctx')
- grad_down: float32 [2, 16, 512, 1536], P(None, 'fsdp', 'ctx')
Inputs may be any that keep to these rules, and one draw needn't show every extreme that they name: `expert_ids`: 8 different experts for each token and layer; of the 128 rows of one device in a layer, at most 96 choose one expert, and some expert is chosen by exactly 96 of them.
All inputs are finite; a program needn't handle non-finite values.
Results may differ from a plain program's by a relative error of at most 0.033.
Values may be sent and summed in bfloat16 or wider, within the bound.
No kernel may reach another device: no remote copies, remote signals or barrier semaphores. Data moves between devices by JAX's collectives and lax.ppermute only.
A program may use at most 384 MiB of HBM per device.

v0:
```python
import math

import jax
import jax.numpy as jnp
from jax import lax
from jax.sharding import PartitionSpec as P

HEADS = 24
KV_HEADS = 8
HEAD_DIM = 64
FE = 512
TOP = 8


highest = lax.Precision.HIGHEST
epsilon = 1e-06
rope_base = 10000.0
masked_score = -1e30


def row_positions(first_row, row_total, row_count, shards):
    indices = first_row + jnp.arange(row_total, dtype=jnp.int32)
    shard_of = indices // row_count
    within = indices % row_count
    half_rows = row_count // 2
    return jnp.where(
        within < half_rows,
        shard_of * half_rows + within,
        (2 * shards - 1 - shard_of) * half_rows + within - half_rows,
    )


def rotate(values_in, places, direction):
    half_dim = values_in.shape[-1] // 2
    frequency = rope_base ** (-jnp.arange(half_dim, dtype=jnp.float32) / half_dim)
    angles = places.astype(jnp.float32)[:, None] * frequency[None, :]
    cosine_part = jnp.cos(angles)[:, None, :]
    sine_part = direction * jnp.sin(angles)[:, None, :]
    front_half = values_in[..., :half_dim]
    back_half = values_in[..., half_dim:]
    return jnp.concatenate(
        [
            front_half * cosine_part - back_half * sine_part,
            back_half * cosine_part + front_half * sine_part,
        ],
        -1,
    )


def rms_scaled(residual, gain_vector):
    inverse_root = lax.rsqrt(jnp.mean(residual * residual, -1, keepdims=True) + epsilon)
    return (residual * inverse_root * gain_vector, inverse_root)


def rms_back(residual, inverse_root, gain_vector, grad_normed):
    grad_gain = jnp.sum(grad_normed * residual * inverse_root, 0)
    weighted = gain_vector * grad_normed
    cubed = inverse_root * inverse_root * inverse_root
    grad_residual = inverse_root * weighted - residual * cubed * jnp.mean(
        residual * weighted, -1, keepdims=True
    )
    return (grad_residual, grad_gain)


def route_table(routing_rows, expert_total, row_count, capacity):
    top_count = routing_rows.shape[1]
    chosen_mask = (
        routing_rows[:, :, None] == jnp.arange(expert_total, dtype=jnp.int32)[None, None, :]
    )
    expert_used = jnp.sum(chosen_mask.astype(jnp.int32), 1)
    slot_all = jnp.cumsum(expert_used, 0) - expert_used
    slot_taken = jnp.sum(jnp.where(chosen_mask, slot_all[:, None, :], 0), -1)
    target_slots = routing_rows * capacity + slot_taken
    entry_rows = jnp.full((expert_total * capacity,), row_count * top_count, jnp.int32)
    entry_rows = entry_rows.at[target_slots.reshape(-1)].set(
        jnp.arange(row_count * top_count, dtype=jnp.int32)
    )
    return (chosen_mask, target_slots, entry_rows)


def fold_keys(running, key_piece, queries, query_places, row_count, shards, kv_width):
    piece_rows = key_piece.shape[0]
    step_rows = math.gcd(piece_rows, row_count)
    step_total = piece_rows // step_rows
    blocks_in = key_piece.reshape(step_total, step_rows, key_piece.shape[1])
    heads_kv = queries.shape[1]
    head_size = queries.shape[3]
    score_scale = head_size ** (-0.5)

    def fold_one_step(state_in, inputs):
        block_rows, block_index = inputs
        key_places = row_positions(block_index * step_rows, step_rows, row_count, shards)
        key_rows = block_rows[:, :kv_width].reshape(step_rows, heads_kv, head_size)
        value_rows = block_rows[:, kv_width:].reshape(step_rows, heads_kv, head_size)
        scores = (
            jnp.einsum("qhgd,khd->hgqk", queries, key_rows, preferred_element_type=jnp.float32)
            * score_scale
        )
        visible = query_places[:, None] >= key_places[None, :]
        scores = jnp.where(visible, scores, masked_score)
        old_top, old_total, old_sum = state_in
        new_top = jnp.maximum(old_top, jnp.max(scores, -1))
        shrink = jnp.exp(old_top - new_top)
        weights = jnp.where(visible, jnp.exp(scores - new_top[..., None]), 0.0)
        new_total = old_total * shrink + jnp.sum(weights, -1)
        new_sum = old_sum * shrink[..., None] + jnp.einsum(
            "hgqk,khd->hgqd",
            weights.astype(jnp.bfloat16),
            value_rows,
            preferred_element_type=jnp.float32,
        )
        return ((new_top, new_total, new_sum), None)

    running, _ = lax.scan(
        fold_one_step, running, (blocks_in, jnp.arange(step_total, dtype=jnp.int32))
    )
    return running


def attend_back(
    queries,
    query_places,
    gathered,
    out_exact,
    grad_attended,
    log_total,
    row_count,
    shards,
    kv_width,
):
    heads_kv = queries.shape[1]
    head_size = queries.shape[3]
    score_scale = head_size ** (-0.5)
    delta_rows = jnp.transpose(
        jnp.sum(grad_attended.astype(jnp.float32) * out_exact, -1), (1, 2, 0)
    )
    blocks_in = gathered.reshape(shards, row_count, gathered.shape[1])

    def attend_one_step(grad_queries, inputs):
        block_rows, block_index = inputs
        key_places = row_positions(block_index * row_count, row_count, row_count, shards)
        key_rows = block_rows[:, :kv_width].reshape(row_count, heads_kv, head_size)
        value_rows = block_rows[:, kv_width:].reshape(row_count, heads_kv, head_size)
        scores = (
            jnp.einsum("qhgd,khd->hgqk", queries, key_rows, preferred_element_type=jnp.float32)
            * score_scale
        )
        visible = query_places[:, None] >= key_places[None, :]
        probabilities = jnp.where(visible, jnp.exp(scores - log_total[..., None]), 0.0)
        rounded = probabilities.astype(jnp.bfloat16)
        grad_values = jnp.einsum(
            "hgqk,qhgd->khd", rounded, grad_attended, preferred_element_type=jnp.float32
        )
        grad_probs = jnp.einsum(
            "qhgd,khd->hgqk", grad_attended, value_rows, preferred_element_type=jnp.float32
        )
        grad_scores = (probabilities * (grad_probs - delta_rows[..., None])).astype(jnp.bfloat16)
        grad_queries = grad_queries + score_scale * jnp.einsum(
            "hgqk,khd->qhgd", grad_scores, key_rows, preferred_element_type=jnp.float32
        )
        grad_keys = score_scale * jnp.einsum(
            "hgqk,qhgd->khd", grad_scores, queries, preferred_element_type=jnp.float32
        )
        return (
            grad_queries,
            jnp.concatenate(
                [grad_keys.reshape(row_count, kv_width), grad_values.reshape(row_count, kv_width)],
                -1,
            ),
        )

    start_grad = jnp.zeros(queries.shape, jnp.float32)
    grad_queries, grad_blocks = lax.scan(
        attend_one_step, start_grad, (blocks_in, jnp.arange(shards, dtype=jnp.int32))
    )
    return (grad_queries, grad_blocks.reshape(shards * row_count, gathered.shape[1]))


def on_device(
    hidden_in,
    w_query,
    w_key_value,
    w_output,
    w_router,
    norm_gains,
    w_gate_up,
    w_down,
    expert_ids,
    out_grad,
):
    shards = lax.axis_size("ctx")
    groups = lax.axis_size("fsdp")
    shard_index = lax.axis_index("ctx")
    row_count = hidden_in.shape[1]
    model_width = hidden_in.shape[2]
    layer_total = w_query.shape[0]
    experts_here = w_gate_up.shape[1]
    expert_total = experts_here * groups
    capacity = min(row_count, 3 * row_count * TOP // (2 * expert_total))
    kv_width = w_key_value.shape[2] // 2
    group_size = HEADS // KV_HEADS
    query_places = row_positions(shard_index * row_count, row_count, row_count, shards)
    residual = hidden_in.reshape(row_count, model_width).astype(jnp.float32)
    saved = []
    for layer_index in range(layer_total):
        query_weight, key_value_weight, output_weight, router_weight, gains = (
            lax.all_gather(w_query[layer_index], ("ctx", "fsdp"), axis=0, tiled=True),
            lax.all_gather(w_key_value[layer_index], ("ctx", "fsdp"), axis=0, tiled=True),
            lax.all_gather(w_output[layer_index], ("ctx", "fsdp"), axis=0, tiled=True),
            lax.all_gather(w_router[layer_index], ("ctx", "fsdp"), axis=0, tiled=True),
            lax.all_gather(norm_gains[layer_index], ("ctx", "fsdp"), axis=0, tiled=True),
        )
        gate_up_weight, down_weight = (
            lax.all_gather(w_gate_up[layer_index], "ctx", axis=1, tiled=True),
            lax.all_gather(w_down[layer_index], "ctx", axis=1, tiled=True),
        )
        gain_pair = gains.astype(jnp.float32)
        normed_first, root_first = rms_scaled(residual, gain_pair[:, 0])
        normed_first_low = normed_first.astype(jnp.bfloat16)
        query_raw = jnp.dot(normed_first_low, query_weight, preferred_element_type=jnp.float32)
        key_value_raw = jnp.dot(
            normed_first_low, key_value_weight, preferred_element_type=jnp.float32
        )
        queries = rotate(query_raw.reshape(row_count, HEADS, HEAD_DIM), query_places, 1.0).astype(
            jnp.bfloat16
        )
        queries = queries.reshape(row_count, KV_HEADS, group_size, HEAD_DIM)
        key_turned = rotate(
            key_value_raw[:, :kv_width].reshape(row_count, KV_HEADS, HEAD_DIM), query_places, 1.0
        )
        key_value_low = jnp.concatenate(
            [key_turned.reshape(row_count, kv_width), key_value_raw[:, kv_width:]], -1
        ).astype(jnp.bfloat16)
        start_state = (
            jnp.full((KV_HEADS, group_size, row_count), masked_score, jnp.float32),
            jnp.zeros((KV_HEADS, group_size, row_count), jnp.float32),
            jnp.zeros((KV_HEADS, group_size, row_count, HEAD_DIM), jnp.float32),
        )
        top_score, score_total, accumulated = fold_keys(
            start_state,
            lax.all_gather(key_value_low, "ctx", axis=0, tiled=True),
            queries,
            query_places,
            row_count,
            shards,
            kv_width,
        )
        out_exact = jnp.transpose(accumulated / score_total[..., None], (2, 0, 1, 3))
        log_total = top_score + jnp.log(score_total)
        attended = out_exact.reshape(row_count, model_width).astype(jnp.bfloat16)
        middle = residual + jnp.dot(attended, output_weight, preferred_element_type=jnp.float32)
        normed_second, root_second = rms_scaled(middle, gain_pair[:, 1])
        normed_second_low = normed_second.astype(jnp.bfloat16)
        chosen_mask, target_slots, entry_rows = route_table(
            expert_ids[layer_index].reshape(row_count, TOP), expert_total, row_count, capacity
        )
        padded_rows = jnp.concatenate(
            [normed_second_low, jnp.zeros((1, model_width), jnp.bfloat16)], 0
        )
        send_buffer = padded_rows[jnp.minimum(entry_rows // TOP, row_count)].reshape(
            groups, experts_here, capacity, model_width
        )
        received = lax.all_to_all(send_buffer, "fsdp", split_axis=0, concat_axis=0, tiled=True)
        gate_up = jnp.einsum(
            "serd,edf->serf", received, gate_up_weight, preferred_element_type=jnp.float32
        )
        hidden = (jax.nn.silu(gate_up[..., :FE]) * gate_up[..., FE:]).astype(jnp.bfloat16)
        expert_out = jnp.einsum(
            "serf,efd->serd", hidden, down_weight, preferred_element_type=jnp.float32
        ).astype(jnp.bfloat16)
        returned = lax.all_to_all(
            expert_out, "fsdp", split_axis=0, concat_axis=0, tiled=True
        ).reshape(expert_total * capacity, model_width)
        picked = returned[target_slots]
        logits = jnp.dot(normed_second_low, router_weight, preferred_element_type=jnp.float32)
        chosen_logits = jnp.sum(jnp.where(chosen_mask, logits[:, None, :], 0.0), -1)
        gate_probs = jax.nn.softmax(chosen_logits, axis=-1)
        expert_sum = jnp.sum(gate_probs[..., None] * picked.astype(jnp.float32), 1)
        saved.append(
            (
                residual,
                root_first,
                normed_first_low,
                queries,
                key_value_low,
                out_exact,
                log_total,
                attended,
                middle,
                root_second,
                normed_second_low,
                chosen_mask,
                target_slots,
                entry_rows,
                received,
                gate_up,
                hidden,
                picked,
                gate_probs,
                query_weight,
                key_value_weight,
                output_weight,
                router_weight,
                gain_pair,
                gate_up_weight,
                down_weight,
            )
        )
        residual = middle + expert_sum
    hidden_out = residual.reshape(1, row_count, model_width).astype(jnp.bfloat16)
    grad_residual = out_grad.reshape(row_count, model_width).astype(jnp.float32)
    (
        query_parts,
        key_value_parts,
        output_parts,
        router_parts,
        gain_parts,
        gate_up_parts,
        down_parts,
    ) = ([], [], [], [], [], [], [])
    for layer_index in reversed(range(layer_total)):
        (
            layer_input,
            root_first,
            normed_first_low,
            queries,
            key_value_low,
            out_exact,
            log_total,
            attended,
            middle,
            root_second,
            normed_second_low,
            chosen_mask,
            target_slots,
            entry_rows,
            received,
            gate_up,
            hidden,
            picked,
            gate_probs,
            query_weight,
            key_value_weight,
            output_weight,
            router_weight,
            gain_pair,
            gate_up_weight,
            down_weight,
        ) = saved[layer_index]
        grad_gates = jnp.sum(grad_residual[:, None, :] * picked.astype(jnp.float32), -1)
        grad_leaving = (
            (gate_probs[..., None] * grad_residual[:, None, :])
            .astype(jnp.bfloat16)
            .reshape(row_count * TOP, model_width)
        )
        grad_padded = jnp.concatenate([grad_leaving, jnp.zeros((1, model_width), jnp.bfloat16)], 0)
        grad_send = grad_padded[entry_rows].reshape(groups, experts_here, capacity, model_width)
        grad_received = lax.all_to_all(grad_send, "fsdp", split_axis=0, concat_axis=0, tiled=True)
        grad_hidden = jnp.einsum(
            "serd,efd->serf", grad_received, down_weight, preferred_element_type=jnp.float32
        )
        grad_down_part = jnp.einsum(
            "serf,serd->efd", hidden, grad_received, preferred_element_type=jnp.float32
        )
        gate_part = gate_up[..., :FE]
        up_part = gate_up[..., FE:]
        sigmoid_gate = jax.nn.sigmoid(gate_part)
        grad_gate = grad_hidden * up_part * sigmoid_gate * (1.0 + gate_part * (1.0 - sigmoid_gate))
        grad_up = grad_hidden * gate_part * sigmoid_gate
        grad_gate_up_rows = jnp.concatenate([grad_gate, grad_up], -1).astype(jnp.bfloat16)
        grad_gate_up_part = jnp.einsum(
            "serd,serf->edf", received, grad_gate_up_rows, preferred_element_type=jnp.float32
        )
        grad_entering = jnp.einsum(
            "serf,edf->serd", grad_gate_up_rows, gate_up_weight, preferred_element_type=jnp.float32
        ).astype(jnp.bfloat16)
        grad_returned = lax.all_to_all(
            grad_entering, "fsdp", split_axis=0, concat_axis=0, tiled=True
        ).reshape(expert_total * capacity, model_width)
        grad_normed_second = jnp.sum(grad_returned[target_slots].astype(jnp.float32), 1)
        gate_mean = jnp.sum(gate_probs * grad_gates, -1, keepdims=True)
        grad_chosen = gate_probs * (grad_gates - gate_mean)
        grad_logits = jnp.sum(jnp.where(chosen_mask, grad_chosen[..., None], 0.0), 1)
        grad_router_part = jnp.dot(
            normed_second_low.astype(jnp.float32).T, grad_logits, precision=highest
        )
        grad_normed_second = grad_normed_second + jnp.dot(
            grad_logits, router_weight.astype(jnp.float32).T, precision=highest
        )
        grad_middle, grad_gain_second = rms_back(
            middle, root_second, gain_pair[:, 1], grad_normed_second
        )
        grad_middle = grad_middle + grad_residual
        grad_branch = grad_middle.astype(jnp.bfloat16)
        grad_output_part = jnp.einsum(
            "rd,re->de", attended, grad_branch, preferred_element_type=jnp.float32
        )
        grad_attended = jnp.einsum(
            "re,de->rd", grad_branch, output_weight, preferred_element_type=jnp.float32
        ).astype(jnp.bfloat16)
        grad_attended = grad_attended.reshape(row_count, KV_HEADS, group_size, HEAD_DIM)
        gathered = lax.all_gather(key_value_low, "ctx", axis=0, tiled=True)
        grad_queries, grad_key_value_all = attend_back(
            queries,
            query_places,
            gathered,
            out_exact,
            grad_attended,
            log_total,
            row_count,
            shards,
            kv_width,
        )
        grad_key_value_own = lax.psum_scatter(
            grad_key_value_all.astype(jnp.bfloat16), "ctx", scatter_dimension=0, tiled=True
        ).astype(jnp.float32)
        grad_keys = rotate(
            grad_key_value_own[:, :kv_width].reshape(row_count, KV_HEADS, HEAD_DIM),
            query_places,
            -1.0,
        )
        grad_key_value_low = jnp.concatenate(
            [grad_keys.reshape(row_count, kv_width), grad_key_value_own[:, kv_width:]], -1
        ).astype(jnp.bfloat16)
        grad_query_low = (
            rotate(grad_queries.reshape(row_count, HEADS, HEAD_DIM), query_places, -1.0)
            .reshape(row_count, model_width)
            .astype(jnp.bfloat16)
        )
        grad_query_part = jnp.einsum(
            "rd,re->de", normed_first_low, grad_query_low, preferred_element_type=jnp.float32
        )
        grad_key_value_part = jnp.einsum(
            "rd,re->de", normed_first_low, grad_key_value_low, preferred_element_type=jnp.float32
        )
        grad_normed_first = jnp.einsum(
            "re,de->rd", grad_query_low, query_weight, preferred_element_type=jnp.float32
        ) + jnp.einsum(
            "re,de->rd", grad_key_value_low, key_value_weight, preferred_element_type=jnp.float32
        )
        grad_input, grad_gain_first = rms_back(
            layer_input, root_first, gain_pair[:, 0], grad_normed_first
        )
        grad_residual = grad_input + grad_middle
        grad_gain_part = jnp.stack([grad_gain_first, grad_gain_second], -1)
        query_parts.insert(0, grad_query_part)
        key_value_parts.insert(0, grad_key_value_part)
        output_parts.insert(0, grad_output_part)
        router_parts.insert(0, grad_router_part)
        gain_parts.insert(0, grad_gain_part)
        gate_up_parts.insert(0, grad_gate_up_part)
        down_parts.insert(0, grad_down_part)
    stacked_query = jnp.stack(query_parts, 0)
    stacked_key_value = jnp.stack(key_value_parts, 0)
    stacked_output = jnp.stack(output_parts, 0)
    stacked_router = jnp.stack(router_parts, 0)
    stacked_gains = jnp.stack(gain_parts, 0)
    stacked_gate_up = jnp.stack(gate_up_parts, 0)
    stacked_down = jnp.stack(down_parts, 0)
    stacked_query, stacked_key_value, stacked_output, stacked_router, stacked_gains = (
        lax.psum_scatter(stacked_query, ("ctx", "fsdp"), scatter_dimension=1, tiled=True),
        lax.psum_scatter(stacked_key_value, ("ctx", "fsdp"), scatter_dimension=1, tiled=True),
        lax.psum_scatter(stacked_output, ("ctx", "fsdp"), scatter_dimension=1, tiled=True),
        lax.psum_scatter(stacked_router, ("ctx", "fsdp"), scatter_dimension=1, tiled=True),
        lax.psum_scatter(stacked_gains, ("ctx", "fsdp"), scatter_dimension=1, tiled=True),
    )
    stacked_gate_up, stacked_down = (
        lax.psum_scatter(
            stacked_gate_up.astype(jnp.bfloat16), "ctx", scatter_dimension=2, tiled=True
        ).astype(jnp.float32),
        lax.psum_scatter(
            stacked_down.astype(jnp.bfloat16), "ctx", scatter_dimension=2, tiled=True
        ).astype(jnp.float32),
    )
    grad_hidden = grad_residual.reshape(1, row_count, model_width)
    return (
        hidden_out,
        grad_hidden,
        stacked_query,
        stacked_key_value,
        stacked_output,
        stacked_router,
        stacked_gains,
        stacked_gate_up,
        stacked_down,
    )


def solution(mesh):
    return jax.shard_map(
        on_device,
        mesh=mesh,
        in_specs=(
            P("fsdp", "ctx", None),
            P(None, ("ctx", "fsdp"), None),
            P(None, ("ctx", "fsdp"), None),
            P(None, ("ctx", "fsdp"), None),
            P(None, ("ctx", "fsdp"), None),
            P(None, ("ctx", "fsdp"), None),
            P(None, "fsdp", "ctx", None),
            P(None, "fsdp", "ctx", None),
            P(None, "fsdp", "ctx", None),
            P("fsdp", "ctx", None),
        ),
        out_specs=(
            P("fsdp", "ctx", None),
            P("fsdp", "ctx", None),
            P(None, ("ctx", "fsdp"), None),
            P(None, ("ctx", "fsdp"), None),
            P(None, ("ctx", "fsdp"), None),
            P(None, ("ctx", "fsdp"), None),
            P(None, ("ctx", "fsdp"), None),
            P(None, "fsdp", "ctx", None),
            P(None, "fsdp", "ctx", None),
        ),
        check_vma=False,
    )
```

profile of v0, /device:TPU:0, one launch (start us, length us, event | category | flops | bytes accessed | tf_op | source)
XLA Modules:
  0.0 2605.0 jit_solution(18000613665335894341)
XLA Ops:
  10.3 75.1 %all-gather = bf16[1,1536,2]{2,0,1:T(2,128)(2,1)S(1)} all-gather(bf16[1,48,2]{2,0,1:T(2,128)(2,1)S(1)} %copy.353), channel_id=2, replica_groups=mesh['ctx'=4,'fsdp'=8] {'ctx','fsdp'}, dimensions={1}, use_global_device_ids=true | all-gather | bytes 6336 | tf_op jit(solution)/shard_map/all_gather | solution.py:211
  108.4 4.3 scatter_custom_fusion
  116.4 64.9 %all-gather.33.cloned.1.call-done = bf16[1,1536,1536]{2,1,0:T(8,128)(2,1)} async-done(((bf16[1,48,1536]{2,1,0:T(8,128)(2,1)}), bf16[1,1536,1536]{2,1,0:T(8,128)(2,1)}) %all-gather.33.cloned.1.call-update) | async-done | bytes 4718608 | tf_op jit(solution)/shard_map/all_gather | solution.py:207
  181.3 6.6 copy.265
  192.0 14.7 while.64
  206.8 40.3 %all-gather.35.cloned.1.call-done = bf16[1,1536,1536]{2,1,0:T(8,128)(2,1)} async-done(((bf16[1,48,1536]{2,1,0:T(8,128)(2,1)}), bf16[1,1536,1536]{2,1,0:T(8,128)(2,1)}) %all-gather.35.cloned.1.call-update) | async-done | bytes 4718608 | tf_op jit(solution)/shard_map/all_gather | solution.py:209
  251.6 6.2 gather_fusion
  257.8 4.8 all-to-all-start
  264.6 29.2 %all-gather.37.cloned.1.call-done = bf16[1,2,1536,1024]{3,2,1,0:T(8,128)(2,1)} async-done(((bf16[1,2,384,1024]{3,2,1,0:T(8,128)(2,1)}), bf16[1,2,1536,1024]{3,2,1,0:T(8,128)(2,1)}) %all-gather.37.cloned.1.call-update) | async-done | bytes 6291472 | tf_op jit(solution)/shard_map/all_gather | solution.py:214
  293.8 76.0 %all-to-all-done = bf16[8,2,96,1536]{3,2,1,0:T(8,128)(2,1)} async-done(((bf16[8,2,96,1536]{3,2,1,0:T(8,128)(2,1)}), bf16[8,2,96,1536]{3,2,1,0:T(8,128)(2,1)}, u32[]{:S(2)}, u32[]{:S(2)}) %all-to-all-start) | async-done | bytes 4718624 | tf_op jit(solution)/shard_map/all_to_all | solution.py:263
  369.8 8.5 fusion.119
  382.2 5.2 convert_bitcast_fusion.3
  390.0 4.8 all-to-all-start.1
  396.3 174.3 %all-gather.4 = bf16[1,1536,16]{2,0,1:T(2,128)(2,1)S(1)} all-gather(bf16[1,48,16]{2,0,1:T(2,128)(2,1)S(1)} %copy.354), channel_id=6, replica_groups=mesh['ctx'=4,'fsdp'=8] {'ctx','fsdp'}, dimensions={1}, use_global_device_ids=true | all-gather | bytes 50688 | tf_op jit(solution)/shard_map/all_gather | solution.py:210
  571.9 68.3 %all-gather.7 = bf16[1,1536,2]{2,0,1:T(2,128)(2,1)S(1)} all-gather(bf16[1,48,2]{2,0,1:T(2,128)(2,1)S(1)} %copy.355), channel_id=9, replica_groups=mesh['ctx'=4,'fsdp'=8] {'ctx','fsdp'}, dimensions={1}, use_global_device_ids=true | all-gather | bytes 6336 | tf_op jit(solution)/shard_map/all_gather | solution.py:211
  643.6 9.6 gather_fusion.1
  662.2 4.3 scatter_custom_fusion.1
  672.1 4.9 all-gather.29.cloned.1.call-done
  679.9 35.6 %while.65 = (s32[]{:T(128)}, f32[8,3,128]{2,1,0:T(4,128)}, f32[8,3,128]{2,1,0:T(4,128)}, f32[8,3,128,64]{2,3,1,0:T(8,128)S(1)}, s32[4]{0:T(128)}, /*index=5*/bf1...) while((s32[]{:T(128)}, f32[8,3,128]{2,1,0:T(4,128)}, ...), condition=%wide.region_18.19_spmd.clone, body=%wide.region_15.18_spmd.clone.sunk | while | flops 104830976 | bytes 8259741 | solution.py:114
  716.3 27.2 %all-gather.45.cloned.1.call-done = bf16[1,1536,1536]{2,1,0:T(8,128)(2,1)} async-done(((bf16[1,48,1536]{2,1,0:T(8,128)(2,1)}), bf16[1,1536,1536]{2,1,0:T(8,128)(2,1)}) %all-gather.45.cloned.1.call-update) | async-done | bytes 4718608 | tf_op jit(solution)/shard_map/all_gather | solution.py:209
  747.9 6.2 gather_fusion.2
  754.1 4.8 all-to-all-start.2
  759.7 164.2 %all-gather.11 = bf16[1,1536,16]{2,0,1:T(2,128)(2,1)S(1)} all-gather(bf16[1,48,16]{2,0,1:T(2,128)(2,1)S(1)} %copy.356), channel_id=13, replica_groups=mesh['ctx'=4,'fsdp'=8] {'ctx','fsdp'}, dimensions={1}, use_global_device_ids=true | all-gather | bytes 50688 | tf_op jit(solution)/shard_map/all_gather | solution.py:210
  926.0 6.3 gather_fusion.4
  932.2 4.6 all-to-all-start.4
  937.5 10.2 fusion.114
  947.7 21.3 all-gather.49.cloned.1.call-done
  969.0 69.2 %all-to-all-done.4 = bf16[8,2,96,1536]{3,2,1,0:T(8,128)(2,1)} async-done(((bf16[8,2,96,1536]{3,2,1,0:T(8,128)(2,1)}), bf16[8,2,96,1536]{3,2,1,0:T(8,128)(2,1)}, u32[]{:S(2)}, u32[]{:S(2)}) %all-to-all-start.4) | async-done | bytes 4718624 | tf_op jit(solution)/shard_map/all_to_all | solution.py:358
  1038.2 10.6 fusion.99
  1054.0 4.9 all-to-all-start.3
  1058.9 8.1 convert_bitcast_fusion.1
  1069.5 93.1 %all-to-all-done.3 = bf16[8,2,96,1536]{3,2,1,0:T(8,128)(2,1)} async-done(((bf16[8,2,96,1536]{3,2,1,0:T(8,128)(2,1)}), bf16[8,2,96,1536]{3,2,1,0:T(8,128)(2,1)}, u32[]{:S(2)}, u32[]{:S(2)}) %all-to-all-start.3) | async-done | bytes 4718624 | tf_op jit(solution)/shard_map/all_to_all | solution.py:271
  1162.6 4.6 all-to-all-start.5
  1167.8 10.3 gather_fusion.3
  1182.1 88.8 %all-to-all-done.5 = bf16[8,2,96,1536]{3,2,1,0:T(8,128)(2,1)} async-done(((bf16[8,2,96,1536]{3,2,1,0:T(8,128)(2,1)}), bf16[8,2,96,1536]{3,2,1,0:T(8,128)(2,1)}, u32[]{:S(2)}, u32[]{:S(2)}) %all-to-all-start.5) | async-done | bytes 4718624 | tf_op jit(solution)/shard_map/all_to_all | solution.py:377
  1271.0 10.2 gather_fusion.5
  1293.7 22.6 while.66
  1321.5 18.0 reduce-scatter.14.cloned.1.call-done
  1346.0 6.2 gather_fusion.6
  1352.2 110.2 %all_to_all.40 = bf16[8,2,96,1536]{3,2,1,0:T(8,128)(2,1)S(1)} all-to-all(bf16[8,2,96,1536]{3,2,1,0:T(8,128)(2,1)} %bitcast.635), channel_id=1, replica_groups=mesh['ctx'=4,'fsdp'=8] {'fsdp'}, dimensions={0} | all-to-all | bytes 9437184 | tf_op jit(solution)/shard_map/all_to_all | solution.py:358
  1462.4 7.4 fusion.92
  1469.9 5.3 convert_bitcast_fusion
  1477.7 4.9 all-to-all-start.7
  1484.7 101.4 %all-to-all-done.7 = bf16[8,2,96,1536]{3,2,1,0:T(8,128)(2,1)} async-done(((bf16[8,2,96,1536]{3,2,1,0:T(8,128)(2,1)}), bf16[8,2,96,1536]{3,2,1,0:T(8,128)(2,1)}, u32[]{:S(2)}, u32[]{:S(2)}) %all-to-all-start.7) | async-done | bytes 4718624 | tf_op jit(solution)/shard_map/all_to_all | solution.py:377
  1586.1 9.8 gather_fusion.7
  1605.8 22.2 while.67
  1628.1 7.2 fusion.87
  1639.3 7.1 fusion.84
  1648.0 5.1 fusion.68
  1666.2 6.0 pad_maximum_fusion.4
  1672.6 8.2 fusion.77
  1680.8 7.8 fusion.76
  1688.6 5.3 pad_maximum_fusion.3
  1702.4 12.0 pad_maximum_fusion.2
  1718.4 6.8 pad_maximum_fusion.1
  1729.1 6.7 pad_maximum_fusion
  1735.9 15.8 reduce-scatter.28.cloned.1.call-done
  1754.4 96.8 %reduce-scatter.30.cloned.1.call-done = f32[48,4]{1,0:T(8,128)} async-done(((f32[1536,4]{1,0:T(8,128)}), f32[48,4]{1,0:T(8,128)}) %reduce-scatter.30.cloned.1.call-update) | async-done | bytes 784
  1852.7 58.4 %reduce-scatter.26.cloned.1.call-done = bf16[2,2,128,1536]{3,2,1,0:T(8,128)(2,1)} async-done(((bf16[2,2,512,1536]{3,2,1,0:T(8,128)(2,1)}), bf16[2,2,128,1536]{3,2,1,0:T(8,128)(2,1)}) %reduce-scatter.26.cloned.1.call-update) | async-done | bytes 1572880 | tf_op jit(solution)/shard_map/reduce_scatter | solution.py:471
  1914.5 98.2 %reduce-scatter.24.cloned.1.call-done = bf16[2,2,384,1024]{3,2,1,0:T(8,128)(2,1)} async-done(((bf16[2,2,1536,1024]{3,2,1,0:T(8,128)(2,1)}), bf16[2,2,384,1024]{3,2,1,0:T(8,128)(2,1)}) %reduce-scatter.24.cloned.1.call-update) | async-done | bytes 3145744 | tf_op jit(solution)/shard_map/reduce_scatter | solution.py:468
  2012.7 5.3 convert_element_type.292
  2018.1 157.7 %reduce-scatter.20.cloned.1.call-done = f32[2,48,1024]{2,1,0:T(8,128)} async-done(((f32[2,1536,1024]{2,1,0:T(8,128)}), f32[2,48,1024]{2,1,0:T(8,128)}) %reduce-scatter.20.cloned.1.call-update) | async-done | bytes 393232 | tf_op jit(solution)/shard_map/reduce_scatter | solution.py:462
  2175.7 211.1 %reduce-scatter.22.cloned.1.call-done = f32[2,48,1536]{2,1,0:T(8,128)} async-done(((f32[2,1536,1536]{2,1,0:T(8,128)}), f32[2,48,1536]{2,1,0:T(8,128)}) %reduce-scatter.22.cloned.1.call-update) | async-done | bytes 589840 | tf_op jit(solution)/shard_map/reduce_scatter | solution.py:463
  2386.8 210.9 %reduce-scatter.18.cloned.1.call-done = f32[2,48,1536]{2,1,0:T(8,128)} async-done(((f32[2,1536,1536]{2,1,0:T(8,128)}), f32[2,48,1536]{2,1,0:T(8,128)}) %reduce-scatter.18.cloned.1.call-update) | async-done | bytes 589840 | tf_op jit(solution)/shard_map/reduce_scatter | solution.py:461
  (714 shorter events, 254.7 us)
Async XLA Ops:
  7.2 79.0 %copy-start.8 = (bf16[1,128,1536]{2,1,0:T(8,128)(2,1)S(1)}, bf16[1,128,1536]{2,1,0:T(8,128)(2,1)}, u32[]{:S(2)}) copy-start(bf16[1,128,1536]{2,1,0:T(8,128)(2,1)} %param.18) | copy-start | bytes 1179652
  7.2 81.6 %all-gather.31.cloned.1.call-start = ((), (), s32[]{:S(2)}) async-start(), calls=%async_computation.26 | async-start | bytes 3244032 | tf_op jit(solution)/shard_map/all_gather | solution.py:208
  8.9 105.2 %all-gather.27.cloned.1.call-start = ((), (), s32[]{:S(2)}) async-start(), calls=%async_computation.17 | async-start | bytes 1310720 | tf_op jit(solution)/shard_map/all_gather | solution.py:241
  88.8 583.2 %copy-start.58 = (f32[128,32]{0,1:T(8,128)}, f32[128,32]{0,1:T(8,128)S(1)}, u32[]{:S(2)}) copy-start(f32[128,32]{0,1:T(8,128)S(1)} %get-tuple-element.1004) | copy-start | bytes 49156
  99.6 81.7 %all-gather.33.cloned.1.call-start = ((), (), s32[]{:S(2)}) async-start(), calls=%async_computation.27 | async-start | bytes 4866048 | tf_op jit(solution)/shard_map/all_gather | solution.py:207
  101.4 145.8 %all-gather.35.cloned.1.call-start = ((), (), s32[]{:S(2)}) async-start(), calls=%async_computation.28 | async-start | bytes 4866048 | tf_op jit(solution)/shard_map/all_gather | solution.py:209
  103.2 190.6 %all-gather.37.cloned.1.call-start = ((), (), s32[]{:S(2)}) async-start(), calls=%async_computation.29 | async-start | bytes 7864320 | tf_op jit(solution)/shard_map/all_gather | solution.py:214
  106.6 74.7 %copy-start.86 = (s32[128,8]{0,1:T(8,128)}, s32[128,8]{0,1:T(8,128)S(1)}, u32[]{:S(2)}) copy-start(s32[128,8]{0,1:T(8,128)S(1)} %get-tuple-element.1001) | copy-start | bytes 12292
  106.6 74.7 %copy-start.89 = (s32[128,8]{0,1:T(8,128)}, s32[128,8]{0,1:T(8,128)S(1)}, u32[]{:S(2)}) copy-start(s32[128,8]{0,1:T(8,128)S(1)} %get-tuple-element.998) | copy-start | bytes 12292
  108.0 80.0 %copy-start.93 = (s32[128,8]{0,1:T(8,128)}, s32[128,8]{0,1:T(8,128)S(1)}, u32[]{:S(2)}) copy-start(s32[128,8]{0,1:T(8,128)S(1)} %get-tuple-element.1024) | copy-start | bytes 12292
  206.7 43.8 %copy-start = (bf16[128,8,3,64]{0,3,2,1:T(8,128)(2,1)}, bf16[128,8,3,64]{0,3,2,1:T(8,128)(2,1)S(1)}, u32[]{:S(2)}) copy-start(bf16[128,8,3,64]{0,3,2,1:T(8,128)(2,1)S(1)} %get-tuple-element.1466) | copy-start | bytes 1179652
  206.7 43.7 %copy-start.4 = (f32[8,3,128,64]{2,3,1,0:T(8,128)}, f32[8,3,128,64]{2,3,1,0:T(8,128)S(1)}, u32[]{:S(2)}) copy-start(f32[8,3,128,64]{2,3,1,0:T(8,128)S(1)} %get-tuple-element.483) | copy-start | bytes 2359300
  206.7 43.7 %copy-start.51 = (f32[8,3,128]{2,1,0:T(4,128)}, f32[8,3,128]{2,1,0:T(4,128)S(1)}, u32[]{:S(2)}) copy-start(f32[8,3,128]{2,1,0:T(4,128)S(1)} %get-tuple-element.487) | copy-start | bytes 36868
  206.7 43.7 %copy-start.66 = (f32[8,3,128]{2,1,0:T(4,128)}, f32[8,3,128]{2,1,0:T(4,128)S(1)}, u32[]{:S(2)}) copy-start(f32[8,3,128]{2,1,0:T(4,128)S(1)} %get-tuple-element.484) | copy-start | bytes 36868
  206.8 43.6 %copy-start.41 = (bf16[128,8,3,64]{0,3,2,1:T(8,128)(2,1)}, bf16[128,8,3,64]{0,3,2,1:T(8,128)(2,1)S(1)}, u32[]{:S(2)}) copy-start(bf16[128,8,3,64]{0,3,2,1:T(8,128)(2,1)S(1)} %bitcast_convert_fusion.5) | copy-start | bytes 1179652
  251.5 390.6 %copy-start.33 = (bf16[128,1536]{1,0:T(8,128)(2,1)}, bf16[128,1536]{1,0:T(8,128)(2,1)S(1)}, u32[]{:S(2)}) copy-start(bf16[128,1536]{1,0:T(8,128)(2,1)S(1)} %multiply_convert_fusion.4) | copy-start | bytes 1179652
  257.8 112.1 %all-to-all-start = ((bf16[8,2,96,1536]{3,2,1,0:T(8,128)(2,1)}), bf16[8,2,96,1536]{3,2,1,0:T(8,128)(2,1)}, u32[]{:S(2)}, u32[]{:S(2)}) async-start(bf16[8,2,96,1536]{3,2,1,0:T(8,128)(2,1)} %bitcast.633), calls=%async_computation | async-start | bytes 9437184 | tf_op jit(solution)/shard_map/all_to_all | solution.py:263
  262.5 119.7 %all-gather.39.cloned.1.call-start = ((), (), s32[]{:S(2)}) async-start(), calls=%async_computation.30 | async-start | bytes 3932160 | tf_op jit(solution)/shard_map/all_gather | solution.py:215
  263.9 393.5 %all-gather.41.cloned.1.call-start = ((), (), s32[]{:S(2)}) async-start(), calls=%async_computation.31 | async-start | bytes 3244032 | tf_op jit(solution)/shard_map/all_gather | solution.py:208
  390.0 181.0 %copy-start.92 = (s32[128,8]{0,1:T(8,128)S(1)}, s32[128,8]{0,1:T(8,128)}, u32[]{:S(2)}) copy-start(s32[128,8]{0,1:T(8,128)} %get-tuple-element.1023) | copy-start | bytes 12292
  390.0 181.0 %copy-start.94 = (s32[128,8]{0,1:T(8,128)S(1)}, s32[128,8]{0,1:T(8,128)}, u32[]{:S(2)}) copy-start(s32[128,8]{0,1:T(8,128)} %copy-done.93) | copy-start | bytes 12292
  390.0 181.0 %copy-start.97 = (s32[2,1,128,8]{2,3,1,0:T(8,128)S(1)}, s32[2,1,128,8]{2,3,1,0:T(8,128)}, u32[]{:S(2)}) copy-start(s32[2,1,128,8]{2,3,1,0:T(8,128)} %param.26) | copy-start | bytes 24580
  390.0 181.8 %copy-start.116 = (bf16[1,48,2]{1,2,0:T(2,128)(2,1)S(1)}, bf16[1,48,2]{1,2,0:T(2,128)(2,1)}, u32[]{:S(2)}) copy-start(bf16[1,48,2]{1,2,0:T(2,128)(2,1)} %get-tuple-element.1005) | copy-start | bytes 580
  390.0 253.6 %all-to-all-start.1 = ((bf16[8,2,96,1536]{3,2,1,0:T(8,128)(2,1)}), bf16[8,2,96,1536]{3,2,1,0:T(8,128)(2,1)}, u32[]{:S(2)}, u32[]{:S(2)}) async-start(bf16[8,2,96,1536]{3,2,1,0:T(8,128)(2,1)} %copy.276), calls=%async_computation.1 | async-start | bytes 9437184 | tf_op jit(solution)/shard_map/all_to_all | solution.py:271
  394.8 272.9 %all-gather.43.cloned.1.call-start = ((), (), s32[]{:S(2)}) async-start(), calls=%async_computation.32 | async-start | bytes 4866048 | tf_op jit(solution)/shard_map/all_gather | solution.py:207
  395.5 281.5 %all-gather.29.cloned.1.call-start = ((), (), s32[]{:S(2)}) async-start(), calls=%async_computation.18 | async-start | bytes 1310720 | tf_op jit(solution)/shard_map/all_gather | solution.py:241
  396.2 246.1 %copy-start.87 = (s32[128,8]{0,1:T(8,128)S(1)}, s32[128,8]{0,1:T(8,128)}, u32[]{:S(2)}) copy-start(s32[128,8]{0,1:T(8,128)} %copy-done.86) | copy-start | bytes 12292
  570.9 71.5 %copy-start.74 = (bf16[1,1536,16]{1,2,0:T(8,128)(2,1)}, bf16[1,1536,16]{1,2,0:T(8,128)(2,1)S(1)}, u32[]{:S(2)}) copy-start(bf16[1,1536,16]{1,2,0:T(8,128)(2,1)S(1)} %copy.268) | copy-start | bytes 147460
  661.1 82.4 %all-gather.45.cloned.1.call-start = ((), (), s32[]{:S(2)}) async-start(), calls=%async_computation.33 | async-start | bytes 4866048 | tf_op jit(solution)/shard_map/all_gather | solution.py:209
  679.9 63.6 %copy-start.17 = (f32[128,1536]{1,0:T(8,128)S(1)}, f32[128,1536]{1,0:T(8,128)}, u32[]{:S(2)}) copy-start(f32[128,1536]{1,0:T(8,128)} %copy-done.16) | copy-start | bytes 2359300
  715.5 31.3 %copy-start.2 = (bf16[128,8,3,64]{0,3,2,1:T(8,128)(2,1)}, bf16[128,8,3,64]{0,3,2,1:T(8,128)(2,1)S(1)}, u32[]{:S(2)}) copy-start(bf16[128,8,3,64]{0,3,2,1:T(8,128)(2,1)S(1)} %get-tuple-element.1467) | copy-start | bytes 1179652
  715.5 31.3 %copy-start.6 = (f32[8,3,128,64]{2,3,1,0:T(8,128)}, f32[8,3,128,64]{2,3,1,0:T(8,128)S(1)}, u32[]{:S(2)}) copy-start(f32[8,3,128,64]{2,3,1,0:T(8,128)S(1)} %get-tuple-element.485) | copy-start | bytes 2359300
  716.3 30.5 %copy-start.43 = (bf16[128,8,3,64]{0,3,2,1:T(8,128)(2,1)}, bf16[128,8,3,64]{0,3,2,1:T(8,128)(2,1)S(1)}, u32[]{:S(2)}) copy-start(bf16[128,8,3,64]{0,3,2,1:T(8,128)(2,1)S(1)} %bitcast_convert_fusion.4) | copy-start | bytes 1179652
  747.8 176.6 %copy-start.35 = (bf16[128,1536]{1,0:T(8,128)(2,1)}, bf16[128,1536]{1,0:T(8,128)(2,1)S(1)}, u32[]{:S(2)}) copy-start(bf16[128,1536]{1,0:T(8,128)(2,1)S(1)} %multiply_convert_fusion.2) | copy-start | bytes 1179652
  754.1 178.2 %all-to-all-start.2 = ((bf16[8,2,96,1536]{3,2,1,0:T(8,128)(2,1)}), bf16[8,2,96,1536]{3,2,1,0:T(8,128)(2,1)}, u32[]{:S(2)}, u32[]{:S(2)}) async-start(bf16[8,2,96,1536]{3,2,1,0:T(8,128)(2,1)} %bitcast.632), calls=%async_computation.2 | async-start | bytes 9437184 | tf_op jit(solution)/shard_map/all_to_all | solution.py:263
  758.9 165.5 %copy-start.99 = (s32[1536]{0:T(1024)S(1)}, s32[1536]{0:T(1024)}, u32[]{:S(2)}) copy-start(s32[1536]{0:T(1024)} %get-tuple-element.992) | copy-start | bytes 18436
  758.9 165.5 %copy-start.55 = (bf16[1,128,1536]{2,1,0:T(8,128)(2,1)S(1)}, bf16[1,128,1536]{2,1,0:T(8,128)(2,1)}, u32[]{:S(2)}) copy-start(bf16[1,128,1536]{2,1,0:T(8,128)(2,1)} %param.27) | copy-start | bytes 1179652
  758.9 165.8 %copy-start.90 = (s32[128,8]{0,1:T(8,128)S(1)}, s32[128,8]{0,1:T(8,128)}, u32[]{:S(2)}) copy-start(s32[128,8]{0,1:T(8,128)} %copy-done.89) | copy-start | bytes 12292
  758.9 178.6 %all-gather.47.cloned.1.call-start = ((), (), s32[]{:S(2)}) async-start(), calls=%async_computation.34 | async-start | bytes 7864320 | tf_op jit(solution)/shard_map/all_gather | solution.py:214
  932.2 106.0 %all-to-all-start.4 = ((bf16[8,2,96,1536]{3,2,1,0:T(8,128)(2,1)}), bf16[8,2,96,1536]{3,2,1,0:T(8,128)(2,1)}, u32[]{:S(2)}, u32[]{:S(2)}) async-start(bf16[8,2,96,1536]{3,2,1,0:T(8,128)(2,1)} %bitcast.634), calls=%async_computation.4 | async-start | bytes 9437184 | tf_op jit(solution)/shard_map/all_to_all | solution.py:358
  936.9 32.1 %all-gather.49.cloned.1.call-start = ((), (), s32[]{:S(2)}) async-start(), calls=%async_computation.35 | async-start | bytes 3932160 | tf_op jit(solution)/shard_map/all_gather | solution.py:215
  969.0 79.8 %copy-start.121 = (bf16[1,2,512,1536]{3,2,1,0:T(8,128)(2,1)S(1)}, bf16[1,2,512,1536]{3,2,1,0:T(8,128)(2,1)}, u32[]{:S(2)}) copy-start(bf16[1,2,512,1536]{3,2,1,0:T(8,128)(2,1)} %all-gather.49.cloned.1.call-done) | copy-start | bytes 9437188
  1054.0 108.6 %all-to-all-start.3 = ((bf16[8,2,96,1536]{3,2,1,0:T(8,128)(2,1)}), bf16[8,2,96,1536]{3,2,1,0:T(8,128)(2,1)}, u32[]{:S(2)}, u32[]{:S(2)}) async-start(bf16[8,2,96,1536]{3,2,1,0:T(8,128)(2,1)} %copy.292), calls=%async_computation.3 | async-start | bytes 9437184 | tf_op jit(solution)/shard_map/all_to_all | solution.py:271
  1069.5 98.0 %copy-start.104 = (s32[128,8,1]{0,1,2:T(8,128)S(1)}, s32[128,8,1]{0,1,2:T(8,128)}, u32[]{:S(2)}) copy-start(s32[128,8,1]{0,1,2:T(8,128)} %get-tuple-element.996) | copy-start | bytes 12292
  1069.5 98.2 %copy-start.53 = (f32[8,3,128]{2,1,0:T(4,128)S(1)}, f32[8,3,128]{2,1,0:T(4,128)}, u32[]{:S(2)}) copy-start(f32[8,3,128]{2,1,0:T(4,128)} %get-tuple-element.488) | copy-start | bytes 36868
  1069.5 98.2 %copy-start.68 = (f32[8,3,128]{2,1,0:T(4,128)S(1)}, f32[8,3,128]{2,1,0:T(4,128)}, u32[]{:S(2)}) copy-start(f32[8,3,128]{2,1,0:T(4,128)} %get-tuple-element.486) | copy-start | bytes 36868
  1162.6 108.3 %all-to-all-start.5 = ((bf16[8,2,96,1536]{3,2,1,0:T(8,128)(2,1)}), bf16[8,2,96,1536]{3,2,1,0:T(8,128)(2,1)}, u32[]{:S(2)}, u32[]{:S(2)}) async-start(bf16[8,2,96,1536]{3,2,1,0:T(8,128)(2,1)} %copy.297), calls=%async_computation.5 | async-start | bytes 9437184 | tf_op jit(solution)/shard_map/all_to_all | solution.py:377
  1167.2 172.3 %reduce-scatter.14.cloned.1.call-start = ((), (), s32[]{:S(2)}) async-start(), calls=%async_computation.19 | async-start | bytes 1310720 | tf_op jit(solution)/shard_map/reduce_scatter | solution.py:414
  1293.7 22.8 copy-start.76
  1317.4 23.5 copy-start.18
  1317.4 23.5 copy-start.84
  1317.4 23.5 copy-start.115
  1352.2 110.2 %copy-start.120 = (bf16[1,2,512,1536]{3,2,1,0:T(8,128)(2,1)S(1)}, bf16[1,2,512,1536]{3,2,1,0:T(8,128)(2,1)}, u32[]{:S(2)}) copy-start(bf16[1,2,512,1536]{3,2,1,0:T(8,128)(2,1)} %all-gather.39.cloned.1.call-done) | copy-start | bytes 9437188
  1352.2 117.7 %slice-start = ((s8[6291456]{0:T(1024)(128)(4,1)}), s8[4194304]{0:T(1024)(128)(4,1)S(1)}, s32[]{:S(2)}) async-start(s8[6291456]{0:T(1024)(128)(4,1)} %bitcast.685), calls=%async_computation.38 | async-start | bytes 8388608
  1477.7 108.4 %all-to-all-start.7 = ((bf16[8,2,96,1536]{3,2,1,0:T(8,128)(2,1)}), bf16[8,2,96,1536]{3,2,1,0:T(8,128)(2,1)}, u32[]{:S(2)}, u32[]{:S(2)}) async-start(bf16[8,2,96,1536]{3,2,1,0:T(8,128)(2,1)} %copy.306), calls=%async_computation.8 | async-start | bytes 9437184 | tf_op jit(solution)/shard_map/all_to_all | solution.py:377
  1482.6 103.5 %copy-start.40 = (s32[1024]{0:T(1024)S(1)}, s32[1024]{0:T(1024)}, u32[]{:S(2)}) copy-start(s32[1024]{0:T(1024)} %copy-done.39) | copy-start | bytes 12292
  1482.6 170.4 %reduce-scatter.16.cloned.1.call-start = ((), (), s32[]{:S(2)}) async-start(), calls=%async_computation.20 | async-start | bytes 1310720 | tf_op jit(solution)/shard_map/reduce_scatter | solution.py:414
  1628.0 123.6 %reduce-scatter.28.cloned.1.call-start = ((), (), s32[]{:S(2)}) async-start(), calls=%async_computation.36 | async-start | bytes 811008
  1639.1 212.1 %reduce-scatter.30.cloned.1.call-start = ((), (), s32[]{:S(2)}) async-start(), calls=%async_computation.37 | async-start | bytes 811008
  1666.1 244.9 %reduce-scatter.26.cloned.1.call-start = ((), (), s32[]{:S(2)}) async-start(), calls=%async_computation.25 | async-start | bytes 7864320 | tf_op jit(solution)/shard_map/reduce_scatter | solution.py:471
  1672.3 340.4 %reduce-scatter.24.cloned.1.call-start = ((), (), s32[]{:S(2)}) async-start(), calls=%async_computation.24 | async-start | bytes 15728640 | tf_op jit(solution)/shard_map/reduce_scatter | solution.py:468
  1694.0 481.8 %reduce-scatter.20.cloned.1.call-start = ((), (), s32[]{:S(2)}) async-start(), calls=%async_computation.22 | async-start | bytes 12976128 | tf_op jit(solution)/shard_map/reduce_scatter | solution.py:462
  1714.5 672.3 %reduce-scatter.22.cloned.1.call-start = ((), (), s32[]{:S(2)}) async-start(), calls=%async_computation.23 | async-start | bytes 19464192 | tf_op jit(solution)/shard_map/reduce_scatter | solution.py:463
  1725.2 872.4 %reduce-scatter.18.cloned.1.call-start = ((), (), s32[]{:S(2)}) async-start(), calls=%async_computation.21 | async-start | bytes 19464192 | tf_op jit(solution)/shard_map/reduce_scatter | solution.py:461
  (95 other events, 487.1 us)
Sparse Core Ops, SparseCore 0:
  11.5 63.2 all-gather.30
  99.7 14.3 all-gather.26
  117.6 63.6 all-gather.32
  184.7 62.4 all-gather.34
  248.6 45.1 all-gather.36
  295.2 28.5 all-gather.38
  326.7 108.6 all-gather.40
  438.9 116.4 all-gather.42
  661.2 15.7 all-gather.28
  679.8 63.6 all-gather.44
  761.9 47.6 all-gather.46
  939.0 29.9 all-gather.48
  1316.4 23.0 reduce-scatter.13
  1628.1 22.9 reduce-scatter.15
  1656.1 95.5 reduce-scatter.27
  1756.6 94.5 reduce-scatter.29
  1853.6 57.4 reduce-scatter.25
  1913.6 99.0 reduce-scatter.23
  2020.4 155.3 reduce-scatter.19
  2182.6 204.1 reduce-scatter.21
  2393.8 203.8 reduce-scatter.17
where the time goes:
time: 2620 us; the launch traced here: 2610 us
  waiting for transfers between devices  1490 us (57%)
  blocking collectives  592 us (23%)
  local copies, waits for them, and re-layouts  184 us (7%)
  matrix products  179 us (7%)
  other arithmetic  99 us (4%)
  starting transfers between devices  35.9 us (1%)
    all_gather x2, blocking collectives, on_device(): lax.all_gather(w_router[layer_index], ('ctx', 'fsdp'), axis=0, tiled=True)  338 us
    reduce_scatter x1, waiting for transfers between devices, on_device(): lax.psum_scatter(stacked_output, ('ctx', 'fsdp'), scatter_dimension=1, ti...  211 us
    reduce_scatter x1, waiting for transfers between devices, on_device(): lax.psum_scatter(stacked_query, ('ctx', 'fsdp'), scatter_dimension=1, til...  211 us
    all_to_all x2, waiting for transfers between devices, on_device(): lax.all_to_all(grad_entering, 'fsdp', split_axis=0, concat_axis=0, tiled=...  190 us
    reduce_scatter x1, waiting for transfers between devices, on_device(): lax.psum_scatter(stacked_key_value, ('ctx', 'fsdp'), scatter_dimension=1,...  158 us
    all_gather x2, blocking collectives, on_device(): lax.all_gather(norm_gains[layer_index], ('ctx', 'fsdp'), axis=0, tiled=True)  143 us
    unnamed x23, waiting for transfers between devices  115 us
    all_to_all x1, blocking collectives, on_device(): lax.all_to_all(grad_send, 'fsdp', split_axis=0, concat_axis=0, tiled=True)  110 us
  transfers between devices with their start and end apart: 28, of which 20 were waited for; matrix products, arithmetic and copies ran while one was open for 12% of the time, Pallas kernels for 0%

commit v1 on v0

--- a/solution.py
+++ b/solution.py
@@ -486,9 +486,372 @@
     )
 
 
+def rotate_ranks(values_in, axis_name, total, target_of):
+    return lax.ppermute(values_in, axis_name, [(i, target_of(i)) for i in range(total)])
+
+
+def swap_y(values_in):
+    return rotate_ranks(values_in, "fsdp", 8, lambda i: i ^ 1)
+
+
+def move_z(values_in, steps):
+    return rotate_ranks(values_in, "fsdp", 8, lambda i: (i + 2 * steps) % 8)
+
+
+def swap_core(values_in):
+    return rotate_ranks(values_in, "ctx", 4, lambda i: i ^ 1)
+
+
+def swap_x(values_in):
+    return rotate_ranks(values_in, "ctx", 4, lambda i: i ^ 2)
+
+
+def fsdp_members(index):
+    z, y = index // 2, index % 2
+    return [((z + dz) % 4) * 2 + (y ^ dy) for dz in (0, 1, 2, 3) for dy in (0, 1)]
+
+
+def gather_fsdp(block):
+    half = block.shape[0] // 2
+    below = move_z(block, 1)
+    above = move_z(block, -1)
+    own_mirror = swap_y(block)
+    below_mirror = swap_y(below)
+    far_first = move_z(below[:half], 1)
+    above_mirror = swap_y(above)
+    far_second = move_z(above[half:], -1)
+    far = jnp.concatenate([far_first, far_second], 0)
+    far_mirror = swap_y(far)
+    return [block, own_mirror, above, above_mirror, far, far_mirror, below, below_mirror]
+
+
+def scatter_fsdp(parts):
+    def fold(kept, sent):
+        return kept.astype(jnp.float32) + swap_y(sent).astype(jnp.float32)
+
+    half = parts[0].shape[0] // 2
+    far = fold(parts[4], parts[5]).astype(jnp.bfloat16)
+    above = fold(parts[2], parts[3])
+    below = fold(parts[6], parts[7])
+    own = fold(parts[0], parts[1])
+    first = move_z(far[:half], 1).astype(jnp.float32)
+    second = move_z(far[half:], -1).astype(jnp.float32)
+    above = jnp.concatenate([above[:half] + first, above[half:]], 0)
+    below = jnp.concatenate([below[:half], below[half:] + second], 0)
+    from_below = move_z(above.astype(jnp.bfloat16), 1).astype(jnp.float32)
+    from_above = move_z(below.astype(jnp.bfloat16), -1).astype(jnp.float32)
+    return own + from_below + from_above
+
+
+def gather_ctx(block):
+    across = swap_x(block)
+    return [block, swap_core(block), across, swap_core(across)]
+
+
+def scatter_ctx(parts):
+    across = parts[2].astype(jnp.float32) + swap_core(parts[3]).astype(jnp.float32)
+    own = parts[0].astype(jnp.float32) + swap_core(parts[1]).astype(jnp.float32)
+    return own + swap_x(across.astype(jnp.bfloat16)).astype(jnp.float32)
+
+
+def split_ranks(
+    hidden_in,
+    w_query,
+    w_key_value,
+    w_output,
+    w_router,
+    norm_gains,
+    w_gate_up,
+    w_down,
+    expert_ids,
+    out_grad,
+):
+    both = ("ctx", "fsdp")
+    ctx_total, groups = 4, 8
+    ctx_index, group_index = lax.axis_index("ctx"), lax.axis_index("fsdp")
+    row_count, model_width = hidden_in.shape[1], hidden_in.shape[2]
+    layer_total, share, _ = w_query.shape
+    experts_here = w_gate_up.shape[1]
+    expert_total = experts_here * groups
+    kv_width = w_key_value.shape[2] // 2
+    q_part, kv_part = model_width // ctx_total, kv_width // ctx_total
+    kv_here, group_size = KV_HEADS // ctx_total, HEADS // KV_HEADS
+    seq_rows = ctx_total * row_count
+    low = jnp.bfloat16
+    f32 = jnp.float32
+    score_scale = HEAD_DIM ** (-0.5)
+
+    def dot(a, b):
+        return jnp.dot(a, b, preferred_element_type=f32)
+
+    def dot_t(a, b):
+        return lax.dot_general(a, b, (((1,), (1,)), ((), ())), preferred_element_type=f32)
+
+    def t_dot(a, b):
+        return lax.dot_general(a, b, (((0,), (0,)), ((), ())), preferred_element_type=f32)
+
+    small = jnp.concatenate(
+        [norm_gains[i] for i in range(layer_total)] + [w_router[i] for i in range(layer_total)], -1
+    )
+    small = lax.all_gather(small, both, axis=0, tiled=True)
+    gains = [small[:, 2 * i : 2 * i + 2].astype(f32) for i in range(layer_total)]
+    routers = [
+        small[:, 2 * layer_total + expert_total * i : 2 * layer_total + expert_total * (i + 1)]
+        for i in range(layer_total)
+    ]
+
+    attention_weights = []
+    for i in range(layer_total):
+        blocks = jnp.concatenate(
+            [
+                w_query[i].reshape(share, ctx_total, q_part),
+                w_key_value[i, :, :kv_width].reshape(share, ctx_total, kv_part),
+                w_key_value[i, :, kv_width:].reshape(share, ctx_total, kv_part),
+            ],
+            -1,
+        ).transpose(1, 0, 2)
+        blocks = lax.all_to_all(blocks, "ctx", split_axis=0, concat_axis=0, tiled=True)
+        packed = jnp.concatenate(
+            [blocks, w_output[i].reshape(share, ctx_total, q_part).transpose(1, 0, 2)], -1
+        )
+        gathered = lax.all_gather(packed, "fsdp", axis=0, tiled=False)
+        qkv_weight = (
+            gathered[..., : q_part + 2 * kv_part]
+            .transpose(1, 0, 2, 3)
+            .reshape(model_width, q_part + 2 * kv_part)
+        )
+        out_weight = (
+            gathered[..., q_part + 2 * kv_part :].transpose(0, 2, 1, 3).reshape(q_part, model_width)
+        )
+        attention_weights.append((qkv_weight, out_weight))
+    expert_weights = [
+        (
+            lax.all_gather(w_gate_up[i], "ctx", axis=1, tiled=True),
+            lax.all_gather(w_down[i], "ctx", axis=1, tiled=True),
+        )
+        for i in range(layer_total)
+    ]
+    members = jnp.stack(fsdp_members(group_index))
+    ids_all = lax.all_gather(expert_ids.reshape(layer_total, row_count, TOP), "fsdp", axis=0)
+    ids_all = jnp.take(ids_all, members, axis=0)
+    expert_range = jnp.arange(expert_total, dtype=jnp.int32)
+    own_experts = [
+        (expert_range == group_index * experts_here + j).astype(f32) for j in range(experts_here)
+    ]
+    places = jnp.concatenate(
+        [row_positions((ctx_index ^ r) * row_count, row_count, row_count, ctx_total) for r in range(4)]
+    )
+    visible = (places[:, None] >= places[None, :])[None, None]
+
+    residual = hidden_in.reshape(row_count, model_width).astype(f32)
+    saved = []
+    for i in range(layer_total):
+        qkv_weight, out_weight = attention_weights[i]
+        gate_up_weight, down_weight = expert_weights[i]
+        normed, root_first = rms_scaled(residual, gains[i][:, 0])
+        rows_first = jnp.concatenate(gather_ctx(normed.astype(low)), 0)
+        raw = dot(rows_first, qkv_weight)
+        queries = rotate(
+            raw[:, :q_part].reshape(seq_rows, kv_here * group_size, HEAD_DIM), places, 1.0
+        ).astype(low).reshape(seq_rows, kv_here, group_size, HEAD_DIM)
+        keys = rotate(
+            raw[:, q_part : q_part + kv_part].reshape(seq_rows, kv_here, HEAD_DIM), places, 1.0
+        ).astype(low)
+        values = raw[:, q_part + kv_part :].reshape(seq_rows, kv_here, HEAD_DIM).astype(low)
+        scores = (
+            jnp.einsum("qhgd,khd->hgqk", queries, keys, preferred_element_type=f32) * score_scale
+        )
+        scores = jnp.where(visible, scores, masked_score)
+        top = jnp.max(scores, -1, keepdims=True)
+        weights = jnp.exp(scores - top)
+        total = jnp.sum(weights, -1, keepdims=True)
+        log_total = top + jnp.log(total)
+        probs = weights / total
+        attended = (
+            jnp.einsum("hgqk,khd->qhgd", probs.astype(low), values, preferred_element_type=f32)
+            .astype(low)
+            .reshape(seq_rows, q_part)
+        )
+        branch = dot(attended, out_weight).astype(low).reshape(ctx_total, row_count, model_width)
+        middle = residual + scatter_ctx([branch[r] for r in range(4)])
+        normed_second, root_second = rms_scaled(middle, gains[i][:, 1])
+        rows_second = jnp.concatenate(gather_fsdp(normed_second.astype(low)), 0)
+        logits = dot(rows_second, routers[i])
+        ids = ids_all[:, i].reshape(groups * row_count, TOP)
+        chosen = jnp.any(ids[:, :, None] == expert_range[None, None, :], 1)
+        logits = jnp.where(chosen, logits, masked_score)
+        gate = jnp.exp(logits - jnp.max(logits, -1, keepdims=True))
+        gate = gate / jnp.sum(gate, -1, keepdims=True)
+        gates = [jnp.sum(gate * own, -1, keepdims=True) for own in own_experts]
+        gate_ups, hiddens = [], []
+        for j in range(experts_here):
+            gate_up = dot(rows_second, gate_up_weight[j])
+            hidden = jax.nn.silu(gate_up[:, :FE]) * gate_up[:, FE:]
+            gate_ups.append(gate_up)
+            hiddens.append((gates[j] * hidden).astype(low))
+        partial = sum(dot(hiddens[j], down_weight[j]) for j in range(experts_here)).astype(low)
+        partial = partial.reshape(groups, row_count, model_width)
+        expert_sum = scatter_fsdp([partial[r] for r in range(groups)])
+        saved.append(
+            (
+                residual, root_first, rows_first, queries, keys, values, log_total, attended,
+                middle, root_second, rows_second, gates, gate_ups, hiddens, expert_sum,
+            )
+        )
+        residual = middle + expert_sum
+    hidden_out = residual.reshape(1, row_count, model_width).astype(low)
+    grad = out_grad.reshape(row_count, model_width).astype(f32)
+    attention_grads, expert_grads, small_grads = [], [], []
+    for i in reversed(range(layer_total)):
+        (
+            residual, root_first, rows_first, queries, keys, values, log_total, attended,
+            middle, root_second, rows_second, gates, gate_ups, hiddens, expert_sum,
+        ) = saved[i]
+        qkv_weight, out_weight = attention_weights[i]
+        gate_up_weight, down_weight = expert_weights[i]
+        mean_gate = jnp.sum(grad * expert_sum, -1, keepdims=True)
+        mean_high = mean_gate.astype(low)
+        mean_low = (mean_gate - mean_high.astype(f32)).astype(low)
+        sent = jnp.concatenate(
+            [
+                grad.astype(low),
+                mean_high,
+                mean_low,
+                jnp.zeros((row_count, 126), low),
+            ],
+            -1,
+        )
+        received = jnp.concatenate(gather_fsdp(sent), 0)
+        mean_gates = received[:, model_width : model_width + 1].astype(f32) + received[
+            :, model_width + 1 : model_width + 2
+        ].astype(f32)
+        received = received[:, :model_width]
+        entering = 0.0
+        gate_up_grads, down_grads, logit_grads = [], [], []
+        for j in range(experts_here):
+            plain = dot_t(received, down_weight[j])
+            gate_part, up_part = gate_ups[j][:, :FE], gate_ups[j][:, FE:]
+            sigmoid_gate = jax.nn.sigmoid(gate_part)
+            silu_gate = gate_part * sigmoid_gate
+            grad_gate_prob = jnp.sum(plain * (silu_gate * up_part), -1, keepdims=True)
+            logit_grads.append(gates[j] * (grad_gate_prob - mean_gates))
+            plain = plain * gates[j]
+            grad_rows = jnp.concatenate(
+                [
+                    plain * up_part * sigmoid_gate * (1.0 + gate_part * (1.0 - sigmoid_gate)),
+                    plain * silu_gate,
+                ],
+                -1,
+            ).astype(low)
+            entering = entering + dot_t(grad_rows, gate_up_weight[j])
+            down_grads.append(t_dot(hiddens[j], received).astype(low))
+            gate_up_grads.append(t_dot(rows_second, grad_rows).astype(low))
+        grad_logits = sum(logit_grads[j] * own_experts[j][None, :] for j in range(experts_here))
+        entering = entering + dot_t(grad_logits.astype(low), routers[i])
+        grad_router = t_dot(rows_second, grad_logits.astype(low))
+        expert_grads.insert(
+            0,
+            (
+                lax.psum_scatter(
+                    jnp.stack(gate_up_grads), "ctx", scatter_dimension=1, tiled=True
+                ),
+                lax.psum_scatter(jnp.stack(down_grads), "ctx", scatter_dimension=1, tiled=True),
+            ),
+        )
+        entering = entering.astype(low).reshape(groups, row_count, model_width)
+        grad_second = scatter_fsdp([entering[r] for r in range(groups)])
+        grad_middle, gain_second = rms_back(middle, root_second, gains[i][:, 1], grad_second)
+        grad_middle = grad_middle + grad
+        rows_branch = jnp.concatenate(gather_ctx(grad_middle.astype(low)), 0)
+        grad_attended = (
+            dot_t(rows_branch, out_weight).astype(low).reshape(seq_rows, kv_here, group_size, HEAD_DIM)
+        )
+        out_weight_grad = t_dot(attended, rows_branch).astype(low)
+        scores = (
+            jnp.einsum("qhgd,khd->hgqk", queries, keys, preferred_element_type=f32) * score_scale
+        )
+        probs = jnp.where(visible, jnp.exp(scores - log_total), 0.0)
+        grad_values = jnp.einsum(
+            "hgqk,qhgd->khd", probs.astype(low), grad_attended, preferred_element_type=f32
+        )
+        grad_probs = jnp.einsum("qhgd,khd->hgqk", grad_attended, values, preferred_element_type=f32)
+        grad_scores = (
+            probs * (grad_probs - jnp.sum(probs * grad_probs, -1, keepdims=True))
+        ).astype(low)
+        grad_queries = score_scale * jnp.einsum(
+            "hgqk,khd->qhgd", grad_scores, keys, preferred_element_type=f32
+        )
+        grad_keys = score_scale * jnp.einsum(
+            "hgqk,qhgd->khd", grad_scores, queries, preferred_element_type=f32
+        )
+        grad_qkv = jnp.concatenate(
+            [
+                rotate(
+                    grad_queries.reshape(seq_rows, kv_here * group_size, HEAD_DIM), places, -1.0
+                ).reshape(seq_rows, q_part),
+                rotate(grad_keys, places, -1.0).reshape(seq_rows, kv_part),
+                grad_values.reshape(seq_rows, kv_part),
+            ],
+            -1,
+        ).astype(low)
+        back = dot_t(grad_qkv, qkv_weight).astype(low).reshape(ctx_total, row_count, model_width)
+        grad_first = scatter_ctx([back[r] for r in range(4)])
+        qkv_weight_grad = t_dot(rows_first, grad_qkv).astype(low)
+        grad_input, gain_first = rms_back(residual, root_first, gains[i][:, 0], grad_first)
+        grad = grad_input + grad_middle
+        packed = jnp.concatenate(
+            [
+                qkv_weight_grad.reshape(ctx_total, groups, share, q_part + 2 * kv_part).transpose(
+                    1, 0, 2, 3
+                ),
+                out_weight_grad.reshape(groups, share, ctx_total, q_part).transpose(0, 2, 1, 3),
+            ],
+            -1,
+        )
+        packed = packed.reshape(groups * ctx_total, share, packed.shape[-1])
+        packed = lax.psum_scatter(packed, "fsdp", scatter_dimension=0, tiled=True)
+        query_blocks = lax.all_to_all(
+            packed[..., : q_part + 2 * kv_part], "ctx", split_axis=0, concat_axis=0, tiled=True
+        )
+        query_blocks = query_blocks.transpose(1, 0, 2).astype(f32)
+        attention_grads.insert(
+            0,
+            (
+                query_blocks[..., :q_part].reshape(share, model_width),
+                jnp.concatenate(
+                    [
+                        query_blocks[..., q_part : q_part + kv_part].reshape(share, kv_width),
+                        query_blocks[..., q_part + kv_part :].reshape(share, kv_width),
+                    ],
+                    -1,
+                ),
+                packed[..., q_part + 2 * kv_part :]
+                .transpose(1, 0, 2)
+                .reshape(share, model_width)
+                .astype(f32),
+            ),
+        )
+        small_grads.insert(
+            0, jnp.concatenate([grad_router, gain_first[:, None], gain_second[:, None]], -1)
+        )
+    small_sum = lax.psum_scatter(jnp.stack(small_grads), both, scatter_dimension=1, tiled=True)
+    return (
+        hidden_out,
+        grad.reshape(1, row_count, model_width),
+        jnp.stack([g[0] for g in attention_grads]),
+        jnp.stack([g[1] for g in attention_grads]),
+        jnp.stack([g[2] for g in attention_grads]),
+        small_sum[..., :expert_total],
+        small_sum[..., expert_total:],
+        jnp.stack([g[0] for g in expert_grads]).astype(f32),
+        jnp.stack([g[1] for g in expert_grads]).astype(f32),
+    )
+
+
 def solution(mesh):
+    split = mesh.shape["ctx"] == 4 and mesh.shape["fsdp"] == 8
     return jax.shard_map(
-        on_device,
+        split_ranks if split else on_device,
         mesh=mesh,
         in_specs=(
             P("fsdp", "ctx", None),

time: 2620 us -> 1400 us (0.53)
  waiting for transfers between devices: 1490 us -> 758 us
  blocking collectives: 592 us -> 109 us
  starting transfers between devices: 35.9 us -> 134 us
  local copies, waits for them, and re-layouts: 184 us -> 123 us
    reduce_scatter x7 -> x6, waiting for transfers between devices: 754 us -> 327 us  [the longest x2 150 us: split_ranks(): packed = lax.psum_scatter(packed, 'fsdp', scatter_dimension=0, tiled=True)]
    all_to_all x7 -> x4, waiting for transfers between devices: 429 us -> 12.3 us  [the longest x2 9.74 us: split_ranks(): lax.all_to_all(packed[..., :q_part + 2 * kv_part], 'ctx', split_axis=0, c...]
    ppermute x0 -> x88, waiting for transfers between devices: none -> 399 us  [rotate_ranks(): lax.ppermute(values_in, axis_name, [(i, target_of(i)) for i in range(tota...]
    all_gather x4 -> x2, blocking collectives: 482 us -> 109 us  [the longest x1 71.8 us: split_ranks(): small = lax.all_gather(small, both, axis=0, tiled=True)]
    all_gather x12 -> x6, waiting for transfers between devices: 188 us -> 0.07 us  [the longest x2 0.04 us: split_ranks(): lax.all_gather(w_gate_up[i], 'ctx', axis=1, tiled=True)]
    ppermute x0 -> x88, starting transfers between devices: none -> 119 us  [rotate_ranks(): lax.ppermute(values_in, axis_name, [(i, target_of(i)) for i in range(tota...]
    all_to_all x1 -> x0, blocking collectives: 110 us -> none  [on_device(): lax.all_to_all(grad_send, 'fsdp', split_axis=0, concat_axis=0, tiled=True)]
    unnamed x23 -> x14, waiting for transfers between devices: 115 us -> 20.5 us
  transfers between devices with their start and end apart: 28 -> 105, of which waited for: 20 -> 76; matrix products, arithmetic and copies ran while one was open for 12% -> 16% of each run, Pallas kernels for 0% -> 0%
where the time goes in v1:
time: 1400 us; the launch traced here: 1380 us
  waiting for transfers between devices  758 us (54%)
  matrix products  157 us (11%)
  starting transfers between devices  134 us (10%)
  local copies, waits for them, and re-layouts  123 us (9%)
  blocking collectives  109 us (8%)
  other arithmetic  83.1 us (6%)
  between operations  18.5 us (1%)
    ppermute x88, waiting for transfers between devices, rotate_ranks(): lax.ppermute(values_in, axis_name, [(i, target_of(i)) for i in range(tota...  399 us
    reduce_scatter x2, waiting for transfers between devices, split_ranks(): packed = lax.psum_scatter(packed, 'fsdp', scatter_dimension=0, tiled=True)  150 us
    ppermute x88, starting transfers between devices, rotate_ranks(): lax.ppermute(values_in, axis_name, [(i, target_of(i)) for i in range(tota...  119 us
    reduce_scatter x2, waiting for transfers between devices, split_ranks(): lax.psum_scatter(jnp.stack(gate_up_grads), 'ctx', scatter_dimension=1, ti...  108 us
    all_gather x1, blocking collectives, split_ranks(): small = lax.all_gather(small, both, axis=0, tiled=True)  71.8 us
    reduce_scatter x2, waiting for transfers between devices, split_ranks(): lax.psum_scatter(jnp.stack(down_grads), 'ctx', scatter_dimension=1, tiled...  69 us
    dot_general x14, matrix products, dot(): return jnp.dot(a, b, preferred_element_type=f32)  50.8 us
    dot_general x14, matrix products, t_dot(): lax.dot_general(a, b, (((0,), (0,)), ((), ())), preferred_element_type=f32)  44.4 us
  transfers between devices with their start and end apart: 105, of which 76 were waited for; matrix products, arithmetic and copies ran while one was open for 16% of the time, Pallas kernels for 0%

profile of v1, /device:TPU:0, one launch (start us, length us, event | category | flops | bytes accessed | tf_op | source)
XLA Modules:
  0.0 1383.5 jit_solution(6024349743792712779)
XLA Ops:
  25.5 71.8 %all-gather.7 = bf16[32,48,36]{1,2,0:T(8,128)(2,1)S(1)} all-gather(bf16[1,48,36]{1,2,0:T(8,128)(2,1)S(1)} %maximum_bitcast_fusion.12), channel_id=1, replica_groups=mesh['ctx'=4,'fsdp'=8] {'ctx','fsdp'}, dimensions={0}, use_global_device_ids=true | all-gather | bytes 114048 | tf_op jit(solution)/shard_map/all_gather | solution.py:596
  102.5 13.5 collective-permute-done.1
  149.2 6.2 collective-permute-done.5
  159.1 37.0 %all-gather.1 = s32[16,1,128,8]{2,3,1,0:T(8,128)S(1)} all-gather(s32[2,1,128,8]{2,3,1,0:T(8,128)S(1)} %copy-done.163), channel_id=3, replica_groups=mesh['ctx'=4,'fsdp'=8] {'fsdp'}, dimensions={0}, use_global_device_ids=true | all-gather | bytes 73728 | tf_op jit(solution)/shard_map/all_gather | solution.py:635
  215.7 10.5 collective-permute-done.13
  234.7 5.0 concatenate.215
  241.5 5.5 fusion.31
  259.8 12.4 add_convert_fusion.3
  277.7 6.6 collective-permute-done.15
  284.4 5.5 collective-permute-done.16
  289.9 7.1 collective-permute-done.19
  304.2 8.1 collective-permute-done.17
  319.2 5.3 collective-permute-done.18
  332.3 7.4 collective-permute-done.23
  359.8 12.0 collective-permute-done.27
  376.7 8.4 collective-permute-done.29
  402.0 7.7 collective-permute-done.32
  416.5 8.4 collective-permute-done.35
  429.4 5.3 concatenate.226
  436.5 5.5 fusion.35
  463.4 8.7 collective-permute-done.37
  472.1 7.7 collective-permute-done.38
  479.7 5.1 collective-permute-done.41
  490.8 7.5 collective-permute-done.39
  522.4 5.2 concatenate.229
  529.6 16.1 %collective-permute-done.45 = bf16[128,1664]{0,1:T(8,128)(2,1)S(1)} collective-permute-done((bf16[128,1664]{0,1:T(8,128)(2,1)}, bf16[128,1664]{0,1:T(8,128)(2,1)S(1)}, u32[]{:S(2)}, u32[]{:S(2)}) %collective-permute-start.45) | collective-permute-done | bytes 426016 | tf_op jit(solution)/shard_map/ppermute | solution.py:490
  545.9 4.8 collective-permute-done.47
  554.4 9.9 collective-permute-done.49
  573.0 9.1 collective-permute-done.51
  582.9 5.5 collective-permute-done.50
  588.4 6.1 concatenate.231
  594.6 6.4 multiply_convert_fusion.5
  617.3 8.1 collective-permute-done.53
  625.4 8.4 collective-permute-done.54
  645.2 7.7 collective-permute-done.55
  669.8 5.2 collective-permute-done.59
  677.6 6.7 collective-permute-done.61
  704.9 9.9 collective-permute-done.65
  728.7 10.6 collective-permute-done.67
  743.7 5.1 collective-permute-done.69
  757.5 8.1 collective-permute-done.70
  768.0 4.8 collective-permute-done.68
  772.9 9.1 collective-permute-done.73
  786.7 6.2 concatenate.242
  793.0 6.4 multiply_convert_fusion.3
  815.4 8.4 collective-permute-done.75
  824.1 6.7 collective-permute-done.76
  830.8 5.8 collective-permute-done.79
  842.8 5.9 collective-permute-done.77
  853.1 5.3 collective-permute-done.80
  859.1 5.0 collective-permute-done.78
  871.2 6.6 collective-permute-done.83
  901.7 9.2 collective-permute-done.87
  961.5 6.1 fusion.18
  976.0 5.4 fusion.16
  993.7 20.3 %reduce-scatter.22.cloned.1.call-done = f32[48,36]{1,0:T(8,128)} async-done(((f32[1536,36]{1,0:T(8,128)}), f32[48,36]{1,0:T(8,128)}) %reduce-scatter.22.cloned.1.call-update) | async-done | bytes 6928
  1016.3 75.2 %reduce-scatter.12.cloned.1.call-done = bf16[4,48,1024]{2,1,0:T(8,128)(2,1)} async-done(((bf16[32,48,1024]{2,1,0:T(8,128)(2,1)}), bf16[4,48,1024]{2,1,0:T(8,128)(2,1)}) %reduce-scatter.12.cloned.1.call-update) | async-done | bytes 393232 | tf_op jit(solution)/shard_map/reduce_scatter | solution.py:812
  1102.8 28.5 %reduce-scatter.20.cloned.1.call-done = bf16[2,128,1536]{2,1,0:T(8,128)(2,1)} async-done(((bf16[2,512,1536]{2,1,0:T(8,128)(2,1)}), bf16[2,128,1536]{2,1,0:T(8,128)(2,1)}) %reduce-scatter.20.cloned.1.call-update) | async-done | bytes 786448 | tf_op jit(solution)/shard_map/reduce_scatter | solution.py:758
  1131.4 40.5 %reduce-scatter.18.cloned.1.call-done = bf16[2,128,1536]{2,1,0:T(8,128)(2,1)} async-done(((bf16[2,512,1536]{2,1,0:T(8,128)(2,1)}), bf16[2,128,1536]{2,1,0:T(8,128)(2,1)}) %reduce-scatter.18.cloned.1.call-update) | async-done | bytes 786448 | tf_op jit(solution)/shard_map/reduce_scatter | solution.py:758
  1175.1 74.8 %reduce-scatter.10.cloned.1.call-done = bf16[4,48,1024]{2,1,0:T(8,128)(2,1)} async-done(((bf16[32,48,1024]{2,1,0:T(8,128)(2,1)}), bf16[4,48,1024]{2,1,0:T(8,128)(2,1)}) %reduce-scatter.10.cloned.1.call-update) | async-done | bytes 393232 | tf_op jit(solution)/shard_map/reduce_scatter | solution.py:812
  1256.9 5.0 all-to-all-done.2
  1263.9 46.5 %reduce-scatter.16.cloned.1.call-done = bf16[2,384,1024]{2,1,0:T(8,128)(2,1)} async-done(((bf16[2,1536,1024]{2,1,0:T(8,128)(2,1)}), bf16[2,384,1024]{2,1,0:T(8,128)(2,1)}) %reduce-scatter.16.cloned.1.call-update) | async-done | bytes 1572880 | tf_op jit(solution)/shard_map/reduce_scatter | solution.py:755
  1310.4 61.1 %reduce-scatter.14.cloned.1.call-done = bf16[2,384,1024]{2,1,0:T(8,128)(2,1)} async-done(((bf16[2,1536,1024]{2,1,0:T(8,128)(2,1)}), bf16[2,384,1024]{2,1,0:T(8,128)(2,1)}) %reduce-scatter.14.cloned.1.call-update) | async-done | bytes 1572880 | tf_op jit(solution)/shard_map/reduce_scatter | solution.py:755
  1371.5 5.0 maximum_convert_fusion
  (906 shorter events, 505.9 us)
Async XLA Ops:
  15.7 101.3 %all-gather.15.cloned.1.call-start = ((), (), s32[]{:S(2)}) async-start(), calls=%async_computation.17 | async-start | bytes 3538944 | tf_op jit(solution)/shard_map/all_gather | solution.py:617
  23.3 218.2 %all-gather.17.cloned.1.call-start = ((), (), s32[]{:S(2)}) async-start(), calls=%async_computation.18 | async-start | bytes 7864320 | tf_op jit(solution)/shard_map/all_gather | solution.py:629
  25.3 230.1 %all-gather.19.cloned.1.call-start = ((), (), s32[]{:S(2)}) async-start(), calls=%async_computation.19 | async-start | bytes 3932160 | tf_op jit(solution)/shard_map/all_gather | solution.py:630
  99.8 16.2 %collective-permute-start.1 = (bf16[128,1536]{0,1:T(8,128)(2,1)S(1)}, bf16[128,1536]{0,1:T(8,128)(2,1)S(1)}, u32[]{:S(2)}, u32[]{:S(2)}) collective-permute-start(bf16[128,1536]{0,1:T(8,128)(2,1)S(1)} %fusion.79), channel_id=1, source_target_pairs={{0,16},{8,24},{16,0},{24,8},{1,17},{9,25},{17,1},{25,9},{2,18},{10... | collective-permute-start | bytes 1179656 | tf_op jit(solution)/shard_map/ppermute | solution.py:490
  100.9 18.0 %collective-permute-start = (bf16[128,1536]{0,1:T(8,128)(2,1)S(1)}, bf16[128,1536]{0,1:T(8,128)(2,1)}, u32[]{:S(2)}, u32[]{:S(2)}) collective-permute-start(bf16[128,1536]{0,1:T(8,128)(2,1)S(1)} %fusion.79), channel_id=1, source_target_pairs={{0,8},{8,0},{16,24},{24,16},{1,9},{9,1},{17,25},{25,17},{2,10},{10... | collective-permute-start | bytes 1179656 | tf_op jit(solution)/shard_map/ppermute | solution.py:490
  145.0 54.9 %all-to-all-start.1 = ((bf16[4,48,640]{2,1,0:T(8,128)(2,1)}), bf16[4,48,640]{2,1,0:T(8,128)(2,1)S(1)}, u32[]{:S(2)}, u32[]{:S(2)}) async-start(bf16[4,48,640]{2,1,0:T(8,128)(2,1)} %copy.291), calls=%async_computation.1 | async-start | bytes 491520 | tf_op jit(solution)/shard_map/all_to_all | solution.py:613
  148.4 191.3 %all-gather.21.cloned.1.call-start = ((), (), s32[]{:S(2)}) async-start(), calls=%async_computation.20 | async-start | bytes 3538944 | tf_op jit(solution)/shard_map/all_gather | solution.py:617
  156.8 39.9 %collective-permute-start.7 = (bf16[128,1536]{0,1:T(8,128)(2,1)S(1)}, bf16[128,1536]{0,1:T(8,128)(2,1)S(1)}, u32[]{:S(2)}, u32[]{:S(2)}) collective-permute-start(bf16[128,1536]{0,1:T(8,128)(2,1)S(1)} %multiply_convert_fusion.14), channel_id=1, source_target_pairs={{0,6},{1,7},{2,0},{3,1},{4,2},{5,3},{6,4},{7,5},{8,14},{9,15},{10,... | collective-permute-start | bytes 1179656 | tf_op jit(solution)/shard_map/ppermute | solution.py:490
  156.8 41.3 %collective-permute-start.9 = (bf16[128,1536]{0,1:T(8,128)(2,1)S(1)}, bf16[128,1536]{0,1:T(8,128)(2,1)S(1)}, u32[]{:S(2)}, u32[]{:S(2)}) collective-permute-start(bf16[128,1536]{0,1:T(8,128)(2,1)S(1)} %multiply_convert_fusion.14), channel_id=1, source_target_pairs={{0,2},{1,3},{2,4},{3,5},{4,6},{5,7},{6,0},{7,1},{8,10},{9,11},{10,... | collective-permute-start | bytes 1179656 | tf_op jit(solution)/shard_map/ppermute | solution.py:490
  200.7 235.8 %all-gather.23.cloned.1.call-start = ((), (), s32[]{:S(2)}) async-start(), calls=%async_computation.21 | async-start | bytes 7864320 | tf_op jit(solution)/shard_map/all_gather | solution.py:629
  200.8 14.9 %collective-permute-start.6 = (bf16[128,1536]{0,1:T(8,128)(2,1)S(1)}, bf16[128,1536]{0,1:T(8,128)(2,1)S(1)}, u32[]{:S(2)}, u32[]{:S(2)}) collective-permute-start(bf16[128,1536]{0,1:T(8,128)(2,1)S(1)} %multiply_convert_fusion.14), channel_id=1, source_target_pairs={{0,1},{1,0},{2,3},{3,2},{4,5},{5,4},{6,7},{7,6},{8,9},{9,8},{10,11... | collective-permute-start | bytes 1179656 | tf_op jit(solution)/shard_map/ppermute | solution.py:490
  204.4 21.8 %collective-permute-start.13 = (bf16[128,1536]{0,1:T(8,128)(2,1)S(1)}, bf16[128,1536]{0,1:T(8,128)(2,1)S(1)}, u32[]{:S(2)}, u32[]{:S(2)}) collective-permute-start(bf16[128,1536]{0,1:T(8,128)(2,1)S(1)} %collective-permute-done.9), channel_id=1, source_target_pairs={{0,1},{1,0},{2,3},{3,2},{4,5},{5,4},{6,7},{7,6},{8,9},{9,8},{10,11... | collective-permute-start | bytes 1179656 | tf_op jit(solution)/shard_map/ppermute | solution.py:490
  204.5 25.9 %collective-permute-start.8 = (bf16[128,1536]{0,1:T(8,128)(2,1)S(1)}, bf16[128,1536]{0,1:T(8,128)(2,1)S(1)}, u32[]{:S(2)}, u32[]{:S(2)}) collective-permute-start(bf16[128,1536]{0,1:T(8,128)(2,1)S(1)} %collective-permute-done.7), channel_id=1, source_target_pairs={{0,1},{1,0},{2,3},{3,2},{4,5},{5,4},{6,7},{7,6},{8,9},{9,8},{10,11... | collective-permute-start | bytes 1179656 | tf_op jit(solution)/shard_map/ppermute | solution.py:490
  210.1 24.7 %collective-permute-start.12 = (bf16[128,1536]{0,1:T(8,128)(2,1)S(1)}, bf16[128,1536]{0,1:T(8,128)(2,1)}, u32[]{:S(2)}, u32[]{:S(2)}) collective-permute-start(bf16[128,1536]{0,1:T(8,128)(2,1)S(1)} %pad_maximum_fusion.29), channel_id=1, source_target_pairs={{0,1},{1,0},{2,3},{3,2},{4,5},{5,4},{6,7},{7,6},{8,9},{9,8},{10,11... | collective-permute-start | bytes 1179656 | tf_op jit(solution)/shard_map/ppermute | solution.py:490
  275.6 14.2 %collective-permute-start.16 = (bf16[128,1536]{0,1:T(8,128)(2,1)}, bf16[128,1536]{0,1:T(8,128)(2,1)}, u32[]{:S(2)}, u32[]{:S(2)}) collective-permute-start(bf16[128,1536]{0,1:T(8,128)(2,1)} %get-tuple-element.88), channel_id=1, source_target_pairs={{0,1},{1,0},{2,3},{3,2},{4,5},{5,4},{6,7},{7,6},{8,9},{9,8},{10,11... | collective-permute-start | bytes 1179656 | tf_op jit(solution)/shard_map/ppermute | solution.py:490
  275.9 21.1 %collective-permute-start.19 = (bf16[128,1536]{0,1:T(8,128)(2,1)}, bf16[128,1536]{0,1:T(8,128)(2,1)}, u32[]{:S(2)}, u32[]{:S(2)}) collective-permute-start(bf16[128,1536]{0,1:T(8,128)(2,1)} %get-tuple-element.87), channel_id=1, source_target_pairs={{0,1},{1,0},{2,3},{3,2},{4,5},{5,4},{6,7},{7,6},{8,9},{9,8},{10,11... | collective-permute-start | bytes 1179656 | tf_op jit(solution)/shard_map/ppermute | solution.py:490
  277.7 175.1 %all-gather.25.cloned.1.call-start = ((), (), s32[]{:S(2)}) async-start(), calls=%async_computation.22 | async-start | bytes 3932160 | tf_op jit(solution)/shard_map/all_gather | solution.py:630
  298.8 20.4 %collective-permute-start.14 = (bf16[128,1536]{0,1:T(8,128)(2,1)S(1)}, bf16[128,1536]{0,1:T(8,128)(2,1)S(1)}, u32[]{:S(2)}, u32[]{:S(2)}) collective-permute-start(bf16[128,1536]{0,1:T(8,128)(2,1)S(1)} %copy-done.103), channel_id=1, source_target_pairs={{0,1},{1,0},{2,3},{3,2},{4,5},{5,4},{6,7},{7,6},{8,9},{9,8},{10,11... | collective-permute-start | bytes 1179656 | tf_op jit(solution)/shard_map/ppermute | solution.py:490
  300.3 16.1 %collective-permute-start.20 = (bf16[64,1536]{0,1:T(8,128)(2,1)S(1)}, bf16[64,1536]{0,1:T(8,128)(2,1)S(1)}, u32[]{:S(2)}, u32[]{:S(2)}) collective-permute-start(bf16[64,1536]{0,1:T(8,128)(2,1)S(1)} %get-tuple-element.128), channel_id=1, source_target_pairs={{0,6},{1,7},{2,0},{3,1},{4,2},{5,3},{6,4},{7,5},{8,14},{9,15},{10,... | collective-permute-start | bytes 589832 | tf_op jit(solution)/shard_map/ppermute | solution.py:490
  359.7 654.3 %reduce-scatter.22.cloned.1.call-start = ((), (), s32[]{:S(2)}) async-start(), calls=%async_computation.23 | async-start | bytes 811008
  375.5 18.5 %collective-permute-start.31 = (bf16[128,1536]{0,1:T(8,128)(2,1)S(1)}, bf16[128,1536]{0,1:T(8,128)(2,1)S(1)}, u32[]{:S(2)}, u32[]{:S(2)}) collective-permute-start(bf16[128,1536]{0,1:T(8,128)(2,1)S(1)} %multiply_convert_fusion.12), channel_id=1, source_target_pairs={{0,2},{1,3},{2,4},{3,5},{4,6},{5,7},{6,0},{7,1},{8,10},{9,11},{10,... | collective-permute-start | bytes 1179656 | tf_op jit(solution)/shard_map/ppermute | solution.py:490
  385.3 16.7 %collective-permute-start.33 = (bf16[64,1536]{0,1:T(8,128)(2,1)S(1)}, bf16[64,1536]{0,1:T(8,128)(2,1)S(1)}, u32[]{:S(2)}, u32[]{:S(2)}) collective-permute-start(bf16[64,1536]{0,1:T(8,128)(2,1)S(1)} %slice.813), channel_id=1, source_target_pairs={{0,6},{1,7},{2,0},{3,1},{4,2},{5,3},{6,4},{7,5},{8,14},{9,15},{10,... | collective-permute-start | bytes 589832 | tf_op jit(solution)/shard_map/ppermute | solution.py:490
  394.0 15.7 %collective-permute-start.32 = (bf16[64,1536]{0,1:T(8,128)(2,1)S(1)}, bf16[64,1536]{0,1:T(8,128)(2,1)S(1)}, u32[]{:S(2)}, u32[]{:S(2)}) collective-permute-start(bf16[64,1536]{0,1:T(8,128)(2,1)S(1)} %bitcast.490), channel_id=1, source_target_pairs={{0,2},{1,3},{2,4},{3,5},{4,6},{5,7},{6,0},{7,1},{8,10},{9,11},{10,... | collective-permute-start | bytes 589832 | tf_op jit(solution)/shard_map/ppermute | solution.py:490
  396.0 16.0 %collective-permute-start.28 = (bf16[128,1536]{0,1:T(8,128)(2,1)S(1)}, bf16[128,1536]{0,1:T(8,128)(2,1)S(1)}, u32[]{:S(2)}, u32[]{:S(2)}) collective-permute-start(bf16[128,1536]{0,1:T(8,128)(2,1)S(1)} %multiply_convert_fusion.12), channel_id=1, source_target_pairs={{0,1},{1,0},{2,3},{3,2},{4,5},{5,4},{6,7},{7,6},{8,9},{9,8},{10,11... | collective-permute-start | bytes 1179656 | tf_op jit(solution)/shard_map/ppermute | solution.py:490
  397.4 19.1 %collective-permute-start.30 = (bf16[128,1536]{0,1:T(8,128)(2,1)S(1)}, bf16[128,1536]{0,1:T(8,128)(2,1)S(1)}, u32[]{:S(2)}, u32[]{:S(2)}) collective-permute-start(bf16[128,1536]{0,1:T(8,128)(2,1)S(1)} %collective-permute-done.29), channel_id=1, source_target_pairs={{0,1},{1,0},{2,3},{3,2},{4,5},{5,4},{6,7},{7,6},{8,9},{9,8},{10,11... | collective-permute-start | bytes 1179656 | tf_op jit(solution)/shard_map/ppermute | solution.py:490
  398.0 26.9 %collective-permute-start.35 = (bf16[128,1536]{0,1:T(8,128)(2,1)S(1)}, bf16[128,1536]{0,1:T(8,128)(2,1)S(1)}, u32[]{:S(2)}, u32[]{:S(2)}) collective-permute-start(bf16[128,1536]{0,1:T(8,128)(2,1)S(1)} %collective-permute-done.31), channel_id=1, source_target_pairs={{0,1},{1,0},{2,3},{3,2},{4,5},{5,4},{6,7},{7,6},{8,9},{9,8},{10,11... | collective-permute-start | bytes 1179656 | tf_op jit(solution)/shard_map/ppermute | solution.py:490
  409.9 19.5 %collective-permute-start.34 = (bf16[128,1536]{0,1:T(8,128)(2,1)S(1)}, bf16[128,1536]{0,1:T(8,128)(2,1)}, u32[]{:S(2)}, u32[]{:S(2)}) collective-permute-start(bf16[128,1536]{0,1:T(8,128)(2,1)S(1)} %pad_maximum_fusion.34), channel_id=1, source_target_pairs={{0,1},{1,0},{2,3},{3,2},{4,5},{5,4},{6,7},{7,6},{8,9},{9,8},{10,11... | collective-permute-start | bytes 1179656 | tf_op jit(solution)/shard_map/ppermute | solution.py:490
  461.4 18.4 %collective-permute-start.38 = (bf16[128,1536]{0,1:T(8,128)(2,1)S(1)}, bf16[128,1536]{0,1:T(8,128)(2,1)S(1)}, u32[]{:S(2)}, u32[]{:S(2)}) collective-permute-start(bf16[128,1536]{0,1:T(8,128)(2,1)S(1)} %get-tuple-element.79), channel_id=1, source_target_pairs={{0,1},{1,0},{2,3},{3,2},{4,5},{5,4},{6,7},{7,6},{8,9},{9,8},{10,11... | collective-permute-start | bytes 1179656 | tf_op jit(solution)/shard_map/ppermute | solution.py:490
  462.0 22.8 %collective-permute-start.41 = (bf16[128,1536]{0,1:T(8,128)(2,1)S(1)}, bf16[128,1536]{0,1:T(8,128)(2,1)S(1)}, u32[]{:S(2)}, u32[]{:S(2)}) collective-permute-start(bf16[128,1536]{0,1:T(8,128)(2,1)S(1)} %get-tuple-element.78), channel_id=1, source_target_pairs={{0,1},{1,0},{2,3},{3,2},{4,5},{5,4},{6,7},{7,6},{8,9},{9,8},{10,11... | collective-permute-start | bytes 1179656 | tf_op jit(solution)/shard_map/ppermute | solution.py:490
  485.4 24.0 %collective-permute-start.36 = (bf16[128,1536]{0,1:T(8,128)(2,1)}, bf16[128,1536]{0,1:T(8,128)(2,1)}, u32[]{:S(2)}, u32[]{:S(2)}) collective-permute-start(bf16[128,1536]{0,1:T(8,128)(2,1)} %get-tuple-element.77), channel_id=1, source_target_pairs={{0,1},{1,0},{2,3},{3,2},{4,5},{5,4},{6,7},{7,6},{8,9},{9,8},{10,11... | collective-permute-start | bytes 1179656 | tf_op jit(solution)/shard_map/ppermute | solution.py:490
  487.0 18.1 %collective-permute-start.42 = (bf16[64,1536]{0,1:T(8,128)(2,1)S(1)}, bf16[64,1536]{0,1:T(8,128)(2,1)S(1)}, u32[]{:S(2)}, u32[]{:S(2)}) collective-permute-start(bf16[64,1536]{0,1:T(8,128)(2,1)S(1)} %get-tuple-element.124), channel_id=1, source_target_pairs={{0,6},{1,7},{2,0},{3,1},{4,2},{5,3},{6,4},{7,5},{8,14},{9,15},{10,... | collective-permute-start | bytes 589832 | tf_op jit(solution)/shard_map/ppermute | solution.py:490
  499.4 14.4 %collective-permute-start.40 = (bf16[128,1536]{0,1:T(8,128)(2,1)}, bf16[128,1536]{0,1:T(8,128)(2,1)}, u32[]{:S(2)}, u32[]{:S(2)}) collective-permute-start(bf16[128,1536]{0,1:T(8,128)(2,1)} %pad_maximum_fusion.35), channel_id=1, source_target_pairs={{0,2},{1,3},{2,4},{3,5},{4,6},{5,7},{6,0},{7,1},{8,10},{9,11},{10,... | collective-permute-start | bytes 1179656 | tf_op jit(solution)/shard_map/ppermute | solution.py:490
  527.6 18.1 %collective-permute-start.45 = (bf16[128,1664]{0,1:T(8,128)(2,1)}, bf16[128,1664]{0,1:T(8,128)(2,1)S(1)}, u32[]{:S(2)}, u32[]{:S(2)}) collective-permute-start(bf16[128,1664]{0,1:T(8,128)(2,1)} %concatenate.229), channel_id=1, source_target_pairs={{0,6},{1,7},{2,0},{3,1},{4,2},{5,3},{6,4},{7,5},{8,14},{9,15},{10,... | collective-permute-start | bytes 1277960 | tf_op jit(solution)/shard_map/ppermute | solution.py:490
  528.8 21.9 %collective-permute-start.47 = (bf16[128,1664]{0,1:T(8,128)(2,1)}, bf16[128,1664]{0,1:T(8,128)(2,1)S(1)}, u32[]{:S(2)}, u32[]{:S(2)}) collective-permute-start(bf16[128,1664]{0,1:T(8,128)(2,1)} %concatenate.229), channel_id=1, source_target_pairs={{0,2},{1,3},{2,4},{3,5},{4,6},{5,7},{6,0},{7,1},{8,10},{9,11},{10,... | collective-permute-start | bytes 1277960 | tf_op jit(solution)/shard_map/ppermute | solution.py:490
  545.9 18.5 %collective-permute-start.49 = (bf16[64,1664]{0,1:T(8,128)(2,1)S(1)}, bf16[64,1664]{0,1:T(8,128)(2,1)S(1)}, u32[]{:S(2)}, u32[]{:S(2)}) collective-permute-start(bf16[64,1664]{0,1:T(8,128)(2,1)S(1)} %slice.837), channel_id=1, source_target_pairs={{0,6},{1,7},{2,0},{3,1},{4,2},{5,3},{6,4},{7,5},{8,14},{9,15},{10,... | collective-permute-start | bytes 638984 | tf_op jit(solution)/shard_map/ppermute | solution.py:490
  550.9 18.8 %collective-permute-start.44 = (bf16[128,1664]{0,1:T(8,128)(2,1)}, bf16[128,1664]{0,1:T(8,128)(2,1)S(1)}, u32[]{:S(2)}, u32[]{:S(2)}) collective-permute-start(bf16[128,1664]{0,1:T(8,128)(2,1)} %concatenate.229), channel_id=1, source_target_pairs={{0,1},{1,0},{2,3},{3,2},{4,5},{5,4},{6,7},{7,6},{8,9},{9,8},{10,11... | collective-permute-start | bytes 1277960 | tf_op jit(solution)/shard_map/ppermute | solution.py:490
  552.4 20.6 %collective-permute-start.46 = (bf16[128,1664]{0,1:T(8,128)(2,1)S(1)}, bf16[128,1664]{0,1:T(8,128)(2,1)S(1)}, u32[]{:S(2)}, u32[]{:S(2)}) collective-permute-start(bf16[128,1664]{0,1:T(8,128)(2,1)S(1)} %collective-permute-done.45), channel_id=1, source_target_pairs={{0,1},{1,0},{2,3},{3,2},{4,5},{5,4},{6,7},{7,6},{8,9},{9,8},{10,11... | collective-permute-start | bytes 1277960 | tf_op jit(solution)/shard_map/ppermute | solution.py:490
  552.9 29.2 %collective-permute-start.51 = (bf16[128,1664]{0,1:T(8,128)(2,1)S(1)}, bf16[128,1664]{0,1:T(8,128)(2,1)S(1)}, u32[]{:S(2)}, u32[]{:S(2)}) collective-permute-start(bf16[128,1664]{0,1:T(8,128)(2,1)S(1)} %collective-permute-done.47), channel_id=1, source_target_pairs={{0,1},{1,0},{2,3},{3,2},{4,5},{5,4},{6,7},{7,6},{8,9},{9,8},{10,11... | collective-permute-start | bytes 1277960 | tf_op jit(solution)/shard_map/ppermute | solution.py:490
  565.9 22.5 %collective-permute-start.50 = (bf16[128,1664]{0,1:T(8,128)(2,1)S(1)}, bf16[128,1664]{0,1:T(8,128)(2,1)}, u32[]{:S(2)}, u32[]{:S(2)}) collective-permute-start(bf16[128,1664]{0,1:T(8,128)(2,1)S(1)} %pad_maximum_fusion.25), channel_id=1, source_target_pairs={{0,1},{1,0},{2,3},{3,2},{4,5},{5,4},{6,7},{7,6},{8,9},{9,8},{10,11... | collective-permute-start | bytes 1277960 | tf_op jit(solution)/shard_map/ppermute | solution.py:490
  614.9 18.9 %collective-permute-start.54 = (bf16[128,1536]{0,1:T(8,128)(2,1)S(1)}, bf16[128,1536]{0,1:T(8,128)(2,1)S(1)}, u32[]{:S(2)}, u32[]{:S(2)}) collective-permute-start(bf16[128,1536]{0,1:T(8,128)(2,1)S(1)} %get-tuple-element.72), channel_id=1, source_target_pairs={{0,1},{1,0},{2,3},{3,2},{4,5},{5,4},{6,7},{7,6},{8,9},{9,8},{10,11... | collective-permute-start | bytes 1179656 | tf_op jit(solution)/shard_map/ppermute | solution.py:490
  615.4 23.0 %collective-permute-start.57 = (bf16[128,1536]{0,1:T(8,128)(2,1)S(1)}, bf16[128,1536]{0,1:T(8,128)(2,1)S(1)}, u32[]{:S(2)}, u32[]{:S(2)}) collective-permute-start(bf16[128,1536]{0,1:T(8,128)(2,1)S(1)} %get-tuple-element.71), channel_id=1, source_target_pairs={{0,1},{1,0},{2,3},{3,2},{4,5},{5,4},{6,7},{7,6},{8,9},{9,8},{10,11... | collective-permute-start | bytes 1179656 | tf_op jit(solution)/shard_map/ppermute | solution.py:490
  638.8 14.0 %collective-permute-start.55 = (bf16[64,1536]{0,1:T(8,128)(2,1)S(1)}, bf16[64,1536]{0,1:T(8,128)(2,1)S(1)}, u32[]{:S(2)}, u32[]{:S(2)}) collective-permute-start(bf16[64,1536]{0,1:T(8,128)(2,1)S(1)} %get-tuple-element.121), channel_id=1, source_target_pairs={{0,2},{1,3},{2,4},{3,5},{4,6},{5,7},{6,0},{7,1},{8,10},{9,11},{10,... | collective-permute-start | bytes 589832 | tf_op jit(solution)/shard_map/ppermute | solution.py:490
  643.3 22.9 %collective-permute-start.52 = (bf16[128,1536]{0,1:T(8,128)(2,1)S(1)}, bf16[128,1536]{0,1:T(8,128)(2,1)S(1)}, u32[]{:S(2)}, u32[]{:S(2)}) collective-permute-start(bf16[128,1536]{0,1:T(8,128)(2,1)S(1)} %get-tuple-element.70), channel_id=1, source_target_pairs={{0,1},{1,0},{2,3},{3,2},{4,5},{5,4},{6,7},{7,6},{8,9},{9,8},{10,11... | collective-permute-start | bytes 1179656 | tf_op jit(solution)/shard_map/ppermute | solution.py:490
  645.0 17.1 %collective-permute-start.58 = (bf16[64,1536]{0,1:T(8,128)(2,1)S(1)}, bf16[64,1536]{0,1:T(8,128)(2,1)S(1)}, u32[]{:S(2)}, u32[]{:S(2)}) collective-permute-start(bf16[64,1536]{0,1:T(8,128)(2,1)S(1)} %get-tuple-element.122), channel_id=1, source_target_pairs={{0,6},{1,7},{2,0},{3,1},{4,2},{5,3},{6,4},{7,5},{8,14},{9,15},{10,... | collective-permute-start | bytes 589832 | tf_op jit(solution)/shard_map/ppermute | solution.py:490
  653.2 16.6 %collective-permute-start.56 = (bf16[128,1536]{0,1:T(8,128)(2,1)S(1)}, bf16[128,1536]{0,1:T(8,128)(2,1)S(1)}, u32[]{:S(2)}, u32[]{:S(2)}) collective-permute-start(bf16[128,1536]{0,1:T(8,128)(2,1)S(1)} %pad_maximum_fusion.37), channel_id=1, source_target_pairs={{0,2},{1,3},{2,4},{3,5},{4,6},{5,7},{6,0},{7,1},{8,10},{9,11},{10,... | collective-permute-start | bytes 1179656 | tf_op jit(solution)/shard_map/ppermute | solution.py:490
  724.4 14.9 %collective-permute-start.67 = (bf16[128,1664]{0,1:T(8,128)(2,1)}, bf16[128,1664]{0,1:T(8,128)(2,1)S(1)}, u32[]{:S(2)}, u32[]{:S(2)}) collective-permute-start(bf16[128,1664]{0,1:T(8,128)(2,1)} %concatenate.240), channel_id=1, source_target_pairs={{0,6},{1,7},{2,0},{3,1},{4,2},{5,3},{6,4},{7,5},{8,14},{9,15},{10,... | collective-permute-start | bytes 1277960 | tf_op jit(solution)/shard_map/ppermute | solution.py:490
  728.7 20.1 %collective-permute-start.69 = (bf16[128,1664]{0,1:T(8,128)(2,1)}, bf16[128,1664]{0,1:T(8,128)(2,1)S(1)}, u32[]{:S(2)}, u32[]{:S(2)}) collective-permute-start(bf16[128,1664]{0,1:T(8,128)(2,1)} %concatenate.240), channel_id=1, source_target_pairs={{0,2},{1,3},{2,4},{3,5},{4,6},{5,7},{6,0},{7,1},{8,10},{9,11},{10,... | collective-permute-start | bytes 1277960 | tf_op jit(solution)/shard_map/ppermute | solution.py:490
  739.4 18.0 %collective-permute-start.71 = (bf16[64,1664]{0,1:T(8,128)(2,1)S(1)}, bf16[64,1664]{0,1:T(8,128)(2,1)S(1)}, u32[]{:S(2)}, u32[]{:S(2)}) collective-permute-start(bf16[64,1664]{0,1:T(8,128)(2,1)S(1)} %slice.864), channel_id=1, source_target_pairs={{0,6},{1,7},{2,0},{3,1},{4,2},{5,3},{6,4},{7,5},{8,14},{9,15},{10,... | collective-permute-start | bytes 638984 | tf_op jit(solution)/shard_map/ppermute | solution.py:490
  748.8 16.8 %collective-permute-start.70 = (bf16[64,1664]{0,1:T(8,128)(2,1)S(1)}, bf16[64,1664]{0,1:T(8,128)(2,1)S(1)}, u32[]{:S(2)}, u32[]{:S(2)}) collective-permute-start(bf16[64,1664]{0,1:T(8,128)(2,1)S(1)} %bitcast.488), channel_id=1, source_target_pairs={{0,2},{1,3},{2,4},{3,5},{4,6},{5,7},{6,0},{7,1},{8,10},{9,11},{10,... | collective-permute-start | bytes 638984 | tf_op jit(solution)/shard_map/ppermute | solution.py:490
  750.8 17.2 %collective-permute-start.66 = (bf16[128,1664]{0,1:T(8,128)(2,1)}, bf16[128,1664]{0,1:T(8,128)(2,1)S(1)}, u32[]{:S(2)}, u32[]{:S(2)}) collective-permute-start(bf16[128,1664]{0,1:T(8,128)(2,1)} %concatenate.240), channel_id=1, source_target_pairs={{0,1},{1,0},{2,3},{3,2},{4,5},{5,4},{6,7},{7,6},{8,9},{9,8},{10,11... | collective-permute-start | bytes 1277960 | tf_op jit(solution)/shard_map/ppermute | solution.py:490
  752.4 20.4 %collective-permute-start.68 = (bf16[128,1664]{0,1:T(8,128)(2,1)S(1)}, bf16[128,1664]{0,1:T(8,128)(2,1)S(1)}, u32[]{:S(2)}, u32[]{:S(2)}) collective-permute-start(bf16[128,1664]{0,1:T(8,128)(2,1)S(1)} %collective-permute-done.67), channel_id=1, source_target_pairs={{0,1},{1,0},{2,3},{3,2},{4,5},{5,4},{6,7},{7,6},{8,9},{9,8},{10,11... | collective-permute-start | bytes 1277960 | tf_op jit(solution)/shard_map/ppermute | solution.py:490
  752.8 29.2 %collective-permute-start.73 = (bf16[128,1664]{0,1:T(8,128)(2,1)S(1)}, bf16[128,1664]{0,1:T(8,128)(2,1)S(1)}, u32[]{:S(2)}, u32[]{:S(2)}) collective-permute-start(bf16[128,1664]{0,1:T(8,128)(2,1)S(1)} %collective-permute-done.69), channel_id=1, source_target_pairs={{0,1},{1,0},{2,3},{3,2},{4,5},{5,4},{6,7},{7,6},{8,9},{9,8},{10,11... | collective-permute-start | bytes 1277960 | tf_op jit(solution)/shard_map/ppermute | solution.py:490
  766.4 20.3 %collective-permute-start.72 = (bf16[128,1664]{0,1:T(8,128)(2,1)S(1)}, bf16[128,1664]{0,1:T(8,128)(2,1)}, u32[]{:S(2)}, u32[]{:S(2)}) collective-permute-start(bf16[128,1664]{0,1:T(8,128)(2,1)S(1)} %pad_maximum_fusion.26), channel_id=1, source_target_pairs={{0,1},{1,0},{2,3},{3,2},{4,5},{5,4},{6,7},{7,6},{8,9},{9,8},{10,11... | collective-permute-start | bytes 1277960 | tf_op jit(solution)/shard_map/ppermute | solution.py:490
  813.4 17.5 %collective-permute-start.76 = (bf16[128,1536]{0,1:T(8,128)(2,1)S(1)}, bf16[128,1536]{0,1:T(8,128)(2,1)S(1)}, u32[]{:S(2)}, u32[]{:S(2)}) collective-permute-start(bf16[128,1536]{0,1:T(8,128)(2,1)S(1)} %get-tuple-element.65), channel_id=1, source_target_pairs={{0,1},{1,0},{2,3},{3,2},{4,5},{5,4},{6,7},{7,6},{8,9},{9,8},{10,11... | collective-permute-start | bytes 1179656 | tf_op jit(solution)/shard_map/ppermute | solution.py:490
  813.7 22.8 %collective-permute-start.79 = (bf16[128,1536]{0,1:T(8,128)(2,1)S(1)}, bf16[128,1536]{0,1:T(8,128)(2,1)S(1)}, u32[]{:S(2)}, u32[]{:S(2)}) collective-permute-start(bf16[128,1536]{0,1:T(8,128)(2,1)S(1)} %get-tuple-element.64), channel_id=1, source_target_pairs={{0,1},{1,0},{2,3},{3,2},{4,5},{5,4},{6,7},{7,6},{8,9},{9,8},{10,11... | collective-permute-start | bytes 1179656 | tf_op jit(solution)/shard_map/ppermute | solution.py:490
  837.1 22.0 %collective-permute-start.74 = (bf16[128,1536]{0,1:T(8,128)(2,1)S(1)}, bf16[128,1536]{0,1:T(8,128)(2,1)S(1)}, u32[]{:S(2)}, u32[]{:S(2)}) collective-permute-start(bf16[128,1536]{0,1:T(8,128)(2,1)S(1)} %get-tuple-element.63), channel_id=1, source_target_pairs={{0,1},{1,0},{2,3},{3,2},{4,5},{5,4},{6,7},{7,6},{8,9},{9,8},{10,11... | collective-permute-start | bytes 1179656 | tf_op jit(solution)/shard_map/ppermute | solution.py:490
  839.0 19.5 %collective-permute-start.80 = (bf16[64,1536]{0,1:T(8,128)(2,1)S(1)}, bf16[64,1536]{0,1:T(8,128)(2,1)S(1)}, u32[]{:S(2)}, u32[]{:S(2)}) collective-permute-start(bf16[64,1536]{0,1:T(8,128)(2,1)S(1)} %get-tuple-element.118), channel_id=1, source_target_pairs={{0,6},{1,7},{2,0},{3,1},{4,2},{5,3},{6,4},{7,5},{8,14},{9,15},{10,... | collective-permute-start | bytes 589832 | tf_op jit(solution)/shard_map/ppermute | solution.py:490
  849.0 15.0 %collective-permute-start.78 = (bf16[128,1536]{0,1:T(8,128)(2,1)S(1)}, bf16[128,1536]{0,1:T(8,128)(2,1)S(1)}, u32[]{:S(2)}, u32[]{:S(2)}) collective-permute-start(bf16[128,1536]{0,1:T(8,128)(2,1)S(1)} %pad_maximum_fusion.40), channel_id=1, source_target_pairs={{0,2},{1,3},{2,4},{3,5},{4,6},{5,7},{6,0},{7,1},{8,10},{9,11},{10,... | collective-permute-start | bytes 1179656 | tf_op jit(solution)/shard_map/ppermute | solution.py:490
  918.7 172.8 %reduce-scatter.12.cloned.1.call-start = ((), (), s32[]{:S(2)}) async-start(), calls=%async_computation.12 | async-start | bytes 3538944 | tf_op jit(solution)/shard_map/reduce_scatter | solution.py:812
  930.6 200.8 %reduce-scatter.20.cloned.1.call-start = ((), (), s32[]{:S(2)}) async-start(), calls=%async_computation.16 | async-start | bytes 3932160 | tf_op jit(solution)/shard_map/reduce_scatter | solution.py:758
  938.8 233.1 %reduce-scatter.18.cloned.1.call-start = ((), (), s32[]{:S(2)}) async-start(), calls=%async_computation.15 | async-start | bytes 3932160 | tf_op jit(solution)/shard_map/reduce_scatter | solution.py:758
  946.8 303.1 %reduce-scatter.10.cloned.1.call-start = ((), (), s32[]{:S(2)}) async-start(), calls=%async_computation.11 | async-start | bytes 3538944 | tf_op jit(solution)/shard_map/reduce_scatter | solution.py:812
  961.4 349.0 %reduce-scatter.16.cloned.1.call-start = ((), (), s32[]{:S(2)}) async-start(), calls=%async_computation.14 | async-start | bytes 7864320 | tf_op jit(solution)/shard_map/reduce_scatter | solution.py:755
  975.7 395.8 %reduce-scatter.14.cloned.1.call-start = ((), (), s32[]{:S(2)}) async-start(), calls=%async_computation.13 | async-start | bytes 7864320 | tf_op jit(solution)/shard_map/reduce_scatter | solution.py:755
  (263 other events, 3150.6 us)
Sparse Core Ops, SparseCore 0:
  23.4 64.8 all-gather.14
  90.4 50.5 all-gather.16
  143.2 30.8 all-gather.18
  200.8 66.0 all-gather.20
  277.8 45.9 all-gather.22
  359.8 28.8 all-gather.24
  918.9 95.0 reduce-scatter.21
  1018.1 73.3 reduce-scatter.11
  1094.1 37.2 reduce-scatter.19
  1133.9 37.9 reduce-scatter.17
  1175.5 74.4 reduce-scatter.9
  1252.9 57.4 reduce-scatter.15
  1313.1 58.3 reduce-scatter.13

commit v2 on v0

--- a/solution.py
+++ b/solution.py
@@ -3,6 +3,8 @@
 import jax
 import jax.numpy as jnp
 from jax import lax
+from jax.experimental import pallas as pl
+from jax.experimental.pallas import tpu as pltpu
 from jax.sharding import PartitionSpec as P
 
 HEADS = 24
@@ -486,9 +488,784 @@
     )
 
 
+NN = (((1,), (0,)), ((), ()))
+NT = (((1,), (1,)), ((), ()))
+TN = (((0,), (0,)), ((), ()))
+FE_STEP = 256
+
+
+def mm(a, b, dims=NN):
+    return lax.dot_general(a, b, dims, preferred_element_type=jnp.float32)
+
+
+def whole(shape):
+    return pl.BlockSpec(shape, lambda *_: (0,) * len(shape))
+
+
+def anywhere():
+    return pl.BlockSpec(memory_space=pl.ANY)
+
+
+def kernel_params(mebibytes):
+    return pltpu.CompilerParams(vmem_limit_bytes=mebibytes * 1024 * 1024)
+
+
+def shaped(shape, dtype=jnp.bfloat16):
+    return jax.ShapeDtypeStruct(shape, dtype)
+
+
+def experts_forward_body(
+    rows_0, rows_1, mask, router, own, w_gate, w_up, w_down, *refs
+):
+    out_0, out_1, all_rows, all_gate, all_up, all_probs, total = refs[-7:]
+    expert, piece = pl.program_id(0), pl.program_id(1)
+    first = jnp.logical_and(expert == 0, piece == 0)
+    last = jnp.logical_and(expert == pl.num_programs(0) - 1, piece == pl.num_programs(1) - 1)
+    count = rows_0.shape[0]
+
+    @pl.when(first)
+    def _():
+        all_rows[:count, :] = rows_0[...]
+        all_rows[count:, :] = rows_1[...]
+        logits = mm(all_rows[...], router[...]) + mask[...]
+        weights = jnp.exp(logits - jnp.max(logits, -1, keepdims=True))
+        all_probs[...] = weights / jnp.sum(weights, -1, keepdims=True)
+        total[...] = jnp.zeros_like(total)
+
+    chosen = jnp.sum(all_probs[...] * own[pl.ds(expert, 1), :], -1, keepdims=True)
+    gate = mm(all_rows[...], w_gate[0])
+    up = mm(all_rows[...], w_up[0])
+    all_gate[...] = gate.astype(jnp.bfloat16)
+    all_up[...] = up.astype(jnp.bfloat16)
+    hidden = (gate * jax.nn.sigmoid(gate) * up * chosen).astype(jnp.bfloat16)
+    total[...] += mm(hidden, w_down[0])
+
+    @pl.when(last)
+    def _():
+        out_0[...] = total[:count, :].astype(jnp.bfloat16)
+        out_1[...] = total[count:, :].astype(jnp.bfloat16)
+
+
+def experts_forward(group, groups, rows, mask, router, own, w_gate_up, w_down, kept):
+    block, width = rows[0].shape
+    count = 2 * block
+    expert_count, hidden_width = w_down.shape[0], w_down.shape[1]
+    steps = hidden_width // FE_STEP
+    flat = shaped((groups * count, expert_count * hidden_width))
+    flat_spec = pl.BlockSpec((count, FE_STEP), lambda e, p: (group, e * steps + p))
+    lanes_spec = pl.BlockSpec((count, 128), lambda e, p: (group, 0))
+    inputs = [*rows, mask, router, own, w_gate_up, w_gate_up, w_down, *kept]
+    return pl.pallas_call(
+        experts_forward_body,
+        grid=(expert_count, steps),
+        in_specs=[
+            whole((block, width)),
+            whole((block, width)),
+            lanes_spec,
+            whole(router.shape),
+            whole(own.shape),
+            pl.BlockSpec((1, width, FE_STEP), lambda e, p: (e, 0, p)),
+            pl.BlockSpec((1, width, FE_STEP), lambda e, p: (e, 0, steps + p)),
+            pl.BlockSpec((1, FE_STEP, width), lambda e, p: (e, p, 0)),
+        ]
+        + [anywhere()] * len(kept),
+        out_specs=[
+            whole((block, width)),
+            whole((block, width)),
+            pl.BlockSpec((count, width), lambda e, p: (group, 0)),
+            flat_spec,
+            flat_spec,
+            lanes_spec,
+        ],
+        out_shape=[
+            shaped((block, width)),
+            shaped((block, width)),
+            shaped((groups * count, width)),
+            flat,
+            flat,
+            shaped((groups * count, 128), jnp.float32),
+        ],
+        input_output_aliases={8 + i: 2 + i for i in range(len(kept))},
+        scratch_shapes=[pltpu.VMEM((count, width), jnp.float32)],
+        compiler_params=kernel_params(24),
+        cost_estimate=pl.CostEstimate(
+            flops=6 * count * width * expert_count * hidden_width,
+            bytes_accessed=6 * width * expert_count * hidden_width,
+            transcendentals=count * expert_count * hidden_width,
+        ),
+    )(*inputs)
+
+
+def experts_backward_body(
+    grads_0, grads_1, probs, gate_in, up_in, router, own, w_gate, w_up, w_down, *refs
+):
+    out_0, out_1, all_grads, all_grad_gate, all_grad_up, all_hidden, all_logits = refs[-10:-3]
+    total, dots, mean = refs[-3:]
+    expert, piece = pl.program_id(0), pl.program_id(1)
+    first = jnp.logical_and(expert == 0, piece == 0)
+    last_piece = piece == pl.num_programs(1) - 1
+    last = jnp.logical_and(expert == pl.num_programs(0) - 1, last_piece)
+    count, width = out_0.shape
+
+    @pl.when(first)
+    def _():
+        for at, grads in ((0, grads_0), (count, grads_1)):
+            all_grads[at : at + count, :] = grads[:, :width]
+            mean[at : at + count, :] = grads[:, width : width + 1].astype(jnp.float32) + grads[
+                :, width + 1 : width + 2
+            ].astype(jnp.float32)
+        total[...] = jnp.zeros_like(total)
+        all_logits[...] = jnp.zeros_like(all_logits)
+
+    @pl.when(piece == 0)
+    def _():
+        dots[...] = jnp.zeros_like(dots)
+
+    mine = own[pl.ds(expert, 1), :]
+    chosen = jnp.sum(probs[...] * mine, -1, keepdims=True)
+    plain = mm(all_grads[...], w_down[0], NT)
+    gate = gate_in[...].astype(jnp.float32)
+    up = up_in[...].astype(jnp.float32)
+    sigmoid_gate = jax.nn.sigmoid(gate)
+    silu_gate = gate * sigmoid_gate
+    hidden = silu_gate * up
+    dots[...] += jnp.sum(plain * hidden, -1, keepdims=True)
+    all_hidden[...] = (hidden * chosen).astype(jnp.bfloat16)
+    plain = plain * chosen
+    grad_gate = (plain * up * sigmoid_gate * (1.0 + gate * (1.0 - sigmoid_gate))).astype(
+        jnp.bfloat16
+    )
+    grad_up = (plain * silu_gate).astype(jnp.bfloat16)
+    all_grad_gate[...] = grad_gate
+    all_grad_up[...] = grad_up
+    total[...] += mm(grad_gate, w_gate[0], NT) + mm(grad_up, w_up[0], NT)
+
+    @pl.when(last_piece)
+    def _():
+        all_logits[...] += (chosen * (dots[...] - mean[...]) * mine).astype(jnp.bfloat16)
+
+    @pl.when(last)
+    def _():
+        result = (total[...] + mm(all_logits[...], router[...], NT)).astype(jnp.bfloat16)
+        out_0[...] = result[:count, :]
+        out_1[...] = result[count:, :]
+
+
+def experts_backward(group, groups, grads, probs, gate, up, router, own, w_gate_up, w_down, kept):
+    block, width = grads[0].shape[0], w_down.shape[2]
+    count = 2 * block
+    expert_count, hidden_width = w_down.shape[0], w_down.shape[1]
+    steps = hidden_width // FE_STEP
+    flat = shaped((groups * count, expert_count * hidden_width))
+    flat_spec = pl.BlockSpec((count, FE_STEP), lambda e, p: (group, e * steps + p))
+    lanes_spec = pl.BlockSpec((count, 128), lambda e, p: (group, 0))
+    inputs = [*grads, probs, gate, up, router, own, w_gate_up, w_gate_up, w_down, *kept]
+    return pl.pallas_call(
+        experts_backward_body,
+        grid=(expert_count, steps),
+        in_specs=[
+            whole(grads[0].shape),
+            whole(grads[1].shape),
+            lanes_spec,
+            flat_spec,
+            flat_spec,
+            whole(router.shape),
+            whole(own.shape),
+            pl.BlockSpec((1, width, FE_STEP), lambda e, p: (e, 0, p)),
+            pl.BlockSpec((1, width, FE_STEP), lambda e, p: (e, 0, steps + p)),
+            pl.BlockSpec((1, FE_STEP, width), lambda e, p: (e, p, 0)),
+        ]
+        + [anywhere()] * len(kept),
+        out_specs=[
+            whole((block, width)),
+            whole((block, width)),
+            pl.BlockSpec((count, width), lambda e, p: (group, 0)),
+            flat_spec,
+            flat_spec,
+            flat_spec,
+            lanes_spec,
+        ],
+        out_shape=[
+            shaped((block, width)),
+            shaped((block, width)),
+            shaped((groups * count, width)),
+            flat,
+            flat,
+            flat,
+            shaped((groups * count, 128)),
+        ],
+        input_output_aliases={10 + i: 2 + i for i in range(len(kept))},
+        scratch_shapes=[
+            pltpu.VMEM((count, width), jnp.float32),
+            pltpu.VMEM((count, 1), jnp.float32),
+            pltpu.VMEM((count, 1), jnp.float32),
+        ],
+        compiler_params=kernel_params(24),
+        cost_estimate=pl.CostEstimate(
+            flops=6 * count * width * expert_count * hidden_width,
+            bytes_accessed=6 * width * expert_count * hidden_width,
+            transcendentals=count * expert_count * hidden_width,
+        ),
+    )(*inputs)
+
+
+def turn(block, cosine, sine, lane):
+    half = HEAD_DIM // 2
+    other = jnp.where(
+        lane % HEAD_DIM < half, pltpu.roll(block, 128 - half, 1), pltpu.roll(block, half, 1)
+    )
+    return block * cosine + other * sine
+
+
+def attention_forward_body(
+    rows_0, rows_1, rows_2, rows_3, w_qkv, w_out, cosine, sine, place_column, place_row,
+    out_0, out_1, out_2, out_3, all_rows, qkv, attended, logs,
+):
+    rows, outs = (rows_0, rows_1, rows_2, rows_3), (out_0, out_1, out_2, out_3)
+    count = rows_0.shape[0]
+    q_width, total_width = attended.shape[1], qkv.shape[1]
+    kv_width = (total_width - q_width) // 2
+    group = HEADS // KV_HEADS
+    for r in range(4):
+        span = pl.ds(r * count, count)
+        all_rows[span, :] = rows[r][...]
+        raw = mm(rows[r][...], w_qkv[:, :total_width])
+        lane = lax.broadcasted_iota(jnp.int32, (count, 128), 1)
+        for j in range((q_width + kv_width) // 128):
+            turned = turn(raw[:, 128 * j : 128 * j + 128], cosine[span, :], sine[span, :], lane)
+            if 128 * j < q_width:
+                turned = turned * HEAD_DIM ** (-0.5)
+            qkv[span, 128 * j : 128 * j + 128] = turned.astype(jnp.bfloat16)
+        qkv[span, q_width + kv_width :] = raw[:, q_width + kv_width :].astype(jnp.bfloat16)
+    visible = place_column[...] >= place_row[...]
+    for head in range(q_width // HEAD_DIM):
+        at, of = head * HEAD_DIM, (head // group) * HEAD_DIM
+        queries = qkv[:, at : at + HEAD_DIM]
+        keys = qkv[:, q_width + of : q_width + of + HEAD_DIM]
+        values = qkv[:, q_width + kv_width + of : q_width + kv_width + of + HEAD_DIM]
+        scores = jnp.where(visible, mm(queries, keys, NT), masked_score)
+        top = jnp.max(scores, -1, keepdims=True)
+        weights = jnp.exp(scores - top)
+        total = jnp.sum(weights, -1, keepdims=True)
+        logs[:, head : head + 1] = top + jnp.log(total)
+        probs = (weights * (1.0 / total)).astype(jnp.bfloat16)
+        attended[:, at : at + HEAD_DIM] = mm(probs, values).astype(jnp.bfloat16)
+    for r in range(4):
+        outs[r][...] = mm(attended[pl.ds(r * count, count), :], w_out[...]).astype(jnp.bfloat16)
+
+
+def attention_forward(rows, w_qkv, w_out, total_width, tables):
+    count, width = rows[0].shape
+    seq = 4 * count
+    q_width = w_out.shape[0]
+    outs = pl.pallas_call(
+        attention_forward_body,
+        out_shape=[shaped((count, width))] * 4
+        + [
+            shaped((seq, width)),
+            shaped((seq, total_width)),
+            shaped((seq, q_width)),
+            shaped((seq, 128), jnp.float32),
+        ],
+        compiler_params=kernel_params(24),
+        cost_estimate=pl.CostEstimate(
+            flops=2 * seq * width * (total_width + q_width) + 4 * seq * seq * q_width,
+            bytes_accessed=2 * (seq * width * 2 + width * (total_width + q_width)),
+            transcendentals=seq * seq * (q_width // HEAD_DIM),
+        ),
+    )(*rows, w_qkv, w_out, *tables)
+    return outs[:4], outs[4], outs[5], outs[6], outs[7]
+
+
+def attention_backward_body(
+    grad_0, grad_1, grad_2, grad_3, rows,
+    w_qkv, w_out, qkv, logs, cosine, sine, place_column, place_row,
+    out_0, out_1, out_2, out_3, all_grads, grad_qkv, gain_sum, grad_attended, raw,
+):
+    grads, outs = (grad_0, grad_1, grad_2, grad_3), (out_0, out_1, out_2, out_3)
+    count, seq = grad_0.shape[0], qkv.shape[0]
+    q_width, total_width = grad_attended.shape[1], qkv.shape[1]
+    kv_width = (total_width - q_width) // 2
+    group = HEADS // KV_HEADS
+    scale = HEAD_DIM ** (-0.5)
+    for r in range(4):
+        span = pl.ds(r * count, count)
+        all_grads[span, :] = grads[r][...]
+        grad_attended[span, :] = mm(grads[r][...], w_out[...], NT).astype(jnp.bfloat16)
+    visible = place_column[...] >= place_row[...]
+    for kv_head in range(kv_width // HEAD_DIM):
+        k_at = q_width + kv_head * HEAD_DIM
+        v_at = k_at + kv_width
+        keys, values = qkv[:, k_at : k_at + HEAD_DIM], qkv[:, v_at : v_at + HEAD_DIM]
+        grad_keys = jnp.zeros((HEAD_DIM, seq), jnp.float32)
+        grad_values = jnp.zeros((HEAD_DIM, seq), jnp.float32)
+        for head in range(kv_head * group, (kv_head + 1) * group):
+            at = head * HEAD_DIM
+            queries = qkv[:, at : at + HEAD_DIM]
+            grad_head = grad_attended[:, at : at + HEAD_DIM]
+            scores = mm(queries, keys, NT)
+            probs = jnp.where(visible, jnp.exp(scores - logs[:, head : head + 1]), 0.0)
+            grad_values += mm(grad_head.T, probs.astype(jnp.bfloat16))
+            weighted = probs * mm(grad_head, values, NT)
+            grad_scores = (weighted - probs * jnp.sum(weighted, -1, keepdims=True)).astype(
+                jnp.bfloat16
+            )
+            raw[:, at : at + HEAD_DIM] = mm(grad_scores, keys) * scale
+            grad_keys += mm(queries.T, grad_scores)
+        raw[:, k_at : k_at + HEAD_DIM] = grad_keys.T
+        raw[:, v_at : v_at + HEAD_DIM] = grad_values.T
+    gain_sum[...] = jnp.zeros_like(gain_sum)
+    for r in range(4):
+        span = pl.ds(r * count, count)
+        lane = lax.broadcasted_iota(jnp.int32, (count, 128), 1)
+        for j in range((q_width + kv_width) // 128):
+            part = slice(128 * j, 128 * j + 128)
+            grad_qkv[span, part] = turn(
+                raw[span, part], cosine[span, :], -sine[span, :], lane
+            ).astype(jnp.bfloat16)
+        grad_qkv[span, q_width + kv_width :] = raw[span, q_width + kv_width :].astype(jnp.bfloat16)
+        back = mm(grad_qkv[span, :], w_qkv[:, :total_width], NT)
+        outs[r][...] = back.astype(jnp.bfloat16)
+        gain_sum[...] += jnp.sum(back * rows[span, :].astype(jnp.float32), 0, keepdims=True)
+
+
+def attention_backward(grads, rows, w_qkv, w_out, qkv, logs, tables):
+    count, width = grads[0].shape
+    seq = 4 * count
+    q_width, total_width = w_out.shape[0], qkv.shape[1]
+    outs = pl.pallas_call(
+        attention_backward_body,
+        out_shape=[shaped((count, width))] * 4
+        + [
+            shaped((seq, width)),
+            shaped((seq, total_width)),
+            shaped((1, width), jnp.float32),
+        ],
+        scratch_shapes=[
+            pltpu.VMEM((seq, q_width), jnp.bfloat16),
+            pltpu.VMEM((seq, total_width), jnp.float32),
+        ],
+        compiler_params=kernel_params(32),
+        cost_estimate=pl.CostEstimate(
+            flops=2 * seq * width * (total_width + q_width) + 10 * seq * seq * q_width,
+            bytes_accessed=2 * (seq * width * 3 + width * (total_width + q_width)),
+            transcendentals=seq * seq * (q_width // HEAD_DIM),
+        ),
+    )(*grads, rows, w_qkv, w_out, qkv, logs, *tables)
+    return outs[:4], outs[4], outs[5], outs[6]
+
+
+def assemble_body(members, *refs):
+    shards, (qkv, out), sems = refs[:8], refs[8:10], refs[10]
+    share = shards[0].shape[1]
+    q_part = out.shape[1] // 4
+    front = qkv.shape[3]
+    copies = []
+    for r in range(8):
+        copies.append(
+            pltpu.make_async_copy(
+                shards[r].at[:, :, :front], qkv.at[:, members[r]], sems.at[5 * r]
+            )
+        )
+        for j in range(4):
+            copies.append(
+                pltpu.make_async_copy(
+                    shards[r].at[j, :, front:],
+                    out.at[
+                        pl.ds(pl.multiple_of(members[r] * share, share), share),
+                        j * q_part : (j + 1) * q_part,
+                    ],
+                    sems.at[5 * r + 1 + j],
+                )
+            )
+    for copy in copies:
+        copy.start()
+    for copy in copies:
+        copy.wait()
+
+
+def assemble(members, shards, front):
+    four, share, width = shards[0].shape
+    q_part = width - front
+    return pl.pallas_call(
+        assemble_body,
+        in_specs=[pl.BlockSpec(memory_space=pltpu.SMEM)] + [anywhere()] * 8,
+        out_specs=[anywhere()] * 2,
+        out_shape=[shaped((four, 8, share, front)), shaped((8 * share, four * q_part))],
+        scratch_shapes=[pltpu.SemaphoreType.DMA((40,))],
+    )(members, *shards)
+
+
+def rotate_ranks(values_in, axis_name, total, target_of):
+    return lax.ppermute(values_in, axis_name, [(i, target_of(i)) for i in range(total)])
+
+
+def swap_y(values_in):
+    return rotate_ranks(values_in, "fsdp", 8, lambda i: i ^ 1)
+
+
+def move_z(values_in, steps):
+    return rotate_ranks(values_in, "fsdp", 8, lambda i: (i + 2 * steps) % 8)
+
+
+def swap_core(values_in):
+    return rotate_ranks(values_in, "ctx", 4, lambda i: i ^ 1)
+
+
+def swap_x(values_in):
+    return rotate_ranks(values_in, "ctx", 4, lambda i: i ^ 2)
+
+
+def after(value, *others):
+    return lax.optimization_barrier((value, *others))[0]
+
+
+def wide(value):
+    return value.astype(jnp.float32)
+
+
+def fsdp_members(index):
+    z, y = index // 2, index % 2
+    return [((z + dz) % 4) * 2 + (y ^ dy) for dz in (0, 3, 1, 2) for dy in (0, 1)]
+
+
+def gather_fsdp(block, work):
+    half = block.shape[0] // 2
+    below = move_z(block, 1)
+    own = (block, swap_y(block))
+    work(0, own)
+    above = move_z(after(block, below), -1)
+    below = (below, swap_y(below))
+    work(1, below)
+    far_first = move_z(after(below[0][:half], above), 1)
+    far_second = move_z(above[half:], -1)
+    above = (above, swap_y(above))
+    work(2, above)
+    far = jnp.concatenate([far_first, far_second], 0)
+    far = (far, swap_y(far))
+    work(3, far)
+    return [*own, *below, *above, *far]
+
+
+def scatter_fsdp(parts, beside=(0.0, 0.0, 0.0)):
+    half = parts[0].shape[0] // 2
+    low = jnp.bfloat16
+    far = (wide(parts[6]) + wide(swap_y(parts[7]))).astype(low)
+    above = wide(parts[4]) + wide(swap_y(parts[5]))
+    far = after(far, beside[0])
+    first, second = move_z(far[:half], 1), move_z(far[half:], -1)
+    below = wide(parts[2]) + wide(swap_y(after(parts[3], far)))
+    above = jnp.concatenate([above[:half] + wide(first), above[half:]], 0).astype(low)
+    from_below = move_z(after(above, beside[1]), 1)
+    own = wide(parts[0]) + wide(swap_y(after(parts[1], above)))
+    below = jnp.concatenate([below[:half], below[half:] + wide(second)], 0).astype(low)
+    from_above = move_z(after(below, beside[2]), -1)
+    return own + wide(from_below) + wide(from_above)
+
+
+def gather_ctx(block):
+    across = swap_x(block)
+    return [block, swap_core(block), across, swap_core(across)]
+
+
+def scatter_ctx(parts, *beside):
+    across = wide(parts[2]) + wide(swap_core(parts[3]))
+    own = wide(parts[0]) + wide(swap_core(parts[1]))
+    across = swap_x(across.astype(jnp.bfloat16))
+    if beside:
+        across = after(across, *beside)
+    return own + wide(across)
+
+
+def split_ranks(
+    hidden_in,
+    w_query,
+    w_key_value,
+    w_output,
+    w_router,
+    norm_gains,
+    w_gate_up,
+    w_down,
+    expert_ids,
+    out_grad,
+):
+    both = ("ctx", "fsdp")
+    ctx_total, groups = 4, 8
+    ctx_index, group_index = lax.axis_index("ctx"), lax.axis_index("fsdp")
+    row_count, model_width = hidden_in.shape[1], hidden_in.shape[2]
+    layer_total, share, _ = w_query.shape
+    experts_here = w_gate_up.shape[1]
+    expert_total = experts_here * groups
+    kv_width = w_key_value.shape[2] // 2
+    q_part, kv_part = model_width // ctx_total, kv_width // ctx_total
+    qkv_part = q_part + 2 * kv_part
+    pair_total = groups // 2
+    low = jnp.bfloat16
+    f32 = jnp.float32
+
+    def dot_tn(a, b):
+        return mm(a, b, TN)
+
+    members = jnp.stack(fsdp_members(group_index)).astype(jnp.int32)
+    expert_lane = jnp.arange(128, dtype=jnp.int32)
+    own_experts = (
+        expert_lane[None, :] == group_index * experts_here + jnp.arange(8, dtype=jnp.int32)[:, None]
+    ).astype(f32)
+    places = jnp.concatenate(
+        [row_positions((ctx_index ^ r) * row_count, row_count, row_count, ctx_total) for r in range(4)]
+    )
+    half_dim = HEAD_DIM // 2
+    frequency = rope_base ** (-jnp.arange(half_dim, dtype=f32) / half_dim)
+    angles = places.astype(f32)[:, None] * frequency[None, :]
+    cosine, sine = jnp.cos(angles), jnp.sin(angles)
+    tables = (
+        jnp.concatenate([cosine] * 4, -1),
+        jnp.concatenate([-sine, sine, -sine, sine], -1),
+        places[:, None],
+        places[None, :],
+    )
+
+    hidden_rows = gather_ctx(hidden_in.reshape(row_count, model_width))
+    small = jnp.concatenate(
+        [norm_gains[i] for i in range(layer_total)] + [w_router[i] for i in range(layer_total)], -1
+    )
+    small_width = small.shape[1]
+    ids = expert_ids.reshape(layer_total, row_count, TOP)
+
+    def weight_blocks(i, *more):
+        blocks = jnp.concatenate(
+            [
+                w_query[i].reshape(share, ctx_total, q_part),
+                w_key_value[i, :, :kv_width].reshape(share, ctx_total, kv_part),
+                w_key_value[i, :, kv_width:].reshape(share, ctx_total, kv_part),
+                *more,
+            ],
+            -1,
+        ).transpose(1, 0, 2)
+        return lax.all_to_all(blocks, "ctx", split_axis=0, concat_axis=0, tiled=True)
+
+    def out_blocks(i):
+        return w_output[i].reshape(share, ctx_total, q_part).transpose(1, 0, 2)
+
+    front = qkv_part + 128
+    blocks = weight_blocks(
+        0, jnp.broadcast_to(small[:, None, :], (share, ctx_total, small_width))
+    )
+    ids_low = jnp.concatenate([ids[i] for i in range(layer_total)], -1).astype(low)
+    ids_width = ids_low.shape[1]
+    ids_low = jnp.pad(ids_low, ((0, ctx_total * share - row_count), (0, 0)))
+    packed = jnp.concatenate(
+        [
+            blocks,
+            ids_low.reshape(ctx_total, share, ids_width),
+            jnp.zeros((ctx_total, share, front - qkv_part - small_width - ids_width), low),
+            out_blocks(0),
+        ],
+        -1,
+    )
+    shards = gather_fsdp(packed.reshape(ctx_total * share, front + q_part), lambda *_: None)
+    shards = [shard.reshape(ctx_total, share, front + q_part) for shard in shards]
+    qkv_weight, out_weight = assemble(members, shards, front)
+    qkv_weight = qkv_weight.reshape(model_width, front)
+    small = qkv_weight[:, qkv_part : qkv_part + small_width]
+    ids_all = jnp.concatenate(
+        [
+            shard[..., qkv_part + small_width : qkv_part + small_width + ids_width].reshape(
+                ctx_total * share, ids_width
+            )[:row_count]
+            for shard in shards
+        ],
+        0,
+    ).astype(jnp.int32)
+    gains = [wide(small[:, 2 * i : 2 * i + 2]) for i in range(layer_total)]
+    routers, masks = [], []
+    for i in range(layer_total):
+        at = 2 * layer_total + expert_total * i
+        routers.append(jnp.pad(small[:, at : at + expert_total], ((0, 0), (0, 128 - expert_total))))
+        chosen = jnp.any(
+            ids_all[:, TOP * i : TOP * (i + 1), None] == expert_lane[None, None, :], 1
+        )
+        masks.append(jnp.where(chosen, 0.0, masked_score).astype(f32))
+
+    attention_weights = [(qkv_weight, out_weight)]
+    for i in range(1, layer_total):
+        packed = jnp.concatenate([weight_blocks(i), out_blocks(i)], -1)
+        gathered = lax.all_gather(packed, "fsdp", axis=0, tiled=False)
+        attention_weights.append(
+            (
+                gathered[..., :qkv_part].transpose(1, 0, 2, 3).reshape(model_width, qkv_part),
+                gathered[..., qkv_part:].transpose(0, 2, 1, 3).reshape(q_part, model_width),
+            )
+        )
+    expert_weights = [
+        (
+            lax.all_gather(w_gate_up[i], "ctx", axis=1, tiled=True),
+            lax.all_gather(w_down[i], "ctx", axis=1, tiled=True),
+        )
+        for i in range(layer_total)
+    ]
+
+    residual = wide(hidden_in.reshape(row_count, model_width))
+    saved = []
+    for i in range(layer_total):
+        qkv_weight, out_weight = attention_weights[i]
+        normed, root_first = rms_scaled(residual, gains[i][:, 0])
+        if i == 0:
+            rows = [
+                rms_scaled(wide(block), gains[i][:, 0])[0].astype(low) for block in hidden_rows
+            ]
+        else:
+            rows = gather_ctx(normed.astype(low))
+        branch, rows_first, qkv, attended, logs = attention_forward(
+            rows, qkv_weight, out_weight, qkv_part, tables
+        )
+        middle = residual + scatter_ctx(branch)
+        normed_second, root_second = rms_scaled(middle, gains[i][:, 1])
+        parts, kept = [None] * groups, []
+
+        def forward_work(group, pair):
+            outs = experts_forward(
+                group, pair_total, pair, masks[i], routers[i], own_experts, *expert_weights[i], kept
+            )
+            parts[2 * group], parts[2 * group + 1] = outs[:2]
+            kept[:] = outs[2:]
+
+        gather_fsdp(normed_second.astype(low), forward_work)
+        rows_second, gate, up, probs = kept
+        expert_sum = scatter_fsdp(parts)
+        saved.append(
+            (
+                residual, root_first, rows_first, qkv, attended, logs,
+                middle, root_second, rows_second, gate, up, probs, expert_sum,
+            )
+        )
+        residual = middle + expert_sum
+    hidden_out = residual.reshape(1, row_count, model_width).astype(low)
+    grad = wide(out_grad.reshape(row_count, model_width))
+    attention_grads, expert_grads, small_grads = [], [], []
+    for i in reversed(range(layer_total)):
+        (
+            residual, root_first, rows_first, qkv, attended, logs,
+            middle, root_second, rows_second, gate, up, probs, expert_sum,
+        ) = saved[i]
+        qkv_weight, out_weight = attention_weights[i]
+        mean_gate = jnp.sum(grad * expert_sum, -1, keepdims=True)
+        mean_high = mean_gate.astype(low)
+        mean_low = (mean_gate - wide(mean_high)).astype(low)
+        sent = jnp.concatenate(
+            [grad.astype(low), mean_high, mean_low, jnp.zeros((row_count, 126), low)], -1
+        )
+        parts, kept = [None] * groups, []
+
+        def backward_work(group, pair):
+            outs = experts_backward(
+                group, pair_total, pair, probs, gate, up, routers[i], own_experts,
+                *expert_weights[i], kept,
+            )
+            parts[2 * group], parts[2 * group + 1] = outs[:2]
+            kept[:] = outs[2:]
+
+        gather_fsdp(sent, backward_work)
+        grads_second, grad_gate, grad_up, hidden, grad_logits = kept
+        gate_grads = dot_tn(rows_second, grad_gate).astype(low)
+        up_grads = dot_tn(rows_second, grad_up).astype(low)
+        down_grads = dot_tn(hidden, grads_second).astype(low)
+        grad_router = dot_tn(rows_second, grad_logits)[:, :expert_total]
+        grad_second = scatter_fsdp(parts, (gate_grads, up_grads, down_grads))
+        expert_grads.insert(
+            0,
+            (
+                lax.psum_scatter(gate_grads, "ctx", scatter_dimension=0, tiled=True),
+                lax.psum_scatter(up_grads, "ctx", scatter_dimension=0, tiled=True),
+                lax.psum_scatter(
+                    down_grads.reshape(experts_here, FE, model_width),
+                    "ctx",
+                    scatter_dimension=1,
+                    tiled=True,
+                ),
+            ),
+        )
+        grad_middle, gain_second = rms_back(middle, root_second, gains[i][:, 1], grad_second)
+        grad_middle = grad_middle + grad
+        back, rows_branch, grad_qkv, gain_first = attention_backward(
+            gather_ctx(grad_middle.astype(low)), rows_first, qkv_weight, out_weight, qkv, logs, tables
+        )
+        gain_first = gain_first[0] / gains[i][:, 0]
+        qkv_grads = dot_tn(rows_first, grad_qkv).astype(low)
+        out_grads = dot_tn(attended, rows_branch).astype(low)
+        grad_first = scatter_ctx(back, qkv_grads, out_grads)
+        grad_input, _ = rms_back(residual, root_first, gains[i][:, 0], grad_first)
+        grad = grad_input + grad_middle
+        qkv_grads = qkv_grads.reshape(ctx_total, groups, share, qkv_part)
+        out_grads = out_grads.reshape(groups, share, ctx_total, q_part)
+        if i == 0:
+            packs = [
+                jnp.concatenate(
+                    [
+                        lax.dynamic_index_in_dim(qkv_grads, members[r], 1, False),
+                        lax.dynamic_index_in_dim(out_grads, members[r], 0, False).transpose(1, 0, 2),
+                    ],
+                    -1,
+                ).reshape(ctx_total * share, qkv_part + q_part)
+                for r in range(groups)
+            ]
+            packed = scatter_fsdp(packs).reshape(ctx_total, share, qkv_part + q_part)
+        else:
+            packed = jnp.concatenate(
+                [qkv_grads.transpose(1, 0, 2, 3), out_grads.transpose(0, 2, 1, 3)], -1
+            ).reshape(groups * ctx_total, share, qkv_part + q_part)
+            packed = lax.psum_scatter(packed, "fsdp", scatter_dimension=0, tiled=True)
+        query_blocks = lax.all_to_all(
+            packed[..., :qkv_part].astype(low), "ctx", split_axis=0, concat_axis=0, tiled=True
+        )
+        query_blocks = wide(query_blocks.transpose(1, 0, 2))
+        attention_grads.insert(
+            0,
+            (
+                query_blocks[..., :q_part].reshape(share, model_width),
+                jnp.concatenate(
+                    [
+                        query_blocks[..., q_part : q_part + kv_part].reshape(share, kv_width),
+                        query_blocks[..., q_part + kv_part :].reshape(share, kv_width),
+                    ],
+                    -1,
+                ),
+                wide(packed[..., qkv_part:].transpose(1, 0, 2).reshape(share, model_width)),
+            ),
+        )
+        small_grads.insert(
+            0,
+            lax.psum_scatter(
+                jnp.concatenate([grad_router, gain_first[:, None], gain_second[:, None]], -1),
+                both,
+                scatter_dimension=0,
+                tiled=True,
+            ),
+        )
+    small_sum = jnp.stack(small_grads)
+    gate_up_out = [
+        jnp.concatenate(
+            [part.reshape(model_width // ctx_total, experts_here, FE) for part in grads[:2]], -1
+        ).transpose(1, 0, 2)
+        for grads in expert_grads
+    ]
+    return (
+        hidden_out,
+        grad.reshape(1, row_count, model_width),
+        jnp.stack([g[0] for g in attention_grads]),
+        jnp.stack([g[1] for g in attention_grads]),
+        jnp.stack([g[2] for g in attention_grads]),
+        small_sum[..., :expert_total],
+        small_sum[..., expert_total:],
+        wide(jnp.stack(gate_up_out)),
+        wide(jnp.stack([g[2] for g in expert_grads])),
+    )
+
+
 def solution(mesh):
+    split = mesh.shape["ctx"] == 4 and mesh.shape["fsdp"] == 8
     return jax.shard_map(
-        on_device,
+        split_ranks if split else on_device,
         mesh=mesh,
         in_specs=(
             P("fsdp", "ctx", None),

time: 2620 us -> 1310 us (0.50)
  waiting for transfers between devices: 1490 us -> 562 us
  blocking collectives: 592 us -> 0 us
  Pallas kernels: 0 us -> 259 us
  matrix products: 179 us -> 54.4 us
  starting transfers between devices: 35.9 us -> 133 us
    reduce_scatter x7, waiting for transfers between devices: 754 us -> 173 us  [the longest x2 79.9 us: split_ranks(): lax.psum_scatter(down_grads.reshape(experts_here, FE, model_width), 'ctx'...]
    all_gather x4 -> x0, blocking collectives: 482 us -> none  [the longest x2 338 us: on_device(): lax.all_gather(w_router[layer_index], ('ctx', 'fsdp'), axis=0, tiled=True)]
    all_to_all x7 -> x4, waiting for transfers between devices: 429 us -> 36.7 us  [the longest x2 26.1 us: weight_blocks(): lax.all_to_all(blocks, 'ctx', split_axis=0, concat_axis=0, tiled=True)]
    ppermute x0 -> x104, waiting for transfers between devices: none -> 288 us  [rotate_ranks(): lax.ppermute(values_in, axis_name, [(i, target_of(i)) for i in range(tota...]
    pallas_call x0 -> x21, Pallas kernels: none -> 259 us  [the longest x1 109 us: assemble(): pl.pallas_call(assemble_body, in_specs=[pl.BlockSpec(memory_space=pltpu.S...]
    all_gather x12 -> x5, waiting for transfers between devices: 188 us -> 0.01 us  [the longest x2 0.01 us: split_ranks(): lax.all_gather(w_down[i], 'ctx', axis=1, tiled=True)]
    dot_general x92 -> x12, matrix products: 179 us -> 54.4 us  [mm(): return lax.dot_general(a, b, dims, preferred_element_type=jnp.float32)]
    ppermute x0 -> x104, starting transfers between devices: none -> 117 us  [rotate_ranks(): lax.ppermute(values_in, axis_name, [(i, target_of(i)) for i in range(tota...]
  transfers between devices with their start and end apart: 28 -> 122, of which waited for: 20 -> 66; matrix products, arithmetic and copies ran while one was open for 12% -> 17% of each run, Pallas kernels for 0% -> 19%
where the time goes in v2:
time: 1310 us; the launch traced here: 1300 us
  waiting for transfers between devices  562 us (43%)
  Pallas kernels  259 us (20%)
  local copies, waits for them, and re-layouts  188 us (14%)
  starting transfers between devices  133 us (10%)
  other arithmetic  87.8 us (7%)
  matrix products  54.4 us (4%)
  between operations  17.2 us (1%)
    ppermute x104, waiting for transfers between devices, rotate_ranks(): lax.ppermute(values_in, axis_name, [(i, target_of(i)) for i in range(tota...  288 us
    ppermute x104, starting transfers between devices, rotate_ranks(): lax.ppermute(values_in, axis_name, [(i, target_of(i)) for i in range(tota...  117 us
    pallas_call x1, Pallas kernels, assemble(): pl.pallas_call(assemble_body, in_specs=[pl.BlockSpec(memory_space=pltpu.S...  109 us
    unnamed x460, local copies, waits for them, and re-layouts  104 us
    reduce_scatter x2, waiting for transfers between devices, split_ranks(): lax.psum_scatter(down_grads.reshape(experts_here, FE, model_width), 'ctx'...  79.9 us
    unnamed x16, waiting for transfers between devices  65.1 us
    pallas_call x8, Pallas kernels, experts_backward(): pl.pallas_call(experts_backward_body, grid=(expert_count, steps), in_spec...  64.5 us
    dot_general x12, matrix products, mm(): return lax.dot_general(a, b, dims, preferred_element_type=jnp.float32)  54.4 us
  transfers between devices with their start and end apart: 122, of which 66 were waited for; matrix products, arithmetic and copies ran while one was open for 17% of the time, Pallas kernels for 19%

profile of v2, /device:TPU:0, one launch (start us, length us, event | category | flops | bytes accessed | tf_op | source)
XLA Modules:
  0.0 1301.2 jit_solution(5838150242825422338)
XLA Ops:
  18.3 7.4 all-to-all-done.1
  33.8 18.7 %all-to-all-done = bf16[4,48,676]{2,1,0:T(8,128)(2,1)S(1)} async-done(((bf16[4,48,676]{2,1,0:T(8,128)(2,1)}), bf16[4,48,676]{2,1,0:T(8,128)(2,1)S(1)}, u32[]{:S(2)}, u32[]{:S(2)}) %all-to-all-start) | async-done | bytes 259616 | tf_op jit(solution)/shard_map/all_to_all | solution.py:1045
  56.6 9.7 collective-permute-done.1
  79.7 4.4 collective-permute-start.6
  93.8 9.5 collective-permute-done.4
  103.2 6.2 collective-permute-done.7
  110.3 109.3 %shard_map.169 = (bf16[4,8,48,768]{3,2,1,0:T(8,128)(2,1)}, bf16[384,1536]{1,0:T(8,128)(2,1)}) custom-call(s32[8]{0:T(128)} %stack.78.members, bf16[4,48,1152]{2,1,0:T(8,128)(2,1)} %concatenate.191.refs_0_, bf16[4,48,1152]{2,1,0:T(8,128)(2,1)} %bitcast.20.refs_1_, bf16[4,48,1152]{2,1,0:T(8,128)(2,1)} %bitcast.315, bf16[4,48,1152]{2,1,0:T(8,128)(2,1)} %bitcast.348, ...), custom_call_target="tpu_custom_call" | custom-call | tf_op jit(solution)/shard_map/pallas_call | solution.py:890
  225.2 8.1 shard_map.170
  278.3 11.3 collective-permute-done.15.rows_0
  290.5 5.8 fusion
  321.3 5.2 shard_map.171
  326.5 6.2 shard_map.172
  333.5 6.1 shard_map.173
  341.1 6.8 shard_map.174
  356.0 9.6 collective-permute-done.23
  398.5 10.3 collective-permute-done.31.rows_2
  414.0 8.9 shard_map.175
  425.4 11.0 collective-permute-done.35
  442.9 8.0 collective-permute-done.37.rows_0
  452.4 6.7 fusion.1
  472.3 6.3 shard_map.176
  486.8 6.2 shard_map.177
  495.2 6.0 shard_map.178
  501.2 5.3 shard_map.179
  510.2 8.7 collective-permute-done.45
  519.0 6.6 collective-permute-done.41
  530.1 5.6 collective-permute-done.49
  557.6 13.8 %collective-permute-done.53.grads_0 = bf16[128,1664]{1,0:T(8,128)(2,1)S(1)} collective-permute-done((bf16[128,1664]{1,0:T(8,128)(2,1)}, bf16[128,1664]{1,0:T(8,128)(2,1)S(1)}, u32[]{:S(2)}, u32[]{:S(2)}) %collective-permute-start.53) | collective-permute-done | bytes 426016 | tf_op jit(solution)/shard_map/ppermute | solution.py:900
  574.7 7.3 collective-permute-done.54.grads_0
  592.9 7.5 shard_map.180
  609.8 7.5 shard_map.181
  618.9 8.2 shard_map.182
  628.0 8.2 shard_map.183
  643.2 5.3 convolution_convert_fusion.5
  648.5 7.6 convolution_convert_fusion.4
  656.1 7.8 convolution_convert_fusion.3
  667.4 4.3 collective-permute-start.66
  677.5 4.6 collective-permute-start.67
  693.1 7.2 collective-permute-done.69.grad_2
  702.3 9.5 shard_map.184
  736.9 4.4 collective-permute-done.73
  753.2 11.9 collective-permute-done.75.grads_0
  769.4 7.1 collective-permute-done.76.grads_0
  788.8 8.3 shard_map.185
  800.6 4.7 collective-permute-done.81
  806.4 8.3 shard_map.186
  816.2 8.9 shard_map.187
  826.2 7.5 shard_map.188
  840.3 4.9 convolution_convert_fusion.1
  845.1 6.7 convolution_convert_fusion.2
  852.9 7.7 convolution_convert_fusion
  889.0 16.2 %collective-permute-done.91.grad_2 = bf16[128,1536]{1,0:T(8,128)(2,1)} collective-permute-done((bf16[128,1536]{1,0:T(8,128)(2,1)S(1)}, bf16[128,1536]{1,0:T(8,128)(2,1)}, u32[]{:S(2)}, u32[]{:S(2)}) %collective-permute-start.91) | collective-permute-done | bytes 393248 | tf_op jit(solution)/shard_map/ppermute | solution.py:900
  915.2 11.0 shard_map.189
  966.0 61.8 %reduce-scatter.28.cloned.1.call-done = f32[48,18]{1,0:T(8,128)} async-done(((f32[1536,18]{1,0:T(8,128)}), f32[48,18]{1,0:T(8,128)}) %reduce-scatter.28.cloned.1.call-update) | async-done | bytes 3472
  1044.0 8.2 collective-permute-done.101
  1058.1 16.5 %collective-permute-done.100 = bf16[192,1024]{1,0:T(8,128)(2,1)S(1)} collective-permute-done((bf16[192,1024]{1,0:T(8,128)(2,1)S(1)}, bf16[192,1024]{1,0:T(8,128)(2,1)S(1)}, u32[]{:S(2)}, u32[]{:S(2)}) %collective-permute-start.100) | collective-permute-done | bytes 393248 | tf_op jit(solution)/shard_map/ppermute | solution.py:900
  1074.6 11.8 collective-permute-done.103
  1091.7 5.6 all-to-all-done.2
  1098.6 27.1 %reduce-scatter.14.cloned.1.call-done = bf16[4,48,1024]{2,1,0:T(8,128)(2,1)} async-done(((bf16[32,48,1024]{2,1,0:T(8,128)(2,1)}), bf16[4,48,1024]{2,1,0:T(8,128)(2,1)}) %reduce-scatter.14.cloned.1.call-update) | async-done | bytes 393232 | tf_op jit(solution)/shard_map/reduce_scatter | solution.py:1217
  1132.9 5.0 all-to-all-done.3
  1139.9 26.3 %reduce-scatter.18.cloned.1.call-done = bf16[384,1024]{1,0:T(8,128)(2,1)} async-done(((bf16[1536,1024]{1,0:T(8,128)(2,1)}), bf16[384,1024]{1,0:T(8,128)(2,1)}) %reduce-scatter.18.cloned.1.call-update) | async-done | bytes 786448 | tf_op jit(solution)/shard_map/reduce_scatter | solution.py:1179
  1167.4 39.4 %reduce-scatter.16.cloned.1.call-done = bf16[384,1024]{1,0:T(8,128)(2,1)} async-done(((bf16[1536,1024]{1,0:T(8,128)(2,1)}), bf16[384,1024]{1,0:T(8,128)(2,1)}) %reduce-scatter.16.cloned.1.call-update) | async-done | bytes 786448 | tf_op jit(solution)/shard_map/reduce_scatter | solution.py:1178
  1207.9 39.3 %reduce-scatter.26.cloned.1.call-done = bf16[2,128,1536]{2,1,0:T(8,128)(2,1)} async-done(((bf16[2,512,1536]{2,1,0:T(8,128)(2,1)}), bf16[2,128,1536]{2,1,0:T(8,128)(2,1)}) %reduce-scatter.26.cloned.1.call-update) | async-done | bytes 786448 | tf_op jit(solution)/shard_map/reduce_scatter | solution.py:1180
  1247.3 40.6 %reduce-scatter.24.cloned.1.call-done = bf16[2,128,1536]{2,1,0:T(8,128)(2,1)} async-done(((bf16[2,512,1536]{2,1,0:T(8,128)(2,1)}), bf16[2,128,1536]{2,1,0:T(8,128)(2,1)}) %reduce-scatter.24.cloned.1.call-update) | async-done | bytes 786448 | tf_op jit(solution)/shard_map/reduce_scatter | solution.py:1180
  (945 shorter events, 482.3 us)
Async XLA Ops:
  7.2 306.4 %all-gather.13.cloned.1.call-start = ((), (), s32[]{:S(2)}) async-start(), calls=%async_computation.21 | async-start | bytes 3932160 | tf_op jit(solution)/shard_map/all_gather | solution.py:1103
  10.0 303.5 %all-gather.11.cloned.1.call-start = ((), (), s32[]{:S(2)}) async-start(), calls=%async_computation.20 | async-start | bytes 7864320 | tf_op jit(solution)/shard_map/all_gather | solution.py:1102
  18.2 390.7 %all-gather.15.cloned.1.call-start = ((), (), s32[]{:S(2)}) async-start(), calls=%async_computation.22 | async-start | bytes 3538944 | tf_op jit(solution)/shard_map/all_gather | solution.py:1093
  26.5 46.9 %collective-permute-start.9 = (bf16[128,1536]{1,0:T(8,128)(2,1)S(1)}, bf16[128,1536]{1,0:T(8,128)(2,1)S(1)}, u32[]{:S(2)}, u32[]{:S(2)}) collective-permute-start(bf16[128,1536]{1,0:T(8,128)(2,1)S(1)} %bitcast.294), channel_id=1, source_target_pairs={{0,16},{8,24},{16,0},{24,8},{1,17},{9,25},{17,1},{25,9},{2,18},{10... | collective-permute-start | bytes 1179656 | tf_op jit(solution)/shard_map/ppermute | solution.py:900
  26.6 47.0 %collective-permute-start.8 = (bf16[128,1536]{1,0:T(8,128)(2,1)S(1)}, bf16[128,1536]{1,0:T(8,128)(2,1)S(1)}, u32[]{:S(2)}, u32[]{:S(2)}) collective-permute-start(bf16[128,1536]{1,0:T(8,128)(2,1)S(1)} %bitcast.295), channel_id=1, source_target_pairs={{0,8},{8,0},{16,24},{24,16},{1,9},{9,1},{17,25},{25,17},{2,10},{10... | collective-permute-start | bytes 1179656 | tf_op jit(solution)/shard_map/ppermute | solution.py:900
  27.8 24.7 %all-to-all-start = ((bf16[4,48,676]{2,1,0:T(8,128)(2,1)}), bf16[4,48,676]{2,1,0:T(8,128)(2,1)S(1)}, u32[]{:S(2)}, u32[]{:S(2)}) async-start(bf16[4,48,676]{2,1,0:T(8,128)(2,1)} %maximum_bitcast_fusion.2), calls=%async_computation | async-start | bytes 589824 | tf_op jit(solution)/shard_map/all_to_all | solution.py:1045
  31.2 434.4 %all-gather.19.cloned.1.call-start = ((), (), s32[]{:S(2)}) async-start(), calls=%async_computation.24 | async-start | bytes 3932160 | tf_op jit(solution)/shard_map/all_gather | solution.py:1103
  31.8 433.8 %all-gather.17.cloned.1.call-start = ((), (), s32[]{:S(2)}) async-start(), calls=%async_computation.23 | async-start | bytes 7864320 | tf_op jit(solution)/shard_map/all_gather | solution.py:1102
  52.6 13.6 %collective-permute-start.1 = (bf16[192,1152]{1,0:T(8,128)(2,1)S(1)}, bf16[192,1152]{1,0:T(8,128)(2,1)S(1)}, u32[]{:S(2)}, u32[]{:S(2)}) collective-permute-start(bf16[192,1152]{1,0:T(8,128)(2,1)S(1)} %concatenate.194), channel_id=1, source_target_pairs={{0,2},{1,3},{2,4},{3,5},{4,6},{5,7},{6,0},{7,1},{8,10},{9,11},{10,... | collective-permute-start | bytes 1327112 | tf_op jit(solution)/shard_map/ppermute | solution.py:900
  71.0 19.6 %collective-permute-start = (bf16[192,1152]{1,0:T(8,128)(2,1)}, bf16[192,1152]{1,0:T(8,128)(2,1)}, u32[]{:S(2)}, u32[]{:S(2)}) collective-permute-start(bf16[192,1152]{1,0:T(8,128)(2,1)} %copy-done.184), channel_id=1, source_target_pairs={{0,1},{1,0},{2,3},{3,2},{4,5},{5,4},{6,7},{7,6},{8,9},{9,8},{10,11... | collective-permute-start | bytes 1327112 | tf_op jit(solution)/shard_map/ppermute | solution.py:900
  73.5 16.4 %collective-permute-start.10 = (bf16[128,1536]{1,0:T(8,128)(2,1)S(1)}, bf16[128,1536]{1,0:T(8,128)(2,1)S(1)}, u32[]{:S(2)}, u32[]{:S(2)}) collective-permute-start(bf16[128,1536]{1,0:T(8,128)(2,1)S(1)} %collective-permute-done.9), channel_id=1, source_target_pairs={{0,8},{8,0},{16,24},{24,16},{1,9},{9,1},{17,25},{25,17},{2,10},{10... | collective-permute-start | bytes 1179656 | tf_op jit(solution)/shard_map/ppermute | solution.py:900
  77.5 16.2 %collective-permute-start.2 = (bf16[192,1152]{1,0:T(8,128)(2,1)S(1)}, bf16[192,1152]{1,0:T(8,128)(2,1)S(1)}, u32[]{:S(2)}, u32[]{:S(2)}) collective-permute-start(bf16[192,1152]{1,0:T(8,128)(2,1)S(1)} %collective-permute-done.1), channel_id=1, source_target_pairs={{0,1},{1,0},{2,3},{3,2},{4,5},{5,4},{6,7},{7,6},{8,9},{9,8},{10,11... | collective-permute-start | bytes 1327112 | tf_op jit(solution)/shard_map/ppermute | solution.py:900
  86.7 16.5 %collective-permute-start.4 = (bf16[192,1152]{1,0:T(8,128)(2,1)S(1)}, bf16[192,1152]{1,0:T(8,128)(2,1)S(1)}, u32[]{:S(2)}, u32[]{:S(2)}) collective-permute-start(bf16[192,1152]{1,0:T(8,128)(2,1)S(1)} %collective-permute-done.3), channel_id=1, source_target_pairs={{0,1},{1,0},{2,3},{3,2},{4,5},{5,4},{6,7},{7,6},{8,9},{9,8},{10,11... | collective-permute-start | bytes 1327112 | tf_op jit(solution)/shard_map/ppermute | solution.py:900
  88.3 21.2 %collective-permute-start.7 = (bf16[192,1152]{1,0:T(8,128)(2,1)S(1)}, bf16[192,1152]{1,0:T(8,128)(2,1)S(1)}, u32[]{:S(2)}, u32[]{:S(2)}) collective-permute-start(bf16[192,1152]{1,0:T(8,128)(2,1)S(1)} %constant_dynamic-update-slice_fusion), channel_id=1, source_target_pairs={{0,1},{1,0},{2,3},{3,2},{4,5},{5,4},{6,7},{7,6},{8,9},{9,8},{10,11... | collective-permute-start | bytes 1327112 | tf_op jit(solution)/shard_map/ppermute | solution.py:900
  237.5 18.8 %collective-permute-start.12 = (bf16[128,1536]{1,0:T(8,128)(2,1)}, bf16[128,1536]{1,0:T(8,128)(2,1)}, u32[]{:S(2)}, u32[]{:S(2)}) collective-permute-start(bf16[128,1536]{1,0:T(8,128)(2,1)} %get-tuple-element.189), channel_id=1, source_target_pairs={{0,8},{8,0},{16,24},{24,16},{1,9},{9,1},{17,25},{25,17},{2,10},{10... | collective-permute-start | bytes 1179656 | tf_op jit(solution)/shard_map/ppermute | solution.py:900
  255.9 18.3 %collective-permute-start.11 = (bf16[128,1536]{1,0:T(8,128)(2,1)}, bf16[128,1536]{1,0:T(8,128)(2,1)}, u32[]{:S(2)}, u32[]{:S(2)}) collective-permute-start(bf16[128,1536]{1,0:T(8,128)(2,1)} %copy-done.110), channel_id=1, source_target_pairs={{0,8},{8,0},{16,24},{24,16},{1,9},{9,1},{17,25},{25,17},{2,10},{10... | collective-permute-start | bytes 1179656 | tf_op jit(solution)/shard_map/ppermute | solution.py:900
  258.2 16.0 %collective-permute-start.13 = (bf16[128,1536]{1,0:T(8,128)(2,1)}, bf16[128,1536]{1,0:T(8,128)(2,1)S(1)}, u32[]{:S(2)}, u32[]{:S(2)}) collective-permute-start(bf16[128,1536]{1,0:T(8,128)(2,1)} %add_convert_fusion.9), channel_id=1, source_target_pairs={{0,16},{8,24},{16,0},{24,8},{1,17},{9,25},{17,1},{25,9},{2,18},{10... | collective-permute-start | bytes 1179656 | tf_op jit(solution)/shard_map/ppermute | solution.py:900
  302.0 24.5 %collective-permute-start.18 = (bf16[128,1536]{1,0:T(8,128)(2,1)}, bf16[128,1536]{1,0:T(8,128)(2,1)}, u32[]{:S(2)}, u32[]{:S(2)}) collective-permute-start(bf16[128,1536]{1,0:T(8,128)(2,1)} %collective-permute-done.15.rows_0), channel_id=1, source_target_pairs={{0,1},{1,0},{2,3},{3,2},{4,5},{5,4},{6,7},{7,6},{8,9},{9,8},{10,11... | collective-permute-start | bytes 1179656 | tf_op jit(solution)/shard_map/ppermute | solution.py:900
  307.3 26.2 %collective-permute-start.17 = (bf16[128,1536]{1,0:T(8,128)(2,1)}, bf16[128,1536]{1,0:T(8,128)(2,1)}, u32[]{:S(2)}, u32[]{:S(2)}) collective-permute-start(bf16[128,1536]{1,0:T(8,128)(2,1)} %collective-permute-done.16.rows_0), channel_id=1, source_target_pairs={{0,1},{1,0},{2,3},{3,2},{4,5},{5,4},{6,7},{7,6},{8,9},{9,8},{10,11... | collective-permute-start | bytes 1179656 | tf_op jit(solution)/shard_map/ppermute | solution.py:900
  311.2 29.9 %collective-permute-start.22 = (bf16[128,1536]{1,0:T(8,128)(2,1)}, bf16[128,1536]{1,0:T(8,128)(2,1)}, u32[]{:S(2)}, u32[]{:S(2)}) collective-permute-start(bf16[128,1536]{1,0:T(8,128)(2,1)} %constant_dynamic-update-slice_fusion.10.rows_0), channel_id=1, source_target_pairs={{0,1},{1,0},{2,3},{3,2},{4,5},{5,4},{6,7},{7,6},{8,9},{9,8},{10,11... | collective-permute-start | bytes 1179656 | tf_op jit(solution)/shard_map/ppermute | solution.py:900
  355.1 585.5 %reduce-scatter.30.cloned.1.call-start = ((), (), s32[]{:S(2)}) async-start(), calls=%async_computation.26 | async-start | bytes 811008
  355.2 16.2 %collective-permute-start.19 = (bf16[128,1536]{1,0:T(8,128)(2,1)}, bf16[128,1536]{1,0:T(8,128)(2,1)S(1)}, u32[]{:S(2)}, u32[]{:S(2)}) collective-permute-start(bf16[128,1536]{1,0:T(8,128)(2,1)} %copy-done.112), channel_id=1, source_target_pairs={{0,1},{1,0},{2,3},{3,2},{4,5},{5,4},{6,7},{7,6},{8,9},{9,8},{10,11... | collective-permute-start | bytes 1179656 | tf_op jit(solution)/shard_map/ppermute | solution.py:900
  398.5 15.1 %collective-permute-start.30 = (bf16[128,1536]{1,0:T(8,128)(2,1)}, bf16[128,1536]{1,0:T(8,128)(2,1)}, u32[]{:S(2)}, u32[]{:S(2)}) collective-permute-start(bf16[128,1536]{1,0:T(8,128)(2,1)} %multiply_convert_fusion.1.rows_0), channel_id=1, source_target_pairs={{0,8},{8,0},{16,24},{24,16},{1,9},{9,1},{17,25},{25,17},{2,10},{10... | collective-permute-start | bytes 1179656 | tf_op jit(solution)/shard_map/ppermute | solution.py:900
  441.4 24.2 %collective-permute-start.36 = (bf16[128,1536]{1,0:T(8,128)(2,1)}, bf16[128,1536]{1,0:T(8,128)(2,1)}, u32[]{:S(2)}, u32[]{:S(2)}) collective-permute-start(bf16[128,1536]{1,0:T(8,128)(2,1)} %multiply_convert_fusion.rows_0), channel_id=1, source_target_pairs={{0,1},{1,0},{2,3},{3,2},{4,5},{5,4},{6,7},{7,6},{8,9},{9,8},{10,11... | collective-permute-start | bytes 1179656 | tf_op jit(solution)/shard_map/ppermute | solution.py:900
  450.9 14.1 %collective-permute-start.38 = (bf16[128,1536]{1,0:T(8,128)(2,1)}, bf16[128,1536]{1,0:T(8,128)(2,1)}, u32[]{:S(2)}, u32[]{:S(2)}) collective-permute-start(bf16[128,1536]{1,0:T(8,128)(2,1)} %multiply_convert_fusion.rows_0), channel_id=1, source_target_pairs={{0,6},{1,7},{2,0},{3,1},{4,2},{5,3},{6,4},{7,5},{8,14},{9,15},{10,... | collective-permute-start | bytes 1179656 | tf_op jit(solution)/shard_map/ppermute | solution.py:900
  461.8 24.9 %collective-permute-start.40 = (bf16[128,1536]{1,0:T(8,128)(2,1)}, bf16[128,1536]{1,0:T(8,128)(2,1)}, u32[]{:S(2)}, u32[]{:S(2)}) collective-permute-start(bf16[128,1536]{1,0:T(8,128)(2,1)} %collective-permute-done.37.rows_0), channel_id=1, source_target_pairs={{0,1},{1,0},{2,3},{3,2},{4,5},{5,4},{6,7},{7,6},{8,9},{9,8},{10,11... | collective-permute-start | bytes 1179656 | tf_op jit(solution)/shard_map/ppermute | solution.py:900
  464.9 18.5 %collective-permute-start.42 = (bf16[64,1536]{1,0:T(8,128)(2,1)}, bf16[64,1536]{1,0:T(8,128)(2,1)}, u32[]{:S(2)}, u32[]{:S(2)}) collective-permute-start(bf16[64,1536]{1,0:T(8,128)(2,1)} %slice.461), channel_id=1, source_target_pairs={{0,2},{1,3},{2,4},{3,5},{4,6},{5,7},{6,0},{7,1},{8,10},{9,11},{10,... | collective-permute-start | bytes 589832 | tf_op jit(solution)/shard_map/ppermute | solution.py:900
  486.1 15.1 %collective-permute-start.44 = (bf16[128,1536]{1,0:T(8,128)(2,1)S(1)}, bf16[128,1536]{1,0:T(8,128)(2,1)S(1)}, u32[]{:S(2)}, u32[]{:S(2)}) collective-permute-start(bf16[128,1536]{1,0:T(8,128)(2,1)S(1)} %constant_dynamic-update-slice_fusion.12.rows_0), channel_id=1, source_target_pairs={{0,1},{1,0},{2,3},{3,2},{4,5},{5,4},{6,7},{7,6},{8,9},{9,8},{10,11... | collective-permute-start | bytes 1179656 | tf_op jit(solution)/shard_map/ppermute | solution.py:900
  508.7 17.0 %collective-permute-start.41 = (bf16[128,1536]{1,0:T(8,128)(2,1)S(1)}, bf16[128,1536]{1,0:T(8,128)(2,1)S(1)}, u32[]{:S(2)}, u32[]{:S(2)}) collective-permute-start(bf16[128,1536]{1,0:T(8,128)(2,1)S(1)} %get-tuple-element.233), channel_id=1, source_target_pairs={{0,1},{1,0},{2,3},{3,2},{4,5},{5,4},{6,7},{7,6},{8,9},{9,8},{10,11... | collective-permute-start | bytes 1179656 | tf_op jit(solution)/shard_map/ppermute | solution.py:900
  557.2 14.2 %collective-permute-start.53 = (bf16[128,1664]{1,0:T(8,128)(2,1)}, bf16[128,1664]{1,0:T(8,128)(2,1)S(1)}, u32[]{:S(2)}, u32[]{:S(2)}) collective-permute-start(bf16[128,1664]{1,0:T(8,128)(2,1)} %concatenate.208.grads_0), channel_id=1, source_target_pairs={{0,2},{1,3},{2,4},{3,5},{4,6},{5,7},{6,0},{7,1},{8,10},{9,11},{10,... | collective-permute-start | bytes 1277960 | tf_op jit(solution)/shard_map/ppermute | solution.py:900
  572.7 37.2 %collective-permute-start.56 = (bf16[128,1664]{1,0:T(8,128)(2,1)S(1)}, bf16[128,1664]{1,0:T(8,128)(2,1)S(1)}, u32[]{:S(2)}, u32[]{:S(2)}) collective-permute-start(bf16[128,1664]{1,0:T(8,128)(2,1)S(1)} %collective-permute-done.53.grads_0), channel_id=1, source_target_pairs={{0,1},{1,0},{2,3},{3,2},{4,5},{5,4},{6,7},{7,6},{8,9},{9,8},{10,11... | collective-permute-start | bytes 1277960 | tf_op jit(solution)/shard_map/ppermute | solution.py:900
  582.0 24.4 %collective-permute-start.58 = (bf16[64,1664]{1,0:T(8,128)(2,1)S(1)}, bf16[64,1664]{1,0:T(8,128)(2,1)S(1)}, u32[]{:S(2)}, u32[]{:S(2)}) collective-permute-start(bf16[64,1664]{1,0:T(8,128)(2,1)S(1)} %slice.467), channel_id=1, source_target_pairs={{0,2},{1,3},{2,4},{3,5},{4,6},{5,7},{6,0},{7,1},{8,10},{9,11},{10,... | collective-permute-start | bytes 638984 | tf_op jit(solution)/shard_map/ppermute | solution.py:900
  605.3 13.6 %collective-permute-start.55 = (bf16[128,1664]{1,0:T(8,128)(2,1)S(1)}, bf16[128,1664]{1,0:T(8,128)(2,1)S(1)}, u32[]{:S(2)}, u32[]{:S(2)}) collective-permute-start(bf16[128,1664]{1,0:T(8,128)(2,1)S(1)} %collective-permute-done.54.grads_0), channel_id=1, source_target_pairs={{0,1},{1,0},{2,3},{3,2},{4,5},{5,4},{6,7},{7,6},{8,9},{9,8},{10,11... | collective-permute-start | bytes 1277960 | tf_op jit(solution)/shard_map/ppermute | solution.py:900
  608.7 19.3 %collective-permute-start.60 = (bf16[128,1664]{1,0:T(8,128)(2,1)S(1)}, bf16[128,1664]{1,0:T(8,128)(2,1)S(1)}, u32[]{:S(2)}, u32[]{:S(2)}) collective-permute-start(bf16[128,1664]{1,0:T(8,128)(2,1)S(1)} %constant_dynamic-update-slice_fusion.14.grads_0), channel_id=1, source_target_pairs={{0,1},{1,0},{2,3},{3,2},{4,5},{5,4},{6,7},{7,6},{8,9},{9,8},{10,11... | collective-permute-start | bytes 1277960 | tf_op jit(solution)/shard_map/ppermute | solution.py:900
  627.1 38.1 %collective-permute-start.57 = (bf16[128,1536]{1,0:T(8,128)(2,1)}, bf16[128,1536]{1,0:T(8,128)(2,1)}, u32[]{:S(2)}, u32[]{:S(2)}) collective-permute-start(bf16[128,1536]{1,0:T(8,128)(2,1)} %get-tuple-element.265), channel_id=1, source_target_pairs={{0,1},{1,0},{2,3},{3,2},{4,5},{5,4},{6,7},{7,6},{8,9},{9,8},{10,11... | collective-permute-start | bytes 1179656 | tf_op jit(solution)/shard_map/ppermute | solution.py:900
  642.1 21.8 %collective-permute-start.61 = (bf16[128,1536]{1,0:T(8,128)(2,1)}, bf16[128,1536]{1,0:T(8,128)(2,1)}, u32[]{:S(2)}, u32[]{:S(2)}) collective-permute-start(bf16[128,1536]{1,0:T(8,128)(2,1)} %get-tuple-element.273), channel_id=1, source_target_pairs={{0,1},{1,0},{2,3},{3,2},{4,5},{5,4},{6,7},{7,6},{8,9},{9,8},{10,11... | collective-permute-start | bytes 1179656 | tf_op jit(solution)/shard_map/ppermute | solution.py:900
  725.6 236.7 %reduce-scatter.22.cloned.1.call-start = ((), (), s32[]{:S(2)}) async-start(), calls=%async_computation.17 | async-start | bytes 3932160 | tf_op jit(solution)/shard_map/reduce_scatter | solution.py:1179
  726.3 238.0 %reduce-scatter.20.cloned.1.call-start = ((), (), s32[]{:S(2)}) async-start(), calls=%async_computation.16 | async-start | bytes 3932160 | tf_op jit(solution)/shard_map/reduce_scatter | solution.py:1178
  727.1 14.1 %collective-permute-start.71 = (bf16[128,1536]{1,0:T(8,128)(2,1)}, bf16[128,1536]{1,0:T(8,128)(2,1)S(1)}, u32[]{:S(2)}, u32[]{:S(2)}) collective-permute-start(bf16[128,1536]{1,0:T(8,128)(2,1)} %copy-done.111), channel_id=1, source_target_pairs={{0,8},{8,0},{16,24},{24,16},{1,9},{9,1},{17,25},{25,17},{2,10},{10... | collective-permute-start | bytes 1179656 | tf_op jit(solution)/shard_map/ppermute | solution.py:900
  751.7 13.4 %collective-permute-start.75 = (bf16[128,1664]{1,0:T(8,128)(2,1)}, bf16[128,1664]{1,0:T(8,128)(2,1)}, u32[]{:S(2)}, u32[]{:S(2)}) collective-permute-start(bf16[128,1664]{1,0:T(8,128)(2,1)} %concatenate.212.grads_0), channel_id=1, source_target_pairs={{0,2},{1,3},{2,4},{3,5},{4,6},{5,7},{6,0},{7,1},{8,10},{9,11},{10,... | collective-permute-start | bytes 1277960 | tf_op jit(solution)/shard_map/ppermute | solution.py:900
  766.2 14.5 %collective-permute-start.74 = (bf16[128,1664]{1,0:T(8,128)(2,1)}, bf16[128,1664]{1,0:T(8,128)(2,1)}, u32[]{:S(2)}, u32[]{:S(2)}) collective-permute-start(bf16[128,1664]{1,0:T(8,128)(2,1)} %concatenate.212.grads_0), channel_id=1, source_target_pairs={{0,1},{1,0},{2,3},{3,2},{4,5},{5,4},{6,7},{7,6},{8,9},{9,8},{10,11... | collective-permute-start | bytes 1277960 | tf_op jit(solution)/shard_map/ppermute | solution.py:900
  767.3 260.5 %reduce-scatter.28.cloned.1.call-start = ((), (), s32[]{:S(2)}) async-start(), calls=%async_computation.25 | async-start | bytes 811008
  767.4 39.1 %collective-permute-start.78 = (bf16[128,1664]{1,0:T(8,128)(2,1)}, bf16[128,1664]{1,0:T(8,128)(2,1)S(1)}, u32[]{:S(2)}, u32[]{:S(2)}) collective-permute-start(bf16[128,1664]{1,0:T(8,128)(2,1)} %collective-permute-done.75.grads_0), channel_id=1, source_target_pairs={{0,1},{1,0},{2,3},{3,2},{4,5},{5,4},{6,7},{7,6},{8,9},{9,8},{10,11... | collective-permute-start | bytes 1277960 | tf_op jit(solution)/shard_map/ppermute | solution.py:900
  776.5 24.0 %collective-permute-start.80 = (bf16[64,1664]{1,0:T(8,128)(2,1)S(1)}, bf16[64,1664]{1,0:T(8,128)(2,1)S(1)}, u32[]{:S(2)}, u32[]{:S(2)}) collective-permute-start(bf16[64,1664]{1,0:T(8,128)(2,1)S(1)} %slice.473), channel_id=1, source_target_pairs={{0,2},{1,3},{2,4},{3,5},{4,6},{5,7},{6,0},{7,1},{8,10},{9,11},{10,... | collective-permute-start | bytes 638984 | tf_op jit(solution)/shard_map/ppermute | solution.py:900
  799.4 16.8 %collective-permute-start.77 = (bf16[128,1664]{1,0:T(8,128)(2,1)}, bf16[128,1664]{1,0:T(8,128)(2,1)S(1)}, u32[]{:S(2)}, u32[]{:S(2)}) collective-permute-start(bf16[128,1664]{1,0:T(8,128)(2,1)} %collective-permute-done.76.grads_0), channel_id=1, source_target_pairs={{0,1},{1,0},{2,3},{3,2},{4,5},{5,4},{6,7},{7,6},{8,9},{9,8},{10,11... | collective-permute-start | bytes 1277960 | tf_op jit(solution)/shard_map/ppermute | solution.py:900
  805.3 20.8 %collective-permute-start.82 = (bf16[128,1664]{1,0:T(8,128)(2,1)S(1)}, bf16[128,1664]{1,0:T(8,128)(2,1)S(1)}, u32[]{:S(2)}, u32[]{:S(2)}) collective-permute-start(bf16[128,1664]{1,0:T(8,128)(2,1)S(1)} %constant_dynamic-update-slice_fusion.16.grads_0), channel_id=1, source_target_pairs={{0,1},{1,0},{2,3},{3,2},{4,5},{5,4},{6,7},{7,6},{8,9},{9,8},{10,11... | collective-permute-start | bytes 1277960 | tf_op jit(solution)/shard_map/ppermute | solution.py:900
  825.2 36.7 %collective-permute-start.79 = (bf16[128,1536]{1,0:T(8,128)(2,1)}, bf16[128,1536]{1,0:T(8,128)(2,1)}, u32[]{:S(2)}, u32[]{:S(2)}) collective-permute-start(bf16[128,1536]{1,0:T(8,128)(2,1)} %get-tuple-element.314), channel_id=1, source_target_pairs={{0,1},{1,0},{2,3},{3,2},{4,5},{5,4},{6,7},{7,6},{8,9},{9,8},{10,11... | collective-permute-start | bytes 1179656 | tf_op jit(solution)/shard_map/ppermute | solution.py:900
  888.3 16.9 %collective-permute-start.91 = (bf16[128,1536]{1,0:T(8,128)(2,1)S(1)}, bf16[128,1536]{1,0:T(8,128)(2,1)}, u32[]{:S(2)}, u32[]{:S(2)}) collective-permute-start(bf16[128,1536]{1,0:T(8,128)(2,1)S(1)} %get-tuple-element.363.grad_0), channel_id=1, source_target_pairs={{0,16},{8,24},{16,0},{24,8},{1,17},{9,25},{17,1},{25,9},{2,18},{10... | collective-permute-start | bytes 1179656 | tf_op jit(solution)/shard_map/ppermute | solution.py:900
  889.0 25.5 %collective-permute-start.90 = (bf16[128,1536]{1,0:T(8,128)(2,1)S(1)}, bf16[128,1536]{1,0:T(8,128)(2,1)}, u32[]{:S(2)}, u32[]{:S(2)}) collective-permute-start(bf16[128,1536]{1,0:T(8,128)(2,1)S(1)} %get-tuple-element.363.grad_0), channel_id=1, source_target_pairs={{0,8},{8,0},{16,24},{24,16},{1,9},{9,1},{17,25},{25,17},{2,10},{10... | collective-permute-start | bytes 1179656 | tf_op jit(solution)/shard_map/ppermute | solution.py:900
  934.7 191.1 %reduce-scatter.14.cloned.1.call-start = ((), (), s32[]{:S(2)}) async-start(), calls=%async_computation.13 | async-start | bytes 3538944 | tf_op jit(solution)/shard_map/reduce_scatter | solution.py:1217
  938.2 227.9 %reduce-scatter.18.cloned.1.call-start = ((), (), s32[]{:S(2)}) async-start(), calls=%async_computation.15 | async-start | bytes 3932160 | tf_op jit(solution)/shard_map/reduce_scatter | solution.py:1179
  939.0 267.8 %reduce-scatter.16.cloned.1.call-start = ((), (), s32[]{:S(2)}) async-start(), calls=%async_computation.14 | async-start | bytes 3932160 | tf_op jit(solution)/shard_map/reduce_scatter | solution.py:1178
  939.6 307.7 %reduce-scatter.26.cloned.1.call-start = ((), (), s32[]{:S(2)}) async-start(), calls=%async_computation.19 | async-start | bytes 3932160 | tf_op jit(solution)/shard_map/reduce_scatter | solution.py:1180
  940.3 347.5 %reduce-scatter.24.cloned.1.call-start = ((), (), s32[]{:S(2)}) async-start(), calls=%async_computation.18 | async-start | bytes 3932160 | tf_op jit(solution)/shard_map/reduce_scatter | solution.py:1180
  954.5 80.0 %collective-permute-start.96 = (bf16[192,1024]{1,0:T(8,128)(2,1)}, bf16[192,1024]{1,0:T(8,128)(2,1)}, u32[]{:S(2)}, u32[]{:S(2)}) collective-permute-start(bf16[192,1024]{1,0:T(8,128)(2,1)} %pad_maximum_fusion.13), channel_id=1, source_target_pairs={{0,1},{1,0},{2,3},{3,2},{4,5},{5,4},{6,7},{7,6},{8,9},{9,8},{10,11... | collective-permute-start | bytes 1179656 | tf_op jit(solution)/shard_map/ppermute | solution.py:900
  956.9 75.0 %collective-permute-start.97 = (bf16[192,1024]{1,0:T(8,128)(2,1)}, bf16[192,1024]{1,0:T(8,128)(2,1)}, u32[]{:S(2)}, u32[]{:S(2)}) collective-permute-start(bf16[192,1024]{1,0:T(8,128)(2,1)} %pad_maximum_fusion.14), channel_id=1, source_target_pairs={{0,1},{1,0},{2,3},{3,2},{4,5},{5,4},{6,7},{7,6},{8,9},{9,8},{10,11... | collective-permute-start | bytes 1179656 | tf_op jit(solution)/shard_map/ppermute | solution.py:900
  959.4 80.4 %collective-permute-start.94 = (bf16[128,1536]{1,0:T(8,128)(2,1)S(1)}, bf16[128,1536]{1,0:T(8,128)(2,1)}, u32[]{:S(2)}, u32[]{:S(2)}) collective-permute-start(bf16[128,1536]{1,0:T(8,128)(2,1)S(1)} %get-tuple-element.341), channel_id=1, source_target_pairs={{0,8},{8,0},{16,24},{24,16},{1,9},{9,1},{17,25},{25,17},{2,10},{10... | collective-permute-start | bytes 1179656 | tf_op jit(solution)/shard_map/ppermute | solution.py:900
  959.4 96.9 %collective-permute-start.93 = (bf16[128,1536]{1,0:T(8,128)(2,1)S(1)}, bf16[128,1536]{1,0:T(8,128)(2,1)S(1)}, u32[]{:S(2)}, u32[]{:S(2)}) collective-permute-start(bf16[128,1536]{1,0:T(8,128)(2,1)S(1)} %get-tuple-element.339), channel_id=1, source_target_pairs={{0,8},{8,0},{16,24},{24,16},{1,9},{9,1},{17,25},{25,17},{2,10},{10... | collective-permute-start | bytes 1179656 | tf_op jit(solution)/shard_map/ppermute | solution.py:900
  1035.8 16.3 %collective-permute-start.101 = (bf16[192,1024]{1,0:T(8,128)(2,1)S(1)}, bf16[192,1024]{1,0:T(8,128)(2,1)S(1)}, u32[]{:S(2)}, u32[]{:S(2)}) collective-permute-start(bf16[192,1024]{1,0:T(8,128)(2,1)S(1)} %copy-done.186), channel_id=1, source_target_pairs={{0,1},{1,0},{2,3},{3,2},{4,5},{5,4},{6,7},{7,6},{8,9},{9,8},{10,11... | collective-permute-start | bytes 1179656 | tf_op jit(solution)/shard_map/ppermute | solution.py:900
  1037.4 17.4 %collective-permute-start.102 = (bf16[96,1024]{1,0:T(8,128)(2,1)S(1)}, bf16[96,1024]{1,0:T(8,128)(2,1)S(1)}, u32[]{:S(2)}, u32[]{:S(2)}) collective-permute-start(bf16[96,1024]{1,0:T(8,128)(2,1)S(1)} %get-tuple-element.406), channel_id=1, source_target_pairs={{0,6},{1,7},{2,0},{3,1},{4,2},{5,3},{6,4},{7,5},{8,14},{9,15},{10,... | collective-permute-start | bytes 589832 | tf_op jit(solution)/shard_map/ppermute | solution.py:900
  1040.9 15.4 %collective-permute-start.95 = (bf16[128,1536]{1,0:T(8,128)(2,1)S(1)}, bf16[128,1536]{1,0:T(8,128)(2,1)S(1)}, u32[]{:S(2)}, u32[]{:S(2)}) collective-permute-start(bf16[128,1536]{1,0:T(8,128)(2,1)S(1)} %add_convert_fusion.1), channel_id=1, source_target_pairs={{0,16},{8,24},{16,0},{24,8},{1,17},{9,25},{17,1},{25,9},{2,18},{10... | collective-permute-start | bytes 1179656 | tf_op jit(solution)/shard_map/ppermute | solution.py:900
  1043.6 14.5 %collective-permute-start.99 = (bf16[192,1024]{1,0:T(8,128)(2,1)S(1)}, bf16[192,1024]{1,0:T(8,128)(2,1)S(1)}, u32[]{:S(2)}, u32[]{:S(2)}) collective-permute-start(bf16[192,1024]{1,0:T(8,128)(2,1)S(1)} %copy-done.185), channel_id=1, source_target_pairs={{0,1},{1,0},{2,3},{3,2},{4,5},{5,4},{6,7},{7,6},{8,9},{9,8},{10,11... | collective-permute-start | bytes 1179656 | tf_op jit(solution)/shard_map/ppermute | solution.py:900
  1052.2 22.4 %collective-permute-start.100 = (bf16[192,1024]{1,0:T(8,128)(2,1)S(1)}, bf16[192,1024]{1,0:T(8,128)(2,1)S(1)}, u32[]{:S(2)}, u32[]{:S(2)}) collective-permute-start(bf16[192,1024]{1,0:T(8,128)(2,1)S(1)} %pad_maximum_fusion.15), channel_id=1, source_target_pairs={{0,2},{1,3},{2,4},{3,5},{4,6},{5,7},{6,0},{7,1},{8,10},{9,11},{10,... | collective-permute-start | bytes 1179656 | tf_op jit(solution)/shard_map/ppermute | solution.py:900
  1054.8 31.5 %collective-permute-start.103 = (bf16[192,1024]{1,0:T(8,128)(2,1)S(1)}, bf16[192,1024]{1,0:T(8,128)(2,1)S(1)}, u32[]{:S(2)}, u32[]{:S(2)}) collective-permute-start(bf16[192,1024]{1,0:T(8,128)(2,1)S(1)} %pad_maximum_fusion.17), channel_id=1, source_target_pairs={{0,6},{1,7},{2,0},{3,1},{4,2},{5,3},{6,4},{7,5},{8,14},{9,15},{10,... | collective-permute-start | bytes 1179656 | tf_op jit(solution)/shard_map/ppermute | solution.py:900
  (275 other events, 2480.4 us)
Sparse Core Ops, SparseCore 0:
  10.1 43.8 all-gather.12
  56.2 46.7 all-gather.10
  105.2 60.4 all-gather.14
  167.1 27.1 all-gather.18
  355.2 48.7 all-gather.16
  725.7 95.6 reduce-scatter.29
  823.9 36.8 reduce-scatter.21
  863.5 45.5 reduce-scatter.19
  934.8 92.9 reduce-scatter.27
  1031.8 93.8 reduce-scatter.13
  1128.9 37.2 reduce-scatter.17
  1168.7 37.9 reduce-scatter.15
  1209.3 37.9 reduce-scatter.25
  1249.8 37.9 reduce-scatter.23

commit v3 on v2

--- a/solution.py
+++ b/solution.py
@@ -1,3 +1,4 @@
+import functools
 import math
 
 import jax
@@ -492,6 +493,7 @@
 NT = (((1,), (1,)), ((), ()))
 TN = (((0,), (0,)), ((), ()))
 FE_STEP = 256
+EXPERT_MIB = 58
 
 
 def mm(a, b, dims=NN):
@@ -515,7 +517,7 @@
 
 
 def experts_forward_body(
-    rows_0, rows_1, mask, router, own, w_gate, w_up, w_down, *refs
+    first_id, rows_0, rows_1, ids, router, own, w_gate, w_up, w_down, *refs
 ):
     out_0, out_1, all_rows, all_gate, all_up, all_probs, total = refs[-7:]
     expert, piece = pl.program_id(0), pl.program_id(1)
@@ -527,7 +529,13 @@
     def _():
         all_rows[:count, :] = rows_0[...]
         all_rows[count:, :] = rows_1[...]
-        logits = mm(all_rows[...], router[...]) + mask[...]
+        lane = lax.broadcasted_iota(jnp.int32, all_probs.shape, 1).astype(jnp.float32)
+        chosen_ids = ids[...].astype(jnp.float32)
+        listed = lane == chosen_ids[:, first_id : first_id + 1]
+        for k in range(1, TOP):
+            at = first_id + k
+            listed = jnp.logical_or(listed, lane == chosen_ids[:, at : at + 1])
+        logits = jnp.where(listed, mm(all_rows[...], router[...]), masked_score)
         weights = jnp.exp(logits - jnp.max(logits, -1, keepdims=True))
         all_probs[...] = weights / jnp.sum(weights, -1, keepdims=True)
         total[...] = jnp.zeros_like(total)
@@ -546,7 +554,7 @@
         out_1[...] = total[count:, :].astype(jnp.bfloat16)
 
 
-def experts_forward(group, groups, rows, mask, router, own, w_gate_up, w_down, kept):
+def experts_forward(group, groups, rows, ids, first_id, router, own, w_gate_up, w_down, kept):
     block, width = rows[0].shape
     count = 2 * block
     expert_count, hidden_width = w_down.shape[0], w_down.shape[1]
@@ -554,14 +562,14 @@
     flat = shaped((groups * count, expert_count * hidden_width))
     flat_spec = pl.BlockSpec((count, FE_STEP), lambda e, p: (group, e * steps + p))
     lanes_spec = pl.BlockSpec((count, 128), lambda e, p: (group, 0))
-    inputs = [*rows, mask, router, own, w_gate_up, w_gate_up, w_down, *kept]
+    inputs = [*rows, ids, router, own, w_gate_up, w_gate_up, w_down, *kept]
     return pl.pallas_call(
-        experts_forward_body,
+        functools.partial(experts_forward_body, first_id),
         grid=(expert_count, steps),
         in_specs=[
             whole((block, width)),
             whole((block, width)),
-            lanes_spec,
+            pl.BlockSpec((count, ids.shape[1]), lambda e, p: (group, 0)),
             whole(router.shape),
             whole(own.shape),
             pl.BlockSpec((1, width, FE_STEP), lambda e, p: (e, 0, p)),
@@ -587,7 +595,7 @@
         ],
         input_output_aliases={8 + i: 2 + i for i in range(len(kept))},
         scratch_shapes=[pltpu.VMEM((count, width), jnp.float32)],
-        compiler_params=kernel_params(24),
+        compiler_params=kernel_params(EXPERT_MIB),
         cost_estimate=pl.CostEstimate(
             flops=6 * count * width * expert_count * hidden_width,
             bytes_accessed=6 * width * expert_count * hidden_width,
@@ -700,7 +708,7 @@
             pltpu.VMEM((count, 1), jnp.float32),
             pltpu.VMEM((count, 1), jnp.float32),
         ],
-        compiler_params=kernel_params(24),
+        compiler_params=kernel_params(EXPERT_MIB),
         cost_estimate=pl.CostEstimate(
             flops=6 * count * width * expert_count * hidden_width,
             bytes_accessed=6 * width * expert_count * hidden_width,
@@ -855,44 +863,30 @@
     return outs[:4], outs[4], outs[5], outs[6]
 
 
-def assemble_body(members, *refs):
-    shards, (qkv, out), sems = refs[:8], refs[8:10], refs[10]
+def place_body(members, *refs):
+    shards, outs = refs[:8], refs[8:]
     share = shards[0].shape[1]
-    q_part = out.shape[1] // 4
-    front = qkv.shape[3]
-    copies = []
+    front = outs[0].shape[3]
     for r in range(8):
-        copies.append(
-            pltpu.make_async_copy(
-                shards[r].at[:, :, :front], qkv.at[:, members[r]], sems.at[5 * r]
-            )
-        )
-        for j in range(4):
-            copies.append(
-                pltpu.make_async_copy(
-                    shards[r].at[j, :, front:],
-                    out.at[
-                        pl.ds(pl.multiple_of(members[r] * share, share), share),
-                        j * q_part : (j + 1) * q_part,
-                    ],
-                    sems.at[5 * r + 1 + j],
-                )
-            )
-    for copy in copies:
-        copy.start()
-    for copy in copies:
-        copy.wait()
-
-
-def assemble(members, shards, front):
+        for c in range(4):
+            outs[0][c, members[r]] = shards[r][c, :, :front]
+        for out in outs[1:]:
+            q_part = out.shape[1] // 4
+            span = pl.ds(pl.multiple_of(members[r] * share, share), share)
+            for j in range(4):
+                out[span, j * q_part : (j + 1) * q_part] = shards[r][j, :, front:]
+
+
+def place(members, shards, front):
     four, share, width = shards[0].shape
-    q_part = width - front
+    outs = [shaped((four, 8, share, front))]
+    if width > front:
+        outs.append(shaped((8 * share, four * (width - front))))
     return pl.pallas_call(
-        assemble_body,
-        in_specs=[pl.BlockSpec(memory_space=pltpu.SMEM)] + [anywhere()] * 8,
-        out_specs=[anywhere()] * 2,
-        out_shape=[shaped((four, 8, share, front)), shaped((8 * share, four * q_part))],
-        scratch_shapes=[pltpu.SemaphoreType.DMA((40,))],
+        place_body,
+        in_specs=[pl.BlockSpec(memory_space=pltpu.SMEM)] + [pl.BlockSpec(memory_space=pltpu.VMEM)] * 8,
+        out_shape=outs,
+        compiler_params=kernel_params(16),
     )(members, *shards)
 
 
@@ -929,38 +923,60 @@
     return [((z + dz) % 4) * 2 + (y ^ dy) for dz in (0, 3, 1, 2) for dy in (0, 1)]
 
 
-def gather_fsdp(block, work):
+def gather_fsdp(block, work=None):
     half = block.shape[0] // 2
+    work = work or (lambda *_: 0.0)
     below = move_z(block, 1)
     own = (block, swap_y(block))
-    work(0, own)
     above = move_z(after(block, below), -1)
-    below = (below, swap_y(below))
-    work(1, below)
-    far_first = move_z(after(below[0][:half], above), 1)
+    below_mirror = swap_y(below)
+    done = work(0, (after(own[0], below), own[1]))
+    far_first = move_z(after(below[:half], above, done), 1)
     far_second = move_z(above[half:], -1)
-    above = (above, swap_y(above))
-    work(2, above)
+    above_mirror = swap_y(above)
+    below = (below, below_mirror)
+    done = work(1, (after(below[0], above), below[1]))
     far = jnp.concatenate([far_first, far_second], 0)
-    far = (far, swap_y(far))
+    far_mirror = swap_y(after(far, done))
+    above = (above, above_mirror)
+    work(2, (after(above[0], far), above[1]))
+    far = (far, far_mirror)
     work(3, far)
     return [*own, *below, *above, *far]
 
 
-def scatter_fsdp(parts, beside=(0.0, 0.0, 0.0)):
+def gather_small(block):
+    own = jnp.stack([block, swap_y(block)])
+    return jnp.concatenate([own, move_z(own, 1), move_z(own, -1), move_z(own, 2)], 0)
+
+
+def scatter_fsdp(parts, beside=None):
     half = parts[0].shape[0] // 2
     low = jnp.bfloat16
-    far = (wide(parts[6]) + wide(swap_y(parts[7]))).astype(low)
-    above = wide(parts[4]) + wide(swap_y(parts[5]))
-    far = after(far, beside[0])
+    results = []
+
+    def run(start):
+        if beside:
+            results.append(beside[len(results)](start))
+            return results[-1:]
+        return []
+
+    far_mirror, above_mirror = swap_y(parts[7]), swap_y(parts[5])
+    far = (wide(parts[6]) + wide(far_mirror)).astype(low)
     first, second = move_z(far[:half], 1), move_z(far[half:], -1)
-    below = wide(parts[2]) + wide(swap_y(after(parts[3], far)))
+    below_mirror = swap_y(after(parts[3], far))
+    done = run(far)
+    above = wide(parts[4]) + wide(above_mirror)
     above = jnp.concatenate([above[:half] + wide(first), above[half:]], 0).astype(low)
-    from_below = move_z(after(above, beside[1]), 1)
-    own = wide(parts[0]) + wide(swap_y(after(parts[1], above)))
+    from_below = move_z(after(above, *done), 1)
+    own_mirror = swap_y(after(parts[1], above))
+    done = run(above)
+    below = wide(parts[2]) + wide(below_mirror)
     below = jnp.concatenate([below[:half], below[half:] + wide(second)], 0).astype(low)
-    from_above = move_z(after(below, beside[2]), -1)
-    return own + wide(from_below) + wide(from_above)
+    from_above = move_z(after(below, *done), -1)
+    done = run(below)
+    own = wide(parts[0]) + wide(own_mirror)
+    return after(own + wide(from_below), *done) + wide(from_above), results
 
 
 def gather_ctx(block):
@@ -1003,6 +1019,18 @@
     low = jnp.bfloat16
     f32 = jnp.float32
 
+    core, across = ctx_index % 2, ctx_index // 2
+
+    def cross_core(whole_sum):
+        sent = lax.dynamic_index_in_dim(whole_sum, 1 - core, 1, False)
+        held = lax.dynamic_index_in_dim(whole_sum, core, 1, False)
+        return (wide(held) + wide(swap_core(sent))).astype(low)
+
+    def cross_x(half_sum):
+        sent = lax.dynamic_index_in_dim(half_sum, 1 - across, 0, False)
+        held = lax.dynamic_index_in_dim(half_sum, across, 0, False)
+        return wide(held) + wide(swap_x(sent))
+
     def dot_tn(a, b):
         return mm(a, b, TN)
 
@@ -1030,80 +1058,68 @@
         [norm_gains[i] for i in range(layer_total)] + [w_router[i] for i in range(layer_total)], -1
     )
     small_width = small.shape[1]
-    ids = expert_ids.reshape(layer_total, row_count, TOP)
-
-    def weight_blocks(i, *more):
-        blocks = jnp.concatenate(
-            [
-                w_query[i].reshape(share, ctx_total, q_part),
-                w_key_value[i, :, :kv_width].reshape(share, ctx_total, kv_part),
-                w_key_value[i, :, kv_width:].reshape(share, ctx_total, kv_part),
-                *more,
-            ],
-            -1,
-        ).transpose(1, 0, 2)
-        return lax.all_to_all(blocks, "ctx", split_axis=0, concat_axis=0, tiled=True)
-
-    def out_blocks(i):
-        return w_output[i].reshape(share, ctx_total, q_part).transpose(1, 0, 2)
-
-    front = qkv_part + 128
-    blocks = weight_blocks(
-        0, jnp.broadcast_to(small[:, None, :], (share, ctx_total, small_width))
-    )
-    ids_low = jnp.concatenate([ids[i] for i in range(layer_total)], -1).astype(low)
+    parts = []
+    for i in range(layer_total):
+        parts += [
+            w_query[i].reshape(share, ctx_total, q_part),
+            w_key_value[i, :, :kv_width].reshape(share, ctx_total, kv_part),
+            w_key_value[i, :, kv_width:].reshape(share, ctx_total, kv_part),
+        ]
+    parts.append(jnp.broadcast_to(small[:, None, :], (share, ctx_total, small_width)))
+    blocks = jnp.concatenate(parts, -1).transpose(1, 0, 2)
+    blocks = lax.all_to_all(blocks, "ctx", split_axis=0, concat_axis=0, tiled=True)
+
+    def layer_shard(i):
+        out_blocks = w_output[i].reshape(share, ctx_total, q_part).transpose(1, 0, 2)
+        return jnp.concatenate([blocks[..., i * qkv_part : (i + 1) * qkv_part], out_blocks], -1)
+
+    packed = layer_shard(0).reshape(ctx_total * share, qkv_part + q_part)
+    shards = gather_fsdp(packed)
+    shards = [shard.reshape(ctx_total, share, qkv_part + q_part) for shard in shards]
+    qkv_weight, out_weight = place(members, shards, qkv_part)
+    attention_weights = [(qkv_weight.reshape(model_width, qkv_part), out_weight)]
+
+    ids_low = jnp.concatenate(
+        [expert_ids[i].reshape(row_count, TOP) for i in range(layer_total)], -1
+    ).astype(low)
     ids_width = ids_low.shape[1]
     ids_low = jnp.pad(ids_low, ((0, ctx_total * share - row_count), (0, 0)))
-    packed = jnp.concatenate(
+    small_rows = jnp.concatenate(
         [
-            blocks,
-            ids_low.reshape(ctx_total, share, ids_width),
-            jnp.zeros((ctx_total, share, front - qkv_part - small_width - ids_width), low),
-            out_blocks(0),
+            blocks[..., layer_total * qkv_part :].reshape(ctx_total * share, small_width),
+            ids_low,
+            jnp.zeros((ctx_total * share, 128 - small_width - ids_width), low),
         ],
         -1,
     )
-    shards = gather_fsdp(packed.reshape(ctx_total * share, front + q_part), lambda *_: None)
-    shards = [shard.reshape(ctx_total, share, front + q_part) for shard in shards]
-    qkv_weight, out_weight = assemble(members, shards, front)
-    qkv_weight = qkv_weight.reshape(model_width, front)
-    small = qkv_weight[:, qkv_part : qkv_part + small_width]
-    ids_all = jnp.concatenate(
-        [
-            shard[..., qkv_part + small_width : qkv_part + small_width + ids_width].reshape(
-                ctx_total * share, ids_width
-            )[:row_count]
-            for shard in shards
-        ],
-        0,
-    ).astype(jnp.int32)
+    small_all = gather_small(small_rows)
+    ids_all = small_all[:, :row_count, small_width : small_width + ids_width].reshape(
+        groups * row_count, ids_width
+    )
+    small_all = small_all.reshape(groups, ctx_total, share, 128)
+    small = place(members, [small_all[r] for r in range(groups)], 128)[0].reshape(model_width, 128)
     gains = [wide(small[:, 2 * i : 2 * i + 2]) for i in range(layer_total)]
-    routers, masks = [], []
+    routers = []
     for i in range(layer_total):
         at = 2 * layer_total + expert_total * i
         routers.append(jnp.pad(small[:, at : at + expert_total], ((0, 0), (0, 128 - expert_total))))
-        chosen = jnp.any(
-            ids_all[:, TOP * i : TOP * (i + 1), None] == expert_lane[None, None, :], 1
-        )
-        masks.append(jnp.where(chosen, 0.0, masked_score).astype(f32))
-
-    attention_weights = [(qkv_weight, out_weight)]
-    for i in range(1, layer_total):
-        packed = jnp.concatenate([weight_blocks(i), out_blocks(i)], -1)
-        gathered = lax.all_gather(packed, "fsdp", axis=0, tiled=False)
-        attention_weights.append(
-            (
-                gathered[..., :qkv_part].transpose(1, 0, 2, 3).reshape(model_width, qkv_part),
-                gathered[..., qkv_part:].transpose(0, 2, 1, 3).reshape(q_part, model_width),
+
+    expert_weights = []
+    for i in range(layer_total):
+        if i > 0:
+            gathered = lax.all_gather(
+                after(layer_shard(i), *expert_weights[-1]), "fsdp", axis=0, tiled=False
             )
-        )
-    expert_weights = [
-        (
-            lax.all_gather(w_gate_up[i], "ctx", axis=1, tiled=True),
-            lax.all_gather(w_down[i], "ctx", axis=1, tiled=True),
-        )
-        for i in range(layer_total)
-    ]
+            attention_weights.append(
+                (
+                    gathered[..., :qkv_part].transpose(1, 0, 2, 3).reshape(model_width, qkv_part),
+                    gathered[..., qkv_part:].transpose(0, 2, 1, 3).reshape(q_part, model_width),
+                )
+            )
+        gate_up = w_gate_up[i] if i == 0 else after(w_gate_up[i], gathered)
+        gate_up = lax.all_gather(gate_up, "ctx", axis=1, tiled=True)
+        down = lax.all_gather(after(w_down[i], gate_up), "ctx", axis=1, tiled=True)
+        expert_weights.append((gate_up, down))
 
     residual = wide(hidden_in.reshape(row_count, model_width))
     saved = []
@@ -1125,14 +1141,16 @@
 
         def forward_work(group, pair):
             outs = experts_forward(
-                group, pair_total, pair, masks[i], routers[i], own_experts, *expert_weights[i], kept
+                group, pair_total, pair, ids_all, TOP * i, routers[i], own_experts,
+                *expert_weights[i], kept,
             )
             parts[2 * group], parts[2 * group + 1] = outs[:2]
             kept[:] = outs[2:]
+            return outs[0]
 
         gather_fsdp(normed_second.astype(low), forward_work)
         rows_second, gate, up, probs = kept
-        expert_sum = scatter_fsdp(parts)
+        expert_sum, _ = scatter_fsdp(parts)
         saved.append(
             (
                 residual, root_first, rows_first, qkv, attended, logs,
@@ -1164,27 +1182,29 @@
             )
             parts[2 * group], parts[2 * group + 1] = outs[:2]
             kept[:] = outs[2:]
+            return outs[0]
 
         gather_fsdp(sent, backward_work)
         grads_second, grad_gate, grad_up, hidden, grad_logits = kept
-        gate_grads = dot_tn(rows_second, grad_gate).astype(low)
-        up_grads = dot_tn(rows_second, grad_up).astype(low)
-        down_grads = dot_tn(hidden, grads_second).astype(low)
+        grad_second, (gate_grads, up_grads, down_grads) = scatter_fsdp(
+            parts,
+            (
+                lambda start: dot_tn(after(rows_second, start), grad_gate).astype(low),
+                lambda start: dot_tn(after(rows_second, start), grad_up).astype(low),
+                lambda start: dot_tn(after(hidden, start), grads_second).astype(low),
+            ),
+        )
         grad_router = dot_tn(rows_second, grad_logits)[:, :expert_total]
-        grad_second = scatter_fsdp(parts, (gate_grads, up_grads, down_grads))
-        expert_grads.insert(
-            0,
-            (
-                lax.psum_scatter(gate_grads, "ctx", scatter_dimension=0, tiled=True),
-                lax.psum_scatter(up_grads, "ctx", scatter_dimension=0, tiled=True),
-                lax.psum_scatter(
-                    down_grads.reshape(experts_here, FE, model_width),
-                    "ctx",
-                    scatter_dimension=1,
-                    tiled=True,
-                ),
+        cross = [
+            cross_core(gate_grads.reshape(2, 2, model_width // ctx_total, -1)),
+            cross_core(up_grads.reshape(2, 2, model_width // ctx_total, -1)),
+            cross_core(
+                down_grads.reshape(experts_here, 2, 2, FE // ctx_total, model_width).transpose(
+                    1, 2, 0, 3, 4
+                )
             ),
-        )
+        ]
+        expert_grads.insert(0, [cross_x(part) for part in cross])
         grad_middle, gain_second = rms_back(middle, root_second, gains[i][:, 1], grad_second)
         grad_middle = grad_middle + grad
         back, rows_branch, grad_qkv, gain_first = attention_backward(
@@ -1209,7 +1229,7 @@
                 ).reshape(ctx_total * share, qkv_part + q_part)
                 for r in range(groups)
             ]
-            packed = scatter_fsdp(packs).reshape(ctx_total, share, qkv_part + q_part)
+            packed = scatter_fsdp(packs)[0].reshape(ctx_total, share, qkv_part + q_part)
         else:
             packed = jnp.concatenate(
                 [qkv_grads.transpose(1, 0, 2, 3), out_grads.transpose(0, 2, 1, 3)], -1

time: 1310 us -> 1070 us (0.82)
  waiting for transfers between devices: 562 us -> 425 us
  Pallas kernels: 259 us -> 194 us
  local copies, waits for them, and re-layouts: 188 us -> 146 us
  starting transfers between devices: 133 us -> 148 us
    reduce_scatter x6 -> x0, waiting for transfers between devices: 146 us -> none  [the longest x2 79.9 us: split_ranks(): lax.psum_scatter(down_grads.reshape(experts_here, FE, model_width), 'ctx'...]
    pallas_call x9 -> x10, Pallas kernels: 157 us -> 72 us  [the longest x8 70.7 us: experts_forward(): pl.pallas_call(functools.partial(experts_forward_body, first_id), grid=(e...]
    all_gather x5, waiting for transfers between devices: 0.01 us -> 58.4 us  [the longest x2 46.6 us: split_ranks(): gate_up = lax.all_gather(gate_up, 'ctx', axis=1, tiled=True)]
    unnamed x460 -> x389, local copies, waits for them, and re-layouts: 104 us -> 62.5 us
    reduce_scatter x1, waiting for transfers between devices: 27.1 us -> 0.02 us  [split_ranks(): packed = lax.psum_scatter(packed, 'fsdp', scatter_dimension=0, tiled=True)]
    dynamic_slice x0 -> x10, local copies, waits for them, and re-layouts: none -> 26.6 us  [the longest x6 16.3 us: cross_core(): held = lax.dynamic_index_in_dim(whole_sum, core, 1, False)]
    pallas_call x8, Pallas kernels: 64.5 us -> 85.6 us  [experts_backward(): pl.pallas_call(experts_backward_body, grid=(expert_count, steps), in_spec...]
    unnamed x16 -> x10, waiting for transfers between devices: 65.1 us -> 44 us
  transfers between devices with their start and end apart: 122 -> 131, of which waited for: 66 -> 54; matrix products, arithmetic and copies ran while one was open for 17% -> 20% of each run, Pallas kernels for 19% -> 18%
where the time goes in v3:
time: 1070 us; the launch traced here: 1050 us
  waiting for transfers between devices  425 us (40%)
  Pallas kernels  194 us (18%)
  starting transfers between devices  148 us (14%)
  local copies, waits for them, and re-layouts  146 us (14%)
  other arithmetic  77.1 us (7%)
  matrix products  45.8 us (4%)
  between operations  17.6 us (2%)
    ppermute x120, waiting for transfers between devices, rotate_ranks(): lax.ppermute(values_in, axis_name, [(i, target_of(i)) for i in range(tota...  301 us
    ppermute x120, starting transfers between devices, rotate_ranks(): lax.ppermute(values_in, axis_name, [(i, target_of(i)) for i in range(tota...  137 us
    pallas_call x8, Pallas kernels, experts_backward(): pl.pallas_call(experts_backward_body, grid=(expert_count, steps), in_spec...  85.6 us
    pallas_call x8, Pallas kernels, experts_forward(): pl.pallas_call(functools.partial(experts_forward_body, first_id), grid=(e...  70.7 us
    unnamed x389, local copies, waits for them, and re-layouts  62.5 us
    all_gather x2, waiting for transfers between devices, split_ranks(): gate_up = lax.all_gather(gate_up, 'ctx', axis=1, tiled=True)  46.6 us
    dot_general x12, matrix products, mm(): return lax.dot_general(a, b, dims, preferred_element_type=jnp.float32)  45.8 us
    unnamed x10, waiting for transfers between devices  44 us
  transfers between devices with their start and end apart: 131, of which 54 were waited for; matrix products, arithmetic and copies ran while one was open for 20% of the time, Pallas kernels for 18%

profile of v3, /device:TPU:0, one launch (start us, length us, event | category | flops | bytes accessed | tf_op | source)
XLA Modules:
  0.0 1053.7 jit_solution(11408317023617343618)
XLA Ops:
  13.7 46.6 %all-gather.14.cloned.1.call-done = bf16[1,2,1536,1024]{3,2,1,0:T(8,128)(2,1)} async-done(((bf16[1,2,384,1024]{3,2,1,0:T(8,128)(2,1)}), bf16[1,2,1536,1024]{3,2,1,0:T(8,128)(2,1)}) %all-gather.14.cloned.1.call-update) | async-done | bytes 6291472 | tf_op jit(solution)/shard_map/all_gather | solution.py:1120
  69.7 14.3 %all-to-all-done = bf16[4,48,1316]{2,1,0:T(8,128)(2,1)S(1)} async-done(((bf16[4,48,1316]{2,1,0:T(8,128)(2,1)}), bf16[4,48,1316]{2,1,0:T(8,128)(2,1)S(1)}, u32[]{:S(2)}, u32[]{:S(2)}) %all-to-all-start) | async-done | bytes 505376 | tf_op jit(solution)/shard_map/all_to_all | solution.py:1070
  84.8 11.8 %all-gather.8.cloned.1.call-done.w_down = bf16[2,512,1536]{2,1,0:T(8,128)(2,1)} async-done(((bf16[2,128,1536]{2,1,0:T(8,128)(2,1)}), bf16[2,512,1536]{2,1,0:T(8,128)(2,1)}) %all-gather.8.cloned.1.call-update) | async-done | bytes 3145744 | tf_op jit(solution)/shard_map/all_gather | solution.py:1121
  104.4 12.6 %collective-permute-done = bf16[192,128]{1,0:T(8,128)(2,1)S(1)} collective-permute-done((bf16[192,128]{1,0:T(8,128)(2,1)S(1)}, bf16[192,128]{1,0:T(8,128)(2,1)S(1)}, u32[]{:S(2)}, u32[]{:S(2)}) %collective-permute-start) | collective-permute-done | bytes 49184 | tf_op jit(solution)/shard_map/ppermute | solution.py:894
  120.9 5.7 collective-permute-done.1
  126.6 4.5 collective-permute-start.3
  139.2 20.9 %collective-permute-done.10 = bf16[192,1024]{1,0:T(8,128)(2,1)S(1)} collective-permute-done((bf16[192,1024]{1,0:T(8,128)(2,1)S(1)}, bf16[192,1024]{1,0:T(8,128)(2,1)S(1)}, u32[]{:S(2)}, u32[]{:S(2)}) %collective-permute-start.10) | collective-permute-done | bytes 393248 | tf_op jit(solution)/shard_map/ppermute | solution.py:894
  164.3 6.1 collective-permute-start.11
  173.4 6.0 collective-permute-done.13
  180.6 7.1 collective-permute-done.14
  188.6 7.4 shard_map.171
  202.1 16.8 %collective-permute-done.17 = bf16[128,1536]{1,0:T(8,128)(2,1)S(1)} collective-permute-done((bf16[128,1536]{1,0:T(8,128)(2,1)}, bf16[128,1536]{1,0:T(8,128)(2,1)S(1)}, u32[]{:S(2)}, u32[]{:S(2)}) %collective-permute-start.17) | collective-permute-done | bytes 393248 | tf_op jit(solution)/shard_map/ppermute | solution.py:894
  223.0 11.4 %collective-permute-done.18.rows_0 = bf16[128,1536]{1,0:T(8,128)(2,1)S(1)} collective-permute-done((bf16[128,1536]{1,0:T(8,128)(2,1)S(1)}, bf16[128,1536]{1,0:T(8,128)(2,1)S(1)}, u32[]{:S(2)}, u32[]{:S(2)}) %collective-permute-start.18) | collective-permute-done | bytes 393248 | tf_op jit(solution)/shard_map/ppermute | solution.py:894
  247.2 8.8 shard_map.172
  257.6 8.8 shard_map.173
  268.8 8.8 shard_map.174
  278.4 8.9 shard_map.175
  290.2 6.7 collective-permute-done.27
  298.3 7.0 collective-permute-done.25
  305.8 5.7 collective-permute-start.32
  314.8 4.5 collective-permute-start.33
  329.6 6.4 collective-permute-done.35.rows_2
  340.4 7.5 shard_map.176
  351.5 11.1 %collective-permute-done.39 = bf16[128,1536]{1,0:T(8,128)(2,1)S(1)} collective-permute-done((bf16[128,1536]{1,0:T(8,128)(2,1)S(1)}, bf16[128,1536]{1,0:T(8,128)(2,1)S(1)}, u32[]{:S(2)}, u32[]{:S(2)}) %collective-permute-start.39) | collective-permute-done | bytes 393248 | tf_op jit(solution)/shard_map/ppermute | solution.py:894
  365.3 11.3 %collective-permute-done.40.rows_0 = bf16[128,1536]{1,0:T(8,128)(2,1)} collective-permute-done((bf16[128,1536]{1,0:T(8,128)(2,1)S(1)}, bf16[128,1536]{1,0:T(8,128)(2,1)}, u32[]{:S(2)}, u32[]{:S(2)}) %collective-permute-start.40) | collective-permute-done | bytes 393248 | tf_op jit(solution)/shard_map/ppermute | solution.py:894
  381.9 4.8 collective-permute-done.42.rows_0
  393.2 8.8 shard_map.177
  402.3 8.8 shard_map.178
  412.8 8.8 shard_map.179
  422.4 8.9 shard_map.180
  433.4 10.2 collective-permute-done.49
  455.3 5.7 collective-permute-done.53
  484.0 13.2 %collective-permute-done.56.grads_0 = bf16[128,1664]{1,0:T(8,128)(2,1)S(1)} collective-permute-done((bf16[128,1664]{1,0:T(8,128)(2,1)}, bf16[128,1664]{1,0:T(8,128)(2,1)S(1)}, u32[]{:S(2)}, u32[]{:S(2)}) %collective-permute-start.56) | collective-permute-done | bytes 426016 | tf_op jit(solution)/shard_map/ppermute | solution.py:894
  500.5 10.7 %shard_map.181 = (bf16[128,1536]{1,0:T(8,128)(2,1)}, bf16[128,1536]{1,0:T(8,128)(2,1)}, bf16[1024,1536]{1,0:T(8,128)(2,1)}, bf16[1024,1024]{1,0:T(8,128)(2,1)}, ...) custom-call(bf16[128,1664]{1,0:T(8,128)(2,1)} %concatenate.206.grads_0, ...), custom_call_target="tpu_custom_call" | custom-call | flops 2415919104 | bytes 9437184 | tf_op jit(solution)/shard_map/pallas_call | solution.py:671
  516.9 10.6 %shard_map.182 = (bf16[128,1536]{1,0:T(8,128)(2,1)}, bf16[128,1536]{1,0:T(8,128)(2,1)}, bf16[1024,1536]{1,0:T(8,128)(2,1)}, bf16[1024,1024]{1,0:T(8,128)(2,1)}, ...) custom-call(bf16[128,1664]{1,0:T(8,128)(2,1)} %copy-done.105, ...), custom_call_target="tpu_custom_call", output_to_operand_aliasing={{2}: (10, {}), {3}: (11, {}), {4}: (12, {}), {5}: (13, {}),... | custom-call | flops 2415919104 | bytes 9437184 | tf_op jit(solution)/shard_map/pallas_call | solution.py:671
  530.0 10.7 %shard_map.183 = (bf16[128,1536]{1,0:T(8,128)(2,1)}, bf16[128,1536]{1,0:T(8,128)(2,1)}, bf16[1024,1536]{1,0:T(8,128)(2,1)}, bf16[1024,1024]{1,0:T(8,128)(2,1)}, ...) custom-call(bf16[128,1664]{1,0:T(8,128)(2,1)} %copy-done.104, ...), custom_call_target="tpu_custom_call", output_to_operand_aliasing={{2}: (10, {}), {3}: (11, {}), {4}: (12, {}), {5}: (13, {}),... | custom-call | flops 2415919104 | bytes 9437184 | tf_op jit(solution)/shard_map/pallas_call | solution.py:671
  542.1 10.7 %shard_map.184 = (bf16[128,1536]{1,0:T(8,128)(2,1)}, bf16[128,1536]{1,0:T(8,128)(2,1)}, bf16[1024,1536]{1,0:T(8,128)(2,1)}, bf16[1024,1024]{1,0:T(8,128)(2,1)}, ...) custom-call(bf16[128,1664]{1,0:T(8,128)(2,1)} %copy-done.106, ...), custom_call_target="tpu_custom_call", output_to_operand_aliasing={{2}: (10, {}), {3}: (11, {}), {4}: (12, {}), {5}: (13, {}),... | custom-call | flops 2415919104 | bytes 9437184 | tf_op jit(solution)/shard_map/pallas_call | solution.py:671
  554.4 10.1 collective-permute-done.65
  570.6 6.6 convolution_convert_fusion.5
  578.4 4.9 convolution_convert_fusion.3
  587.5 5.0 convolution_convert_fusion.4
  595.8 7.9 collective-permute-done.73.grad_2
  621.9 11.8 %shard_map.185 = (bf16[128,1536]{1,0:T(8,128)(2,1)S(1)}, bf16[128,1536]{1,0:T(8,128)(2,1)S(1)}, bf16[128,1536]{1,0:T(8,128)(2,1)S(1)}, bf16[128,1536]{1,0:T(8,12...) custom-call(bf16[128,1536]{1,0:T(8,128)(2,1)S(1)} %copy-done.3, ...), custom_call_target="tpu_custom_call" | custom-call | flops 2617245696 | bytes 7864320 | tf_op jit(solution)/shard_map/pallas_call | solution.py:844
  654.3 4.8 collective-permute-done.77
  672.9 4.7 collective-permute-done.78.grads_0
  686.0 10.6 %shard_map.186 = (bf16[128,1536]{1,0:T(8,128)(2,1)}, bf16[128,1536]{1,0:T(8,128)(2,1)}, bf16[1024,1536]{1,0:T(8,128)(2,1)}, bf16[1024,1024]{1,0:T(8,128)(2,1)}, ...) custom-call(bf16[128,1664]{1,0:T(8,128)(2,1)} %concatenate.210.grads_0, ...), custom_call_target="tpu_custom_call" | custom-call | flops 2415919104 | bytes 9437184 | tf_op jit(solution)/shard_map/pallas_call | solution.py:671
  700.6 11.0 %shard_map.187 = (bf16[128,1536]{1,0:T(8,128)(2,1)}, bf16[128,1536]{1,0:T(8,128)(2,1)}, bf16[1024,1536]{1,0:T(8,128)(2,1)}, bf16[1024,1024]{1,0:T(8,128)(2,1)}, ...) custom-call(bf16[128,1664]{1,0:T(8,128)(2,1)} %collective-permute-do, ...), custom_call_target="tpu_custom_call", output_to_operand_aliasing={{2}: (10, {}), {3}: (11, {}), {4}: (12, {}), {5}: (13, {}),... | custom-call | flops 2415919104 | bytes 9437184 | tf_op jit(solution)/shard_map/pallas_call | solution.py:671
  713.9 12.0 %collective-permute-done.83.grads_1 = bf16[128,1664]{1,0:T(8,128)(2,1)S(1)} collective-permute-done((bf16[128,1664]{1,0:T(8,128)(2,1)S(1)}, bf16[128,1664]{1,0:T(8,128)(2,1)S(1)}, u32[]{:S(2)}, u32[]{:S(2)}) %collective-permute-start.83) | collective-permute-done | bytes 426016 | tf_op jit(solution)/shard_map/ppermute | solution.py:894
  726.6 10.7 %shard_map.188 = (bf16[128,1536]{1,0:T(8,128)(2,1)}, bf16[128,1536]{1,0:T(8,128)(2,1)}, bf16[1024,1536]{1,0:T(8,128)(2,1)}, bf16[1024,1024]{1,0:T(8,128)(2,1)}, ...) custom-call(bf16[128,1664]{1,0:T(8,128)(2,1)} %copy-done.103, ...), custom_call_target="tpu_custom_call", output_to_operand_aliasing={{2}: (10, {}), {3}: (11, {}), {4}: (12, {}), {5}: (13, {}),... | custom-call | flops 2415919104 | bytes 9437184 | tf_op jit(solution)/shard_map/pallas_call | solution.py:671
  744.4 10.7 %shard_map.189 = (bf16[128,1536]{1,0:T(8,128)(2,1)}, bf16[128,1536]{1,0:T(8,128)(2,1)}, bf16[1024,1536]{1,0:T(8,128)(2,1)}, bf16[1024,1024]{1,0:T(8,128)(2,1)}, ...) custom-call(bf16[128,1664]{1,0:T(8,128)(2,1)} %copy-done.107, ...), custom_call_target="tpu_custom_call", output_to_operand_aliasing={{2}: (10, {}), {3}: (11, {}), {4}: (12, {}), {5}: (13, {}),... | custom-call | flops 2415919104 | bytes 9437184 | tf_op jit(solution)/shard_map/pallas_call | solution.py:671
  756.3 9.1 collective-permute-done.87
  767.7 6.6 convolution_convert_fusion.2
  778.3 5.0 convolution_convert_fusion
  785.1 4.9 convolution_convert_fusion.1
  794.2 4.8 collective-permute-done.93
  812.9 9.6 shard_map.190
  886.0 43.8 %reduce-scatter.10.cloned.1.call-done = f32[48,18]{1,0:T(8,128)} async-done(((f32[1536,18]{1,0:T(8,128)}), f32[48,18]{1,0:T(8,128)}) %reduce-scatter.10.cloned.1.call-update) | async-done | bytes 3472
  947.5 6.4 collective-permute-done.102
  955.4 25.8 %collective-permute-done.99 = bf16[128,1536]{1,0:T(8,128)(2,1)S(1)} collective-permute-done((bf16[128,1536]{1,0:T(8,128)(2,1)S(1)}, bf16[128,1536]{1,0:T(8,128)(2,1)S(1)}, u32[]{:S(2)}, u32[]{:S(2)}) %collective-permute-start.99) | collective-permute-done | bytes 393248 | tf_op jit(solution)/shard_map/ppermute | solution.py:894
  992.5 4.5 collective-permute-done.103
  996.9 6.2 collective-permute-done.104
  1008.5 6.6 copy.307
  1015.1 4.9 collective-permute-done.107
  1039.6 5.0 all-to-all-done.2
  (894 shorter events, 403.3 us)
Async XLA Ops:
  7.2 53.2 %all-gather.14.cloned.1.call-start = ((), (), s32[]{:S(2)}) async-start(), calls=%async_computation.10 | async-start | bytes 7864320 | tf_op jit(solution)/shard_map/all_gather | solution.py:1120
  11.1 85.5 %all-gather.8.cloned.1.call-start = ((), (), s32[]{:S(2)}) async-start(), calls=%async_computation.6 | async-start | bytes 3932160 | tf_op jit(solution)/shard_map/all_gather | solution.py:1121
  60.4 43.7 %collective-permute-start.5 = (bf16[128,1536]{1,0:T(8,128)(2,1)S(1)}, bf16[128,1536]{1,0:T(8,128)(2,1)S(1)}, u32[]{:S(2)}, u32[]{:S(2)}) collective-permute-start(bf16[128,1536]{1,0:T(8,128)(2,1)S(1)} %bitcast.357), channel_id=1, source_target_pairs={{0,16},{8,24},{16,0},{24,8},{1,17},{9,25},{17,1},{25,9},{2,18},{10... | collective-permute-start | bytes 1179656 | tf_op jit(solution)/shard_map/ppermute | solution.py:894
  60.8 43.5 %collective-permute-start.4 = (bf16[128,1536]{1,0:T(8,128)(2,1)S(1)}, bf16[128,1536]{1,0:T(8,128)(2,1)S(1)}, u32[]{:S(2)}, u32[]{:S(2)}) collective-permute-start(bf16[128,1536]{1,0:T(8,128)(2,1)S(1)} %bitcast.358), channel_id=1, source_target_pairs={{0,8},{8,0},{16,24},{24,16},{1,9},{9,1},{17,25},{25,17},{2,10},{10... | collective-permute-start | bytes 1179656 | tf_op jit(solution)/shard_map/ppermute | solution.py:894
  65.7 18.3 %all-to-all-start = ((bf16[4,48,1316]{2,1,0:T(8,128)(2,1)}), bf16[4,48,1316]{2,1,0:T(8,128)(2,1)S(1)}, u32[]{:S(2)}, u32[]{:S(2)}) async-start(bf16[4,48,1316]{2,1,0:T(8,128)(2,1)} %bitcast.13), calls=%async_computation | async-start | bytes 1081344 | tf_op jit(solution)/shard_map/all_to_all | solution.py:1070
  69.2 128.8 %all-gather.16.cloned.1.call-start = ((), (), s32[]{:S(2)}) async-start(), calls=%async_computation.11 | async-start | bytes 3538944 | tf_op jit(solution)/shard_map/all_gather | solution.py:1110
  96.7 230.5 %all-gather.10.cloned.1.call-start = ((), (), s32[]{:S(2)}) async-start(), calls=%async_computation.7 | async-start | bytes 7864320 | tf_op jit(solution)/shard_map/all_gather | solution.py:1120
  99.5 35.3 %collective-permute-start.8 = (bf16[192,1024]{1,0:T(8,128)(2,1)S(1)}, bf16[192,1024]{1,0:T(8,128)(2,1)S(1)}, u32[]{:S(2)}, u32[]{:S(2)}) collective-permute-start(bf16[192,1024]{1,0:T(8,128)(2,1)S(1)} %bitcast.303), channel_id=1, source_target_pairs={{0,2},{1,3},{2,4},{3,5},{4,6},{5,7},{6,0},{7,1},{8,10},{9,11},{10,... | collective-permute-start | bytes 1179656 | tf_op jit(solution)/shard_map/ppermute | solution.py:894
  101.2 79.4 %collective-permute-start.7 = (bf16[192,1024]{1,0:T(8,128)(2,1)S(1)}, bf16[192,1024]{1,0:T(8,128)(2,1)S(1)}, u32[]{:S(2)}, u32[]{:S(2)}) collective-permute-start(bf16[192,1024]{1,0:T(8,128)(2,1)S(1)} %bitcast.304), channel_id=1, source_target_pairs={{0,1},{1,0},{2,3},{3,2},{4,5},{5,4},{6,7},{7,6},{8,9},{9,8},{10,11... | collective-permute-start | bytes 1179656 | tf_op jit(solution)/shard_map/ppermute | solution.py:894
  118.6 20.4 %collective-permute-start.6 = (bf16[128,1536]{1,0:T(8,128)(2,1)S(1)}, bf16[128,1536]{1,0:T(8,128)(2,1)S(1)}, u32[]{:S(2)}, u32[]{:S(2)}) collective-permute-start(bf16[128,1536]{1,0:T(8,128)(2,1)S(1)} %collective-permute-done.5), channel_id=1, source_target_pairs={{0,8},{8,0},{16,24},{24,16},{1,9},{9,1},{17,25},{25,17},{2,10},{10... | collective-permute-start | bytes 1179656 | tf_op jit(solution)/shard_map/ppermute | solution.py:894
  134.8 25.3 %collective-permute-start.10 = (bf16[192,1024]{1,0:T(8,128)(2,1)S(1)}, bf16[192,1024]{1,0:T(8,128)(2,1)S(1)}, u32[]{:S(2)}, u32[]{:S(2)}) collective-permute-start(bf16[192,1024]{1,0:T(8,128)(2,1)S(1)} %bitcast.305), channel_id=1, source_target_pairs={{0,6},{1,7},{2,0},{3,1},{4,2},{5,3},{6,4},{7,5},{8,14},{9,15},{10,... | collective-permute-start | bytes 1179656 | tf_op jit(solution)/shard_map/ppermute | solution.py:894
  136.9 43.7 %collective-permute-start.9 = (bf16[192,1024]{1,0:T(8,128)(2,1)S(1)}, bf16[192,1024]{1,0:T(8,128)(2,1)S(1)}, u32[]{:S(2)}, u32[]{:S(2)}) collective-permute-start(bf16[192,1024]{1,0:T(8,128)(2,1)S(1)} %collective-permute-done.8), channel_id=1, source_target_pairs={{0,1},{1,0},{2,3},{3,2},{4,5},{5,4},{6,7},{7,6},{8,9},{9,8},{10,11... | collective-permute-start | bytes 1179656 | tf_op jit(solution)/shard_map/ppermute | solution.py:894
  160.2 19.2 %collective-permute-start.13 = (bf16[96,1024]{1,0:T(8,128)(2,1)S(1)}, bf16[96,1024]{1,0:T(8,128)(2,1)S(1)}, u32[]{:S(2)}, u32[]{:S(2)}) collective-permute-start(bf16[96,1024]{1,0:T(8,128)(2,1)S(1)} %slice.421), channel_id=1, source_target_pairs={{0,6},{1,7},{2,0},{3,1},{4,2},{5,3},{6,4},{7,5},{8,14},{9,15},{10,... | collective-permute-start | bytes 589832 | tf_op jit(solution)/shard_map/ppermute | solution.py:894
  164.3 16.3 %collective-permute-start.11 = (bf16[192,1024]{1,0:T(8,128)(2,1)S(1)}, bf16[192,1024]{1,0:T(8,128)(2,1)S(1)}, u32[]{:S(2)}, u32[]{:S(2)}) collective-permute-start(bf16[192,1024]{1,0:T(8,128)(2,1)S(1)} %collective-permute-done.10), channel_id=1, source_target_pairs={{0,1},{1,0},{2,3},{3,2},{4,5},{5,4},{6,7},{7,6},{8,9},{9,8},{10,11... | collective-permute-start | bytes 1179656 | tf_op jit(solution)/shard_map/ppermute | solution.py:894
  198.0 195.2 %all-gather.12.cloned.1.call-start = ((), (), s32[]{:S(2)}) async-start(), calls=%async_computation.8 | async-start | bytes 3932160 | tf_op jit(solution)/shard_map/all_gather | solution.py:1121
  201.6 17.2 %collective-permute-start.17 = (bf16[128,1536]{1,0:T(8,128)(2,1)}, bf16[128,1536]{1,0:T(8,128)(2,1)S(1)}, u32[]{:S(2)}, u32[]{:S(2)}) collective-permute-start(bf16[128,1536]{1,0:T(8,128)(2,1)} %add_convert_fusion.9), channel_id=1, source_target_pairs={{0,16},{8,24},{16,0},{24,8},{1,17},{9,25},{17,1},{25,9},{2,18},{10... | collective-permute-start | bytes 1179656 | tf_op jit(solution)/shard_map/ppermute | solution.py:894
  222.4 24.0 %collective-permute-start.19 = (bf16[128,1536]{1,0:T(8,128)(2,1)S(1)}, bf16[128,1536]{1,0:T(8,128)(2,1)S(1)}, u32[]{:S(2)}, u32[]{:S(2)}) collective-permute-start(bf16[128,1536]{1,0:T(8,128)(2,1)S(1)} %multiply_convert_fusion.2.rows_0), channel_id=1, source_target_pairs={{0,1},{1,0},{2,3},{3,2},{4,5},{5,4},{6,7},{7,6},{8,9},{9,8},{10,11... | collective-permute-start | bytes 1179656 | tf_op jit(solution)/shard_map/ppermute | solution.py:894
  236.0 20.7 %collective-permute-start.24 = (bf16[128,1536]{1,0:T(8,128)(2,1)S(1)}, bf16[128,1536]{1,0:T(8,128)(2,1)S(1)}, u32[]{:S(2)}, u32[]{:S(2)}) collective-permute-start(bf16[128,1536]{1,0:T(8,128)(2,1)S(1)} %collective-permute-done.18.rows_0), channel_id=1, source_target_pairs={{0,1},{1,0},{2,3},{3,2},{4,5},{5,4},{6,7},{7,6},{8,9},{9,8},{10,11... | collective-permute-start | bytes 1179656 | tf_op jit(solution)/shard_map/ppermute | solution.py:894
  244.0 22.3 %collective-permute-start.22 = (bf16[64,1536]{1,0:T(8,128)(2,1)S(1)}, bf16[64,1536]{1,0:T(8,128)(2,1)S(1)}, u32[]{:S(2)}, u32[]{:S(2)}) collective-permute-start(bf16[64,1536]{1,0:T(8,128)(2,1)S(1)} %slice.426), channel_id=1, source_target_pairs={{0,6},{1,7},{2,0},{3,1},{4,2},{5,3},{6,4},{7,5},{8,14},{9,15},{10,... | collective-permute-start | bytes 589832 | tf_op jit(solution)/shard_map/ppermute | solution.py:894
  245.9 22.1 %collective-permute-start.23 = (bf16[128,1536]{1,0:T(8,128)(2,1)S(1)}, bf16[128,1536]{1,0:T(8,128)(2,1)S(1)}, u32[]{:S(2)}, u32[]{:S(2)}) collective-permute-start(bf16[128,1536]{1,0:T(8,128)(2,1)S(1)} %collective-permute-done.20.rows_0), channel_id=1, source_target_pairs={{0,1},{1,0},{2,3},{3,2},{4,5},{5,4},{6,7},{7,6},{8,9},{9,8},{10,11... | collective-permute-start | bytes 1179656 | tf_op jit(solution)/shard_map/ppermute | solution.py:894
  288.6 16.7 %collective-permute-start.25 = (bf16[128,1536]{1,0:T(8,128)(2,1)S(1)}, bf16[128,1536]{1,0:T(8,128)(2,1)S(1)}, u32[]{:S(2)}, u32[]{:S(2)}) collective-permute-start(bf16[128,1536]{1,0:T(8,128)(2,1)S(1)} %copy-done.177), channel_id=1, source_target_pairs={{0,1},{1,0},{2,3},{3,2},{4,5},{5,4},{6,7},{7,6},{8,9},{9,8},{10,11... | collective-permute-start | bytes 1179656 | tf_op jit(solution)/shard_map/ppermute | solution.py:894
  327.1 506.8 %reduce-scatter.12.cloned.1.call-start = ((), (), s32[]{:S(2)}) async-start(), calls=%async_computation.13 | async-start | bytes 811008
  378.1 15.1 %collective-permute-start.41 = (bf16[128,1536]{1,0:T(8,128)(2,1)S(1)}, bf16[128,1536]{1,0:T(8,128)(2,1)}, u32[]{:S(2)}, u32[]{:S(2)}) collective-permute-start(bf16[128,1536]{1,0:T(8,128)(2,1)S(1)} %multiply_convert_fusion.rows_0), channel_id=1, source_target_pairs={{0,1},{1,0},{2,3},{3,2},{4,5},{5,4},{6,7},{7,6},{8,9},{9,8},{10,11... | collective-permute-start | bytes 1179656 | tf_op jit(solution)/shard_map/ppermute | solution.py:894
  379.6 22.7 %collective-permute-start.46 = (bf16[128,1536]{1,0:T(8,128)(2,1)}, bf16[128,1536]{1,0:T(8,128)(2,1)}, u32[]{:S(2)}, u32[]{:S(2)}) collective-permute-start(bf16[128,1536]{1,0:T(8,128)(2,1)} %collective-permute-done.40.rows_0), channel_id=1, source_target_pairs={{0,1},{1,0},{2,3},{3,2},{4,5},{5,4},{6,7},{7,6},{8,9},{9,8},{10,11... | collective-permute-start | bytes 1179656 | tf_op jit(solution)/shard_map/ppermute | solution.py:894
  388.4 22.8 %collective-permute-start.44 = (bf16[64,1536]{1,0:T(8,128)(2,1)}, bf16[64,1536]{1,0:T(8,128)(2,1)}, u32[]{:S(2)}, u32[]{:S(2)}) collective-permute-start(bf16[64,1536]{1,0:T(8,128)(2,1)} %slice.441), channel_id=1, source_target_pairs={{0,6},{1,7},{2,0},{3,1},{4,2},{5,3},{6,4},{7,5},{8,14},{9,15},{10,... | collective-permute-start | bytes 589832 | tf_op jit(solution)/shard_map/ppermute | solution.py:894
  391.8 21.1 %collective-permute-start.45 = (bf16[128,1536]{1,0:T(8,128)(2,1)}, bf16[128,1536]{1,0:T(8,128)(2,1)}, u32[]{:S(2)}, u32[]{:S(2)}) collective-permute-start(bf16[128,1536]{1,0:T(8,128)(2,1)} %collective-permute-done.42.rows_0), channel_id=1, source_target_pairs={{0,1},{1,0},{2,3},{3,2},{4,5},{5,4},{6,7},{7,6},{8,9},{9,8},{10,11... | collective-permute-start | bytes 1179656 | tf_op jit(solution)/shard_map/ppermute | solution.py:894
  432.9 16.2 %collective-permute-start.47 = (bf16[128,1536]{1,0:T(8,128)(2,1)S(1)}, bf16[128,1536]{1,0:T(8,128)(2,1)S(1)}, u32[]{:S(2)}, u32[]{:S(2)}) collective-permute-start(bf16[128,1536]{1,0:T(8,128)(2,1)S(1)} %copy-done.178), channel_id=1, source_target_pairs={{0,1},{1,0},{2,3},{3,2},{4,5},{5,4},{6,7},{7,6},{8,9},{9,8},{10,11... | collective-permute-start | bytes 1179656 | tf_op jit(solution)/shard_map/ppermute | solution.py:894
  483.2 16.6 %collective-permute-start.57 = (bf16[128,1664]{1,0:T(8,128)(2,1)}, bf16[128,1664]{1,0:T(8,128)(2,1)S(1)}, u32[]{:S(2)}, u32[]{:S(2)}) collective-permute-start(bf16[128,1664]{1,0:T(8,128)(2,1)} %concatenate.206.grads_0), channel_id=1, source_target_pairs={{0,1},{1,0},{2,3},{3,2},{4,5},{5,4},{6,7},{7,6},{8,9},{9,8},{10,11... | collective-permute-start | bytes 1277960 | tf_op jit(solution)/shard_map/ppermute | solution.py:894
  498.3 17.9 %collective-permute-start.62 = (bf16[128,1664]{1,0:T(8,128)(2,1)S(1)}, bf16[128,1664]{1,0:T(8,128)(2,1)S(1)}, u32[]{:S(2)}, u32[]{:S(2)}) collective-permute-start(bf16[128,1664]{1,0:T(8,128)(2,1)S(1)} %collective-permute-done.56.grads_0), channel_id=1, source_target_pairs={{0,1},{1,0},{2,3},{3,2},{4,5},{5,4},{6,7},{7,6},{8,9},{9,8},{10,11... | collective-permute-start | bytes 1277960 | tf_op jit(solution)/shard_map/ppermute | solution.py:894
  511.2 16.3 %collective-permute-start.59 = (bf16[64,1664]{1,0:T(8,128)(2,1)S(1)}, bf16[64,1664]{1,0:T(8,128)(2,1)S(1)}, u32[]{:S(2)}, u32[]{:S(2)}) collective-permute-start(bf16[64,1664]{1,0:T(8,128)(2,1)S(1)} %slice.448), channel_id=1, source_target_pairs={{0,2},{1,3},{2,4},{3,5},{4,6},{5,7},{6,0},{7,1},{8,10},{9,11},{10,... | collective-permute-start | bytes 638984 | tf_op jit(solution)/shard_map/ppermute | solution.py:894
  511.3 16.2 %collective-permute-start.60 = (bf16[64,1664]{1,0:T(8,128)(2,1)S(1)}, bf16[64,1664]{1,0:T(8,128)(2,1)S(1)}, u32[]{:S(2)}, u32[]{:S(2)}) collective-permute-start(bf16[64,1664]{1,0:T(8,128)(2,1)S(1)} %slice.449), channel_id=1, source_target_pairs={{0,6},{1,7},{2,0},{3,1},{4,2},{5,3},{6,4},{7,5},{8,14},{9,15},{10,... | collective-permute-start | bytes 638984 | tf_op jit(solution)/shard_map/ppermute | solution.py:894
  565.8 17.5 %collective-permute-start.69 = (bf16[128,1536]{1,0:T(8,128)(2,1)S(1)}, bf16[128,1536]{1,0:T(8,128)(2,1)S(1)}, u32[]{:S(2)}, u32[]{:S(2)}) collective-permute-start(bf16[128,1536]{1,0:T(8,128)(2,1)S(1)} %copy-done.174), channel_id=1, source_target_pairs={{0,1},{1,0},{2,3},{3,2},{4,5},{5,4},{6,7},{7,6},{8,9},{9,8},{10,11... | collective-permute-start | bytes 1179656 | tf_op jit(solution)/shard_map/ppermute | solution.py:894
  566.9 16.5 %collective-permute-start.70 = (bf16[64,1536]{1,0:T(8,128)(2,1)S(1)}, bf16[64,1536]{1,0:T(8,128)(2,1)S(1)}, u32[]{:S(2)}, u32[]{:S(2)}) collective-permute-start(bf16[64,1536]{1,0:T(8,128)(2,1)S(1)} %get-tuple-element.485), channel_id=1, source_target_pairs={{0,6},{1,7},{2,0},{3,1},{4,2},{5,3},{6,4},{7,5},{8,14},{9,15},{10,... | collective-permute-start | bytes 589832 | tf_op jit(solution)/shard_map/ppermute | solution.py:894
  577.3 15.3 %collective-permute-start.67 = (bf16[128,1536]{1,0:T(8,128)(2,1)S(1)}, bf16[128,1536]{1,0:T(8,128)(2,1)S(1)}, u32[]{:S(2)}, u32[]{:S(2)}) collective-permute-start(bf16[128,1536]{1,0:T(8,128)(2,1)S(1)} %copy-done.170), channel_id=1, source_target_pairs={{0,1},{1,0},{2,3},{3,2},{4,5},{5,4},{6,7},{7,6},{8,9},{9,8},{10,11... | collective-permute-start | bytes 1179656 | tf_op jit(solution)/shard_map/ppermute | solution.py:894
  595.8 18.8 %collective-permute-start.72 = (bf16[128,1536]{1,0:T(8,128)(2,1)S(1)}, bf16[128,1536]{1,0:T(8,128)(2,1)}, u32[]{:S(2)}, u32[]{:S(2)}) collective-permute-start(bf16[128,1536]{1,0:T(8,128)(2,1)S(1)} %get-tuple-element.431.grad_0), channel_id=1, source_target_pairs={{0,8},{8,0},{16,24},{24,16},{1,9},{9,1},{17,25},{25,17},{2,10},{10... | collective-permute-start | bytes 1179656 | tf_op jit(solution)/shard_map/ppermute | solution.py:894
  611.5 67.7 %collective-permute-start.112 = (bf16[2,384,1024]{1,2,0:T(8,128)(2,1)}, bf16[2,384,1024]{1,2,0:T(8,128)(2,1)}, u32[]{:S(2)}, u32[]{:S(2)}) collective-permute-start(bf16[2,384,1024]{1,2,0:T(8,128)(2,1)} %bitcast.380), channel_id=1, source_target_pairs={{0,8},{8,0},{16,24},{24,16},{1,9},{9,1},{17,25},{25,17},{2,10},{10... | collective-permute-start | bytes 4718600 | tf_op jit(solution)/shard_map/ppermute | solution.py:894
  639.1 99.3 %collective-permute-start.114 = (bf16[2,384,1024]{1,2,0:T(8,128)(2,1)}, bf16[2,384,1024]{1,2,0:T(8,128)(2,1)}, u32[]{:S(2)}, u32[]{:S(2)}) collective-permute-start(bf16[2,384,1024]{1,2,0:T(8,128)(2,1)} %bitcast.379), channel_id=1, source_target_pairs={{0,8},{8,0},{16,24},{24,16},{1,9},{9,1},{17,25},{25,17},{2,10},{10... | collective-permute-start | bytes 4718600 | tf_op jit(solution)/shard_map/ppermute | solution.py:894
  645.4 156.4 %collective-permute-start.118 = (bf16[2,2,128,1536]{3,2,1,0:T(8,128)(2,1)}, bf16[2,2,128,1536]{3,2,1,0:T(8,128)(2,1)}, u32[]{:S(2)}, u32[]{:S(2)}) collective-permute-start(bf16[2,2,128,1536]{3,2,1,0:T(8,128)(2,1)} %bitcast.290), channel_id=1, source_target_pairs={{0,8},{8,0},{16,24},{24,16},{1,9},{9,1},{17,25},{25,17},{2,10},{10... | collective-permute-start | bytes 4718600 | tf_op jit(solution)/shard_map/ppermute | solution.py:894
  668.3 261.6 %reduce-scatter.10.cloned.1.call-start = ((), (), s32[]{:S(2)}) async-start(), calls=%async_computation.12 | async-start | bytes 811008
  677.6 19.0 %collective-permute-start.80 = (bf16[128,1664]{1,0:T(8,128)(2,1)}, bf16[128,1664]{1,0:T(8,128)(2,1)S(1)}, u32[]{:S(2)}, u32[]{:S(2)}) collective-permute-start(bf16[128,1664]{1,0:T(8,128)(2,1)} %concatenate.210.grads_0), channel_id=1, source_target_pairs={{0,6},{1,7},{2,0},{3,1},{4,2},{5,3},{6,4},{7,5},{8,14},{9,15},{10,... | collective-permute-start | bytes 1277960 | tf_op jit(solution)/shard_map/ppermute | solution.py:894
  679.2 18.0 %collective-permute-start.84 = (bf16[128,1664]{1,0:T(8,128)(2,1)}, bf16[128,1664]{1,0:T(8,128)(2,1)S(1)}, u32[]{:S(2)}, u32[]{:S(2)}) collective-permute-start(bf16[128,1664]{1,0:T(8,128)(2,1)} %collective-permute-done.78.grads_0), channel_id=1, source_target_pairs={{0,1},{1,0},{2,3},{3,2},{4,5},{5,4},{6,7},{7,6},{8,9},{9,8},{10,11... | collective-permute-start | bytes 1277960 | tf_op jit(solution)/shard_map/ppermute | solution.py:894
  685.2 150.1 %collective-permute-start.113 = (bf16[384,1024]{0,1:T(8,128)(2,1)}, bf16[384,1024]{0,1:T(8,128)(2,1)}, u32[]{:S(2)}, u32[]{:S(2)}) collective-permute-start(bf16[384,1024]{0,1:T(8,128)(2,1)} %dynamic-slice_bitcast_fusion.3), channel_id=1, source_target_pairs={{0,16},{8,24},{16,0},{24,8},{1,17},{9,25},{17,1},{25,9},{2,18},{10... | collective-permute-start | bytes 2359304 | tf_op jit(solution)/shard_map/ppermute | solution.py:894
  696.6 15.0 %collective-permute-start.81 = (bf16[64,1664]{1,0:T(8,128)(2,1)S(1)}, bf16[64,1664]{1,0:T(8,128)(2,1)S(1)}, u32[]{:S(2)}, u32[]{:S(2)}) collective-permute-start(bf16[64,1664]{1,0:T(8,128)(2,1)S(1)} %slice.456), channel_id=1, source_target_pairs={{0,2},{1,3},{2,4},{3,5},{4,6},{5,7},{6,0},{7,1},{8,10},{9,11},{10,... | collective-permute-start | bytes 638984 | tf_op jit(solution)/shard_map/ppermute | solution.py:894
  697.2 15.6 %collective-permute-start.82 = (bf16[64,1664]{1,0:T(8,128)(2,1)S(1)}, bf16[64,1664]{1,0:T(8,128)(2,1)S(1)}, u32[]{:S(2)}, u32[]{:S(2)}) collective-permute-start(bf16[64,1664]{1,0:T(8,128)(2,1)S(1)} %slice.457), channel_id=1, source_target_pairs={{0,6},{1,7},{2,0},{3,1},{4,2},{5,3},{6,4},{7,5},{8,14},{9,15},{10,... | collective-permute-start | bytes 638984 | tf_op jit(solution)/shard_map/ppermute | solution.py:894
  712.8 30.9 %collective-permute-start.86 = (bf16[128,1664]{1,0:T(8,128)(2,1)S(1)}, bf16[128,1664]{1,0:T(8,128)(2,1)S(1)}, u32[]{:S(2)}, u32[]{:S(2)}) collective-permute-start(bf16[128,1664]{1,0:T(8,128)(2,1)S(1)} %constant_dynamic-update-slice_fusion.14.grads_0), channel_id=1, source_target_pairs={{0,1},{1,0},{2,3},{3,2},{4,5},{5,4},{6,7},{7,6},{8,9},{9,8},{10,11... | collective-permute-start | bytes 1277960 | tf_op jit(solution)/shard_map/ppermute | solution.py:894
  737.3 18.9 %collective-permute-start.85 = (bf16[128,1536]{1,0:T(8,128)(2,1)}, bf16[128,1536]{1,0:T(8,128)(2,1)S(1)}, u32[]{:S(2)}, u32[]{:S(2)}) collective-permute-start(bf16[128,1536]{1,0:T(8,128)(2,1)} %get-tuple-element.342), channel_id=1, source_target_pairs={{0,1},{1,0},{2,3},{3,2},{4,5},{5,4},{6,7},{7,6},{8,9},{9,8},{10,11... | collective-permute-start | bytes 1179656 | tf_op jit(solution)/shard_map/ppermute | solution.py:894
  742.3 94.7 %collective-permute-start.115 = (bf16[384,1024]{0,1:T(8,128)(2,1)}, bf16[384,1024]{0,1:T(8,128)(2,1)}, u32[]{:S(2)}, u32[]{:S(2)}) collective-permute-start(bf16[384,1024]{0,1:T(8,128)(2,1)} %dynamic-slice_bitcast_fusion.2), channel_id=1, source_target_pairs={{0,16},{8,24},{16,0},{24,8},{1,17},{9,25},{17,1},{25,9},{2,18},{10... | collective-permute-start | bytes 2359304 | tf_op jit(solution)/shard_map/ppermute | solution.py:894
  766.6 16.7 %collective-permute-start.91 = (bf16[128,1536]{1,0:T(8,128)(2,1)S(1)}, bf16[128,1536]{1,0:T(8,128)(2,1)S(1)}, u32[]{:S(2)}, u32[]{:S(2)}) collective-permute-start(bf16[128,1536]{1,0:T(8,128)(2,1)S(1)} %copy-done.173), channel_id=1, source_target_pairs={{0,1},{1,0},{2,3},{3,2},{4,5},{5,4},{6,7},{7,6},{8,9},{9,8},{10,11... | collective-permute-start | bytes 1179656 | tf_op jit(solution)/shard_map/ppermute | solution.py:894
  809.3 31.2 %collective-permute-start.119 = (bf16[2,128,1536]{2,1,0:T(8,128)(2,1)}, bf16[2,128,1536]{2,1,0:T(8,128)(2,1)}, u32[]{:S(2)}, u32[]{:S(2)}) collective-permute-start(bf16[2,128,1536]{2,1,0:T(8,128)(2,1)} %dynamic-slice_bitcast_fusion), channel_id=1, source_target_pairs={{0,16},{8,24},{16,0},{24,8},{1,17},{9,25},{17,1},{25,9},{2,18},{10... | collective-permute-start | bytes 2359304 | tf_op jit(solution)/shard_map/ppermute | solution.py:894
  829.5 202.9 %reduce-scatter.8.cloned.1.call-start = ((), (), s32[]{:S(2)}) async-start(), calls=%async_computation.9 | async-start | bytes 3538944 | tf_op jit(solution)/shard_map/reduce_scatter | solution.py:1237
  847.9 34.0 %collective-permute-start.108 = (bf16[2,384,1024]{1,2,0:T(8,128)(2,1)}, bf16[2,384,1024]{1,2,0:T(8,128)(2,1)}, u32[]{:S(2)}, u32[]{:S(2)}) collective-permute-start(bf16[2,384,1024]{1,2,0:T(8,128)(2,1)} %bitcast.382), channel_id=1, source_target_pairs={{0,8},{8,0},{16,24},{24,16},{1,9},{9,1},{17,25},{25,17},{2,10},{10... | collective-permute-start | bytes 4718600 | tf_op jit(solution)/shard_map/ppermute | solution.py:894
  857.3 76.6 %collective-permute-start.110 = (bf16[2,384,1024]{1,2,0:T(8,128)(2,1)}, bf16[2,384,1024]{1,2,0:T(8,128)(2,1)}, u32[]{:S(2)}, u32[]{:S(2)}) collective-permute-start(bf16[2,384,1024]{1,2,0:T(8,128)(2,1)} %bitcast.381), channel_id=1, source_target_pairs={{0,8},{8,0},{16,24},{24,16},{1,9},{9,1},{17,25},{25,17},{2,10},{10... | collective-permute-start | bytes 4718600 | tf_op jit(solution)/shard_map/ppermute | solution.py:894
  864.8 78.3 %collective-permute-start.116 = (bf16[2,2,128,1536]{3,2,1,0:T(8,128)(2,1)}, bf16[2,2,128,1536]{3,2,1,0:T(8,128)(2,1)}, u32[]{:S(2)}, u32[]{:S(2)}) collective-permute-start(bf16[2,2,128,1536]{3,2,1,0:T(8,128)(2,1)} %bitcast.291), channel_id=1, source_target_pairs={{0,8},{8,0},{16,24},{24,16},{1,9},{9,1},{17,25},{25,17},{2,10},{10... | collective-permute-start | bytes 4718600 | tf_op jit(solution)/shard_map/ppermute | solution.py:894
  875.4 60.6 %collective-permute-start.101 = (bf16[192,1024]{1,0:T(8,128)(2,1)}, bf16[192,1024]{1,0:T(8,128)(2,1)}, u32[]{:S(2)}, u32[]{:S(2)}) collective-permute-start(bf16[192,1024]{1,0:T(8,128)(2,1)} %pad_maximum_fusion.17), channel_id=1, source_target_pairs={{0,1},{1,0},{2,3},{3,2},{4,5},{5,4},{6,7},{7,6},{8,9},{9,8},{10,11... | collective-permute-start | bytes 1179656 | tf_op jit(solution)/shard_map/ppermute | solution.py:894
  877.9 62.6 %collective-permute-start.100 = (bf16[192,1024]{1,0:T(8,128)(2,1)}, bf16[192,1024]{1,0:T(8,128)(2,1)}, u32[]{:S(2)}, u32[]{:S(2)}) collective-permute-start(bf16[192,1024]{1,0:T(8,128)(2,1)} %pad_maximum_fusion.16), channel_id=1, source_target_pairs={{0,1},{1,0},{2,3},{3,2},{4,5},{5,4},{6,7},{7,6},{8,9},{9,8},{10,11... | collective-permute-start | bytes 1179656 | tf_op jit(solution)/shard_map/ppermute | solution.py:894
  881.9 56.8 %collective-permute-start.98 = (bf16[128,1536]{1,0:T(8,128)(2,1)S(1)}, bf16[128,1536]{1,0:T(8,128)(2,1)}, u32[]{:S(2)}, u32[]{:S(2)}) collective-permute-start(bf16[128,1536]{1,0:T(8,128)(2,1)S(1)} %get-tuple-element.372), channel_id=1, source_target_pairs={{0,8},{8,0},{16,24},{24,16},{1,9},{9,1},{17,25},{25,17},{2,10},{10... | collective-permute-start | bytes 1179656 | tf_op jit(solution)/shard_map/ppermute | solution.py:894
  933.9 49.7 %collective-permute-start.97 = (bf16[128,1536]{1,0:T(8,128)(2,1)S(1)}, bf16[128,1536]{1,0:T(8,128)(2,1)S(1)}, u32[]{:S(2)}, u32[]{:S(2)}) collective-permute-start(bf16[128,1536]{1,0:T(8,128)(2,1)S(1)} %get-tuple-element.370), channel_id=1, source_target_pairs={{0,8},{8,0},{16,24},{24,16},{1,9},{9,1},{17,25},{25,17},{2,10},{10... | collective-permute-start | bytes 1179656 | tf_op jit(solution)/shard_map/ppermute | solution.py:894
  936.0 53.2 %collective-permute-start.109 = (bf16[384,1024]{0,1:T(8,128)(2,1)S(1)}, bf16[384,1024]{0,1:T(8,128)(2,1)S(1)}, u32[]{:S(2)}, u32[]{:S(2)}) collective-permute-start(bf16[384,1024]{0,1:T(8,128)(2,1)S(1)} %copy-done.112), channel_id=1, source_target_pairs={{0,16},{8,24},{16,0},{24,8},{1,17},{9,25},{17,1},{25,9},{2,18},{10... | collective-permute-start | bytes 2359304 | tf_op jit(solution)/shard_map/ppermute | solution.py:894
  938.7 64.6 %collective-permute-start.111 = (bf16[384,1024]{0,1:T(8,128)(2,1)S(1)}, bf16[384,1024]{0,1:T(8,128)(2,1)S(1)}, u32[]{:S(2)}, u32[]{:S(2)}) collective-permute-start(bf16[384,1024]{0,1:T(8,128)(2,1)S(1)} %dynamic-slice_bitcast_fusion.4), channel_id=1, source_target_pairs={{0,16},{8,24},{16,0},{24,8},{1,17},{9,25},{17,1},{25,9},{2,18},{10... | collective-permute-start | bytes 2359304 | tf_op jit(solution)/shard_map/ppermute | solution.py:894
  943.1 38.1 %collective-permute-start.99 = (bf16[128,1536]{1,0:T(8,128)(2,1)S(1)}, bf16[128,1536]{1,0:T(8,128)(2,1)S(1)}, u32[]{:S(2)}, u32[]{:S(2)}) collective-permute-start(bf16[128,1536]{1,0:T(8,128)(2,1)S(1)} %add_convert_fusion.1), channel_id=1, source_target_pairs={{0,16},{8,24},{16,0},{24,8},{1,17},{9,25},{17,1},{25,9},{2,18},{10... | collective-permute-start | bytes 1179656 | tf_op jit(solution)/shard_map/ppermute | solution.py:894
  953.9 32.8 %collective-permute-start.105 = (bf16[192,1024]{1,0:T(8,128)(2,1)S(1)}, bf16[192,1024]{1,0:T(8,128)(2,1)S(1)}, u32[]{:S(2)}, u32[]{:S(2)}) collective-permute-start(bf16[192,1024]{1,0:T(8,128)(2,1)S(1)} %copy-done.126), channel_id=1, source_target_pairs={{0,1},{1,0},{2,3},{3,2},{4,5},{5,4},{6,7},{7,6},{8,9},{9,8},{10,11... | collective-permute-start | bytes 1179656 | tf_op jit(solution)/shard_map/ppermute | solution.py:894
  983.6 42.7 %collective-permute-start.117 = (bf16[2,128,1536]{2,1,0:T(8,128)(2,1)}, bf16[2,128,1536]{2,1,0:T(8,128)(2,1)}, u32[]{:S(2)}, u32[]{:S(2)}) collective-permute-start(bf16[2,128,1536]{2,1,0:T(8,128)(2,1)} %dynamic-slice_bitcast_fusion.1), channel_id=1, source_target_pairs={{0,16},{8,24},{16,0},{24,8},{1,17},{9,25},{17,1},{25,9},{2,18},{10... | collective-permute-start | bytes 2359304 | tf_op jit(solution)/shard_map/ppermute | solution.py:894
  987.7 15.5 %collective-permute-start.104 = (bf16[192,1024]{1,0:T(8,128)(2,1)S(1)}, bf16[192,1024]{1,0:T(8,128)(2,1)S(1)}, u32[]{:S(2)}, u32[]{:S(2)}) collective-permute-start(bf16[192,1024]{1,0:T(8,128)(2,1)S(1)} %pad_maximum_fusion.18), channel_id=1, source_target_pairs={{0,2},{1,3},{2,4},{3,5},{4,6},{5,7},{6,0},{7,1},{8,10},{9,11},{10,... | collective-permute-start | bytes 1179656 | tf_op jit(solution)/shard_map/ppermute | solution.py:894
  989.2 30.8 %collective-permute-start.107 = (bf16[192,1024]{1,0:T(8,128)(2,1)S(1)}, bf16[192,1024]{1,0:T(8,128)(2,1)}, u32[]{:S(2)}, u32[]{:S(2)}) collective-permute-start(bf16[192,1024]{1,0:T(8,128)(2,1)S(1)} %pad_maximum_fusion.20), channel_id=1, source_target_pairs={{0,6},{1,7},{2,0},{3,1},{4,2},{5,3},{6,4},{7,5},{8,14},{9,15},{10,... | collective-permute-start | bytes 1179656 | tf_op jit(solution)/shard_map/ppermute | solution.py:894
  (246 other events, 2956.6 us)
Sparse Core Ops, SparseCore 0:
  11.2 49.0 all-gather.13
  62.5 34.1 all-gather.7
  99.4 81.0 all-gather.15
  198.1 50.2 all-gather.9
  327.3 29.5 all-gather.11
  668.4 96.1 reduce-scatter.11
  829.7 100.1 reduce-scatter.9
  933.4 87.7 reduce-scatter.7

commit v4 on v0

--- a/solution.py
+++ b/solution.py
@@ -1,8 +1,11 @@
+import functools
 import math
 
 import jax
 import jax.numpy as jnp
 from jax import lax
+from jax.experimental import pallas as pl
+from jax.experimental.pallas import tpu as pltpu
 from jax.sharding import PartitionSpec as P
 
 HEADS = 24
@@ -486,9 +489,1207 @@
     )
 
 
+NN = (((1,), (0,)), ((), ()))
+NT = (((1,), (1,)), ((), ()))
+TN = (((0,), (0,)), ((), ()))
+FE_STEP = 512
+KERNEL_MIB = 58
+
+
+def mm(a, b, dims=NN):
+    return lax.dot_general(a, b, dims, preferred_element_type=jnp.float32)
+
+
+def whole(shape):
+    return pl.BlockSpec(shape, lambda *_: (0,) * len(shape))
+
+
+def anywhere():
+    return pl.BlockSpec(memory_space=pl.ANY)
+
+
+def kernel_params():
+    return pltpu.CompilerParams(vmem_limit_bytes=KERNEL_MIB * 1024 * 1024)
+
+
+def shaped(shape, dtype=jnp.bfloat16):
+    return jax.ShapeDtypeStruct(shape, dtype)
+
+
+RING = (0, 2, 1, 3)
+
+
+def bring_expert_weights(bring, ctx_ref, quarters, w_gate_up_here, w_down_here, e, p):
+    gate_up, down = quarters[:4], quarters[4:]
+    hidden_width = w_down_here.shape[1]
+    copies = []
+    for r in range(4):
+        rows = gate_up[r].shape[1]
+        at = pl.ds(pl.multiple_of((ctx_ref[0] ^ r) * rows, rows), rows)
+        for side in range(2):
+            span = slice(side * hidden_width + p * FE_STEP, side * hidden_width + (p + 1) * FE_STEP)
+            copies.append(bring(gate_up[r].at[e, :, span], w_gate_up_here.at[e, at, span]))
+    if p == 0:
+        for r in range(4):
+            rows = down[r].shape[1]
+            at = pl.ds(pl.multiple_of((ctx_ref[0] ^ r) * rows, rows), rows)
+            copies.append(bring(down[r].at[e], w_down_here.at[e, at, :]))
+    return copies
+
+
+def experts_forward_body(group, first_id, lane_offset, ctx_ref, rows_0, rows_1, ids_in, router_in, own_in, *refs):
+    (out_0, out_1, all_rows, all_gate, all_up, all_probs) = refs[-19:-13]
+    (
+        rows, w_gate_up_here, w_down_here, gate_here, up_here, probs, ring_rows,
+        ids, router, own, result, in_sems, out_sems,
+    ) = refs[-13:]
+    block, width = rows_0.shape
+    count = 2 * block
+    expert_count, hidden_width = w_down_here.shape[0], w_down_here.shape[1]
+    steps = hidden_width // FE_STEP
+    incoming = []
+
+    def bring(source, target):
+        copy = pltpu.make_async_copy(source, target, in_sems.at[len(incoming)])
+        copy.start()
+        incoming.append(copy)
+        return copy
+
+    span = pl.ds(group * count, count)
+    row_copies = [
+        bring(rows_0, rows.at[:block]),
+        bring(rows_1, rows.at[block:]),
+        bring(ids_in.at[span], ids),
+        bring(router_in, router),
+        bring(own_in, own),
+    ]
+    weight_copies = []
+    for e in range(expert_count):
+        for p in range(steps):
+            weight_copies.append(
+                bring_expert_weights(bring, ctx_ref, refs[:8], w_gate_up_here, w_down_here, e, p)
+            )
+    outgoing = []
+
+    def send(source, target):
+        copy = pltpu.make_async_copy(source, target, out_sems.at[len(outgoing)])
+        copy.start()
+        outgoing.append(copy)
+
+    for copy in row_copies:
+        copy.wait()
+    lane = lax.broadcasted_iota(jnp.int32, probs.shape, 1).astype(jnp.float32)
+    chosen_ids = ids[...].astype(jnp.float32) + lane_offset
+    listed = lane == chosen_ids[:, first_id : first_id + 1]
+    for k in range(1, TOP):
+        at = first_id + k
+        listed = jnp.logical_or(listed, lane == chosen_ids[:, at : at + 1])
+    logits = jnp.where(listed, mm(rows[...], router[...]), masked_score)
+    weights = jnp.exp(logits - jnp.max(logits, -1, keepdims=True))
+    gates = weights / jnp.sum(weights, -1, keepdims=True)
+    probs[...] = gates
+    part = width // 4
+    for place, r in enumerate(RING):
+        at = pl.multiple_of((ctx_ref[0] ^ r) * part, part)
+        ring_rows[:, place * part : (place + 1) * part] = rows[:, pl.ds(at, part)]
+    send(ring_rows, all_rows.at[span])
+    send(probs, all_probs.at[span])
+    total = jnp.zeros((count, width), jnp.float32)
+    for e in range(expert_count):
+        chosen = jnp.sum(gates * own[e : e + 1, :], -1, keepdims=True)
+        for p in range(steps):
+            for copy in weight_copies[e * steps + p]:
+                copy.wait()
+            lower = slice(p * FE_STEP, (p + 1) * FE_STEP)
+            upper = slice(hidden_width + p * FE_STEP, hidden_width + (p + 1) * FE_STEP)
+            gate = mm(rows[...], w_gate_up_here[e, :, lower])
+            up = mm(rows[...], w_gate_up_here[e, :, upper])
+            flat = slice(e * hidden_width + p * FE_STEP, e * hidden_width + (p + 1) * FE_STEP)
+            gate_here[:, flat] = gate.astype(jnp.bfloat16)
+            up_here[:, flat] = up.astype(jnp.bfloat16)
+            hidden = (gate * jax.nn.sigmoid(gate) * up * chosen).astype(jnp.bfloat16)
+            total = total + mm(hidden, w_down_here[e, lower, :])
+    send(gate_here, all_gate.at[span])
+    send(up_here, all_up.at[span])
+    result[...] = total.astype(jnp.bfloat16)
+    send(result.at[:block], out_0)
+    send(result.at[block:], out_1)
+    for copy in outgoing:
+        copy.wait()
+
+
+def vmem():
+    return pl.BlockSpec(memory_space=pltpu.VMEM)
+
+
+def smem():
+    return pl.BlockSpec(memory_space=pltpu.SMEM)
+
+
+def expert_shapes(weights):
+    (count, rows, width), (_, down_rows, down_width) = weights[0].shape, weights[4].shape
+    return (count, 4 * rows, width), (count, 4 * down_rows, down_width)
+
+
+def expert_cost(count, width, expert_count, hidden_width):
+    return pl.CostEstimate(
+        flops=6 * count * width * expert_count * hidden_width,
+        bytes_accessed=6 * width * expert_count * hidden_width,
+        transcendentals=count * expert_count * hidden_width,
+    )
+
+
+def experts_forward(
+    group, groups, ctx_ref, rows, ids, first_id, lane_offset, router, own, weights, kept
+):
+    block, width = rows[0].shape
+    count = 2 * block
+    gate_up_shape, down_shape = expert_shapes(weights)
+    expert_count, hidden_width = down_shape[0], down_shape[1]
+    flat = expert_count * hidden_width
+    low, f32 = jnp.bfloat16, jnp.float32
+    inputs = [ctx_ref, *rows, ids, router, own, *weights, *kept]
+    return pl.pallas_call(
+        functools.partial(experts_forward_body, group, first_id, lane_offset),
+        in_specs=[smem()] + [anywhere()] * (13 + len(kept)),
+        out_specs=[anywhere()] * 6,
+        out_shape=[
+            shaped((block, width)),
+            shaped((block, width)),
+            shaped((groups * count, width)),
+            shaped((groups * count, flat)),
+            shaped((groups * count, flat)),
+            shaped((groups * count, 128), f32),
+        ],
+        input_output_aliases={14 + i: 2 + i for i in range(len(kept))},
+        scratch_shapes=[
+            pltpu.VMEM((count, width), low),
+            pltpu.VMEM(gate_up_shape, low),
+            pltpu.VMEM(down_shape, low),
+            pltpu.VMEM((count, flat), low),
+            pltpu.VMEM((count, flat), low),
+            pltpu.VMEM((count, 128), f32),
+            pltpu.VMEM((count, width), low),
+            pltpu.VMEM((count, ids.shape[1]), low),
+            pltpu.VMEM(router.shape, low),
+            pltpu.VMEM(own.shape, f32),
+            pltpu.VMEM((count, width), low),
+            pltpu.SemaphoreType.DMA((5 + 8 * flat // FE_STEP + 4 * expert_count,)),
+            pltpu.SemaphoreType.DMA((6,)),
+        ],
+        compiler_params=kernel_params(),
+        cost_estimate=expert_cost(count, width, expert_count, hidden_width),
+    )(*inputs)
+
+
+def experts_backward_body(group, ctx_ref, grads_0, grads_1, probs_in, gate_in, up_in, router_in, own_in, *refs):
+    out_0, out_1, all_grads, all_grad_gate, all_grad_up, all_hidden, all_logits = refs[-23:-16]
+    (
+        sent, w_gate_up_here, w_down_here, gates, ups, probs, grads, grad_gates, grad_ups,
+        hiddens, logits, router, own, result, in_sems, out_sems,
+    ) = refs[-16:]
+    block, width = out_0.shape
+    count = 2 * block
+    expert_count, hidden_width = w_down_here.shape[0], w_down_here.shape[1]
+    steps = hidden_width // FE_STEP
+    rows_here = pl.ds(group * count, count)
+    incoming = []
+
+    def bring(source, target):
+        copy = pltpu.make_async_copy(source, target, in_sems.at[len(incoming)])
+        copy.start()
+        incoming.append(copy)
+        return copy
+
+    first_copies = [
+        bring(grads_0, sent.at[:block]),
+        bring(grads_1, sent.at[block:]),
+        bring(probs_in.at[rows_here], probs),
+        bring(router_in, router),
+        bring(own_in, own),
+    ]
+    weight_copies = []
+    for e in range(expert_count):
+        for p in range(steps):
+            flat = slice(e * hidden_width + p * FE_STEP, e * hidden_width + (p + 1) * FE_STEP)
+            weight_copies.append(
+                [
+                    bring(gate_in.at[rows_here, flat], gates.at[:, flat]),
+                    bring(up_in.at[rows_here, flat], ups.at[:, flat]),
+                ]
+                + bring_expert_weights(bring, ctx_ref, refs[:8], w_gate_up_here, w_down_here, e, p)
+            )
+    outgoing = []
+
+    def send(source, target):
+        copy = pltpu.make_async_copy(source, target, out_sems.at[len(outgoing)])
+        copy.start()
+        outgoing.append(copy)
+
+    for copy in first_copies:
+        copy.wait()
+    grads[...] = sent[:, :width]
+    mean = sent[:, width : width + 1].astype(jnp.float32) + sent[:, width + 1 : width + 2].astype(
+        jnp.float32
+    )
+    send(grads, all_grads.at[rows_here])
+    total = jnp.zeros((count, width), jnp.float32)
+    grad_logits = jnp.zeros(probs.shape, jnp.float32)
+    quarter = hidden_width // 4
+    for e in range(expert_count):
+        mine = own[e : e + 1, :]
+        chosen = jnp.sum(probs[...] * mine, -1, keepdims=True)
+        dots = jnp.zeros((count, 1), jnp.float32)
+        for p in range(steps):
+            for copy in weight_copies[e * steps + p]:
+                copy.wait()
+            lower = slice(p * FE_STEP, (p + 1) * FE_STEP)
+            upper = slice(hidden_width + p * FE_STEP, hidden_width + (p + 1) * FE_STEP)
+            flat = slice(e * hidden_width + p * FE_STEP, e * hidden_width + (p + 1) * FE_STEP)
+            plain = mm(grads[...], w_down_here[e, lower, :], NT)
+            gate = gates[:, flat].astype(jnp.float32)
+            up = ups[:, flat].astype(jnp.float32)
+            sigmoid_gate = jax.nn.sigmoid(gate)
+            silu_gate = gate * sigmoid_gate
+            hidden = silu_gate * up
+            dots = dots + jnp.sum(plain * hidden, -1, keepdims=True)
+            hidden = (hidden * chosen).astype(jnp.bfloat16)
+            for q in range(FE_STEP // quarter):
+                r = ctx_ref[0] ^ (p * (FE_STEP // quarter) + q)
+                at = jnp.where(r == 1, 2, jnp.where(r == 2, 1, r)) * expert_count + e
+                hiddens[:, pl.ds(pl.multiple_of(at * quarter, quarter), quarter)] = hidden[
+                    :, q * quarter : (q + 1) * quarter
+                ]
+            plain = plain * chosen
+            grad_gate = (
+                plain * up * sigmoid_gate * (1.0 + gate * (1.0 - sigmoid_gate))
+            ).astype(jnp.bfloat16)
+            grad_up = (plain * silu_gate).astype(jnp.bfloat16)
+            grad_gates[:, flat] = grad_gate
+            grad_ups[:, flat] = grad_up
+            total = (
+                total
+                + mm(grad_gate, w_gate_up_here[e, :, lower], NT)
+                + mm(grad_up, w_gate_up_here[e, :, upper], NT)
+            )
+        grad_logits = grad_logits + chosen * (dots - mean) * mine
+    send(grad_gates, all_grad_gate.at[rows_here])
+    send(grad_ups, all_grad_up.at[rows_here])
+    send(hiddens, all_hidden.at[rows_here])
+    low_logits = grad_logits.astype(jnp.bfloat16)
+    logits[...] = low_logits
+    send(logits, all_logits.at[rows_here])
+    result[...] = (total + mm(low_logits, router[...], NT)).astype(jnp.bfloat16)
+    send(result.at[:block], out_0)
+    send(result.at[block:], out_1)
+    for copy in outgoing:
+        copy.wait()
+
+
+def experts_backward(
+    group, groups, ctx_ref, grads, probs, gate, up, router, own, weights, kept
+):
+    gate_up_shape, down_shape = expert_shapes(weights)
+    expert_count, hidden_width, width = down_shape
+    block = grads[0].shape[0]
+    count = 2 * block
+    flat = expert_count * hidden_width
+    low, f32 = jnp.bfloat16, jnp.float32
+    inputs = [ctx_ref, *grads, probs, gate, up, router, own, *weights, *kept]
+    return pl.pallas_call(
+        functools.partial(experts_backward_body, group),
+        in_specs=[smem()] + [anywhere()] * (15 + len(kept)),
+        out_specs=[anywhere()] * 7,
+        out_shape=[
+            shaped((block, width)),
+            shaped((block, width)),
+            shaped((groups * count, width)),
+            shaped((groups * count, flat)),
+            shaped((groups * count, flat)),
+            shaped((groups * count, flat)),
+            shaped((groups * count, 128)),
+        ],
+        input_output_aliases={16 + i: 2 + i for i in range(len(kept))},
+        scratch_shapes=[
+            pltpu.VMEM((count, grads[0].shape[1]), low),
+            pltpu.VMEM(gate_up_shape, low),
+            pltpu.VMEM(down_shape, low),
+            pltpu.VMEM((count, flat), low),
+            pltpu.VMEM((count, flat), low),
+            pltpu.VMEM((count, 128), f32),
+            pltpu.VMEM((count, width), low),
+            pltpu.VMEM((count, flat), low),
+            pltpu.VMEM((count, flat), low),
+            pltpu.VMEM((count, flat), low),
+            pltpu.VMEM((count, 128), low),
+            pltpu.VMEM(router.shape, low),
+            pltpu.VMEM(own.shape, f32),
+            pltpu.VMEM((count, width), low),
+            pltpu.SemaphoreType.DMA((5 + 10 * flat // FE_STEP + 4 * expert_count,)),
+            pltpu.SemaphoreType.DMA((7,)),
+        ],
+        compiler_params=kernel_params(),
+        cost_estimate=expert_cost(count, width, expert_count, hidden_width),
+    )(*inputs)
+
+
+def turn(block, cosine, sine, lane):
+    half = HEAD_DIM // 2
+    other = jnp.where(
+        lane % HEAD_DIM < half, pltpu.roll(block, 128 - half, 1), pltpu.roll(block, half, 1)
+    )
+    return block * cosine + other * sine
+
+
+def row_places(ctx, count, axis):
+    half = count // 2
+    blocks = []
+    for r in range(4):
+        c = ctx ^ r
+        within = lax.broadcasted_iota(jnp.int32, (count, 1) if axis == 0 else (1, count), axis)
+        blocks.append(
+            jnp.where(within < half, c * half + within, (7 - c) * half + within - half)
+        )
+    return jnp.concatenate(blocks, axis)
+
+
+class Copies:
+    def __init__(self, sems):
+        self.sems, self.all = sems, []
+
+    def start(self, source, target):
+        copy = pltpu.make_async_copy(source, target, self.sems.at[len(self.all)])
+        copy.start()
+        self.all.append(copy)
+        return copy
+
+    def wait(self):
+        for copy in self.all:
+            copy.wait()
+
+
+def attention_forward_body(
+    ctx_ref, rows_0, rows_1, rows_2, rows_3, w_qkv_in, w_out_in, cosine_in, sine_in,
+    out_0, out_1, out_2, out_3, all_rows, qkv_out, attended_out, logs_out,
+    rows, w_qkv, w_out, cosine, sine, ring_rows, qkv, attended, logs, result, in_sems, out_sems,
+):
+    sources, outs = (rows_0, rows_1, rows_2, rows_3), (out_0, out_1, out_2, out_3)
+    count, width = rows_0.shape
+    q_width, total_width = attended.shape[1], qkv.shape[1]
+    kv_width = (total_width - q_width) // 2
+    group = HEADS // KV_HEADS
+    spans = [slice(r * count, (r + 1) * count) for r in range(4)]
+    incoming, outgoing = Copies(in_sems), Copies(out_sems)
+    first = [incoming.start(w_qkv_in, w_qkv), incoming.start(rows_0, rows.at[spans[0]])]
+    tables = [incoming.start(cosine_in, cosine), incoming.start(sine_in, sine)]
+    later = [incoming.start(sources[r], rows.at[spans[r]]) for r in range(1, 4)]
+    last = incoming.start(w_out_in, w_out)
+    for copy in first + tables:
+        copy.wait()
+    part = width // 4
+    lane = lax.broadcasted_iota(jnp.int32, (count, 128), 1)
+    for r in range(4):
+        span = spans[r]
+        if r:
+            later[r - 1].wait()
+        raw = mm(rows[span, :], w_qkv[...])
+        for j in range((q_width + kv_width) // 128):
+            turned = turn(raw[:, 128 * j : 128 * j + 128], cosine[span, :], sine[span, :], lane)
+            if 128 * j < q_width:
+                turned = turned * HEAD_DIM ** (-0.5)
+            qkv[span, 128 * j : 128 * j + 128] = turned.astype(jnp.bfloat16)
+        qkv[span, q_width + kv_width :] = raw[:, q_width + kv_width :].astype(jnp.bfloat16)
+        for place, distance in enumerate(RING):
+            at = pl.multiple_of((ctx_ref[0] ^ distance) * part, part)
+            ring_rows[span, place * part : (place + 1) * part] = rows[span, pl.ds(at, part)]
+    outgoing.start(qkv, qkv_out)
+    outgoing.start(ring_rows, all_rows)
+    visible = row_places(ctx_ref[0], count, 0) >= row_places(ctx_ref[0], count, 1)
+    for head in range(q_width // HEAD_DIM):
+        at, of = head * HEAD_DIM, (head // group) * HEAD_DIM
+        queries = qkv[:, at : at + HEAD_DIM]
+        keys = qkv[:, q_width + of : q_width + of + HEAD_DIM]
+        values = qkv[:, q_width + kv_width + of : q_width + kv_width + of + HEAD_DIM]
+        scores = jnp.where(visible, mm(queries, keys, NT), masked_score)
+        top = jnp.max(scores, -1, keepdims=True)
+        weights = jnp.exp(scores - top)
+        total = jnp.sum(weights, -1, keepdims=True)
+        logs[:, head : head + 1] = top + jnp.log(total)
+        probs = (weights * (1.0 / total)).astype(jnp.bfloat16)
+        attended[:, at : at + HEAD_DIM] = mm(probs, values).astype(jnp.bfloat16)
+    outgoing.start(logs, logs_out)
+    outgoing.start(attended, attended_out)
+    last.wait()
+    for r in (1, 3, 0, 2):
+        result[spans[r], :] = mm(attended[spans[r], :], w_out[...]).astype(jnp.bfloat16)
+        outgoing.start(result.at[spans[r]], outs[r])
+    outgoing.wait()
+
+
+def attention_forward(ctx_ref, rows, w_qkv, w_out, total_width, tables):
+    count, width = rows[0].shape
+    seq = 4 * count
+    q_width = w_out.shape[0]
+    low, f32 = jnp.bfloat16, jnp.float32
+    outs = pl.pallas_call(
+        attention_forward_body,
+        in_specs=[smem()] + [anywhere()] * 8,
+        out_specs=[anywhere()] * 8,
+        out_shape=[shaped((count, width))] * 4
+        + [
+            shaped((seq, width)),
+            shaped((seq, total_width)),
+            shaped((seq, q_width)),
+            shaped((seq, 128), f32),
+        ],
+        scratch_shapes=[
+            pltpu.VMEM((seq, width), low),
+            pltpu.VMEM(w_qkv.shape, low),
+            pltpu.VMEM(w_out.shape, low),
+            pltpu.VMEM((seq, 128), f32),
+            pltpu.VMEM((seq, 128), f32),
+            pltpu.VMEM((seq, width), low),
+            pltpu.VMEM((seq, total_width), low),
+            pltpu.VMEM((seq, q_width), low),
+            pltpu.VMEM((seq, 128), f32),
+            pltpu.VMEM((seq, width), low),
+            pltpu.SemaphoreType.DMA((8,)),
+            pltpu.SemaphoreType.DMA((8,)),
+        ],
+        compiler_params=kernel_params(),
+        cost_estimate=pl.CostEstimate(
+            flops=2 * seq * width * (total_width + q_width) + 4 * seq * seq * q_width,
+            bytes_accessed=2 * (seq * width * 2 + width * (total_width + q_width)),
+            transcendentals=seq * seq * (q_width // HEAD_DIM),
+        ),
+    )(ctx_ref, *rows, w_qkv, w_out, *tables)
+    return outs[:4], outs[4], outs[5], outs[6], outs[7]
+
+
+def attention_backward_body(
+    ctx_ref, grad_0, grad_1, grad_2, grad_3, rows_in, w_qkv_in, w_out_in, qkv_in, logs_in,
+    cosine_in, sine_in,
+    out_0, out_1, out_2, out_3, all_grads, grad_qkv_out, gain_out,
+    grads, rows, w_qkv, w_out, qkv, logs, cosine, sine, grad_attended, raw, grad_qkv, gain_sum,
+    result, in_sems, out_sems,
+):
+    sources, outs = (grad_0, grad_1, grad_2, grad_3), (out_0, out_1, out_2, out_3)
+    count, width = grad_0.shape
+    seq = 4 * count
+    q_width, total_width = grad_attended.shape[1], qkv.shape[1]
+    kv_width = (total_width - q_width) // 2
+    group = HEADS // KV_HEADS
+    scale = HEAD_DIM ** (-0.5)
+    spans = [slice(r * count, (r + 1) * count) for r in range(4)]
+    incoming, outgoing = Copies(in_sems), Copies(out_sems)
+    first = [incoming.start(w_out_in, w_out)]
+    branches = [incoming.start(sources[r], grads.at[spans[r]]) for r in range(4)]
+    second = [incoming.start(qkv_in, qkv), incoming.start(logs_in, logs)]
+    last = [
+        incoming.start(cosine_in, cosine),
+        incoming.start(sine_in, sine),
+        incoming.start(w_qkv_in, w_qkv),
+        incoming.start(rows_in, rows),
+    ]
+    first[0].wait()
+    for r in range(4):
+        branches[r].wait()
+        grad_attended[spans[r], :] = mm(grads[spans[r], :], w_out[...], NT).astype(jnp.bfloat16)
+    outgoing.start(grads, all_grads)
+    for copy in second:
+        copy.wait()
+    visible = row_places(ctx_ref[0], count, 0) >= row_places(ctx_ref[0], count, 1)
+    for kv_head in range(kv_width // HEAD_DIM):
+        k_at = q_width + kv_head * HEAD_DIM
+        v_at = k_at + kv_width
+        keys, values = qkv[:, k_at : k_at + HEAD_DIM], qkv[:, v_at : v_at + HEAD_DIM]
+        grad_keys = jnp.zeros((HEAD_DIM, seq), jnp.float32)
+        grad_values = jnp.zeros((HEAD_DIM, seq), jnp.float32)
+        for head in range(kv_head * group, (kv_head + 1) * group):
+            at = head * HEAD_DIM
+            queries = qkv[:, at : at + HEAD_DIM]
+            grad_head = grad_attended[:, at : at + HEAD_DIM]
+            scores = mm(queries, keys, NT)
+            probs = jnp.where(visible, jnp.exp(scores - logs[:, head : head + 1]), 0.0)
+            grad_values += mm(grad_head.T, probs.astype(jnp.bfloat16))
+            weighted = probs * mm(grad_head, values, NT)
+            grad_scores = (weighted - probs * jnp.sum(weighted, -1, keepdims=True)).astype(
+                jnp.bfloat16
+            )
+            raw[:, at : at + HEAD_DIM] = mm(grad_scores, keys) * scale
+            grad_keys += mm(queries.T, grad_scores)
+        raw[:, k_at : k_at + HEAD_DIM] = grad_keys.T
+        raw[:, v_at : v_at + HEAD_DIM] = grad_values.T
+    for copy in last:
+        copy.wait()
+    gain_sum[...] = jnp.zeros_like(gain_sum)
+    lane = lax.broadcasted_iota(jnp.int32, (count, 128), 1)
+    part = width // 4
+    for r in (1, 3, 0, 2):
+        span = spans[r]
+        for j in range((q_width + kv_width) // 128):
+            columns = slice(128 * j, 128 * j + 128)
+            grad_qkv[span, columns] = turn(
+                raw[span, columns], cosine[span, :], -sine[span, :], lane
+            ).astype(jnp.bfloat16)
+        grad_qkv[span, q_width + kv_width :] = raw[span, q_width + kv_width :].astype(jnp.bfloat16)
+        result[span, :] = mm(grad_qkv[span, :], w_qkv[...], NT).astype(jnp.bfloat16)
+        outgoing.start(result.at[span], outs[r])
+    outgoing.start(grad_qkv, grad_qkv_out)
+    for r in range(4):
+        span = spans[r]
+        for place, distance in enumerate(RING):
+            at = pl.multiple_of((ctx_ref[0] ^ distance) * part, part)
+            spot = slice(place * part, (place + 1) * part)
+            gain_sum[:, spot] += jnp.sum(
+                result[span, pl.ds(at, part)].astype(jnp.float32)
+                * rows[span, spot].astype(jnp.float32),
+                0,
+                keepdims=True,
+            )
+    outgoing.start(gain_sum, gain_out)
+    outgoing.wait()
+
+
+def attention_backward(ctx_ref, grads, rows, w_qkv, w_out, qkv, logs, tables):
+    count, width = grads[0].shape
+    seq = 4 * count
+    q_width, total_width = w_out.shape[0], qkv.shape[1]
+    low, f32 = jnp.bfloat16, jnp.float32
+    outs = pl.pallas_call(
+        attention_backward_body,
+        in_specs=[smem()] + [anywhere()] * 11,
+        out_specs=[anywhere()] * 7,
+        out_shape=[shaped((count, width))] * 4
+        + [
+            shaped((seq, width)),
+            shaped((seq, total_width)),
+            shaped((1, width), f32),
+        ],
+        scratch_shapes=[
+            pltpu.VMEM((seq, width), low),
+            pltpu.VMEM((seq, width), low),
+            pltpu.VMEM(w_qkv.shape, low),
+            pltpu.VMEM(w_out.shape, low),
+            pltpu.VMEM((seq, total_width), low),
+            pltpu.VMEM((seq, 128), f32),
+            pltpu.VMEM((seq, 128), f32),
+            pltpu.VMEM((seq, 128), f32),
+            pltpu.VMEM((seq, q_width), low),
+            pltpu.VMEM((seq, total_width), f32),
+            pltpu.VMEM((seq, total_width), low),
+            pltpu.VMEM((1, width), f32),
+            pltpu.VMEM((seq, width), low),
+            pltpu.SemaphoreType.DMA((11,)),
+            pltpu.SemaphoreType.DMA((7,)),
+        ],
+        compiler_params=kernel_params(),
+        cost_estimate=pl.CostEstimate(
+            flops=2 * seq * width * (total_width + q_width) + 10 * seq * seq * q_width,
+            bytes_accessed=2 * (seq * width * 3 + width * (total_width + q_width)),
+            transcendentals=seq * seq * (q_width // HEAD_DIM),
+        ),
+    )(ctx_ref, *grads, rows, w_qkv, w_out, qkv, logs, *tables)
+    return outs[:4], outs[4], outs[5], outs[6]
+
+
+def place_body(members, shares, *refs):
+    shards = [refs[0].at[r] for r in range(8)] if refs[0].shape[0] == 8 else refs[:8]
+    outs = refs[1:] if refs[0].shape[0] == 8 else refs[8:]
+    front = outs[0].shape[3]
+    for r in range(8):
+        for c in range(4):
+            outs[0][members[8 + c], members[r]] = shards[r][c, :, :front]
+        for out in outs[1:]:
+            q_part = out.shape[1] // 4
+            span = pl.ds(pl.multiple_of(members[r] * shares, shares), shares)
+            for j in range(4):
+                out[span, j * q_part : (j + 1) * q_part] = shards[r][j, :, front:]
+
+
+def place(members, shards, front):
+    four, share, width = shards[0].shape[-3:]
+    outs = [shaped((four, 8, share, front))]
+    if width > front:
+        outs.append(shaped((8 * share, four * (width - front))))
+    return pl.pallas_call(
+        lambda members_ref, *refs: place_body(members_ref, share, *refs),
+        in_specs=[smem()] + [vmem()] * len(shards),
+        out_shape=outs,
+        compiler_params=kernel_params(),
+    )(members, *shards)
+
+
+def weight_blocks_body(members, w_query, w_key_value, w_router, gains, *outs):
+    layers, share, q_width = w_query.shape
+    kv_width = w_key_value.shape[2] // 2
+    q_part, kv_part = q_width // 4, kv_width // 4
+    experts = w_router.shape[2]
+    small = outs[0].shape[1] - 128
+    for r in range(4):
+        c = members[8 + r]
+        outs[r][:, small:] = jnp.zeros((share, 128), jnp.bfloat16)
+        for i in range(layers):
+            at = i * (q_part + 2 * kv_part)
+            outs[r][:, at : at + q_part] = w_query[
+                i, :, pl.ds(pl.multiple_of(c * q_part, q_part), q_part)
+            ]
+            for side in range(2):
+                to = at + q_part + side * kv_part
+                outs[r][:, to : to + kv_part] = w_key_value[
+                    i, :, pl.ds(pl.multiple_of(side * kv_width + c * kv_part, kv_part), kv_part)
+                ]
+            at = small + i * experts
+            outs[r][:, at : at + experts] = w_router[i]
+            at = small + layers * experts + 2 * i
+            outs[r][:, at : at + 2] = gains[i]
+
+
+def weight_blocks(members, w_query, w_key_value, w_router, gains):
+    layers, share, q_width = w_query.shape
+    block = shaped((share, layers * (q_width + w_key_value.shape[2]) // 4 + 128))
+    return pl.pallas_call(
+        weight_blocks_body,
+        in_specs=[smem()] + [vmem()] * 4,
+        out_shape=[block] * 4,
+        compiler_params=kernel_params(),
+    )(members, w_query, w_key_value, w_router, gains)
+
+
+def pack_shards_body(front, block_0, block_1, block_2, block_3, w_output, ids, *outs):
+    blocks, small_rows = (block_0, block_1, block_2, block_3), outs[-1]
+    layers, share, width = w_output.shape
+    count, top = ids.shape[1:]
+    small_rows[...] = jnp.zeros_like(small_rows)
+    for r in range(4):
+        span = slice(r * share, (r + 1) * share)
+        for i in range(layers):
+            outs[i][span, :front] = blocks[r][:, i * front : (i + 1) * front]
+            outs[i][span, front:] = w_output[i, :, r * (width // 4) : (r + 1) * (width // 4)]
+        small_rows[span, :] = blocks[r][:, layers * front :]
+    for i in range(layers):
+        at = 64 + top * i
+        small_rows[:count, at : at + top] = ids[i].astype(jnp.float32).astype(jnp.bfloat16)
+
+
+def pack_shards(blocks, w_output, ids, front):
+    layers, share, width = w_output.shape
+    return pl.pallas_call(
+        functools.partial(pack_shards_body, front),
+        in_specs=[vmem()] * 6,
+        out_shape=[shaped((4 * share, front + width // 4))] * layers + [shaped((4 * share, 128))],
+        compiler_params=kernel_params(),
+    )(*blocks, w_output, ids)
+
+
+def pack_grads_body(members, qkv, small, out, *parts):
+    front, lanes = qkv.shape[3], small.shape[3]
+    q_part = out.shape[1] // 4
+    share = qkv.shape[2]
+    for r in range(8):
+        m = members[r]
+        part = parts[r] if len(parts) > 1 else parts[0].at[r]
+        for place, distance in enumerate(RING):
+            part[distance, :, :front] = qkv[place, m]
+            part[distance, :, front : front + lanes] = small[place, m]
+        for j in range(4):
+            part[j, :, front + lanes :] = out[
+                pl.ds(pl.multiple_of(m * share, share), share), j * q_part : (j + 1) * q_part
+            ]
+
+
+def pack_grads(members, qkv, small, out, apart):
+    four, eight, share, front = qkv.shape
+    shape = (four, share, front + small.shape[3] + out.shape[1] // 4)
+    return pl.pallas_call(
+        pack_grads_body,
+        in_specs=[smem()] + [vmem()] * 3,
+        out_shape=[shaped(shape)] * 8 if apart else [shaped((eight, *shape))],
+        compiler_params=kernel_params(),
+    )(members, qkv, small, out)
+
+
+def finish_attention_body(layers, members, *refs):
+    blocks, outs = refs[: 5 * layers], refs[5 * layers :]
+    query, key_value, output, router, gains = outs
+    experts, lane_count = router.shape[2], layers * router.shape[2]
+    q_part, kv_part = query.shape[2] // 4, key_value.shape[2] // 8
+    front = q_part + 2 * kv_part
+    kv_width = 4 * kv_part
+    for i in range(layers):
+        lanes = jnp.zeros((query.shape[1], 128), jnp.float32)
+        for r in range(4):
+            c = members[8 + r]
+            block = blocks[5 * i + r]
+            query[i, :, pl.ds(pl.multiple_of(c * q_part, q_part), q_part)] = block[
+                :, :q_part
+            ].astype(jnp.float32)
+            for side in range(2):
+                at = pl.multiple_of(side * kv_width + c * kv_part, kv_part)
+                key_value[i, :, pl.ds(at, kv_part)] = block[
+                    :, q_part + side * kv_part : q_part + (side + 1) * kv_part
+                ].astype(jnp.float32)
+            lanes = lanes + block[:, front:].astype(jnp.float32)
+        router[i] = lanes[:, i * experts : (i + 1) * experts]
+        gains[i] = lanes[:, lane_count : lane_count + 2]
+        own = blocks[5 * i + 4]
+        for j in range(4):
+            output[i, :, j * q_part : (j + 1) * q_part] = own[j].astype(jnp.float32)
+
+
+def finish_attention(members, layers, expert_total):
+    share, q_part = layers[0][4].shape[1:]
+    front = layers[0][0].shape[1] - 128
+    total = len(layers)
+    f32 = jnp.float32
+    return pl.pallas_call(
+        functools.partial(finish_attention_body, total),
+        in_specs=[smem()] + [vmem()] * (5 * total),
+        out_shape=[
+            shaped((total, share, 4 * q_part), f32),
+            shaped((total, share, 4 * (front - q_part)), f32),
+            shaped((total, share, 4 * q_part), f32),
+            shaped((total, share, expert_total), f32),
+            shaped((total, share, 2), f32),
+        ],
+        compiler_params=kernel_params(),
+    )(members, *[block for layer in layers for block in layer])
+
+
+def finish_experts_body(
+    gate_held, gate_sent, up_held, up_sent, down_held, down_sent, *refs
+):
+    gate_up, down = refs[-2:]
+    half = gate_up.shape[3] // 2
+    gate_up[0, 0, :, :half] = gate_held[...].astype(jnp.float32) + gate_sent[...].astype(jnp.float32)
+    gate_up[0, 0, :, half:] = up_held[...].astype(jnp.float32) + up_sent[...].astype(jnp.float32)
+    down[0, 0] = down_held[...].astype(jnp.float32) + down_sent[...].astype(jnp.float32)
+
+
+def finish_experts(layer, layers, experts, held, sent, kept):
+    rows, flat = sent[0].shape
+    half = flat // experts
+    down_rows, width = sent[2].shape[0] // experts, sent[2].shape[1]
+    gate_spec = pl.BlockSpec((rows, half), lambda e: (0, e))
+    down_spec = pl.BlockSpec((down_rows, width), lambda e: (e, 0))
+    return pl.pallas_call(
+        finish_experts_body,
+        grid=(experts,),
+        in_specs=[gate_spec] * 4 + [down_spec] * 2 + [anywhere()] * len(kept),
+        out_specs=[
+            pl.BlockSpec((1, 1, rows, 2 * half), lambda e: (layer, e, 0, 0)),
+            pl.BlockSpec((1, 1, down_rows, width), lambda e: (layer, e, 0, 0)),
+        ],
+        out_shape=[
+            shaped((layers, experts, rows, 2 * half), jnp.float32),
+            shaped((layers, experts, down_rows, width), jnp.float32),
+        ],
+        input_output_aliases={6 + i: i for i in range(len(kept))},
+        compiler_params=kernel_params(),
+    )(held[0], sent[0], held[1], sent[1], held[2], sent[2], *kept)
+
+
+def rotate_ranks(values_in, axis_name, total, target_of):
+    return lax.ppermute(values_in, axis_name, [(i, target_of(i)) for i in range(total)])
+
+
+def swap_y(values_in):
+    return rotate_ranks(values_in, "fsdp", 8, lambda i: i ^ 1)
+
+
+def move_z(values_in, steps):
+    return rotate_ranks(values_in, "fsdp", 8, lambda i: (i + 2 * steps) % 8)
+
+
+def swap_core(values_in):
+    return rotate_ranks(values_in, "ctx", 4, lambda i: i ^ 1)
+
+
+def swap_x(values_in):
+    return rotate_ranks(values_in, "ctx", 4, lambda i: i ^ 2)
+
+
+def swap_both(values_in):
+    return rotate_ranks(values_in, "ctx", 4, lambda i: i ^ 3)
+
+
+def to_members(blocks):
+    return [blocks[0], swap_core(blocks[1]), swap_x(blocks[2]), swap_both(blocks[3])]
+
+
+def after(value, *others):
+    return lax.optimization_barrier((value, *others))[0]
+
+
+def wide(value):
+    return value.astype(jnp.float32)
+
+
+def fsdp_members(index):
+    z, y = index // 2, index % 2
+    return [((z + dz) % 4) * 2 + (y ^ dy) for dz in (0, 3, 2, 1) for dy in (0, 1)]
+
+
+def gather_fsdp(block, work=None):
+    below = move_z(block, 1)
+    own_mirror = swap_y(block)
+    if work is None:
+        far = move_z(after(below, own_mirror), 1)
+        below_mirror = swap_y(after(below, own_mirror))
+        above = move_z(after(block, far, below_mirror), -1)
+        far_mirror = swap_y(after(far, below_mirror))
+        above_mirror = swap_y(after(above, far_mirror))
+        return [block, own_mirror, below, below_mirror, far, far_mirror, above, above_mirror]
+    far = move_z(below, 1)
+    below_mirror = swap_y(below)
+    done = work(0, (after(block, below), own_mirror))
+    above = move_z(after(block, far, done), -1)
+    far_mirror = swap_y(after(far, done))
+    done = work(1, (after(below, far), below_mirror))
+    above_mirror = swap_y(after(above, done))
+    done = work(2, (after(far, above), far_mirror))
+    work(3, (after(above, done), above_mirror))
+
+
+def scatter_fsdp(parts, beside=None):
+    low = jnp.bfloat16
+    results = []
+
+    def run(start):
+        if beside:
+            results.append(beside[len(results)](start))
+            return jax.tree.leaves(results[-1])
+        return []
+
+    far = (wide(parts[4]) + wide(swap_y(parts[5]))).astype(low)
+    from_far = move_z(far, 1)
+    above_mirror = swap_y(parts[7])
+    done = run(far)
+    above = (wide(parts[6]) + wide(above_mirror) + wide(from_far)).astype(low)
+    from_below = move_z(after(above, *done), 1)
+    below_mirror = swap_y(after(parts[3], above))
+    done = run(above)
+    below = (wide(parts[2]) + wide(below_mirror)).astype(low)
+    from_above = move_z(after(below, *done), -1)
+    own_mirror = swap_y(after(parts[1], below))
+    done = run(below)
+    own = wide(parts[0]) + wide(own_mirror) + wide(from_below)
+    return after(own, *done) + wide(from_above), results
+
+
+def gather_ctx(block):
+    across = swap_x(block)
+    return [block, swap_core(block), across, swap_core(across)]
+
+
+def scatter_ctx(parts, *beside):
+    across = wide(parts[2]) + wide(swap_core(parts[3]))
+    own = wide(parts[0]) + wide(swap_core(parts[1]))
+    across = swap_x(across.astype(jnp.bfloat16))
+    if beside:
+        across = after(across, *beside)
+    return own + wide(across)
+
+
+def split_ranks(
+    hidden_in,
+    w_query,
+    w_key_value,
+    w_output,
+    w_router,
+    norm_gains,
+    w_gate_up,
+    w_down,
+    expert_ids,
+    out_grad,
+):
+    both = ("ctx", "fsdp")
+    ctx_total, groups = 4, 8
+    ctx_index, group_index = lax.axis_index("ctx"), lax.axis_index("fsdp")
+    row_count, model_width = hidden_in.shape[1], hidden_in.shape[2]
+    layer_total, share, _ = w_query.shape
+    experts_here = w_gate_up.shape[1]
+    expert_total = experts_here * groups
+    kv_width = w_key_value.shape[2] // 2
+    q_part, kv_part = model_width // ctx_total, kv_width // ctx_total
+    qkv_part = q_part + 2 * kv_part
+    pair_total = groups // 2
+    low = jnp.bfloat16
+    f32 = jnp.float32
+
+    def dot_tn(a, b):
+        return mm(a, b, TN)
+
+    ctx_members = [ctx_index ^ r for r in range(ctx_total)]
+    members = jnp.stack([*fsdp_members(group_index), *ctx_members]).astype(jnp.int32)
+    natural_members = jnp.stack([*range(groups), *ctx_members]).astype(jnp.int32)
+    ring_members = jnp.stack([ctx_members[r] for r in RING])
+    ctx_ref = ctx_index.reshape(1).astype(jnp.int32)
+    expert_lane = jnp.arange(128, dtype=jnp.int32)
+    own_experts = [
+        (
+            expert_lane[None, :]
+            == expert_total * i
+            + group_index * experts_here
+            + jnp.arange(8, dtype=jnp.int32)[:, None]
+        ).astype(f32)
+        for i in range(layer_total)
+    ]
+    gain_lane = expert_total * layer_total
+
+    def ring(vector):
+        return jnp.take(vector.reshape(ctx_total, -1), ring_members, axis=0).reshape(-1)
+
+    def gather_experts(i, start):
+        return [*gather_ctx(after(w_gate_up[i], start)), *gather_ctx(after(w_down[i], start))]
+
+    places = jnp.concatenate(
+        [row_positions((ctx_index ^ r) * row_count, row_count, row_count, ctx_total) for r in range(4)]
+    )
+    half_dim = HEAD_DIM // 2
+    frequency = rope_base ** (-jnp.arange(half_dim, dtype=f32) / half_dim)
+    angles = places.astype(f32)[:, None] * frequency[None, :]
+    cosine, sine = jnp.cos(angles), jnp.sin(angles)
+    tables = (
+        jnp.concatenate([cosine] * 4, -1),
+        jnp.concatenate([-sine, sine, -sine, sine], -1),
+    )
+
+    blocks = to_members(weight_blocks(members, w_query, w_key_value, w_router, norm_gains))
+    hidden_rows = gather_ctx(after(hidden_in.reshape(row_count, model_width), blocks[2]))
+    *layer_shards, small_rows = pack_shards(
+        blocks, w_output, expert_ids.reshape(layer_total, row_count, TOP), qkv_part
+    )
+    shards = gather_fsdp(layer_shards[0])
+    expert_weights = [gather_experts(0, small_rows)]
+    small_pair = jnp.stack([small_rows, swap_y(small_rows)])
+    small_pair = after(small_pair, shards[2])
+    small_all = jnp.concatenate(
+        [small_pair, move_z(small_pair, 1), move_z(small_pair, 2), move_z(small_pair, -1)], 0
+    )
+    small_all = after(small_all, shards[6])
+    ids_all = small_all[:, :row_count, 64 : 64 + layer_total * TOP].reshape(groups * row_count, -1)
+    small = place(members, [small_all.reshape(groups, ctx_total, share, 128)], 128)[0]
+    small = small.reshape(model_width, 128)
+    gains = [
+        wide(small[:, gain_lane + 2 * i : gain_lane + 2 * i + 2]).T for i in range(layer_total)
+    ]
+    ring_gains = [ring(gains[i][0]) for i in range(layer_total)]
+
+    def place_layer(members, shards):
+        shards = [shard.reshape(-1, ctx_total, share, qkv_part + q_part) for shard in shards]
+        if len(shards) > 1:
+            shards = [shard[0] for shard in shards]
+        qkv_weight, out_weight = place(members, shards, qkv_part)
+        return qkv_weight.reshape(model_width, qkv_part), out_weight
+
+    attention_weights = [place_layer(members, shards)]
+    later_weights = [
+        lax.all_gather(after(shard, shards[7]), "fsdp", axis=0, tiled=False)
+        for shard in layer_shards[1:]
+    ]
+
+    residual = wide(hidden_in.reshape(row_count, model_width))
+    saved = []
+    for i in range(layer_total):
+        qkv_weight, out_weight = attention_weights[i]
+        normed, root_first = rms_scaled(residual, gains[i][0])
+        if i == 0:
+            rows = [
+                rms_scaled(wide(block), gains[i][0])[0].astype(low) for block in hidden_rows
+            ]
+        else:
+            rows = gather_ctx(normed.astype(low))
+        branch, rows_first, qkv, attended, logs = attention_forward(
+            ctx_ref, rows, qkv_weight, out_weight, qkv_part, tables
+        )
+        middle = residual + scatter_ctx(branch, *(expert_weights[0] if i == 0 else ()))
+        normed_second, root_second = rms_scaled(middle, gains[i][1])
+        parts, kept = [None] * groups, []
+
+        def forward_work(group, pair):
+            outs = experts_forward(
+                group, pair_total, ctx_ref, pair, ids_all, TOP * i, expert_total * i, small,
+                own_experts[i], expert_weights[i], kept,
+            )
+            parts[2 * group], parts[2 * group + 1] = outs[:2]
+            kept[:] = outs[2:]
+            return outs[0]
+
+        gather_fsdp(normed_second.astype(low), forward_work)
+        rows_second, gate, up, probs = kept
+        beside = None
+        if i + 1 < layer_total:
+            gathered = gather_experts(i + 1, parts[0])
+            beside = (
+                lambda start: [],
+                lambda start: place_layer(natural_members, [after(later_weights[i], start)]),
+                lambda start: gathered,
+            )
+        expert_sum, placed = scatter_fsdp(parts, beside)
+        if beside:
+            attention_weights.append(placed[1])
+            expert_weights.append(gathered)
+        saved.append(
+            (
+                residual, root_first, rows_first, qkv, attended, logs,
+                middle, root_second, rows_second, gate, up, probs, expert_sum,
+            )
+        )
+        residual = middle + expert_sum
+    hidden_out = residual.reshape(1, row_count, model_width).astype(low)
+    grad = wide(out_grad.reshape(row_count, model_width))
+    attention_grads, expert_grads = [], []
+
+    def finish_layer(i, pairs, start, kept):
+        held, sent = [pair[0] for pair in pairs], [pair[1] for pair in pairs]
+        held[0] = after(held[0], start)
+        return finish_experts(i, layer_total, experts_here, held, sent, kept)
+
+    for i in reversed(range(layer_total)):
+        (
+            residual, root_first, rows_first, qkv, attended, logs,
+            middle, root_second, rows_second, gate, up, probs, expert_sum,
+        ) = saved[i]
+        qkv_weight, out_weight = attention_weights[i]
+        mean_gate = jnp.sum(grad * expert_sum, -1, keepdims=True)
+        mean_high = mean_gate.astype(low)
+        mean_low = (mean_gate - wide(mean_high)).astype(low)
+        lanes = jnp.where(expert_lane == 0, mean_high, jnp.where(expert_lane == 1, mean_low, 0))
+        sent = jnp.concatenate([grad.astype(low), lanes.astype(low)], -1)
+        parts, kept = [None] * groups, []
+
+        def backward_work(group, pair):
+            if i + 1 < layer_total:
+                done = (packed, expert_grads[0][0][1], expert_grads[0][1][1], expert_grads[0][2][1])
+                pair = (after(pair[0], done[group]), pair[1])
+            outs = experts_backward(
+                group, pair_total, ctx_ref, pair, probs, gate, up, small, own_experts[i],
+                expert_weights[i], kept,
+            )
+            parts[2 * group], parts[2 * group + 1] = outs[:2]
+            kept[:] = outs[2:]
+            return outs[0]
+
+        gather_fsdp(sent, backward_work)
+        grads_second, grad_gate, grad_up, hidden, grad_logits = kept
+        half_width, half_hidden = model_width // 2, hidden.shape[1] // 2
+
+        def to_other_core(start):
+            ours = after(rows_second, start)[:, half_width:]
+            return [
+                swap_core(dot_tn(part, grads).astype(low))
+                for part, grads in (
+                    (ours, grad_gate),
+                    (ours, grad_up),
+                    (hidden[:, half_hidden:], grads_second),
+                )
+            ]
+
+        def add_core(start):
+            ours = after(rows_second, start)[:, :half_width]
+            return [
+                (dot_tn(part, grads) + wide(other)).astype(low)
+                for part, grads, other in (
+                    (ours, grad_gate, came[0]),
+                    (ours, grad_up, came[1]),
+                    (hidden[:, :half_hidden], grads_second, came[2]),
+                )
+            ]
+
+        came = []
+
+        def first_beside(start):
+            came[:] = to_other_core(start)
+            return came
+
+        def second_beside(start):
+            came[:] = add_core(start)
+            return came
+
+        def third_beside(start):
+            if i + 1 < layer_total:
+                return finish_layer(i + 1, expert_grads[0], start, [])
+            return []
+
+        grad_second, finished = scatter_fsdp(parts, (first_beside, second_beside, third_beside))
+        halves = [(part[: part.shape[0] // 2], part[part.shape[0] // 2 :]) for part in came]
+        small_grads = dot_tn(rows_second, grad_logits)
+        grad_middle, gain_second = rms_back(middle, root_second, gains[i][1], grad_second)
+        grad_middle = grad_middle + grad
+        branch_grads = gather_ctx(grad_middle.astype(low))
+        crossed = []
+        if i == 0:
+            crossed.append(swap_x(halves[0][1]))
+            crossed.append(swap_x(after(halves[1][1], crossed[0], branch_grads[3])))
+            crossed.append(swap_x(after(halves[2][1], crossed[1])))
+            rows_first = after(rows_first, crossed[0])
+        back, rows_branch, grad_qkv, gain_first = attention_backward(
+            ctx_ref, branch_grads, rows_first, qkv_weight, out_weight, qkv,
+            logs, tables,
+        )
+        gain_first = gain_first[0] / ring_gains[i]
+        gain_second = ring(gain_second)
+        small_grads = jnp.where(
+            expert_lane == gain_lane,
+            gain_first[:, None],
+            jnp.where(expert_lane == gain_lane + 1, gain_second[:, None], small_grads),
+        ).astype(low)
+        if crossed:
+            small_grads = after(small_grads, crossed[1])
+        qkv_grads = dot_tn(rows_first, grad_qkv).astype(low)
+        out_grads = dot_tn(attended, rows_branch).astype(low)
+        grad_first = scatter_ctx(back, qkv_grads, out_grads)
+        grad_input, _ = rms_back(residual, root_first, gains[i][0], grad_first)
+        grad = grad_input + grad_middle
+        crossed = crossed or [swap_x(after(sent_half, grad)) for _, sent_half in halves]
+        expert_grads.insert(0, [(half[0], sent) for half, sent in zip(halves, crossed, strict=True)])
+        packs = pack_grads(
+            members if i == 0 else natural_members,
+            qkv_grads.reshape(ctx_total, groups, share, qkv_part),
+            small_grads.reshape(ctx_total, groups, share, 128),
+            out_grads,
+            i == 0,
+        )
+        shard_shape = (ctx_total, share, qkv_part + 128 + q_part)
+        if i == 0:
+            flat = (ctx_total * share, shard_shape[2])
+            packed = scatter_fsdp([pack.reshape(flat) for pack in packs])[0].astype(low)
+        else:
+            packed = packs[0].reshape(groups * ctx_total, *shard_shape[1:])
+            attention_grads.insert(0, lax.psum_scatter(packed, "fsdp", scatter_dimension=0, tiled=True))
+        if i == 0:
+            attention_grads.insert(0, packed.reshape(shard_shape))
+    front = qkv_part + 128
+    blocks = to_members(
+        [jnp.concatenate([part[r, :, :front] for part in attention_grads], -1) for r in range(ctx_total)]
+    )
+    query_out, key_value_out, output_out, router_out, gains_out = finish_attention(
+        members,
+        [
+            [block[:, i * front : (i + 1) * front] for block in blocks] + [part[..., front:]]
+            for i, part in enumerate(attention_grads)
+        ],
+        expert_total,
+    )
+    outs = finish_layer(0, expert_grads[0], attention_grads[0], finished[2])
+    return (
+        hidden_out,
+        grad.reshape(1, row_count, model_width),
+        query_out,
+        key_value_out,
+        output_out,
+        router_out,
+        gains_out,
+        outs[0],
+        outs[1],
+    )
+
+
 def solution(mesh):
+    split = mesh.shape["ctx"] == 4 and mesh.shape["fsdp"] == 8
     return jax.shard_map(
-        on_device,
+        split_ranks if split else on_device,
         mesh=mesh,
         in_specs=(
             P("fsdp", "ctx", None),

time: 2620 us -> 868 us (0.33)
  waiting for transfers between devices: 1490 us -> 365 us
  blocking collectives: 592 us -> 0 us
  Pallas kernels: 0 us -> 207 us
  local copies, waits for them, and re-layouts: 184 us -> 54.1 us
  matrix products: 179 us -> 52.1 us
  starting transfers between devices: 35.9 us -> 112 us
  other arithmetic: 99 us -> 55.3 us
    reduce_scatter x7 -> x1, waiting for transfers between devices: 754 us -> 0.01 us  [split_ranks(): lax.psum_scatter(packed, 'fsdp', scatter_dimension=0, tiled=True)]
    all_gather x4 -> x0, blocking collectives: 482 us -> none  [the longest x2 338 us: on_device(): lax.all_gather(w_router[layer_index], ('ctx', 'fsdp'), axis=0, tiled=True)]
    all_to_all x7 -> x0, waiting for transfers between devices: 429 us -> none  [the longest x2 190 us: on_device(): lax.all_to_all(grad_entering, 'fsdp', split_axis=0, concat_axis=0, tiled=...]
    ppermute x0 -> x128, waiting for transfers between devices: none -> 365 us  [rotate_ranks(): lax.ppermute(values_in, axis_name, [(i, target_of(i)) for i in range(tota...]
    pallas_call x0 -> x30, Pallas kernels: none -> 207 us  [the longest x8 65.8 us: experts_backward(): pl.pallas_call(functools.partial(experts_backward_body, group), in_specs=...]
    all_gather x12 -> x1, waiting for transfers between devices: 188 us -> 0.01 us  [split_ranks(): lax.all_gather(after(shard, shards[7]), 'fsdp', axis=0, tiled=False)]
    dot_general x92 -> x18, matrix products: 179 us -> 52.1 us  [mm(): return lax.dot_general(a, b, dims, preferred_element_type=jnp.float32)]
    unnamed x23 -> x2, waiting for transfers between devices: 115 us -> 0.03 us
  transfers between devices with their start and end apart: 28 -> 130, of which waited for: 20 -> 54; matrix products, arithmetic and copies ran while one was open for 12% -> 15% of each run, Pallas kernels for 0% -> 19%
where the time goes in v4:
time: 868 us; the launch traced here: 862 us
  waiting for transfers between devices  365 us (42%)
  Pallas kernels  207 us (24%)
  starting transfers between devices  112 us (13%)
  other arithmetic  55.3 us (6%)
  local copies, waits for them, and re-layouts  54.1 us (6%)
  matrix products  52.1 us (6%)
  between operations  16.1 us (2%)
    ppermute x128, waiting for transfers between devices, rotate_ranks(): lax.ppermute(values_in, axis_name, [(i, target_of(i)) for i in range(tota...  365 us
    ppermute x128, starting transfers between devices, rotate_ranks(): lax.ppermute(values_in, axis_name, [(i, target_of(i)) for i in range(tota...  112 us
    pallas_call x8, Pallas kernels, experts_backward(): pl.pallas_call(functools.partial(experts_backward_body, group), in_specs=...  65.8 us
    pallas_call x8, Pallas kernels, experts_forward(): pl.pallas_call(functools.partial(experts_forward_body, group, first_id, l...  60 us
    dot_general x18, matrix products, mm(): return lax.dot_general(a, b, dims, preferred_element_type=jnp.float32)  52.1 us
    pallas_call x2, Pallas kernels, attention_backward(): pl.pallas_call(attention_backward_body, in_specs=[smem()] + [anywhere()]...  27.1 us
    unnamed x311, local copies, waits for them, and re-layouts  24.4 us
    pallas_call x2, Pallas kernels, attention_forward(): pl.pallas_call(attention_forward_body, in_specs=[smem()] + [anywhere()] *...  21.9 us
  transfers between devices with their start and end apart: 130, of which 54 were waited for; matrix products, arithmetic and copies ran while one was open for 15% of the time, Pallas kernels for 19%

profile of v4, /device:TPU:0, one launch (start us, length us, event | category | flops | bytes accessed | tf_op | source)
XLA Modules:
  0.0 862.4 jit_solution(1623921031331576211)
XLA Ops:
  33.4 8.3 collective-permute-done.3
  49.8 7.4 collective-permute-done.9
  82.0 4.5 collective-permute-done.16
  90.3 10.9 %shard_map.173 = (bf16[128,1536]{1,0:T(8,128)(2,1)}, bf16[128,1536]{1,0:T(8,128)(2,1)}, bf16[128,1536]{1,0:T(8,128)(2,1)}, bf16[128,1536]{1,0:T(8,128)(2,1)}, bf...) custom-call(s32[1]{0:T(128)} %bitcast.1.ctx_ref, ...), custom_call_target="tpu_custom_call" | custom-call | flops 2013265920 | bytes 6291456 | tf_op jit(solution)/shard_map/pallas_call | solution.py:934
  106.4 10.1 %collective-permute-done.19 = bf16[128,1536]{1,0:T(8,128)(2,1)} collective-permute-done((bf16[128,1536]{1,0:T(8,128)(2,1)}, bf16[128,1536]{1,0:T(8,128)(2,1)}, u32[]{:S(2)}, u32[]{:S(2)}) %collective-permute-start.19) | collective-permute-done | bytes 393248 | tf_op jit(solution)/shard_map/ppermute | solution.py:1293
  120.9 20.7 %collective-permute-done.26.rows_0 = bf16[128,1536]{1,0:T(8,128)(2,1)S(1)} collective-permute-done((bf16[128,1536]{1,0:T(8,128)(2,1)S(1)}, bf16[128,1536]{1,0:T(8,128)(2,1)S(1)}, u32[]{:S(2)}, u32[]{:S(2)}) %collective-permute-start.26) | collective-permute-done | bytes 393248 | tf_op jit(solution)/shard_map/ppermute | solution.py:1293
  145.5 7.8 shard_map.174
  153.3 5.0 collective-permute-done.28.rows_0
  158.4 4.5 collective-permute-start.30
  164.8 7.4 shard_map.175
  172.2 6.3 collective-permute-done.30.rows_0
  179.3 7.4 shard_map.176
  188.8 10.2 %collective-permute-done.34 = bf16[128,1536]{1,0:T(8,128)(2,1)S(1)} collective-permute-done((bf16[128,1536]{1,0:T(8,128)(2,1)}, bf16[128,1536]{1,0:T(8,128)(2,1)S(1)}, u32[]{:S(2)}, u32[]{:S(2)}) %collective-permute-start.34) | collective-permute-done | bytes 393248 | tf_op jit(solution)/shard_map/ppermute | solution.py:1293
  204.3 7.5 shard_map.177
  213.4 7.2 collective-permute-done.33
  225.7 4.8 collective-permute-done.36
  233.8 4.6 collective-permute-done.43.refs_6_
  250.6 7.6 collective-permute-done.45
  259.7 9.7 %collective-permute-done.47.rows_2 = bf16[128,1536]{1,0:T(8,128)(2,1)S(1)} collective-permute-done((bf16[128,1536]{1,0:T(8,128)(2,1)S(1)}, bf16[128,1536]{1,0:T(8,128)(2,1)S(1)}, u32[]{:S(2)}, u32[]{:S(2)}) %collective-permute-start.47) | collective-permute-done | bytes 393248 | tf_op jit(solution)/shard_map/ppermute | solution.py:1293
  271.8 10.9 %shard_map.179 = (bf16[128,1536]{1,0:T(8,128)(2,1)}, bf16[128,1536]{1,0:T(8,128)(2,1)}, bf16[128,1536]{1,0:T(8,128)(2,1)}, bf16[128,1536]{1,0:T(8,128)(2,1)}, bf...) custom-call(s32[1]{0:T(128)} %bitcast.1.ctx_ref, ...), custom_call_target="tpu_custom_call" | custom-call | flops 2013265920 | bytes 6291456 | tf_op jit(solution)/shard_map/pallas_call | solution.py:934
  286.5 10.7 %collective-permute-done.51 = bf16[128,1536]{1,0:T(8,128)(2,1)S(1)} collective-permute-done((bf16[128,1536]{1,0:T(8,128)(2,1)S(1)}, bf16[128,1536]{1,0:T(8,128)(2,1)S(1)}, u32[]{:S(2)}, u32[]{:S(2)}) %collective-permute-start.51) | collective-permute-done | bytes 393248 | tf_op jit(solution)/shard_map/ppermute | solution.py:1293
  300.9 11.2 %collective-permute-done.52.rows_0 = bf16[128,1536]{1,0:T(8,128)(2,1)S(1)} collective-permute-done((bf16[128,1536]{1,0:T(8,128)(2,1)S(1)}, bf16[128,1536]{1,0:T(8,128)(2,1)S(1)}, u32[]{:S(2)}, u32[]{:S(2)}) %collective-permute-start.52) | collective-permute-done | bytes 393248 | tf_op jit(solution)/shard_map/ppermute | solution.py:1293
  314.1 7.5 shard_map.180
  327.9 7.5 shard_map.181
  336.2 7.4 shard_map.182
  345.7 10.2 %collective-permute-done.60 = bf16[128,1536]{1,0:T(8,128)(2,1)S(1)} collective-permute-done((bf16[128,1536]{1,0:T(8,128)(2,1)}, bf16[128,1536]{1,0:T(8,128)(2,1)S(1)}, u32[]{:S(2)}, u32[]{:S(2)}) %collective-permute-start.60) | collective-permute-done | bytes 393248 | tf_op jit(solution)/shard_map/ppermute | solution.py:1293
  361.7 7.5 shard_map.183
  369.6 8.2 collective-permute-done.59
  379.9 9.7 %collective-permute-done.62 = bf16[128,1536]{1,0:T(8,128)(2,1)S(1)} collective-permute-done((bf16[128,1536]{1,0:T(8,128)(2,1)S(1)}, bf16[128,1536]{1,0:T(8,128)(2,1)S(1)}, u32[]{:S(2)}, u32[]{:S(2)}) %collective-permute-start.62) | collective-permute-done | bytes 393248 | tf_op jit(solution)/shard_map/ppermute | solution.py:1293
  393.2 5.4 collective-permute-done.63
  403.7 13.2 %collective-permute-done.66.grads_0 = bf16[128,1664]{1,0:T(8,128)(2,1)S(1)} collective-permute-done((bf16[128,1664]{1,0:T(8,128)(2,1)S(1)}, bf16[128,1664]{1,0:T(8,128)(2,1)S(1)}, u32[]{:S(2)}, u32[]{:S(2)}) %collective-permute-start.66) | collective-permute-done | bytes 426016 | tf_op jit(solution)/shard_map/ppermute | solution.py:1293
  418.7 8.2 shard_map.184
  432.9 8.2 shard_map.185
  442.0 8.2 shard_map.186
  452.3 6.0 collective-permute-done.74
  460.3 4.3 collective-permute-done.72.grads_1
  465.4 8.3 shard_map.187
  485.7 9.3 %collective-permute-done.76 = bf16[128,1536]{1,0:T(8,128)(2,1)S(1)} collective-permute-done((bf16[128,1536]{1,0:T(8,128)(2,1)S(1)}, bf16[128,1536]{1,0:T(8,128)(2,1)S(1)}, u32[]{:S(2)}, u32[]{:S(2)}) %collective-permute-start.76) | collective-permute-done | bytes 393248 | tf_op jit(solution)/shard_map/ppermute | solution.py:1293
  510.2 7.0 collective-permute-done.82
  519.8 9.8 %collective-permute-done.84.grad_2 = bf16[128,1536]{1,0:T(8,128)(2,1)} collective-permute-done((bf16[128,1536]{1,0:T(8,128)(2,1)}, bf16[128,1536]{1,0:T(8,128)(2,1)}, u32[]{:S(2)}, u32[]{:S(2)}) %collective-permute-start.84) | collective-permute-done | bytes 393248 | tf_op jit(solution)/shard_map/ppermute | solution.py:1293
  534.7 13.5 %shard_map.188 = (bf16[128,1536]{1,0:T(8,128)(2,1)}, bf16[128,1536]{1,0:T(8,128)(2,1)}, bf16[128,1536]{1,0:T(8,128)(2,1)}, bf16[128,1536]{1,0:T(8,128)(2,1)}, bf...) custom-call(s32[1]{0:T(128)} %bitcast.1.ctx_ref, ...), custom_call_target="tpu_custom_call" | custom-call | flops 2617245696 | bytes 7864320 | tf_op jit(solution)/shard_map/pallas_call | solution.py:1059
  559.9 5.9 collective-permute-done.88
  572.7 9.2 %collective-permute-done.89.grads_0 = bf16[128,1664]{1,0:T(8,128)(2,1)} collective-permute-done((bf16[128,1664]{1,0:T(8,128)(2,1)}, bf16[128,1664]{1,0:T(8,128)(2,1)}, u32[]{:S(2)}, u32[]{:S(2)}) %collective-permute-start.89) | collective-permute-done | bytes 426016 | tf_op jit(solution)/shard_map/ppermute | solution.py:1293
  584.0 4.1 shard_map.189
  589.1 8.3 shard_map.190
  606.3 8.2 shard_map.191
  615.3 8.2 shard_map.192
  625.7 10.2 %collective-permute-done.100 = bf16[128,1536]{1,0:T(8,128)(2,1)S(1)} collective-permute-done((bf16[128,1536]{1,0:T(8,128)(2,1)}, bf16[128,1536]{1,0:T(8,128)(2,1)S(1)}, u32[]{:S(2)}, u32[]{:S(2)}) %collective-permute-start.100) | collective-permute-done | bytes 393248 | tf_op jit(solution)/shard_map/ppermute | solution.py:1293
  641.8 8.3 shard_map.193
  650.6 4.7 convolution_convert_fusion.7
  664.5 14.7 %collective-permute-done.102 = bf16[128,1536]{1,0:T(8,128)(2,1)} collective-permute-done((bf16[128,1536]{1,0:T(8,128)(2,1)}, bf16[128,1536]{1,0:T(8,128)(2,1)}, u32[]{:S(2)}, u32[]{:S(2)}) %collective-permute-start.102) | collective-permute-done | bytes 393248 | tf_op jit(solution)/shard_map/ppermute | solution.py:1293
  682.9 4.1 shard_map.194
  687.2 4.6 fusion.1
  698.6 4.1 collective-permute-start.108
  702.7 6.2 collective-permute-done.107
  709.1 9.0 %collective-permute-done.108 = bf16[128,1536]{1,0:T(8,128)(2,1)S(1)} collective-permute-done((bf16[128,1536]{1,0:T(8,128)(2,1)S(1)}, bf16[128,1536]{1,0:T(8,128)(2,1)S(1)}, u32[]{:S(2)}, u32[]{:S(2)}) %collective-permute-start.108) | collective-permute-done | bytes 393248 | tf_op jit(solution)/shard_map/ppermute | solution.py:1293
  723.2 9.0 %collective-permute-done.110.grad_2 = bf16[128,1536]{1,0:T(8,128)(2,1)} collective-permute-done((bf16[128,1536]{1,0:T(8,128)(2,1)S(1)}, bf16[128,1536]{1,0:T(8,128)(2,1)}, u32[]{:S(2)}, u32[]{:S(2)}) %collective-permute-start.110) | collective-permute-done | bytes 393248 | tf_op jit(solution)/shard_map/ppermute | solution.py:1293
  734.9 13.2 %collective-permute-done.112.gate_sent = bf16[384,1024]{1,0:T(8,128)(2,1)S(1)} collective-permute-done((bf16[384,1024]{1,0:T(8,128)(2,1)S(1)}, bf16[384,1024]{1,0:T(8,128)(2,1)S(1)}, u32[]{:S(2)}, u32[]{:S(2)}) %collective-permute-start.112) | collective-permute-done | bytes 786464 | tf_op jit(solution)/shard_map/ppermute | solution.py:1293
  749.0 13.7 %shard_map.195 = (bf16[128,1536]{1,0:T(8,128)(2,1)}, bf16[128,1536]{1,0:T(8,128)(2,1)}, bf16[128,1536]{1,0:T(8,128)(2,1)}, bf16[128,1536]{1,0:T(8,128)(2,1)}, bf...) custom-call(s32[1]{0:T(128)} %bitcast.1.ctx_ref, bf16[128,1536]{1,0:T(8,128)(2,1)} %copy-done.71, ...), custom_call_target="tpu_custom_call" | custom-call | flops 2617245696 | bytes 7864320 | tf_op jit(solution)/shard_map/pallas_call | solution.py:1059
  771.3 12.6 %collective-permute-done.116.up_sent = bf16[384,1024]{1,0:T(8,128)(2,1)} collective-permute-done((bf16[384,1024]{1,0:T(8,128)(2,1)}, bf16[384,1024]{1,0:T(8,128)(2,1)}, u32[]{:S(2)}, u32[]{:S(2)}) %collective-permute-start.116) | collective-permute-done | bytes 786464 | tf_op jit(solution)/shard_map/ppermute | solution.py:1293
  783.9 4.1 shard_map.196
  791.7 9.6 %collective-permute-done.118 = bf16[192,1152]{1,0:T(8,128)(2,1)S(1)} collective-permute-done((bf16[192,1152]{1,0:T(8,128)(2,1)}, bf16[192,1152]{1,0:T(8,128)(2,1)S(1)}, u32[]{:S(2)}, u32[]{:S(2)}) %collective-permute-start.118) | collective-permute-done | bytes 442400 | tf_op jit(solution)/shard_map/ppermute | solution.py:1293
  814.2 9.5 %collective-permute-done.120 = bf16[192,1152]{1,0:T(8,128)(2,1)S(1)} collective-permute-done((bf16[192,1152]{1,0:T(8,128)(2,1)S(1)}, bf16[192,1152]{1,0:T(8,128)(2,1)S(1)}, u32[]{:S(2)}, u32[]{:S(2)}) %collective-permute-start.120) | collective-permute-done | bytes 442400 | tf_op jit(solution)/shard_map/ppermute | solution.py:1293
  833.7 4.9 collective-permute-done.123
  (681 shorter events, 315.7 us)
Async XLA Ops:
  7.2 235.8 %all-gather.3.cloned.1.call-start = ((), (), s32[]{:S(2)}) async-start(), calls=%async_computation.2 | async-start | bytes 3538944 | tf_op jit(solution)/shard_map/all_gather | solution.py:1488
  27.6 16.4 %collective-permute-start.4 = (bf16[192,1024]{1,0:T(8,128)(2,1)}, bf16[192,1024]{1,0:T(8,128)(2,1)S(1)}, u32[]{:S(2)}, u32[]{:S(2)}) collective-permute-start(bf16[192,1024]{1,0:T(8,128)(2,1)} %get-tuple-element.259), channel_id=1, source_target_pairs={{0,2},{1,3},{2,4},{3,5},{4,6},{5,7},{6,0},{7,1},{8,10},{9,11},{10,... | collective-permute-start | bytes 1179656 | tf_op jit(solution)/shard_map/ppermute | solution.py:1293
  29.6 14.3 %collective-permute-start.8 = (bf16[192,1024]{1,0:T(8,128)(2,1)}, bf16[192,1024]{1,0:T(8,128)(2,1)S(1)}, u32[]{:S(2)}, u32[]{:S(2)}) collective-permute-start(bf16[192,1024]{1,0:T(8,128)(2,1)} %get-tuple-element.259), channel_id=1, source_target_pairs={{0,1},{1,0},{2,3},{3,2},{4,5},{5,4},{6,7},{7,6},{8,9},{9,8},{10,11... | collective-permute-start | bytes 1179656 | tf_op jit(solution)/shard_map/ppermute | solution.py:1293
  31.2 18.4 %collective-permute-start.13 = (bf16[128,1536]{1,0:T(8,128)(2,1)S(1)}, bf16[128,1536]{1,0:T(8,128)(2,1)S(1)}, u32[]{:S(2)}, u32[]{:S(2)}) collective-permute-start(bf16[128,1536]{1,0:T(8,128)(2,1)S(1)} %bitcast.144), channel_id=1, source_target_pairs={{0,16},{8,24},{16,0},{24,8},{1,17},{9,25},{17,1},{25,9},{2,18},{10... | collective-permute-start | bytes 1179656 | tf_op jit(solution)/shard_map/ppermute | solution.py:1293
  32.7 14.5 %collective-permute-start.12 = (bf16[128,1536]{1,0:T(8,128)(2,1)S(1)}, bf16[128,1536]{1,0:T(8,128)(2,1)S(1)}, u32[]{:S(2)}, u32[]{:S(2)}) collective-permute-start(bf16[128,1536]{1,0:T(8,128)(2,1)S(1)} %bitcast.145), channel_id=1, source_target_pairs={{0,8},{8,0},{16,24},{24,16},{1,9},{9,1},{17,25},{25,17},{2,10},{10... | collective-permute-start | bytes 1179656 | tf_op jit(solution)/shard_map/ppermute | solution.py:1293
  41.7 38.8 %collective-permute-start.21 = (bf16[2,384,1024]{2,1,0:T(8,128)(2,1)S(1)}, bf16[2,384,1024]{2,1,0:T(8,128)(2,1)}, u32[]{:S(2)}, u32[]{:S(2)}) collective-permute-start(bf16[2,384,1024]{2,1,0:T(8,128)(2,1)S(1)} %get-tuple-element.269.refs_0_), channel_id=1, source_target_pairs={{0,16},{8,24},{16,0},{24,8},{1,17},{9,25},{17,1},{25,9},{2,18},{10... | collective-permute-start | bytes 4718600 | tf_op jit(solution)/shard_map/ppermute | solution.py:1293
  45.6 14.6 %collective-permute-start.10 = (bf16[192,1024]{1,0:T(8,128)(2,1)S(1)}, bf16[192,1024]{1,0:T(8,128)(2,1)S(1)}, u32[]{:S(2)}, u32[]{:S(2)}) collective-permute-start(bf16[192,1024]{1,0:T(8,128)(2,1)S(1)} %collective-permute-done.4), channel_id=1, source_target_pairs={{0,1},{1,0},{2,3},{3,2},{4,5},{5,4},{6,7},{7,6},{8,9},{9,8},{10,11... | collective-permute-start | bytes 1179656 | tf_op jit(solution)/shard_map/ppermute | solution.py:1293
  49.6 20.2 %collective-permute-start.14 = (bf16[128,1536]{1,0:T(8,128)(2,1)S(1)}, bf16[128,1536]{1,0:T(8,128)(2,1)S(1)}, u32[]{:S(2)}, u32[]{:S(2)}) collective-permute-start(bf16[128,1536]{1,0:T(8,128)(2,1)S(1)} %collective-permute-done.13), channel_id=1, source_target_pairs={{0,8},{8,0},{16,24},{24,16},{1,9},{9,1},{17,25},{25,17},{2,10},{10... | collective-permute-start | bytes 1179656 | tf_op jit(solution)/shard_map/ppermute | solution.py:1293
  60.3 46.0 %collective-permute-start.20 = (bf16[2,384,1024]{2,1,0:T(8,128)(2,1)S(1)}, bf16[2,384,1024]{2,1,0:T(8,128)(2,1)}, u32[]{:S(2)}, u32[]{:S(2)}) collective-permute-start(bf16[2,384,1024]{2,1,0:T(8,128)(2,1)S(1)} %get-tuple-element.269.refs_0_), channel_id=1, source_target_pairs={{0,8},{8,0},{16,24},{24,16},{1,9},{9,1},{17,25},{25,17},{2,10},{10... | collective-permute-start | bytes 4718600 | tf_op jit(solution)/shard_map/ppermute | solution.py:1293
  69.8 32.0 %collective-permute-start.24 = (bf16[2,128,1536]{2,1,0:T(8,128)(2,1)S(1)}, bf16[2,128,1536]{2,1,0:T(8,128)(2,1)}, u32[]{:S(2)}, u32[]{:S(2)}) collective-permute-start(bf16[2,128,1536]{2,1,0:T(8,128)(2,1)S(1)} %copy-done.3), channel_id=1, source_target_pairs={{0,16},{8,24},{16,0},{24,8},{1,17},{9,25},{17,1},{25,9},{2,18},{10... | collective-permute-start | bytes 2359304 | tf_op jit(solution)/shard_map/ppermute | solution.py:1293
  80.5 36.0 %collective-permute-start.22 = (bf16[2,384,1024]{2,1,0:T(8,128)(2,1)}, bf16[2,384,1024]{2,1,0:T(8,128)(2,1)}, u32[]{:S(2)}, u32[]{:S(2)}) collective-permute-start(bf16[2,384,1024]{2,1,0:T(8,128)(2,1)} %collective-permute-done.21.refs_2_), channel_id=1, source_target_pairs={{0,8},{8,0},{16,24},{24,16},{1,9},{9,1},{17,25},{25,17},{2,10},{10... | collective-permute-start | bytes 4718600 | tf_op jit(solution)/shard_map/ppermute | solution.py:1293
  106.3 720.9 %reduce-scatter.2.cloned.1.call-start = ((), (), s32[]{:S(2)}) async-start(), calls=%async_computation.1 | async-start | bytes 3981312 | tf_op jit(solution)/shard_map/reduce_scatter | solution.py:1660
  119.3 22.2 %collective-permute-start.26 = (bf16[128,1536]{1,0:T(8,128)(2,1)S(1)}, bf16[128,1536]{1,0:T(8,128)(2,1)S(1)}, u32[]{:S(2)}, u32[]{:S(2)}) collective-permute-start(bf16[128,1536]{1,0:T(8,128)(2,1)S(1)} %multiply_convert_fusion.2.rows_0), channel_id=1, source_target_pairs={{0,2},{1,3},{2,4},{3,5},{4,6},{5,7},{6,0},{7,1},{8,10},{9,11},{10,... | collective-permute-start | bytes 1179656 | tf_op jit(solution)/shard_map/ppermute | solution.py:1293
  119.3 25.4 %collective-permute-start.27 = (bf16[128,1536]{1,0:T(8,128)(2,1)S(1)}, bf16[128,1536]{1,0:T(8,128)(2,1)S(1)}, u32[]{:S(2)}, u32[]{:S(2)}) collective-permute-start(bf16[128,1536]{1,0:T(8,128)(2,1)S(1)} %multiply_convert_fusion.2.rows_0), channel_id=1, source_target_pairs={{0,1},{1,0},{2,3},{3,2},{4,5},{5,4},{6,7},{7,6},{8,9},{9,8},{10,11... | collective-permute-start | bytes 1179656 | tf_op jit(solution)/shard_map/ppermute | solution.py:1293
  141.5 16.8 %collective-permute-start.28 = (bf16[128,1536]{1,0:T(8,128)(2,1)S(1)}, bf16[128,1536]{1,0:T(8,128)(2,1)S(1)}, u32[]{:S(2)}, u32[]{:S(2)}) collective-permute-start(bf16[128,1536]{1,0:T(8,128)(2,1)S(1)} %collective-permute-done.26.rows_0), channel_id=1, source_target_pairs={{0,2},{1,3},{2,4},{3,5},{4,6},{5,7},{6,0},{7,1},{8,10},{9,11},{10,... | collective-permute-start | bytes 1179656 | tf_op jit(solution)/shard_map/ppermute | solution.py:1293
  143.2 20.8 %collective-permute-start.29 = (bf16[128,1536]{1,0:T(8,128)(2,1)S(1)}, bf16[128,1536]{1,0:T(8,128)(2,1)S(1)}, u32[]{:S(2)}, u32[]{:S(2)}) collective-permute-start(bf16[128,1536]{1,0:T(8,128)(2,1)S(1)} %collective-permute-done.26.rows_0), channel_id=1, source_target_pairs={{0,1},{1,0},{2,3},{3,2},{4,5},{5,4},{6,7},{7,6},{8,9},{9,8},{10,11... | collective-permute-start | bytes 1179656 | tf_op jit(solution)/shard_map/ppermute | solution.py:1293
  158.4 20.2 %collective-permute-start.30 = (bf16[128,1536]{1,0:T(8,128)(2,1)}, bf16[128,1536]{1,0:T(8,128)(2,1)S(1)}, u32[]{:S(2)}, u32[]{:S(2)}) collective-permute-start(bf16[128,1536]{1,0:T(8,128)(2,1)} %copy-done.42), channel_id=1, source_target_pairs={{0,6},{1,7},{2,0},{3,1},{4,2},{5,3},{6,4},{7,5},{8,14},{9,15},{10,... | collective-permute-start | bytes 1179656 | tf_op jit(solution)/shard_map/ppermute | solution.py:1293
  162.9 15.6 %collective-permute-start.31 = (bf16[128,1536]{1,0:T(8,128)(2,1)S(1)}, bf16[128,1536]{1,0:T(8,128)(2,1)S(1)}, u32[]{:S(2)}, u32[]{:S(2)}) collective-permute-start(bf16[128,1536]{1,0:T(8,128)(2,1)S(1)} %collective-permute-done.28.rows_0), channel_id=1, source_target_pairs={{0,1},{1,0},{2,3},{3,2},{4,5},{5,4},{6,7},{7,6},{8,9},{9,8},{10,11... | collective-permute-start | bytes 1179656 | tf_op jit(solution)/shard_map/ppermute | solution.py:1293
  188.3 35.1 %collective-permute-start.40 = (bf16[2,384,1024]{2,1,0:T(8,128)(2,1)S(1)}, bf16[2,384,1024]{2,1,0:T(8,128)(2,1)S(1)}, u32[]{:S(2)}, u32[]{:S(2)}) collective-permute-start(bf16[2,384,1024]{2,1,0:T(8,128)(2,1)S(1)} %get-tuple-element.301.refs_0_), channel_id=1, source_target_pairs={{0,16},{8,24},{16,0},{24,8},{1,17},{9,25},{17,1},{25,9},{2,18},{10... | collective-permute-start | bytes 4718600 | tf_op jit(solution)/shard_map/ppermute | solution.py:1293
  188.3 15.2 %collective-permute-start.32 = (bf16[128,1536]{1,0:T(8,128)(2,1)S(1)}, bf16[128,1536]{1,0:T(8,128)(2,1)S(1)}, u32[]{:S(2)}, u32[]{:S(2)}) collective-permute-start(bf16[128,1536]{1,0:T(8,128)(2,1)S(1)} %collective-permute-done.30.rows_0), channel_id=1, source_target_pairs={{0,1},{1,0},{2,3},{3,2},{4,5},{5,4},{6,7},{7,6},{8,9},{9,8},{10,11... | collective-permute-start | bytes 1179656 | tf_op jit(solution)/shard_map/ppermute | solution.py:1293
  223.3 15.0 %collective-permute-start.43 = (bf16[2,128,1536]{2,1,0:T(8,128)(2,1)}, bf16[2,128,1536]{2,1,0:T(8,128)(2,1)}, u32[]{:S(2)}, u32[]{:S(2)}) collective-permute-start(bf16[2,128,1536]{2,1,0:T(8,128)(2,1)} %get-tuple-element.302.refs_4_), channel_id=1, source_target_pairs={{0,16},{8,24},{16,0},{24,8},{1,17},{9,25},{17,1},{25,9},{2,18},{10... | collective-permute-start | bytes 2359304 | tf_op jit(solution)/shard_map/ppermute | solution.py:1293
  223.4 27.2 %collective-permute-start.39 = (bf16[2,384,1024]{2,1,0:T(8,128)(2,1)S(1)}, bf16[2,384,1024]{2,1,0:T(8,128)(2,1)}, u32[]{:S(2)}, u32[]{:S(2)}) collective-permute-start(bf16[2,384,1024]{2,1,0:T(8,128)(2,1)S(1)} %get-tuple-element.301.refs_0_), channel_id=1, source_target_pairs={{0,8},{8,0},{16,24},{24,16},{1,9},{9,1},{17,25},{25,17},{2,10},{10... | collective-permute-start | bytes 4718600 | tf_op jit(solution)/shard_map/ppermute | solution.py:1293
  223.4 27.2 %collective-permute-start.41 = (bf16[2,384,1024]{2,1,0:T(8,128)(2,1)S(1)}, bf16[2,384,1024]{2,1,0:T(8,128)(2,1)}, u32[]{:S(2)}, u32[]{:S(2)}) collective-permute-start(bf16[2,384,1024]{2,1,0:T(8,128)(2,1)S(1)} %collective-permute-done.40.refs_2_), channel_id=1, source_target_pairs={{0,8},{8,0},{16,24},{24,16},{1,9},{9,1},{17,25},{25,17},{2,10},{10... | collective-permute-start | bytes 4718600 | tf_op jit(solution)/shard_map/ppermute | solution.py:1293
  223.9 14.5 %collective-permute-start.38 = (bf16[128,1536]{1,0:T(8,128)(2,1)S(1)}, bf16[128,1536]{1,0:T(8,128)(2,1)S(1)}, u32[]{:S(2)}, u32[]{:S(2)}) collective-permute-start(bf16[128,1536]{1,0:T(8,128)(2,1)S(1)} %add_convert_fusion.19), channel_id=1, source_target_pairs={{0,2},{1,3},{2,4},{3,5},{4,6},{5,7},{6,0},{7,1},{8,10},{9,11},{10,... | collective-permute-start | bytes 1179656 | tf_op jit(solution)/shard_map/ppermute | solution.py:1293
  231.3 15.6 %collective-permute-start.37 = (bf16[128,1536]{1,0:T(8,128)(2,1)S(1)}, bf16[128,1536]{1,0:T(8,128)(2,1)}, u32[]{:S(2)}, u32[]{:S(2)}) collective-permute-start(bf16[128,1536]{1,0:T(8,128)(2,1)S(1)} %copy-done.132), channel_id=1, source_target_pairs={{0,1},{1,0},{2,3},{3,2},{4,5},{5,4},{6,7},{7,6},{8,9},{9,8},{10,11... | collective-permute-start | bytes 1179656 | tf_op jit(solution)/shard_map/ppermute | solution.py:1293
  313.0 14.1 %collective-permute-start.55 = (bf16[128,1536]{1,0:T(8,128)(2,1)S(1)}, bf16[128,1536]{1,0:T(8,128)(2,1)S(1)}, u32[]{:S(2)}, u32[]{:S(2)}) collective-permute-start(bf16[128,1536]{1,0:T(8,128)(2,1)S(1)} %collective-permute-done.52.rows_0), channel_id=1, source_target_pairs={{0,1},{1,0},{2,3},{3,2},{4,5},{5,4},{6,7},{7,6},{8,9},{9,8},{10,11... | collective-permute-start | bytes 1179656 | tf_op jit(solution)/shard_map/ppermute | solution.py:1293
  344.2 16.7 %collective-permute-start.58 = (bf16[128,1536]{1,0:T(8,128)(2,1)S(1)}, bf16[128,1536]{1,0:T(8,128)(2,1)S(1)}, u32[]{:S(2)}, u32[]{:S(2)}) collective-permute-start(bf16[128,1536]{1,0:T(8,128)(2,1)S(1)} %collective-permute-done.56.rows_0), channel_id=1, source_target_pairs={{0,1},{1,0},{2,3},{3,2},{4,5},{5,4},{6,7},{7,6},{8,9},{9,8},{10,11... | collective-permute-start | bytes 1179656 | tf_op jit(solution)/shard_map/ppermute | solution.py:1293
  379.5 13.7 %collective-permute-start.64 = (bf16[128,1536]{1,0:T(8,128)(2,1)S(1)}, bf16[128,1536]{1,0:T(8,128)(2,1)S(1)}, u32[]{:S(2)}, u32[]{:S(2)}) collective-permute-start(bf16[128,1536]{1,0:T(8,128)(2,1)S(1)} %add_convert_fusion.15), channel_id=1, source_target_pairs={{0,2},{1,3},{2,4},{3,5},{4,6},{5,7},{6,0},{7,1},{8,10},{9,11},{10,... | collective-permute-start | bytes 1179656 | tf_op jit(solution)/shard_map/ppermute | solution.py:1293
  403.5 13.4 %collective-permute-start.66 = (bf16[128,1664]{1,0:T(8,128)(2,1)S(1)}, bf16[128,1664]{1,0:T(8,128)(2,1)S(1)}, u32[]{:S(2)}, u32[]{:S(2)}) collective-permute-start(bf16[128,1664]{1,0:T(8,128)(2,1)S(1)} %pad_maximum_fusion.grads_0), channel_id=1, source_target_pairs={{0,2},{1,3},{2,4},{3,5},{4,6},{5,7},{6,0},{7,1},{8,10},{9,11},{10,... | collective-permute-start | bytes 1277960 | tf_op jit(solution)/shard_map/ppermute | solution.py:1293
  403.6 14.3 %collective-permute-start.67 = (bf16[128,1664]{1,0:T(8,128)(2,1)S(1)}, bf16[128,1664]{1,0:T(8,128)(2,1)S(1)}, u32[]{:S(2)}, u32[]{:S(2)}) collective-permute-start(bf16[128,1664]{1,0:T(8,128)(2,1)S(1)} %pad_maximum_fusion.grads_0), channel_id=1, source_target_pairs={{0,1},{1,0},{2,3},{3,2},{4,5},{5,4},{6,7},{7,6},{8,9},{9,8},{10,11... | collective-permute-start | bytes 1277960 | tf_op jit(solution)/shard_map/ppermute | solution.py:1293
  416.9 15.3 %collective-permute-start.69 = (bf16[128,1664]{1,0:T(8,128)(2,1)S(1)}, bf16[128,1664]{1,0:T(8,128)(2,1)S(1)}, u32[]{:S(2)}, u32[]{:S(2)}) collective-permute-start(bf16[128,1664]{1,0:T(8,128)(2,1)S(1)} %collective-permute-done.66.grads_0), channel_id=1, source_target_pairs={{0,1},{1,0},{2,3},{3,2},{4,5},{5,4},{6,7},{7,6},{8,9},{9,8},{10,11... | collective-permute-start | bytes 1277960 | tf_op jit(solution)/shard_map/ppermute | solution.py:1293
  460.1 22.6 %collective-permute-start.75 = (bf16[128,1536]{1,0:T(8,128)(2,1)}, bf16[128,1536]{1,0:T(8,128)(2,1)}, u32[]{:S(2)}, u32[]{:S(2)}) collective-permute-start(bf16[128,1536]{1,0:T(8,128)(2,1)} %add_convert_fusion.12), channel_id=1, source_target_pairs={{0,2},{1,3},{2,4},{3,5},{4,6},{5,7},{6,0},{7,1},{8,10},{9,11},{10,... | collective-permute-start | bytes 1179656 | tf_op jit(solution)/shard_map/ppermute | solution.py:1293
  477.6 19.3 %collective-permute-start.78 = (bf16[768,1024]{1,0:T(8,128)(2,1)S(1)}, bf16[768,1024]{1,0:T(8,128)(2,1)S(1)}, u32[]{:S(2)}, u32[]{:S(2)}) collective-permute-start(bf16[768,1024]{1,0:T(8,128)(2,1)S(1)} %convolution_convert_fusion.9), channel_id=1, source_target_pairs={{0,8},{8,0},{16,24},{24,16},{1,9},{9,1},{17,25},{25,17},{2,10},{10... | collective-permute-start | bytes 4718600 | tf_op jit(solution)/shard_map/ppermute | solution.py:1293
  479.6 17.4 %collective-permute-start.79 = (bf16[768,1024]{1,0:T(8,128)(2,1)S(1)}, bf16[768,1024]{1,0:T(8,128)(2,1)S(1)}, u32[]{:S(2)}, u32[]{:S(2)}) collective-permute-start(bf16[768,1024]{1,0:T(8,128)(2,1)S(1)} %convolution_convert_fusion.8), channel_id=1, source_target_pairs={{0,8},{8,0},{16,24},{24,16},{1,9},{9,1},{17,25},{25,17},{2,10},{10... | collective-permute-start | bytes 4718600 | tf_op jit(solution)/shard_map/ppermute | solution.py:1293
  482.1 14.8 %collective-permute-start.80 = (bf16[512,1536]{1,0:T(8,128)(2,1)S(1)}, bf16[512,1536]{1,0:T(8,128)(2,1)S(1)}, u32[]{:S(2)}, u32[]{:S(2)}) collective-permute-start(bf16[512,1536]{1,0:T(8,128)(2,1)S(1)} %convolution_convert_fusion.3), channel_id=1, source_target_pairs={{0,8},{8,0},{16,24},{24,16},{1,9},{9,1},{17,25},{25,17},{2,10},{10... | collective-permute-start | bytes 4718600 | tf_op jit(solution)/shard_map/ppermute | solution.py:1293
  495.1 15.0 %collective-permute-start.77 = (bf16[128,1536]{1,0:T(8,128)(2,1)S(1)}, bf16[128,1536]{1,0:T(8,128)(2,1)S(1)}, u32[]{:S(2)}, u32[]{:S(2)}) collective-permute-start(bf16[128,1536]{1,0:T(8,128)(2,1)S(1)} %copy-done.131), channel_id=1, source_target_pairs={{0,1},{1,0},{2,3},{3,2},{4,5},{5,4},{6,7},{7,6},{8,9},{9,8},{10,11... | collective-permute-start | bytes 1179656 | tf_op jit(solution)/shard_map/ppermute | solution.py:1293
  519.8 14.9 %collective-permute-start.83 = (bf16[128,1536]{1,0:T(8,128)(2,1)}, bf16[128,1536]{1,0:T(8,128)(2,1)}, u32[]{:S(2)}, u32[]{:S(2)}) collective-permute-start(bf16[128,1536]{1,0:T(8,128)(2,1)} %get-tuple-element.533.grad_0), channel_id=1, source_target_pairs={{0,8},{8,0},{16,24},{24,16},{1,9},{9,1},{17,25},{25,17},{2,10},{10... | collective-permute-start | bytes 1179656 | tf_op jit(solution)/shard_map/ppermute | solution.py:1293
  568.4 13.5 %collective-permute-start.89 = (bf16[128,1664]{1,0:T(8,128)(2,1)}, bf16[128,1664]{1,0:T(8,128)(2,1)}, u32[]{:S(2)}, u32[]{:S(2)}) collective-permute-start(bf16[128,1664]{1,0:T(8,128)(2,1)} %pad_maximum_fusion.1.grads_0), channel_id=1, source_target_pairs={{0,2},{1,3},{2,4},{3,5},{4,6},{5,7},{6,0},{7,1},{8,10},{9,11},{10,... | collective-permute-start | bytes 1277960 | tf_op jit(solution)/shard_map/ppermute | solution.py:1293
  570.8 18.3 %collective-permute-start.90 = (bf16[128,1664]{1,0:T(8,128)(2,1)}, bf16[128,1664]{1,0:T(8,128)(2,1)}, u32[]{:S(2)}, u32[]{:S(2)}) collective-permute-start(bf16[128,1664]{1,0:T(8,128)(2,1)} %pad_maximum_fusion.1.grads_0), channel_id=1, source_target_pairs={{0,1},{1,0},{2,3},{3,2},{4,5},{5,4},{6,7},{7,6},{8,9},{9,8},{10,11... | collective-permute-start | bytes 1277960 | tf_op jit(solution)/shard_map/ppermute | solution.py:1293
  571.3 32.8 %collective-permute-start.92 = (bf16[384,1024]{1,0:T(8,128)(2,1)}, bf16[384,1024]{1,0:T(8,128)(2,1)}, u32[]{:S(2)}, u32[]{:S(2)}) collective-permute-start(bf16[384,1024]{1,0:T(8,128)(2,1)} %get-tuple-element.408), channel_id=1, source_target_pairs={{0,16},{8,24},{16,0},{24,8},{1,17},{9,25},{17,1},{25,9},{2,18},{10... | collective-permute-start | bytes 2359304 | tf_op jit(solution)/shard_map/ppermute | solution.py:1293
  581.9 15.5 %collective-permute-start.91 = (bf16[128,1664]{1,0:T(8,128)(2,1)}, bf16[128,1664]{1,0:T(8,128)(2,1)}, u32[]{:S(2)}, u32[]{:S(2)}) collective-permute-start(bf16[128,1664]{1,0:T(8,128)(2,1)} %collective-permute-done.89.grads_0), channel_id=1, source_target_pairs={{0,2},{1,3},{2,4},{3,5},{4,6},{5,7},{6,0},{7,1},{8,10},{9,11},{10,... | collective-permute-start | bytes 1277960 | tf_op jit(solution)/shard_map/ppermute | solution.py:1293
  588.1 26.4 %collective-permute-start.95 = (bf16[384,1024]{1,0:T(8,128)(2,1)S(1)}, bf16[384,1024]{1,0:T(8,128)(2,1)S(1)}, u32[]{:S(2)}, u32[]{:S(2)}) collective-permute-start(bf16[384,1024]{1,0:T(8,128)(2,1)S(1)} %copy-done.54), channel_id=1, source_target_pairs={{0,16},{8,24},{16,0},{24,8},{1,17},{9,25},{17,1},{25,9},{2,18},{10... | collective-permute-start | bytes 2359304 | tf_op jit(solution)/shard_map/ppermute | solution.py:1293
  588.7 16.8 %collective-permute-start.93 = (bf16[128,1664]{1,0:T(8,128)(2,1)}, bf16[128,1664]{1,0:T(8,128)(2,1)S(1)}, u32[]{:S(2)}, u32[]{:S(2)}) collective-permute-start(bf16[128,1664]{1,0:T(8,128)(2,1)} %collective-permute-done.89.grads_0), channel_id=1, source_target_pairs={{0,1},{1,0},{2,3},{3,2},{4,5},{5,4},{6,7},{7,6},{8,9},{9,8},{10,11... | collective-permute-start | bytes 1277960 | tf_op jit(solution)/shard_map/ppermute | solution.py:1293
  597.4 17.1 %collective-permute-start.94 = (bf16[128,1664]{1,0:T(8,128)(2,1)}, bf16[128,1664]{1,0:T(8,128)(2,1)S(1)}, u32[]{:S(2)}, u32[]{:S(2)}) collective-permute-start(bf16[128,1664]{1,0:T(8,128)(2,1)} %pad_maximum_fusion.1.grads_0), channel_id=1, source_target_pairs={{0,6},{1,7},{2,0},{3,1},{4,2},{5,3},{6,4},{7,5},{8,14},{9,15},{10,... | collective-permute-start | bytes 1277960 | tf_op jit(solution)/shard_map/ppermute | solution.py:1293
  604.1 19.9 %collective-permute-start.97 = (bf16[256,1536]{1,0:T(8,128)(2,1)S(1)}, bf16[256,1536]{1,0:T(8,128)(2,1)S(1)}, u32[]{:S(2)}, u32[]{:S(2)}) collective-permute-start(bf16[256,1536]{1,0:T(8,128)(2,1)S(1)} %get-tuple-element.429), channel_id=1, source_target_pairs={{0,16},{8,24},{16,0},{24,8},{1,17},{9,25},{17,1},{25,9},{2,18},{10... | collective-permute-start | bytes 2359304 | tf_op jit(solution)/shard_map/ppermute | solution.py:1293
  624.0 17.1 %collective-permute-start.98 = (bf16[128,1664]{1,0:T(8,128)(2,1)S(1)}, bf16[128,1664]{1,0:T(8,128)(2,1)S(1)}, u32[]{:S(2)}, u32[]{:S(2)}) collective-permute-start(bf16[128,1664]{1,0:T(8,128)(2,1)S(1)} %collective-permute-done.94.grads_0), channel_id=1, source_target_pairs={{0,1},{1,0},{2,3},{3,2},{4,5},{5,4},{6,7},{7,6},{8,9},{9,8},{10,11... | collective-permute-start | bytes 1277960 | tf_op jit(solution)/shard_map/ppermute | solution.py:1293
  637.7 24.2 %collective-permute-start.101 = (bf16[128,1536]{1,0:T(8,128)(2,1)}, bf16[128,1536]{1,0:T(8,128)(2,1)S(1)}, u32[]{:S(2)}, u32[]{:S(2)}) collective-permute-start(bf16[128,1536]{1,0:T(8,128)(2,1)} %add_convert_fusion.8), channel_id=1, source_target_pairs={{0,2},{1,3},{2,4},{3,5},{4,6},{5,7},{6,0},{7,1},{8,10},{9,11},{10,... | collective-permute-start | bytes 1179656 | tf_op jit(solution)/shard_map/ppermute | solution.py:1293
  655.3 31.7 %collective-permute-start.104 = (bf16[768,1024]{1,0:T(8,128)(2,1)}, bf16[768,1024]{1,0:T(8,128)(2,1)}, u32[]{:S(2)}, u32[]{:S(2)}) collective-permute-start(bf16[768,1024]{1,0:T(8,128)(2,1)} %convolution_convert_fusion.7), channel_id=1, source_target_pairs={{0,8},{8,0},{16,24},{24,16},{1,9},{9,1},{17,25},{25,17},{2,10},{10... | collective-permute-start | bytes 4718600 | tf_op jit(solution)/shard_map/ppermute | solution.py:1293
  658.4 28.7 %collective-permute-start.105 = (bf16[768,1024]{1,0:T(8,128)(2,1)}, bf16[768,1024]{1,0:T(8,128)(2,1)}, u32[]{:S(2)}, u32[]{:S(2)}) collective-permute-start(bf16[768,1024]{1,0:T(8,128)(2,1)} %convolution_convert_fusion.6), channel_id=1, source_target_pairs={{0,8},{8,0},{16,24},{24,16},{1,9},{9,1},{17,25},{25,17},{2,10},{10... | collective-permute-start | bytes 4718600 | tf_op jit(solution)/shard_map/ppermute | solution.py:1293
  661.9 25.2 %collective-permute-start.106 = (bf16[512,1536]{1,0:T(8,128)(2,1)}, bf16[512,1536]{1,0:T(8,128)(2,1)}, u32[]{:S(2)}, u32[]{:S(2)}) collective-permute-start(bf16[512,1536]{1,0:T(8,128)(2,1)} %convolution_convert_fusion.2), channel_id=1, source_target_pairs={{0,8},{8,0},{16,24},{24,16},{1,9},{9,1},{17,25},{25,17},{2,10},{10... | collective-permute-start | bytes 4718600 | tf_op jit(solution)/shard_map/ppermute | solution.py:1293
  662.9 16.4 %collective-permute-start.102 = (bf16[128,1536]{1,0:T(8,128)(2,1)}, bf16[128,1536]{1,0:T(8,128)(2,1)}, u32[]{:S(2)}, u32[]{:S(2)}) collective-permute-start(bf16[128,1536]{1,0:T(8,128)(2,1)} %get-tuple-element.440), channel_id=1, source_target_pairs={{0,1},{1,0},{2,3},{3,2},{4,5},{5,4},{6,7},{7,6},{8,9},{9,8},{10,11... | collective-permute-start | bytes 1179656 | tf_op jit(solution)/shard_map/ppermute | solution.py:1293
  681.1 21.6 %collective-permute-start.103 = (bf16[128,1536]{1,0:T(8,128)(2,1)}, bf16[128,1536]{1,0:T(8,128)(2,1)S(1)}, u32[]{:S(2)}, u32[]{:S(2)}) collective-permute-start(bf16[128,1536]{1,0:T(8,128)(2,1)} %get-tuple-element.441), channel_id=1, source_target_pairs={{0,1},{1,0},{2,3},{3,2},{4,5},{5,4},{6,7},{7,6},{8,9},{9,8},{10,11... | collective-permute-start | bytes 1179656 | tf_op jit(solution)/shard_map/ppermute | solution.py:1293
  687.1 21.8 %collective-permute-start.107 = (bf16[128,1536]{1,0:T(8,128)(2,1)S(1)}, bf16[128,1536]{1,0:T(8,128)(2,1)S(1)}, u32[]{:S(2)}, u32[]{:S(2)}) collective-permute-start(bf16[128,1536]{1,0:T(8,128)(2,1)S(1)} %copy-done.76), channel_id=1, source_target_pairs={{0,2},{1,3},{2,4},{3,5},{4,6},{5,7},{6,0},{7,1},{8,10},{9,11},{10,... | collective-permute-start | bytes 1179656 | tf_op jit(solution)/shard_map/ppermute | solution.py:1293
  698.6 19.5 %collective-permute-start.108 = (bf16[128,1536]{1,0:T(8,128)(2,1)S(1)}, bf16[128,1536]{1,0:T(8,128)(2,1)S(1)}, u32[]{:S(2)}, u32[]{:S(2)}) collective-permute-start(bf16[128,1536]{1,0:T(8,128)(2,1)S(1)} %copy-done.78), channel_id=1, source_target_pairs={{0,6},{1,7},{2,0},{3,1},{4,2},{5,3},{6,4},{7,5},{8,14},{9,15},{10,... | collective-permute-start | bytes 1179656 | tf_op jit(solution)/shard_map/ppermute | solution.py:1293
  721.8 26.3 %collective-permute-start.112 = (bf16[384,1024]{1,0:T(8,128)(2,1)S(1)}, bf16[384,1024]{1,0:T(8,128)(2,1)S(1)}, u32[]{:S(2)}, u32[]{:S(2)}) collective-permute-start(bf16[384,1024]{1,0:T(8,128)(2,1)S(1)} %get-tuple-element.548), channel_id=1, source_target_pairs={{0,16},{8,24},{16,0},{24,8},{1,17},{9,25},{17,1},{25,9},{2,18},{10... | collective-permute-start | bytes 2359304 | tf_op jit(solution)/shard_map/ppermute | solution.py:1293
  723.2 24.9 %collective-permute-start.109 = (bf16[128,1536]{1,0:T(8,128)(2,1)S(1)}, bf16[128,1536]{1,0:T(8,128)(2,1)}, u32[]{:S(2)}, u32[]{:S(2)}) collective-permute-start(bf16[128,1536]{1,0:T(8,128)(2,1)S(1)} %get-tuple-element.527.grad_0), channel_id=1, source_target_pairs={{0,8},{8,0},{16,24},{24,16},{1,9},{9,1},{17,25},{25,17},{2,10},{10... | collective-permute-start | bytes 1179656 | tf_op jit(solution)/shard_map/ppermute | solution.py:1293
  732.2 15.9 %collective-permute-start.111 = (bf16[128,1536]{1,0:T(8,128)(2,1)}, bf16[128,1536]{1,0:T(8,128)(2,1)}, u32[]{:S(2)}, u32[]{:S(2)}) collective-permute-start(bf16[128,1536]{1,0:T(8,128)(2,1)} %collective-permute-done.110.grad_2), channel_id=1, source_target_pairs={{0,8},{8,0},{16,24},{24,16},{1,9},{9,1},{17,25},{25,17},{2,10},{10... | collective-permute-start | bytes 1179656 | tf_op jit(solution)/shard_map/ppermute | solution.py:1293
  762.7 26.2 %collective-permute-start.114 = (bf16[128,1536]{1,0:T(8,128)(2,1)}, bf16[128,1536]{1,0:T(8,128)(2,1)}, u32[]{:S(2)}, u32[]{:S(2)}) collective-permute-start(bf16[128,1536]{1,0:T(8,128)(2,1)} %get-tuple-element.462), channel_id=1, source_target_pairs={{0,8},{8,0},{16,24},{24,16},{1,9},{9,1},{17,25},{25,17},{2,10},{10... | collective-permute-start | bytes 1179656 | tf_op jit(solution)/shard_map/ppermute | solution.py:1293
  762.8 42.1 %collective-permute-start.113 = (bf16[128,1536]{1,0:T(8,128)(2,1)}, bf16[128,1536]{1,0:T(8,128)(2,1)}, u32[]{:S(2)}, u32[]{:S(2)}) collective-permute-start(bf16[128,1536]{1,0:T(8,128)(2,1)} %get-tuple-element.460), channel_id=1, source_target_pairs={{0,8},{8,0},{16,24},{24,16},{1,9},{9,1},{17,25},{25,17},{2,10},{10... | collective-permute-start | bytes 1179656 | tf_op jit(solution)/shard_map/ppermute | solution.py:1293
  764.0 19.9 %collective-permute-start.116 = (bf16[384,1024]{1,0:T(8,128)(2,1)}, bf16[384,1024]{1,0:T(8,128)(2,1)}, u32[]{:S(2)}, u32[]{:S(2)}) collective-permute-start(bf16[384,1024]{1,0:T(8,128)(2,1)} %get-tuple-element.469), channel_id=1, source_target_pairs={{0,16},{8,24},{16,0},{24,8},{1,17},{9,25},{17,1},{25,9},{2,18},{10... | collective-permute-start | bytes 2359304 | tf_op jit(solution)/shard_map/ppermute | solution.py:1293
  790.0 14.3 %collective-permute-start.115 = (bf16[128,1536]{1,0:T(8,128)(2,1)S(1)}, bf16[128,1536]{1,0:T(8,128)(2,1)S(1)}, u32[]{:S(2)}, u32[]{:S(2)}) collective-permute-start(bf16[128,1536]{1,0:T(8,128)(2,1)S(1)} %add_convert_fusion.5), channel_id=1, source_target_pairs={{0,16},{8,24},{16,0},{24,8},{1,17},{9,25},{17,1},{25,9},{2,18},{10... | collective-permute-start | bytes 1179656 | tf_op jit(solution)/shard_map/ppermute | solution.py:1293
  791.3 17.7 %collective-permute-start.117 = (bf16[192,1152]{1,0:T(8,128)(2,1)}, bf16[192,1152]{1,0:T(8,128)(2,1)S(1)}, u32[]{:S(2)}, u32[]{:S(2)}) collective-permute-start(bf16[192,1152]{1,0:T(8,128)(2,1)} %bitcast.169), channel_id=1, source_target_pairs={{0,1},{1,0},{2,3},{3,2},{4,5},{5,4},{6,7},{7,6},{8,9},{9,8},{10,11... | collective-permute-start | bytes 1327112 | tf_op jit(solution)/shard_map/ppermute | solution.py:1293
  804.2 38.0 %collective-permute-start.127 = (bf16[256,1536]{1,0:T(8,128)(2,1)S(1)}, bf16[256,1536]{1,0:T(8,128)(2,1)S(1)}, u32[]{:S(2)}, u32[]{:S(2)}) collective-permute-start(bf16[256,1536]{1,0:T(8,128)(2,1)S(1)} %get-tuple-element.487), channel_id=1, source_target_pairs={{0,16},{8,24},{16,0},{24,8},{1,17},{9,25},{17,1},{25,9},{2,18},{10... | collective-permute-start | bytes 2359304 | tf_op jit(solution)/shard_map/ppermute | solution.py:1293
  814.1 17.0 %collective-permute-start.122 = (bf16[192,1152]{1,0:T(8,128)(2,1)S(1)}, bf16[192,1152]{1,0:T(8,128)(2,1)S(1)}, u32[]{:S(2)}, u32[]{:S(2)}) collective-permute-start(bf16[192,1152]{1,0:T(8,128)(2,1)S(1)} %fusion.16), channel_id=1, source_target_pairs={{0,2},{1,3},{2,4},{3,5},{4,6},{5,7},{6,0},{7,1},{8,10},{9,11},{10,... | collective-permute-start | bytes 1327112 | tf_op jit(solution)/shard_map/ppermute | solution.py:1293
  (219 other events, 2951.3 us)
Sparse Core Ops, SparseCore 0:
  106.4 84.7 all-gather.2
  664.7 90.3 reduce-scatter.1

commit v5 on v4

--- a/solution.py
+++ b/solution.py
@@ -519,25 +519,45 @@
 RING = (0, 2, 1, 3)
 
 
-def bring_expert_weights(bring, ctx_ref, quarters, w_gate_up_here, w_down_here, e, p):
-    gate_up, down = quarters[:4], quarters[4:]
-    hidden_width = w_down_here.shape[1]
+def bring_expert_weights(bring, ctx_ref, weights, w_gate_up_here, w_down_here, e, p):
+    hidden_width, width = w_down_here.shape[1:]
     copies = []
-    for r in range(4):
-        rows = gate_up[r].shape[1]
-        at = pl.ds(pl.multiple_of((ctx_ref[0] ^ r) * rows, rows), rows)
-        for side in range(2):
-            span = slice(side * hidden_width + p * FE_STEP, side * hidden_width + (p + 1) * FE_STEP)
-            copies.append(bring(gate_up[r].at[e, :, span], w_gate_up_here.at[e, at, span]))
+    for side in range(2):
+        span = slice(side * hidden_width + p * FE_STEP, side * hidden_width + (p + 1) * FE_STEP)
+        if len(weights) == 1:
+            copies.append(bring(weights[0].at[e, :, span], w_gate_up_here.at[e, :, span]))
+            continue
+        for r in range(4):
+            quarter = weights[4 * e + r]
+            rows = quarter.shape[0]
+            at = pl.ds(pl.multiple_of((ctx_ref[0] ^ r) * rows, rows), rows)
+            copies.append(bring(quarter.at[:, span], w_gate_up_here.at[e, at, span]))
     if p == 0:
+        rows, part = hidden_width // 4, width // 3
         for r in range(4):
-            rows = down[r].shape[1]
-            at = pl.ds(pl.multiple_of((ctx_ref[0] ^ r) * rows, rows), rows)
-            copies.append(bring(down[r].at[e], w_down_here.at[e, at, :]))
+            if len(weights) > 1:
+                at = pl.ds(pl.multiple_of((ctx_ref[0] ^ r) * rows, rows), rows)
+                copies.append(bring(weights[-4 + r].at[e], w_down_here.at[e, at, :]))
+                continue
+            for b in range(3):
+                source = slice((3 * r + b) * rows, (3 * r + b + 1) * rows)
+                copies.append(
+                    bring(
+                        weights[0].at[e, source, 2 * hidden_width :],
+                        w_down_here.at[e, r * rows : (r + 1) * rows, b * part : (b + 1) * part],
+                    )
+                )
     return copies
 
 
-def experts_forward_body(group, first_id, lane_offset, ctx_ref, rows_0, rows_1, ids_in, router_in, own_in, *refs):
+def join_experts(gate_up, down):
+    part = down.shape[2] // 3
+    return jnp.concatenate(
+        [gate_up, jnp.concatenate([down[:, :, b * part : (b + 1) * part] for b in range(3)], 1)], -1
+    )
+
+
+def experts_forward_body(weight_total, group, first_id, lane_offset, ctx_ref, rows_0, rows_1, ids_0, ids_1, router_in, own_in, *refs):
     (out_0, out_1, all_rows, all_gate, all_up, all_probs) = refs[-19:-13]
     (
         rows, w_gate_up_here, w_down_here, gate_here, up_here, probs, ring_rows,
@@ -556,10 +576,12 @@
         return copy
 
     span = pl.ds(group * count, count)
+    ids_at = ids_0.shape[1] - 128
     row_copies = [
         bring(rows_0, rows.at[:block]),
         bring(rows_1, rows.at[block:]),
-        bring(ids_in.at[span], ids),
+        bring(ids_0.at[:block, ids_at:], ids.at[:block]),
+        bring(ids_1.at[:block, ids_at:], ids.at[block:]),
         bring(router_in, router),
         bring(own_in, own),
     ]
@@ -567,7 +589,7 @@
     for e in range(expert_count):
         for p in range(steps):
             weight_copies.append(
-                bring_expert_weights(bring, ctx_ref, refs[:8], w_gate_up_here, w_down_here, e, p)
+                bring_expert_weights(bring, ctx_ref, refs[:weight_total], w_gate_up_here, w_down_here, e, p)
             )
     outgoing = []
 
@@ -627,8 +649,13 @@
 
 
 def expert_shapes(weights):
-    (count, rows, width), (_, down_rows, down_width) = weights[0].shape, weights[4].shape
-    return (count, 4 * rows, width), (count, 4 * down_rows, down_width)
+    if len(weights) == 1:
+        count, width, columns = weights[0].shape
+        hidden_width = (columns - width // 3) // 2
+    else:
+        count, rows, width = weights[-1].shape
+        hidden_width = 4 * rows
+    return (count, width, 2 * hidden_width), (count, hidden_width, width)
 
 
 def expert_cost(count, width, expert_count, hidden_width):
@@ -648,10 +675,10 @@
     expert_count, hidden_width = down_shape[0], down_shape[1]
     flat = expert_count * hidden_width
     low, f32 = jnp.bfloat16, jnp.float32
-    inputs = [ctx_ref, *rows, ids, router, own, *weights, *kept]
+    inputs = [ctx_ref, *rows, *ids, router, own, *weights, *kept]
     return pl.pallas_call(
-        functools.partial(experts_forward_body, group, first_id, lane_offset),
-        in_specs=[smem()] + [anywhere()] * (13 + len(kept)),
+        functools.partial(experts_forward_body, len(weights), group, first_id, lane_offset),
+        in_specs=[smem()] + [anywhere()] * (6 + len(weights) + len(kept)),
         out_specs=[anywhere()] * 6,
         out_shape=[
             shaped((block, width)),
@@ -661,7 +688,7 @@
             shaped((groups * count, flat)),
             shaped((groups * count, 128), f32),
         ],
-        input_output_aliases={14 + i: 2 + i for i in range(len(kept))},
+        input_output_aliases={7 + len(weights) + i: 2 + i for i in range(len(kept))},
         scratch_shapes=[
             pltpu.VMEM((count, width), low),
             pltpu.VMEM(gate_up_shape, low),
@@ -670,11 +697,11 @@
             pltpu.VMEM((count, flat), low),
             pltpu.VMEM((count, 128), f32),
             pltpu.VMEM((count, width), low),
-            pltpu.VMEM((count, ids.shape[1]), low),
+            pltpu.VMEM((count, 128), low),
             pltpu.VMEM(router.shape, low),
             pltpu.VMEM(own.shape, f32),
             pltpu.VMEM((count, width), low),
-            pltpu.SemaphoreType.DMA((5 + 8 * flat // FE_STEP + 4 * expert_count,)),
+            pltpu.SemaphoreType.DMA((6 + 8 * flat // FE_STEP + 24 * expert_count,)),
             pltpu.SemaphoreType.DMA((6,)),
         ],
         compiler_params=kernel_params(),
@@ -682,7 +709,7 @@
     )(*inputs)
 
 
-def experts_backward_body(group, ctx_ref, grads_0, grads_1, probs_in, gate_in, up_in, router_in, own_in, *refs):
+def experts_backward_body(weight_total, ring, group, ctx_ref, grads_0, grads_1, probs_in, gate_in, up_in, router_in, own_in, *refs):
     out_0, out_1, all_grads, all_grad_gate, all_grad_up, all_hidden, all_logits = refs[-23:-16]
     (
         sent, w_gate_up_here, w_down_here, gates, ups, probs, grads, grad_gates, grad_ups,
@@ -717,7 +744,7 @@
                     bring(gate_in.at[rows_here, flat], gates.at[:, flat]),
                     bring(up_in.at[rows_here, flat], ups.at[:, flat]),
                 ]
-                + bring_expert_weights(bring, ctx_ref, refs[:8], w_gate_up_here, w_down_here, e, p)
+                + bring_expert_weights(bring, ctx_ref, refs[:weight_total], w_gate_up_here, w_down_here, e, p)
             )
     outgoing = []
 
@@ -755,8 +782,11 @@
             dots = dots + jnp.sum(plain * hidden, -1, keepdims=True)
             hidden = (hidden * chosen).astype(jnp.bfloat16)
             for q in range(FE_STEP // quarter):
-                r = ctx_ref[0] ^ (p * (FE_STEP // quarter) + q)
-                at = jnp.where(r == 1, 2, jnp.where(r == 2, 1, r)) * expert_count + e
+                at = p * (FE_STEP // quarter) + q
+                if ring:
+                    r = ctx_ref[0] ^ at
+                    at = jnp.where(r == 1, 2, jnp.where(r == 2, 1, r))
+                at = at * expert_count + e
                 hiddens[:, pl.ds(pl.multiple_of(at * quarter, quarter), quarter)] = hidden[
                     :, q * quarter : (q + 1) * quarter
                 ]
@@ -787,7 +817,7 @@
 
 
 def experts_backward(
-    group, groups, ctx_ref, grads, probs, gate, up, router, own, weights, kept
+    group, groups, ctx_ref, grads, probs, gate, up, router, own, weights, kept, ring
 ):
     gate_up_shape, down_shape = expert_shapes(weights)
     expert_count, hidden_width, width = down_shape
@@ -797,8 +827,8 @@
     low, f32 = jnp.bfloat16, jnp.float32
     inputs = [ctx_ref, *grads, probs, gate, up, router, own, *weights, *kept]
     return pl.pallas_call(
-        functools.partial(experts_backward_body, group),
-        in_specs=[smem()] + [anywhere()] * (15 + len(kept)),
+        functools.partial(experts_backward_body, len(weights), ring, group),
+        in_specs=[smem()] + [anywhere()] * (7 + len(weights) + len(kept)),
         out_specs=[anywhere()] * 7,
         out_shape=[
             shaped((block, width)),
@@ -809,7 +839,7 @@
             shaped((groups * count, flat)),
             shaped((groups * count, 128)),
         ],
-        input_output_aliases={16 + i: 2 + i for i in range(len(kept))},
+        input_output_aliases={8 + len(weights) + i: 2 + i for i in range(len(kept))},
         scratch_shapes=[
             pltpu.VMEM((count, grads[0].shape[1]), low),
             pltpu.VMEM(gate_up_shape, low),
@@ -825,7 +855,7 @@
             pltpu.VMEM(router.shape, low),
             pltpu.VMEM(own.shape, f32),
             pltpu.VMEM((count, width), low),
-            pltpu.SemaphoreType.DMA((5 + 10 * flat // FE_STEP + 4 * expert_count,)),
+            pltpu.SemaphoreType.DMA((5 + 10 * flat // FE_STEP + 24 * expert_count,)),
             pltpu.SemaphoreType.DMA((7,)),
         ],
         compiler_params=kernel_params(),
@@ -1093,38 +1123,43 @@
     return outs[:4], outs[4], outs[5], outs[6]
 
 
-def place_body(members, shares, *refs):
-    shards = [refs[0].at[r] for r in range(8)] if refs[0].shape[0] == 8 else refs[:8]
-    outs = refs[1:] if refs[0].shape[0] == 8 else refs[8:]
+def place_body(members, share, first, *refs):
+    shards, outs = refs[:8], refs[8:]
     front = outs[0].shape[3]
     for r in range(8):
         for c in range(4):
-            outs[0][members[8 + c], members[r]] = shards[r][c, :, :front]
+            outs[0][members[8 + c], members[r]] = shards[r][c, :, first : first + front]
         for out in outs[1:]:
             q_part = out.shape[1] // 4
-            span = pl.ds(pl.multiple_of(members[r] * shares, shares), shares)
+            span = pl.ds(pl.multiple_of(members[r] * share, share), share)
             for j in range(4):
-                out[span, j * q_part : (j + 1) * q_part] = shards[r][j, :, front:]
-
-
-def place(members, shards, front):
-    four, share, width = shards[0].shape[-3:]
+                out[span, j * q_part : (j + 1) * q_part] = shards[r][
+                    j, :, first + front : first + front + q_part
+                ]
+
+
+def place(members, shards, first, front, rest):
+    four, share, width = shards[0].shape
     outs = [shaped((four, 8, share, front))]
-    if width > front:
-        outs.append(shaped((8 * share, four * (width - front))))
+    if rest:
+        outs.append(shaped((8 * share, four * rest)))
     return pl.pallas_call(
-        lambda members_ref, *refs: place_body(members_ref, share, *refs),
-        in_specs=[smem()] + [vmem()] * len(shards),
+        lambda members_ref, *refs: place_body(members_ref, share, first, *refs),
+        in_specs=[smem()] + [vmem()] * 8,
         out_shape=outs,
         compiler_params=kernel_params(),
     )(members, *shards)
+
+
+def turned(block):
+    return block.astype(jnp.float32).T.astype(jnp.bfloat16)
 
 
 def weight_blocks_body(members, w_query, w_key_value, w_router, gains, *outs):
     layers, share, q_width = w_query.shape
     kv_width = w_key_value.shape[2] // 2
     q_part, kv_part = q_width // 4, kv_width // 4
-    experts = w_router.shape[2]
+    experts = w_router.shape[1]
     small = outs[0].shape[1] - 128
     for r in range(4):
         c = members[8 + r]
@@ -1140,9 +1175,9 @@
                     i, :, pl.ds(pl.multiple_of(side * kv_width + c * kv_part, kv_part), kv_part)
                 ]
             at = small + i * experts
-            outs[r][:, at : at + experts] = w_router[i]
+            outs[r][:, at : at + experts] = turned(w_router[i])
             at = small + layers * experts + 2 * i
-            outs[r][:, at : at + 2] = gains[i]
+            outs[r][:, at : at + 2] = turned(gains[i])
 
 
 def weight_blocks(members, w_query, w_key_value, w_router, gains):
@@ -1156,20 +1191,22 @@
     )(members, w_query, w_key_value, w_router, gains)
 
 
-def pack_shards_body(front, block_0, block_1, block_2, block_3, w_output, ids, *outs):
-    blocks, small_rows = (block_0, block_1, block_2, block_3), outs[-1]
+def pack_shards_body(front, block_0, block_1, block_2, block_3, w_output, ids, shard):
+    blocks = (block_0, block_1, block_2, block_3)
     layers, share, width = w_output.shape
-    count, top = ids.shape[1:]
-    small_rows[...] = jnp.zeros_like(small_rows)
+    part = front + width // 4
+    top, count = ids.shape[1:]
     for r in range(4):
         span = slice(r * share, (r + 1) * share)
         for i in range(layers):
-            outs[i][span, :front] = blocks[r][:, i * front : (i + 1) * front]
-            outs[i][span, front:] = w_output[i, :, r * (width // 4) : (r + 1) * (width // 4)]
-        small_rows[span, :] = blocks[r][:, layers * front :]
+            shard[span, i * part : i * part + front] = blocks[r][:, i * front : (i + 1) * front]
+            shard[span, i * part + front : (i + 1) * part] = w_output[
+                i, :, r * (width // 4) : (r + 1) * (width // 4)
+            ]
+        shard[span, layers * part :] = blocks[r][:, layers * front :]
     for i in range(layers):
-        at = 64 + top * i
-        small_rows[:count, at : at + top] = ids[i].astype(jnp.float32).astype(jnp.bfloat16)
+        at = layers * part + 64 + top * i
+        shard[:count, at : at + top] = turned(ids[i])
 
 
 def pack_shards(blocks, w_output, ids, front):
@@ -1177,7 +1214,7 @@
     return pl.pallas_call(
         functools.partial(pack_shards_body, front),
         in_specs=[vmem()] * 6,
-        out_shape=[shaped((4 * share, front + width // 4))] * layers + [shaped((4 * share, 128))],
+        out_shape=shaped((4 * share, layers * (front + width // 4) + 128)),
         compiler_params=kernel_params(),
     )(*blocks, w_output, ids)
 
@@ -1212,7 +1249,7 @@
 def finish_attention_body(layers, members, *refs):
     blocks, outs = refs[: 5 * layers], refs[5 * layers :]
     query, key_value, output, router, gains = outs
-    experts, lane_count = router.shape[2], layers * router.shape[2]
+    experts, lane_count = router.shape[1], layers * router.shape[1]
     q_part, kv_part = query.shape[2] // 4, key_value.shape[2] // 8
     front = q_part + 2 * kv_part
     kv_width = 4 * kv_part
@@ -1230,8 +1267,9 @@
                     :, q_part + side * kv_part : q_part + (side + 1) * kv_part
                 ].astype(jnp.float32)
             lanes = lanes + block[:, front:].astype(jnp.float32)
-        router[i] = lanes[:, i * experts : (i + 1) * experts]
-        gains[i] = lanes[:, lane_count : lane_count + 2]
+        lanes = lanes.T
+        router[i] = lanes[i * experts : (i + 1) * experts, :]
+        gains[i] = lanes[lane_count : lane_count + 2, :]
         own = blocks[5 * i + 4]
         for j in range(4):
             output[i, :, j * q_part : (j + 1) * q_part] = own[j].astype(jnp.float32)
@@ -1249,33 +1287,38 @@
             shaped((total, share, 4 * q_part), f32),
             shaped((total, share, 4 * (front - q_part)), f32),
             shaped((total, share, 4 * q_part), f32),
-            shaped((total, share, expert_total), f32),
-            shaped((total, share, 2), f32),
+            shaped((total, expert_total, share), f32),
+            shaped((total, 2, share), f32),
         ],
         compiler_params=kernel_params(),
     )(members, *[block for layer in layers for block in layer])
 
 
-def finish_experts_body(
-    gate_held, gate_sent, up_held, up_sent, down_held, down_sent, *refs
-):
+def finish_experts_body(down_total, *refs):
     gate_up, down = refs[-2:]
     half = gate_up.shape[3] // 2
-    gate_up[0, 0, :, :half] = gate_held[...].astype(jnp.float32) + gate_sent[...].astype(jnp.float32)
-    gate_up[0, 0, :, half:] = up_held[...].astype(jnp.float32) + up_sent[...].astype(jnp.float32)
-    down[0, 0] = down_held[...].astype(jnp.float32) + down_sent[...].astype(jnp.float32)
+
+    def total(first, count):
+        values = [ref[...].astype(jnp.float32) for ref in refs[first : first + count]]
+        return sum(values[1:], values[0])
+
+    gate_up[0, 0, :, :half] = total(0, 2)
+    gate_up[0, 0, :, half:] = total(2, 2)
+    down[0, 0] = total(4, down_total)
 
 
 def finish_experts(layer, layers, experts, held, sent, kept):
-    rows, flat = sent[0].shape
+    rows, flat = held[0].shape
     half = flat // experts
-    down_rows, width = sent[2].shape[0] // experts, sent[2].shape[1]
+    down_rows, width = held[2].shape[0] // experts, held[2].shape[1]
     gate_spec = pl.BlockSpec((rows, half), lambda e: (0, e))
     down_spec = pl.BlockSpec((down_rows, width), lambda e: (e, 0))
+    downs = [part for part in (held[2], sent[2]) if part is not None]
+    inputs = [held[0], sent[0], held[1], sent[1], *downs]
     return pl.pallas_call(
-        finish_experts_body,
+        functools.partial(finish_experts_body, len(downs)),
         grid=(experts,),
-        in_specs=[gate_spec] * 4 + [down_spec] * 2 + [anywhere()] * len(kept),
+        in_specs=[gate_spec] * 4 + [down_spec] * len(downs) + [anywhere()] * len(kept),
         out_specs=[
             pl.BlockSpec((1, 1, rows, 2 * half), lambda e: (layer, e, 0, 0)),
             pl.BlockSpec((1, 1, down_rows, width), lambda e: (layer, e, 0, 0)),
@@ -1284,9 +1327,9 @@
             shaped((layers, experts, rows, 2 * half), jnp.float32),
             shaped((layers, experts, down_rows, width), jnp.float32),
         ],
-        input_output_aliases={6 + i: i for i in range(len(kept))},
+        input_output_aliases={len(inputs) + i: i for i in range(len(kept))},
         compiler_params=kernel_params(),
-    )(held[0], sent[0], held[1], sent[1], held[2], sent[2], *kept)
+    )(*inputs, *kept)
 
 
 def rotate_ranks(values_in, axis_name, total, target_of):
@@ -1330,15 +1373,18 @@
     return [((z + dz) % 4) * 2 + (y ^ dy) for dz in (0, 3, 2, 1) for dy in (0, 1)]
 
 
-def gather_fsdp(block, work=None):
+def gather_fsdp(block, work=None, beside=()):
     below = move_z(block, 1)
     own_mirror = swap_y(block)
     if work is None:
-        far = move_z(after(below, own_mirror), 1)
+        below, own_mirror = after(below, own_mirror, beside[0]), after(own_mirror, below)
+        far = move_z(below, 1)
         below_mirror = swap_y(after(below, own_mirror))
-        above = move_z(after(block, far, below_mirror), -1)
-        far_mirror = swap_y(after(far, below_mirror))
-        above_mirror = swap_y(after(above, far_mirror))
+        far = after(far, below_mirror, beside[1])
+        above = move_z(after(block, far), -1)
+        far_mirror = swap_y(far)
+        above = after(above, far_mirror, beside[2])
+        above_mirror = swap_y(above)
         return [block, own_mirror, below, below_mirror, far, far_mirror, above, above_mirror]
     far = move_z(below, 1)
     below_mirror = swap_y(below)
@@ -1347,11 +1393,12 @@
     far_mirror = swap_y(after(far, done))
     done = work(1, (after(below, far), below_mirror))
     above_mirror = swap_y(after(above, done))
-    done = work(2, (after(far, above), far_mirror))
-    work(3, (after(above, done), above_mirror))
-
-
-def scatter_fsdp(parts, beside=None):
+    work(2, (after(far, above), far_mirror))
+    work(3, (above, above_mirror))
+    return above_mirror
+
+
+def scatter_fsdp(parts, beside=None, start=None, middle=None, late=None):
     low = jnp.bfloat16
     results = []
 
@@ -1361,20 +1408,24 @@
             return jax.tree.leaves(results[-1])
         return []
 
-    far = (wide(parts[4]) + wide(swap_y(parts[5]))).astype(low)
+    def held(value, *others):
+        return after(value, *[other for other in others if other is not None])
+
+    far = (wide(parts[4]) + wide(swap_y(held(parts[5], start)))).astype(low)
     from_far = move_z(far, 1)
-    above_mirror = swap_y(parts[7])
+    above_mirror = swap_y(held(parts[7], start))
     done = run(far)
     above = (wide(parts[6]) + wide(above_mirror) + wide(from_far)).astype(low)
-    from_below = move_z(after(above, *done), 1)
+    above = held(above, middle)
+    from_below = move_z(above, 1)
     below_mirror = swap_y(after(parts[3], above))
-    done = run(above)
-    below = (wide(parts[2]) + wide(below_mirror)).astype(low)
+    later = run(above)
+    below = held((wide(parts[2]) + wide(below_mirror)).astype(low), late)
     from_above = move_z(after(below, *done), -1)
     own_mirror = swap_y(after(parts[1], below))
-    done = run(below)
+    done = later + run(below)
     own = wide(parts[0]) + wide(own_mirror) + wide(from_below)
-    return after(own, *done) + wide(from_above), results
+    return after(own, *done) + wide(from_above), results, below
 
 
 def gather_ctx(block):
@@ -1382,13 +1433,11 @@
     return [block, swap_core(block), across, swap_core(across)]
 
 
-def scatter_ctx(parts, *beside):
+def scatter_ctx(parts, beside=()):
     across = wide(parts[2]) + wide(swap_core(parts[3]))
     own = wide(parts[0]) + wide(swap_core(parts[1]))
     across = swap_x(across.astype(jnp.bfloat16))
-    if beside:
-        across = after(across, *beside)
-    return own + wide(across)
+    return own + wide(after(across, *beside))
 
 
 def split_ranks(
@@ -1440,9 +1489,6 @@
     def ring(vector):
         return jnp.take(vector.reshape(ctx_total, -1), ring_members, axis=0).reshape(-1)
 
-    def gather_experts(i, start):
-        return [*gather_ctx(after(w_gate_up[i], start)), *gather_ctx(after(w_down[i], start))]
-
     places = jnp.concatenate(
         [row_positions((ctx_index ^ r) * row_count, row_count, row_count, ctx_total) for r in range(4)]
     )
@@ -1455,40 +1501,40 @@
         jnp.concatenate([-sine, sine, -sine, sine], -1),
     )
 
-    blocks = to_members(weight_blocks(members, w_query, w_key_value, w_router, norm_gains))
-    hidden_rows = gather_ctx(after(hidden_in.reshape(row_count, model_width), blocks[2]))
-    *layer_shards, small_rows = pack_shards(
-        blocks, w_output, expert_ids.reshape(layer_total, row_count, TOP), qkv_part
-    )
-    shards = gather_fsdp(layer_shards[0])
-    expert_weights = [gather_experts(0, small_rows)]
-    small_pair = jnp.stack([small_rows, swap_y(small_rows)])
-    small_pair = after(small_pair, shards[2])
-    small_all = jnp.concatenate(
-        [small_pair, move_z(small_pair, 1), move_z(small_pair, 2), move_z(small_pair, -1)], 0
-    )
-    small_all = after(small_all, shards[6])
-    ids_all = small_all[:, :row_count, 64 : 64 + layer_total * TOP].reshape(groups * row_count, -1)
-    small = place(members, [small_all.reshape(groups, ctx_total, share, 128)], 128)[0]
-    small = small.reshape(model_width, 128)
+    blocks = to_members(
+        weight_blocks(
+            members, w_query, w_key_value, w_router.transpose(0, 2, 1), norm_gains.transpose(0, 2, 1)
+        )
+    )
+    packed = pack_shards(
+        blocks,
+        w_output,
+        expert_ids.reshape(layer_total, row_count, TOP).transpose(0, 2, 1),
+        qkv_part,
+    )
+    expert_weights, start = [[]], packed
+    for part in [*(w_gate_up[0, e] for e in range(experts_here)), w_down[0]]:
+        expert_weights[0].extend(gather_ctx(after(part, start)))
+        start = expert_weights[0][-2]
+    hidden_rows = gather_ctx(
+        after(hidden_in.reshape(row_count, model_width), expert_weights[0][6])
+    )
+    flat_shards = gather_fsdp(packed, None, [expert_weights[0][2], expert_weights[0][6], 0.0])
+    shards = [shard.reshape(ctx_total, share, -1) for shard in flat_shards]
+    layer_part = qkv_part + q_part
+    small = place(members, shards, layer_total * layer_part, 128, 0)[0].reshape(model_width, 128)
     gains = [
         wide(small[:, gain_lane + 2 * i : gain_lane + 2 * i + 2]).T for i in range(layer_total)
     ]
     ring_gains = [ring(gains[i][0]) for i in range(layer_total)]
 
-    def place_layer(members, shards):
-        shards = [shard.reshape(-1, ctx_total, share, qkv_part + q_part) for shard in shards]
-        if len(shards) > 1:
-            shards = [shard[0] for shard in shards]
-        qkv_weight, out_weight = place(members, shards, qkv_part)
+    def place_layer(i, start):
+        qkv_weight, out_weight = place(
+            members, [after(shards[0], start), *shards[1:]], i * layer_part, qkv_part, q_part
+        )
         return qkv_weight.reshape(model_width, qkv_part), out_weight
 
-    attention_weights = [place_layer(members, shards)]
-    later_weights = [
-        lax.all_gather(after(shard, shards[7]), "fsdp", axis=0, tiled=False)
-        for shard in layer_shards[1:]
-    ]
-
+    attention_weights = [place_layer(0, expert_weights[0][10])]
     residual = wide(hidden_in.reshape(row_count, model_width))
     saved = []
     for i in range(layer_total):
@@ -1503,33 +1549,31 @@
         branch, rows_first, qkv, attended, logs = attention_forward(
             ctx_ref, rows, qkv_weight, out_weight, qkv_part, tables
         )
-        middle = residual + scatter_ctx(branch, *(expert_weights[0] if i == 0 else ()))
+        middle = residual + scatter_ctx(branch)
         normed_second, root_second = rms_scaled(middle, gains[i][1])
         parts, kept = [None] * groups, []
 
         def forward_work(group, pair):
             outs = experts_forward(
-                group, pair_total, ctx_ref, pair, ids_all, TOP * i, expert_total * i, small,
+                group, pair_total, ctx_ref, pair, flat_shards[2 * group : 2 * group + 2],
+                64 + TOP * i, expert_total * i, small,
                 own_experts[i], expert_weights[i], kept,
             )
             parts[2 * group], parts[2 * group + 1] = outs[:2]
             kept[:] = outs[2:]
             return outs[0]
 
-        gather_fsdp(normed_second.astype(low), forward_work)
+        normed_second = normed_second.astype(low)
+        beside = None
+        if i == 0:
+            joined = join_experts(after(w_gate_up[1], middle), w_down[1])
+            expert_weights.append([lax.all_gather(joined, "ctx", axis=1, tiled=True)])
+            beside = (lambda start: [], lambda start: place_layer(1, start), lambda start: [])
+        last = gather_fsdp(normed_second, forward_work)
         rows_second, gate, up, probs = kept
-        beside = None
-        if i + 1 < layer_total:
-            gathered = gather_experts(i + 1, parts[0])
-            beside = (
-                lambda start: [],
-                lambda start: place_layer(natural_members, [after(later_weights[i], start)]),
-                lambda start: gathered,
-            )
-        expert_sum, placed = scatter_fsdp(parts, beside)
+        expert_sum, placed, _ = scatter_fsdp(parts, beside, last)
         if beside:
             attention_weights.append(placed[1])
-            expert_weights.append(gathered)
         saved.append(
             (
                 residual, root_first, rows_first, qkv, attended, logs,
@@ -1539,7 +1583,14 @@
         residual = middle + expert_sum
     hidden_out = residual.reshape(1, row_count, model_width).astype(low)
     grad = wide(out_grad.reshape(row_count, model_width))
-    attention_grads, expert_grads = [], []
+    expert_grads = []
+
+    def add_core(start, pairs, came):
+        sums = [
+            (dot_tn(after(part, start)[:, :half], grads) + wide(other)).astype(low)
+            for (part, half, grads), other in zip(pairs, came, strict=True)
+        ]
+        return [(part[: part.shape[0] // 2], part[part.shape[0] // 2 :]) for part in sums]
 
     def finish_layer(i, pairs, start, kept):
         held, sent = [pair[0] for pair in pairs], [pair[1] for pair in pairs]
@@ -1558,72 +1609,50 @@
         lanes = jnp.where(expert_lane == 0, mean_high, jnp.where(expert_lane == 1, mean_low, 0))
         sent = jnp.concatenate([grad.astype(low), lanes.astype(low)], -1)
         parts, kept = [None] * groups, []
+        if i == 0:
+            halves = add_core(sent, *pending)
+            expert_grads.insert(0, [(half[0], swap_x(half[1])) for half in halves] + [upper_down])
 
         def backward_work(group, pair):
-            if i + 1 < layer_total:
-                done = (packed, expert_grads[0][0][1], expert_grads[0][1][1], expert_grads[0][2][1])
-                pair = (after(pair[0], done[group]), pair[1])
+            if i == 0 and group == 0:
+                pair = (after(pair[0], *jax.tree.leaves(halves)), pair[1])
+            if i == 0 and group == 3:
+                pair = (after(pair[0], expert_grads[0][0][1]), pair[1])
             outs = experts_backward(
                 group, pair_total, ctx_ref, pair, probs, gate, up, small, own_experts[i],
-                expert_weights[i], kept,
+                expert_weights[i], kept, i == 0,
             )
             parts[2 * group], parts[2 * group + 1] = outs[:2]
             kept[:] = outs[2:]
             return outs[0]
 
-        gather_fsdp(sent, backward_work)
+        last = gather_fsdp(sent, backward_work)
         grads_second, grad_gate, grad_up, hidden, grad_logits = kept
         half_width, half_hidden = model_width // 2, hidden.shape[1] // 2
 
-        def to_other_core(start):
-            ours = after(rows_second, start)[:, half_width:]
-            return [
-                swap_core(dot_tn(part, grads).astype(low))
-                for part, grads in (
-                    (ours, grad_gate),
-                    (ours, grad_up),
-                    (hidden[:, half_hidden:], grads_second),
-                )
-            ]
-
-        def add_core(start):
-            ours = after(rows_second, start)[:, :half_width]
-            return [
-                (dot_tn(part, grads) + wide(other)).astype(low)
-                for part, grads, other in (
-                    (ours, grad_gate, came[0]),
-                    (ours, grad_up, came[1]),
-                    (hidden[:, :half_hidden], grads_second, came[2]),
-                )
-            ]
-
-        came = []
+        came, whole_down = [], []
+        pairs = [(rows_second, half_width, grad_gate), (rows_second, half_width, grad_up)]
+        if i == 0:
+            pairs.append((hidden, half_hidden, grads_second))
 
         def first_beside(start):
-            came[:] = to_other_core(start)
-            return came
-
-        def second_beside(start):
-            came[:] = add_core(start)
-            return came
-
-        def third_beside(start):
-            if i + 1 < layer_total:
-                return finish_layer(i + 1, expert_grads[0], start, [])
-            return []
-
-        grad_second, finished = scatter_fsdp(parts, (first_beside, second_beside, third_beside))
-        halves = [(part[: part.shape[0] // 2], part[part.shape[0] // 2 :]) for part in came]
+            for part, half, grads in pairs:
+                came.append(swap_core(dot_tn(after(part, start)[:, half:], grads).astype(low)))
+            if i > 0:
+                whole_down.append(dot_tn(after(hidden, start), grads_second).astype(low))
+            return came + whole_down
+
+        last_gate = [expert_grads[0][1][1]] if i == 0 else []
+        grad_second, _, _ = scatter_fsdp(
+            parts, (lambda start: last_gate, first_beside, lambda start: []), last
+        )
         small_grads = dot_tn(rows_second, grad_logits)
         grad_middle, gain_second = rms_back(middle, root_second, gains[i][1], grad_second)
         grad_middle = grad_middle + grad
-        branch_grads = gather_ctx(grad_middle.astype(low))
-        crossed = []
-        if i == 0:
-            crossed.append(swap_x(halves[0][1]))
-            crossed.append(swap_x(after(halves[1][1], crossed[0], branch_grads[3])))
-            crossed.append(swap_x(after(halves[2][1], crossed[1])))
-            rows_first = after(rows_first, crossed[0])
+        branch_rows = grad_middle.astype(low)
+        branch_grads = gather_ctx(branch_rows)
+        if i > 0:
+            pending = pairs, came
         back, rows_branch, grad_qkv, gain_first = attention_backward(
             ctx_ref, branch_grads, rows_first, qkv_weight, out_weight, qkv,
             logs, tables,
@@ -1635,31 +1664,57 @@
             gain_first[:, None],
             jnp.where(expert_lane == gain_lane + 1, gain_second[:, None], small_grads),
         ).astype(low)
-        if crossed:
-            small_grads = after(small_grads, crossed[1])
+        if i == 0:
+            far = (wide(packs[4]) + wide(swap_y(after(packs[5], grad_second)))).astype(low)
+            above_mirror, from_far = swap_y(after(packs[7], grad_second)), move_z(far, 1)
+            above = (wide(packs[6]) + wide(above_mirror) + wide(from_far)).astype(low)
+            above = after(above, back[0])
+            from_below, below_mirror = move_z(above, 1), swap_y(after(packs[3], above))
+            rows_first = after(rows_first, above)
         qkv_grads = dot_tn(rows_first, grad_qkv).astype(low)
         out_grads = dot_tn(attended, rows_branch).astype(low)
-        grad_first = scatter_ctx(back, qkv_grads, out_grads)
-        grad_input, _ = rms_back(residual, root_first, gains[i][0], grad_first)
-        grad = grad_input + grad_middle
-        crossed = crossed or [swap_x(after(sent_half, grad)) for _, sent_half in halves]
-        expert_grads.insert(0, [(half[0], sent) for half, sent in zip(halves, crossed, strict=True)])
-        packs = pack_grads(
-            members if i == 0 else natural_members,
+        layer_packs = pack_grads(
+            members,
             qkv_grads.reshape(ctx_total, groups, share, qkv_part),
             small_grads.reshape(ctx_total, groups, share, 128),
             out_grads,
-            i == 0,
-        )
-        shard_shape = (ctx_total, share, qkv_part + 128 + q_part)
+            True,
+        )
+        flat_packs = [pack.reshape(ctx_total * share, -1) for pack in layer_packs]
         if i == 0:
-            flat = (ctx_total * share, shard_shape[2])
-            packed = scatter_fsdp([pack.reshape(flat) for pack in packs])[0].astype(low)
-        else:
-            packed = packs[0].reshape(groups * ctx_total, *shard_shape[1:])
-            attention_grads.insert(0, lax.psum_scatter(packed, "fsdp", scatter_dimension=0, tiled=True))
-        if i == 0:
-            attention_grads.insert(0, packed.reshape(shard_shape))
+            below = after((wide(packs[2]) + wide(below_mirror)).astype(low), layer_packs[0])
+            from_above, own_mirror = move_z(below, -1), swap_y(after(packs[1], below))
+            upper = wide(packs[0]) + wide(own_mirror) + wide(from_below) + wide(from_above)
+            halves = add_core(below, pairs[:1], came[:1])
+            crossed = [swap_x(halves[0][1])]
+
+            def second_beside(start):
+                halves.extend(add_core(start, pairs[1:], came[1:]))
+                crossed.extend(swap_x(half[1]) for half in halves[1:])
+                return jax.tree.leaves(halves)
+
+            beside = [
+                second_beside,
+                lambda start: [crossed[0], finish_layer(1, expert_grads[0], start, [])],
+                lambda start: crossed[1],
+            ]
+            lower, finished, _ = scatter_fsdp(flat_packs, beside, below, None, upper)
+            expert_grads.insert(
+                0, [(half[0], other) for half, other in zip(halves, crossed, strict=True)]
+            )
+            attention_grads = [lower, upper]
+            layer_packs = [upper]
+        grad_first = scatter_ctx(back, layer_packs)
+        grad_input, _ = rms_back(residual, root_first, gains[i][0], grad_first)
+        grad = grad_input + grad_middle
+        if i > 0:
+            parts = after(whole_down[0], grad).reshape(ctx_total, -1, model_width)
+            upper_down = lax.psum_scatter(parts, "ctx", scatter_dimension=0, tiled=True)
+            upper_down = (upper_down.reshape(-1, model_width), None)
+        packs = flat_packs
+    attention_grads = [
+        part.astype(low).reshape(ctx_total, share, -1) for part in attention_grads
+    ]
     front = qkv_part + 128
     blocks = to_members(
         [jnp.concatenate([part[r, :, :front] for part in attention_grads], -1) for r in range(ctx_total)]
@@ -1672,15 +1727,15 @@
         ],
         expert_total,
     )
-    outs = finish_layer(0, expert_grads[0], attention_grads[0], finished[2])
+    outs = finish_layer(0, expert_grads[0], attention_grads[0], finished[1][1])
     return (
         hidden_out,
         grad.reshape(1, row_count, model_width),
         query_out,
         key_value_out,
         output_out,
-        router_out,
-        gains_out,
+        router_out.transpose(0, 2, 1),
+        gains_out.transpose(0, 2, 1),
         outs[0],
         outs[1],
     )

time: 868 us -> 788 us (0.908)
  waiting for transfers between devices: 365 us -> 288 us
  matrix products: 52.1 us -> 42.4 us
  Pallas kernels: 207 us -> 216 us
    ppermute x128 -> x126, waiting for transfers between devices: 365 us -> 288 us  [rotate_ranks(): lax.ppermute(values_in, axis_name, [(i, target_of(i)) for i in range(tota...]
    dot_general x18 -> x17, matrix products: 52.1 us -> 42.4 us  [mm(): return lax.dot_general(a, b, dims, preferred_element_type=jnp.float32)]
    ppermute x128 -> x126, starting transfers between devices: 112 us -> 115 us  [rotate_ranks(): lax.ppermute(values_in, axis_name, [(i, target_of(i)) for i in range(tota...]
    unnamed x311 -> x366, local copies, waits for them, and re-layouts: 24.4 us -> 23.6 us
  transfers between devices with their start and end apart: 130 -> 128, of which waited for: 54 -> 55; matrix products, arithmetic and copies ran while one was open for 15% -> 13% of each run, Pallas kernels for 19% -> 23%
where the time goes in v5:
time: 788 us; the launch traced here: 777 us
  waiting for transfers between devices  288 us (37%)
  Pallas kernels  216 us (27%)
  starting transfers between devices  115 us (15%)
  other arithmetic  50.3 us (6%)
  local copies, waits for them, and re-layouts  48.4 us (6%)
  matrix products  42.4 us (5%)
  between operations  16.9 us (2%)
    ppermute x126, waiting for transfers between devices, rotate_ranks(): lax.ppermute(values_in, axis_name, [(i, target_of(i)) for i in range(tota...  288 us
    ppermute x126, starting transfers between devices, rotate_ranks(): lax.ppermute(values_in, axis_name, [(i, target_of(i)) for i in range(tota...  115 us
    pallas_call x8, Pallas kernels, experts_backward(): pl.pallas_call(functools.partial(experts_backward_body, len(weights), rin...  67.9 us
    pallas_call x8, Pallas kernels, experts_forward(): pl.pallas_call(functools.partial(experts_forward_body, len(weights), grou...  62.8 us
    dot_general x17, matrix products, mm(): return lax.dot_general(a, b, dims, preferred_element_type=jnp.float32)  42.4 us
    pallas_call x2, Pallas kernels, attention_backward(): pl.pallas_call(attention_backward_body, in_specs=[smem()] + [anywhere()]...  27.1 us
    unnamed x366, local copies, waits for them, and re-layouts  23.6 us
    pallas_call x2, Pallas kernels, attention_forward(): pl.pallas_call(attention_forward_body, in_specs=[smem()] + [anywhere()] *...  21.9 us
  transfers between devices with their start and end apart: 128, of which 55 were waited for; matrix products, arithmetic and copies ran while one was open for 13% of the time, Pallas kernels for 23%

profile of v5, /device:TPU:0, one launch (start us, length us, event | category | flops | bytes accessed | tf_op | source)
XLA Modules:
  0.0 776.7 jit_solution(4568481231546528624)
XLA Ops:
  13.0 4.5 collective-permute-done.1.block_2
  29.3 17.6 %collective-permute-done.3.refs_2_ = bf16[384,1024]{1,0:T(8,128)(2,1)S(1)} collective-permute-done((bf16[384,1024]{1,0:T(8,128)(2,1)S(1)}, bf16[384,1024]{1,0:T(8,128)(2,1)S(1)}, u32[]{:S(2)}, u32[]{:S(2)}) %collective-permute-start.3) | collective-permute-done | bytes 786464 | tf_op jit(solution)/shard_map/ppermute | solution.py:1336
  53.0 12.3 %collective-permute-done.4.refs_6_ = bf16[384,1024]{1,0:T(8,128)(2,1)} collective-permute-done((bf16[384,1024]{1,0:T(8,128)(2,1)S(1)}, bf16[384,1024]{1,0:T(8,128)(2,1)}, u32[]{:S(2)}, u32[]{:S(2)}) %collective-permute-start.4) | collective-permute-done | bytes 786464 | tf_op jit(solution)/shard_map/ppermute | solution.py:1336
  77.1 7.5 collective-permute-done.13
  89.9 8.6 %collective-permute-done.15.refs_10_ = bf16[2,128,1536]{2,1,0:T(8,128)(2,1)S(1)} collective-permute-done((bf16[2,128,1536]{2,1,0:T(8,128)(2,1)S(1)}, bf16[2,128,1536]{2,1,0:T(8,128)(2,1)S(1)}, u32[]{:S(2)}, u32[]{:S(2)}) %collective-permute-start.15) | collective-permute-done | bytes 786464 | tf_op jit(solution)/shard_map/ppermute | solution.py:1336
  99.6 6.6 collective-permute-done.11.ids_1
  114.0 4.9 shard_map.172
  120.3 11.0 %shard_map.173 = (bf16[128,1536]{1,0:T(8,128)(2,1)}, bf16[128,1536]{1,0:T(8,128)(2,1)}, bf16[128,1536]{1,0:T(8,128)(2,1)}, bf16[128,1536]{1,0:T(8,128)(2,1)}, bf...) custom-call(s32[1]{0:T(128)} %bitcast.1.ctx_ref, ...), custom_call_target="tpu_custom_call" | custom-call | flops 2013265920 | bytes 6291456 | tf_op jit(solution)/shard_map/pallas_call | solution.py:964
  137.5 8.2 %collective-permute-done.18 = bf16[128,1536]{1,0:T(8,128)(2,1)S(1)} collective-permute-done((bf16[128,1536]{1,0:T(8,128)(2,1)S(1)}, bf16[128,1536]{1,0:T(8,128)(2,1)S(1)}, u32[]{:S(2)}, u32[]{:S(2)}) %collective-permute-start.18) | collective-permute-done | bytes 393248 | tf_op jit(solution)/shard_map/ppermute | solution.py:1336
  159.2 8.4 %collective-permute-done.19.rows_0 = bf16[128,1536]{1,0:T(8,128)(2,1)S(1)} collective-permute-done((bf16[128,1536]{1,0:T(8,128)(2,1)S(1)}, bf16[128,1536]{1,0:T(8,128)(2,1)S(1)}, u32[]{:S(2)}, u32[]{:S(2)}) %collective-permute-start.19) | collective-permute-done | bytes 393248 | tf_op jit(solution)/shard_map/ppermute | solution.py:1336
  171.4 7.9 %shard_map.174 = (bf16[128,1536]{1,0:T(8,128)(2,1)}, bf16[128,1536]{1,0:T(8,128)(2,1)}, bf16[1024,1536]{1,0:T(8,128)(2,1)}, bf16[1024,1024]{1,0:T(8,128)(2,1)}, ...) custom-call(s32[1]{0:T(128)} %bitcast.1.ctx_ref, bf16[128,1536]{1,0:T(8,128)(2,1)} %copy-done.52, ...), custom_call_target="tpu_custom_call" | custom-call | flops 2415919104 | bytes 9437184 | tf_op jit(solution)/shard_map/pallas_call | solution.py:679
  184.4 7.8 %shard_map.175 = (bf16[128,1536]{1,0:T(8,128)(2,1)}, bf16[128,1536]{1,0:T(8,128)(2,1)}, bf16[1024,1536]{1,0:T(8,128)(2,1)}, bf16[1024,1024]{1,0:T(8,128)(2,1)}, ...) custom-call(s32[1]{0:T(128)} %bitcast.1.ctx_ref, ...), custom_call_target="tpu_custom_call", output_to_operand_aliasing={{2}: (19, {}), {3}: (20, {}), {4}: (21, {}), {5}: (22, {})} | custom-call | flops 2415919104 | bytes 9437184 | tf_op jit(solution)/shard_map/pallas_call | solution.py:679
  194.5 7.8 %shard_map.176 = (bf16[128,1536]{1,0:T(8,128)(2,1)}, bf16[128,1536]{1,0:T(8,128)(2,1)}, bf16[1024,1536]{1,0:T(8,128)(2,1)}, bf16[1024,1024]{1,0:T(8,128)(2,1)}, ...) custom-call(s32[1]{0:T(128)} %bitcast.1.ctx_ref, ...), custom_call_target="tpu_custom_call", output_to_operand_aliasing={{2}: (19, {}), {3}: (20, {}), {4}: (21, {}), {5}: (22, {})} | custom-call | flops 2415919104 | bytes 9437184 | tf_op jit(solution)/shard_map/pallas_call | solution.py:679
  203.0 7.9 %shard_map.177 = (bf16[128,1536]{1,0:T(8,128)(2,1)}, bf16[128,1536]{1,0:T(8,128)(2,1)}, bf16[1024,1536]{1,0:T(8,128)(2,1)}, bf16[1024,1024]{1,0:T(8,128)(2,1)}, ...) custom-call(s32[1]{0:T(128)} %bitcast.1.ctx_ref, ...), custom_call_target="tpu_custom_call", output_to_operand_aliasing={{2}: (19, {}), {3}: (20, {}), {4}: (21, {}), {5}: (22, {})} | custom-call | flops 2415919104 | bytes 9437184 | tf_op jit(solution)/shard_map/pallas_call | solution.py:679
  212.6 7.6 collective-permute-done.32
  225.0 8.7 %collective-permute-done.35 = bf16[128,1536]{1,0:T(8,128)(2,1)S(1)} collective-permute-done((bf16[128,1536]{1,0:T(8,128)(2,1)S(1)}, bf16[128,1536]{1,0:T(8,128)(2,1)S(1)}, u32[]{:S(2)}, u32[]{:S(2)}) %collective-permute-start.35) | collective-permute-done | bytes 393248 | tf_op jit(solution)/shard_map/ppermute | solution.py:1336
  235.2 4.9 shard_map.178
  241.8 6.3 collective-permute-done.38
  251.4 6.0 collective-permute-done.40.rows_2
  259.8 10.9 %shard_map.179 = (bf16[128,1536]{1,0:T(8,128)(2,1)}, bf16[128,1536]{1,0:T(8,128)(2,1)}, bf16[128,1536]{1,0:T(8,128)(2,1)}, bf16[128,1536]{1,0:T(8,128)(2,1)}, bf...) custom-call(s32[1]{0:T(128)} %bitcast.1.ctx_ref, ...), custom_call_target="tpu_custom_call" | custom-call | flops 2013265920 | bytes 6291456 | tf_op jit(solution)/shard_map/pallas_call | solution.py:964
  275.7 9.4 %collective-permute-done.44 = bf16[128,1536]{1,0:T(8,128)(2,1)S(1)} collective-permute-done((bf16[128,1536]{1,0:T(8,128)(2,1)S(1)}, bf16[128,1536]{1,0:T(8,128)(2,1)S(1)}, u32[]{:S(2)}, u32[]{:S(2)}) %collective-permute-start.44) | collective-permute-done | bytes 393248 | tf_op jit(solution)/shard_map/ppermute | solution.py:1336
  288.6 10.7 %collective-permute-done.45.rows_0 = bf16[128,1536]{1,0:T(8,128)(2,1)S(1)} collective-permute-done((bf16[128,1536]{1,0:T(8,128)(2,1)S(1)}, bf16[128,1536]{1,0:T(8,128)(2,1)S(1)}, u32[]{:S(2)}, u32[]{:S(2)}) %collective-permute-start.45) | collective-permute-done | bytes 393248 | tf_op jit(solution)/shard_map/ppermute | solution.py:1336
  302.2 7.9 %shard_map.180 = (bf16[128,1536]{1,0:T(8,128)(2,1)}, bf16[128,1536]{1,0:T(8,128)(2,1)}, bf16[1024,1536]{1,0:T(8,128)(2,1)}, bf16[1024,1024]{1,0:T(8,128)(2,1)}, ...) custom-call(s32[1]{0:T(128)} %bitcast.1.ctx_ref, bf16[128,1536]{1,0:T(8,128)(2,1)} %copy-done.53, ...), custom_call_target="tpu_custom_call" | custom-call | flops 2415919104 | bytes 9437184 | tf_op jit(solution)/shard_map/pallas_call | solution.py:679
  315.7 7.8 %shard_map.181 = (bf16[128,1536]{1,0:T(8,128)(2,1)}, bf16[128,1536]{1,0:T(8,128)(2,1)}, bf16[1024,1536]{1,0:T(8,128)(2,1)}, bf16[1024,1024]{1,0:T(8,128)(2,1)}, ...) custom-call(s32[1]{0:T(128)} %bitcast.1.ctx_ref, ...), custom_call_target="tpu_custom_call", output_to_operand_aliasing={{2}: (8, {}), {3}: (9, {}), {4}: (10, {}), {5}: (11, {})} | custom-call | flops 2415919104 | bytes 9437184 | tf_op jit(solution)/shard_map/pallas_call | solution.py:679
  325.8 7.9 %shard_map.182 = (bf16[128,1536]{1,0:T(8,128)(2,1)}, bf16[128,1536]{1,0:T(8,128)(2,1)}, bf16[1024,1536]{1,0:T(8,128)(2,1)}, bf16[1024,1024]{1,0:T(8,128)(2,1)}, ...) custom-call(s32[1]{0:T(128)} %bitcast.1.ctx_ref, ...), custom_call_target="tpu_custom_call", output_to_operand_aliasing={{2}: (8, {}), {3}: (9, {}), {4}: (10, {}), {5}: (11, {})} | custom-call | flops 2415919104 | bytes 9437184 | tf_op jit(solution)/shard_map/pallas_call | solution.py:679
  334.4 7.9 %shard_map.183 = (bf16[128,1536]{1,0:T(8,128)(2,1)}, bf16[128,1536]{1,0:T(8,128)(2,1)}, bf16[1024,1536]{1,0:T(8,128)(2,1)}, bf16[1024,1024]{1,0:T(8,128)(2,1)}, ...) custom-call(s32[1]{0:T(128)} %bitcast.1.ctx_ref, ...), custom_call_target="tpu_custom_call", output_to_operand_aliasing={{2}: (8, {}), {3}: (9, {}), {4}: (10, {}), {5}: (11, {})} | custom-call | flops 2415919104 | bytes 9437184 | tf_op jit(solution)/shard_map/pallas_call | solution.py:679
  343.9 6.7 collective-permute-done.52
  355.5 10.1 %collective-permute-done.55 = bf16[128,1536]{1,0:T(8,128)(2,1)S(1)} collective-permute-done((bf16[128,1536]{1,0:T(8,128)(2,1)S(1)}, bf16[128,1536]{1,0:T(8,128)(2,1)S(1)}, u32[]{:S(2)}, u32[]{:S(2)}) %collective-permute-start.55) | collective-permute-done | bytes 393248 | tf_op jit(solution)/shard_map/ppermute | solution.py:1336
  367.9 6.9 collective-permute-done.56
  376.1 5.3 collective-permute-start.60
  381.5 7.6 collective-permute-done.59.grads_0
  389.2 4.2 collective-permute-start.62
  394.2 8.3 %shard_map.184 = (bf16[128,1536]{1,0:T(8,128)(2,1)}, bf16[128,1536]{1,0:T(8,128)(2,1)}, bf16[1024,1536]{1,0:T(8,128)(2,1)}, bf16[1024,1024]{1,0:T(8,128)(2,1)}, ...) custom-call(s32[1]{0:T(128)} %bitcast.1.ctx_ref, bf16[128,1664]{1,0:T(8,128)(2,1)} %copy-done.51, ...), custom_call_target="tpu_custom_call" | custom-call | flops 2415919104 | bytes 9437184 | tf_op jit(solution)/shard_map/pallas_call | solution.py:829
  402.6 3.8 collective-permute-start.63
  407.2 8.4 %shard_map.185 = (bf16[128,1536]{1,0:T(8,128)(2,1)}, bf16[128,1536]{1,0:T(8,128)(2,1)}, bf16[1024,1536]{1,0:T(8,128)(2,1)}, bf16[1024,1024]{1,0:T(8,128)(2,1)}, ...) custom-call(s32[1]{0:T(128)} %bitcast.1.ctx_ref, ...), custom_call_target="tpu_custom_call", output_to_operand_aliasing={{2}: (9, {}), {3}: (10, {}), {4}: (11, {}), {5}: (12, {}), ... | custom-call | flops 2415919104 | bytes 9437184 | tf_op jit(solution)/shard_map/pallas_call | solution.py:829
  418.5 8.3 %shard_map.186 = (bf16[128,1536]{1,0:T(8,128)(2,1)}, bf16[128,1536]{1,0:T(8,128)(2,1)}, bf16[1024,1536]{1,0:T(8,128)(2,1)}, bf16[1024,1024]{1,0:T(8,128)(2,1)}, ...) custom-call(s32[1]{0:T(128)} %bitcast.1.ctx_ref, ...), custom_call_target="tpu_custom_call", output_to_operand_aliasing={{2}: (9, {}), {3}: (10, {}), {4}: (11, {}), {5}: (12, {}), ... | custom-call | flops 2415919104 | bytes 9437184 | tf_op jit(solution)/shard_map/pallas_call | solution.py:829
  427.6 8.5 %shard_map.187 = (bf16[128,1536]{1,0:T(8,128)(2,1)}, bf16[128,1536]{1,0:T(8,128)(2,1)}, bf16[1024,1536]{1,0:T(8,128)(2,1)}, bf16[1024,1024]{1,0:T(8,128)(2,1)}, ...) custom-call(s32[1]{0:T(128)} %bitcast.1.ctx_ref, ...), custom_call_target="tpu_custom_call", output_to_operand_aliasing={{2}: (9, {}), {3}: (10, {}), {4}: (11, {}), {5}: (12, {}), ... | custom-call | flops 2415919104 | bytes 9437184 | tf_op jit(solution)/shard_map/pallas_call | solution.py:829
  437.7 6.5 collective-permute-done.66
  457.6 5.0 convolution_convert_fusion
  466.6 6.0 collective-permute-done.74
  477.6 5.5 collective-permute-done.76.grad_2
  491.1 13.6 %shard_map.188 = (bf16[128,1536]{1,0:T(8,128)(2,1)}, bf16[128,1536]{1,0:T(8,128)(2,1)}, bf16[128,1536]{1,0:T(8,128)(2,1)}, bf16[128,1536]{1,0:T(8,128)(2,1)}, bf...) custom-call(s32[1]{0:T(128)} %bitcast.1.ctx_ref, bf16[128,1536]{1,0:T(8,128)(2,1)} %copy-done.109, ...), custom_call_target="tpu_custom_call" | custom-call | flops 2617245696 | bytes 7864320 | tf_op jit(solution)/shard_map/pallas_call | solution.py:1089
  515.9 4.2 shard_map.189
  531.5 7.7 collective-permute-done.81.grads_0
  542.2 8.6 %shard_map.190 = (bf16[128,1536]{1,0:T(8,128)(2,1)}, bf16[128,1536]{1,0:T(8,128)(2,1)}, bf16[1024,1536]{1,0:T(8,128)(2,1)}, bf16[1024,1024]{1,0:T(8,128)(2,1)}, ...) custom-call(s32[1]{0:T(128)} %bitcast.1.ctx_ref, bf16[128,1664]{1,0:T(8,128)(2,1)} %copy-done.49, ...), custom_call_target="tpu_custom_call" | custom-call | flops 2415919104 | bytes 9437184 | tf_op jit(solution)/shard_map/pallas_call | solution.py:829
  558.6 8.6 %shard_map.191 = (bf16[128,1536]{1,0:T(8,128)(2,1)}, bf16[128,1536]{1,0:T(8,128)(2,1)}, bf16[1024,1536]{1,0:T(8,128)(2,1)}, bf16[1024,1024]{1,0:T(8,128)(2,1)}, ...) custom-call(s32[1]{0:T(128)} %bitcast.1.ctx_ref, ...), custom_call_target="tpu_custom_call", output_to_operand_aliasing={{2}: (20, {}), {3}: (21, {}), {4}: (22, {}), {5}: (23, {}),... | custom-call | flops 2415919104 | bytes 9437184 | tf_op jit(solution)/shard_map/pallas_call | solution.py:829
  568.9 8.5 %shard_map.192 = (bf16[128,1536]{1,0:T(8,128)(2,1)}, bf16[128,1536]{1,0:T(8,128)(2,1)}, bf16[1024,1536]{1,0:T(8,128)(2,1)}, bf16[1024,1024]{1,0:T(8,128)(2,1)}, ...) custom-call(s32[1]{0:T(128)} %bitcast.1.ctx_ref, ...), custom_call_target="tpu_custom_call", output_to_operand_aliasing={{2}: (20, {}), {3}: (21, {}), {4}: (22, {}), {5}: (23, {}),... | custom-call | flops 2415919104 | bytes 9437184 | tf_op jit(solution)/shard_map/pallas_call | solution.py:829
  579.6 8.7 %shard_map.193 = (bf16[128,1536]{1,0:T(8,128)(2,1)}, bf16[128,1536]{1,0:T(8,128)(2,1)}, bf16[1024,1536]{1,0:T(8,128)(2,1)}, bf16[1024,1024]{1,0:T(8,128)(2,1)}, ...) custom-call(s32[1]{0:T(128)} %bitcast.1.ctx_ref, ...), custom_call_target="tpu_custom_call", output_to_operand_aliasing={{2}: (20, {}), {3}: (21, {}), {4}: (22, {}), {5}: (23, {}),... | custom-call | flops 2415919104 | bytes 9437184 | tf_op jit(solution)/shard_map/pallas_call | solution.py:829
  590.1 6.6 collective-permute-done.89
  610.1 12.1 %collective-permute-done.94 = bf16[128,1536]{1,0:T(8,128)(2,1)S(1)} collective-permute-done((bf16[128,1536]{1,0:T(8,128)(2,1)S(1)}, bf16[128,1536]{1,0:T(8,128)(2,1)S(1)}, u32[]{:S(2)}, u32[]{:S(2)}) %collective-permute-start.94) | collective-permute-done | bytes 393248 | tf_op jit(solution)/shard_map/ppermute | solution.py:1336
  623.6 9.3 %collective-permute-done.99 = bf16[128,1536]{1,0:T(8,128)(2,1)S(1)} collective-permute-done((bf16[128,1536]{1,0:T(8,128)(2,1)S(1)}, bf16[128,1536]{1,0:T(8,128)(2,1)S(1)}, u32[]{:S(2)}, u32[]{:S(2)}) %collective-permute-start.99) | collective-permute-done | bytes 393248 | tf_op jit(solution)/shard_map/ppermute | solution.py:1336
  639.1 5.8 collective-permute-done.101.grad_2
  649.6 13.5 %shard_map.194 = (bf16[128,1536]{1,0:T(8,128)(2,1)}, bf16[128,1536]{1,0:T(8,128)(2,1)}, bf16[128,1536]{1,0:T(8,128)(2,1)}, bf16[128,1536]{1,0:T(8,128)(2,1)}, bf...) custom-call(s32[1]{0:T(128)} %bitcast.1.ctx_ref, bf16[128,1536]{1,0:T(8,128)(2,1)} %copy-done.108, ...), custom_call_target="tpu_custom_call" | custom-call | flops 2617245696 | bytes 7864320 | tf_op jit(solution)/shard_map/pallas_call | solution.py:1089
  667.2 4.1 select_convert_fusion
  676.6 4.2 shard_map.195
  685.3 3.9 collective-permute-start.112
  690.1 3.9 add_convert_fusion.1
  695.3 5.3 collective-permute-done.114
  703.1 10.6 %collective-permute-done.110 = bf16[192,1152]{1,0:T(8,128)(2,1)S(1)} collective-permute-done((bf16[192,1152]{1,0:T(8,128)(2,1)S(1)}, bf16[192,1152]{1,0:T(8,128)(2,1)S(1)}, u32[]{:S(2)}, u32[]{:S(2)}) %collective-permute-start.110) | collective-permute-done | bytes 442400 | tf_op jit(solution)/shard_map/ppermute | solution.py:1336
  726.5 10.5 %collective-permute-done.116 = bf16[192,1152]{1,0:T(8,128)(2,1)S(1)} collective-permute-done((bf16[192,1152]{1,0:T(8,128)(2,1)S(1)}, bf16[192,1152]{1,0:T(8,128)(2,1)S(1)}, u32[]{:S(2)}, u32[]{:S(2)}) %collective-permute-start.116) | collective-permute-done | bytes 442400 | tf_op jit(solution)/shard_map/ppermute | solution.py:1336
  741.8 3.9 shard_map.196
  745.7 4.2 collective-permute-start.121
  751.1 4.6 collective-permute-done.121
  760.1 4.0 shard_map.198
  (733 shorter events, 275.4 us)
Async XLA Ops:
  7.2 294.2 %all-gather.2.cloned.1.call-start = ((), (), s32[]{:S(2)}) async-start(), calls=%async_computation.1 | async-start | bytes 11796480 | tf_op jit(solution)/shard_map/all_gather | solution.py:1570
  23.1 25.3 %collective-permute-start.5 = (bf16[192,2176]{1,0:T(8,128)(2,1)}, bf16[192,2176]{1,0:T(8,128)(2,1)S(1)}, u32[]{:S(2)}, u32[]{:S(2)}) collective-permute-start(bf16[192,2176]{1,0:T(8,128)(2,1)} %shard_map.170.ids_0), channel_id=1, source_target_pairs={{0,1},{1,0},{2,3},{3,2},{4,5},{5,4},{6,7},{7,6},{8,9},{9,8},{10,11... | collective-permute-start | bytes 2506760 | tf_op jit(solution)/shard_map/ppermute | solution.py:1336
  24.6 23.8 %collective-permute-start.6 = (bf16[192,2176]{1,0:T(8,128)(2,1)}, bf16[192,2176]{1,0:T(8,128)(2,1)}, u32[]{:S(2)}, u32[]{:S(2)}) collective-permute-start(bf16[192,2176]{1,0:T(8,128)(2,1)} %shard_map.170.ids_0), channel_id=1, source_target_pairs={{0,2},{1,3},{2,4},{3,5},{4,6},{5,7},{6,0},{7,1},{8,10},{9,11},{10,... | collective-permute-start | bytes 2506760 | tf_op jit(solution)/shard_map/ppermute | solution.py:1336
  27.7 19.2 %collective-permute-start.3 = (bf16[384,1024]{1,0:T(8,128)(2,1)S(1)}, bf16[384,1024]{1,0:T(8,128)(2,1)S(1)}, u32[]{:S(2)}, u32[]{:S(2)}) collective-permute-start(bf16[384,1024]{1,0:T(8,128)(2,1)S(1)} %get-tuple-element.267.refs_0_), channel_id=1, source_target_pairs={{0,16},{8,24},{16,0},{24,8},{1,17},{9,25},{17,1},{25,9},{2,18},{10... | collective-permute-start | bytes 2359304 | tf_op jit(solution)/shard_map/ppermute | solution.py:1336
  46.9 18.4 %collective-permute-start.4 = (bf16[384,1024]{1,0:T(8,128)(2,1)S(1)}, bf16[384,1024]{1,0:T(8,128)(2,1)}, u32[]{:S(2)}, u32[]{:S(2)}) collective-permute-start(bf16[384,1024]{1,0:T(8,128)(2,1)S(1)} %get-tuple-element.268.refs_4_), channel_id=1, source_target_pairs={{0,16},{8,24},{16,0},{24,8},{1,17},{9,25},{17,1},{25,9},{2,18},{10... | collective-permute-start | bytes 2359304 | tf_op jit(solution)/shard_map/ppermute | solution.py:1336
  48.4 21.2 %collective-permute-start.8 = (bf16[192,2176]{1,0:T(8,128)(2,1)}, bf16[192,2176]{1,0:T(8,128)(2,1)}, u32[]{:S(2)}, u32[]{:S(2)}) collective-permute-start(bf16[192,2176]{1,0:T(8,128)(2,1)} %collective-permute-done.6.ids_0), channel_id=1, source_target_pairs={{0,2},{1,3},{2,4},{3,5},{4,6},{5,7},{6,0},{7,1},{8,10},{9,11},{10,... | collective-permute-start | bytes 2506760 | tf_op jit(solution)/shard_map/ppermute | solution.py:1336
  50.0 19.0 %collective-permute-start.7 = (bf16[192,2176]{1,0:T(8,128)(2,1)}, bf16[192,2176]{1,0:T(8,128)(2,1)}, u32[]{:S(2)}, u32[]{:S(2)}) collective-permute-start(bf16[192,2176]{1,0:T(8,128)(2,1)} %collective-permute-done.6.ids_0), channel_id=1, source_target_pairs={{0,1},{1,0},{2,3},{3,2},{4,5},{5,4},{6,7},{7,6},{8,9},{9,8},{10,11... | collective-permute-start | bytes 2506760 | tf_op jit(solution)/shard_map/ppermute | solution.py:1336
  69.6 18.4 %collective-permute-start.9 = (bf16[192,2176]{1,0:T(8,128)(2,1)}, bf16[192,2176]{1,0:T(8,128)(2,1)S(1)}, u32[]{:S(2)}, u32[]{:S(2)}) collective-permute-start(bf16[192,2176]{1,0:T(8,128)(2,1)} %collective-permute-done.8.ids_0), channel_id=1, source_target_pairs={{0,1},{1,0},{2,3},{3,2},{4,5},{5,4},{6,7},{7,6},{8,9},{9,8},{10,11... | collective-permute-start | bytes 2506760 | tf_op jit(solution)/shard_map/ppermute | solution.py:1336
  70.1 18.1 %collective-permute-start.10 = (bf16[192,2176]{1,0:T(8,128)(2,1)}, bf16[192,2176]{1,0:T(8,128)(2,1)S(1)}, u32[]{:S(2)}, u32[]{:S(2)}) collective-permute-start(bf16[192,2176]{1,0:T(8,128)(2,1)} %shard_map.170.ids_0), channel_id=1, source_target_pairs={{0,6},{1,7},{2,0},{3,1},{4,2},{5,3},{6,4},{7,5},{8,14},{9,15},{10,... | collective-permute-start | bytes 2506760 | tf_op jit(solution)/shard_map/ppermute | solution.py:1336
  75.8 22.8 %collective-permute-start.15 = (bf16[2,128,1536]{2,1,0:T(8,128)(2,1)S(1)}, bf16[2,128,1536]{2,1,0:T(8,128)(2,1)S(1)}, u32[]{:S(2)}, u32[]{:S(2)}) collective-permute-start(bf16[2,128,1536]{2,1,0:T(8,128)(2,1)S(1)} %get-tuple-element.276.refs_8_), channel_id=1, source_target_pairs={{0,16},{8,24},{16,0},{24,8},{1,17},{9,25},{17,1},{25,9},{2,18},{10... | collective-permute-start | bytes 2359304 | tf_op jit(solution)/shard_map/ppermute | solution.py:1336
  84.5 14.9 %collective-permute-start.14 = (bf16[128,1536]{1,0:T(8,128)(2,1)S(1)}, bf16[128,1536]{1,0:T(8,128)(2,1)S(1)}, u32[]{:S(2)}, u32[]{:S(2)}) collective-permute-start(bf16[128,1536]{1,0:T(8,128)(2,1)S(1)} %collective-permute-done.13), channel_id=1, source_target_pairs={{0,8},{8,0},{16,24},{24,16},{1,9},{9,1},{17,25},{25,17},{2,10},{10... | collective-permute-start | bytes 1179656 | tf_op jit(solution)/shard_map/ppermute | solution.py:1336
  88.2 18.1 %collective-permute-start.11 = (bf16[192,2176]{1,0:T(8,128)(2,1)S(1)}, bf16[192,2176]{1,0:T(8,128)(2,1)S(1)}, u32[]{:S(2)}, u32[]{:S(2)}) collective-permute-start(bf16[192,2176]{1,0:T(8,128)(2,1)S(1)} %collective-permute-done.10.ids_0), channel_id=1, source_target_pairs={{0,1},{1,0},{2,3},{3,2},{4,5},{5,4},{6,7},{7,6},{8,9},{9,8},{10,11... | collective-permute-start | bytes 2506760 | tf_op jit(solution)/shard_map/ppermute | solution.py:1336
  131.4 14.2 %collective-permute-start.16 = (bf16[128,1536]{1,0:T(8,128)(2,1)}, bf16[128,1536]{1,0:T(8,128)(2,1)S(1)}, u32[]{:S(2)}, u32[]{:S(2)}) collective-permute-start(bf16[128,1536]{1,0:T(8,128)(2,1)} %get-tuple-element.281), channel_id=1, source_target_pairs={{0,8},{8,0},{16,24},{24,16},{1,9},{9,1},{17,25},{25,17},{2,10},{10... | collective-permute-start | bytes 1179656 | tf_op jit(solution)/shard_map/ppermute | solution.py:1336
  148.8 593.1 %reduce-scatter.2.cloned.1.call-start = ((), (), s32[]{:S(2)}) async-start(), calls=%async_computation.2 | async-start | bytes 3932160 | tf_op jit(solution)/shard_map/reduce_scatter | solution.py:1712
  149.5 20.2 %collective-permute-start.25 = (bf16[2,128,1536]{2,1,0:T(8,128)(2,1)S(1)}, bf16[2,128,1536]{2,1,0:T(8,128)(2,1)}, u32[]{:S(2)}, u32[]{:S(2)}) collective-permute-start(bf16[2,128,1536]{2,1,0:T(8,128)(2,1)S(1)} %get-tuple-element.276.refs_8_), channel_id=1, source_target_pairs={{0,8},{8,0},{16,24},{24,16},{1,9},{9,1},{17,25},{25,17},{2,10},{10... | collective-permute-start | bytes 2359304 | tf_op jit(solution)/shard_map/ppermute | solution.py:1336
  149.9 18.3 %collective-permute-start.24 = (bf16[384,1024]{1,0:T(8,128)(2,1)}, bf16[384,1024]{1,0:T(8,128)(2,1)}, u32[]{:S(2)}, u32[]{:S(2)}) collective-permute-start(bf16[384,1024]{1,0:T(8,128)(2,1)} %collective-permute-done.4.refs_6_), channel_id=1, source_target_pairs={{0,8},{8,0},{16,24},{24,16},{1,9},{9,1},{17,25},{25,17},{2,10},{10... | collective-permute-start | bytes 2359304 | tf_op jit(solution)/shard_map/ppermute | solution.py:1336
  152.1 17.7 %collective-permute-start.26 = (bf16[2,128,1536]{2,1,0:T(8,128)(2,1)}, bf16[2,128,1536]{2,1,0:T(8,128)(2,1)S(1)}, u32[]{:S(2)}, u32[]{:S(2)}) collective-permute-start(bf16[2,128,1536]{2,1,0:T(8,128)(2,1)} %copy-done.4), channel_id=1, source_target_pairs={{0,8},{8,0},{16,24},{24,16},{1,9},{9,1},{17,25},{25,17},{2,10},{10... | collective-permute-start | bytes 2359304 | tf_op jit(solution)/shard_map/ppermute | solution.py:1336
  154.6 13.0 %collective-permute-start.19 = (bf16[128,1536]{1,0:T(8,128)(2,1)S(1)}, bf16[128,1536]{1,0:T(8,128)(2,1)S(1)}, u32[]{:S(2)}, u32[]{:S(2)}) collective-permute-start(bf16[128,1536]{1,0:T(8,128)(2,1)S(1)} %multiply_convert_fusion.2.rows_0), channel_id=1, source_target_pairs={{0,2},{1,3},{2,4},{3,5},{4,6},{5,7},{6,0},{7,1},{8,10},{9,11},{10,... | collective-permute-start | bytes 1179656 | tf_op jit(solution)/shard_map/ppermute | solution.py:1336
  168.2 15.4 %collective-permute-start.28 = (bf16[128,1536]{1,0:T(8,128)(2,1)S(1)}, bf16[128,1536]{1,0:T(8,128)(2,1)S(1)}, u32[]{:S(2)}, u32[]{:S(2)}) collective-permute-start(bf16[128,1536]{1,0:T(8,128)(2,1)S(1)} %collective-permute-done.19.rows_0), channel_id=1, source_target_pairs={{0,1},{1,0},{2,3},{3,2},{4,5},{5,4},{6,7},{7,6},{8,9},{9,8},{10,11... | collective-permute-start | bytes 1179656 | tf_op jit(solution)/shard_map/ppermute | solution.py:1336
  179.6 12.6 %collective-permute-start.29 = (bf16[128,1536]{1,0:T(8,128)(2,1)}, bf16[128,1536]{1,0:T(8,128)(2,1)S(1)}, u32[]{:S(2)}, u32[]{:S(2)}) collective-permute-start(bf16[128,1536]{1,0:T(8,128)(2,1)} %copy-done.52), channel_id=1, source_target_pairs={{0,6},{1,7},{2,0},{3,1},{4,2},{5,3},{6,4},{7,5},{8,14},{9,15},{10,... | collective-permute-start | bytes 1179656 | tf_op jit(solution)/shard_map/ppermute | solution.py:1336
  225.0 15.9 %collective-permute-start.37 = (bf16[128,1536]{1,0:T(8,128)(2,1)S(1)}, bf16[128,1536]{1,0:T(8,128)(2,1)S(1)}, u32[]{:S(2)}, u32[]{:S(2)}) collective-permute-start(bf16[128,1536]{1,0:T(8,128)(2,1)S(1)} %add_convert_fusion.19), channel_id=1, source_target_pairs={{0,2},{1,3},{2,4},{3,5},{4,6},{5,7},{6,0},{7,1},{8,10},{9,11},{10,... | collective-permute-start | bytes 1179656 | tf_op jit(solution)/shard_map/ppermute | solution.py:1336
  287.1 12.2 %collective-permute-start.45 = (bf16[128,1536]{1,0:T(8,128)(2,1)S(1)}, bf16[128,1536]{1,0:T(8,128)(2,1)S(1)}, u32[]{:S(2)}, u32[]{:S(2)}) collective-permute-start(bf16[128,1536]{1,0:T(8,128)(2,1)S(1)} %multiply_convert_fusion.rows_0), channel_id=1, source_target_pairs={{0,2},{1,3},{2,4},{3,5},{4,6},{5,7},{6,0},{7,1},{8,10},{9,11},{10,... | collective-permute-start | bytes 1179656 | tf_op jit(solution)/shard_map/ppermute | solution.py:1336
  287.2 14.2 %collective-permute-start.46 = (bf16[128,1536]{1,0:T(8,128)(2,1)S(1)}, bf16[128,1536]{1,0:T(8,128)(2,1)S(1)}, u32[]{:S(2)}, u32[]{:S(2)}) collective-permute-start(bf16[128,1536]{1,0:T(8,128)(2,1)S(1)} %multiply_convert_fusion.rows_0), channel_id=1, source_target_pairs={{0,1},{1,0},{2,3},{3,2},{4,5},{5,4},{6,7},{7,6},{8,9},{9,8},{10,11... | collective-permute-start | bytes 1179656 | tf_op jit(solution)/shard_map/ppermute | solution.py:1336
  300.1 14.9 %collective-permute-start.48 = (bf16[128,1536]{1,0:T(8,128)(2,1)S(1)}, bf16[128,1536]{1,0:T(8,128)(2,1)S(1)}, u32[]{:S(2)}, u32[]{:S(2)}) collective-permute-start(bf16[128,1536]{1,0:T(8,128)(2,1)S(1)} %collective-permute-done.45.rows_0), channel_id=1, source_target_pairs={{0,1},{1,0},{2,3},{3,2},{4,5},{5,4},{6,7},{7,6},{8,9},{9,8},{10,11... | collective-permute-start | bytes 1179656 | tf_op jit(solution)/shard_map/ppermute | solution.py:1336
  310.7 12.9 %collective-permute-start.49 = (bf16[128,1536]{1,0:T(8,128)(2,1)}, bf16[128,1536]{1,0:T(8,128)(2,1)S(1)}, u32[]{:S(2)}, u32[]{:S(2)}) collective-permute-start(bf16[128,1536]{1,0:T(8,128)(2,1)} %copy-done.53), channel_id=1, source_target_pairs={{0,6},{1,7},{2,0},{3,1},{4,2},{5,3},{6,4},{7,5},{8,14},{9,15},{10,... | collective-permute-start | bytes 1179656 | tf_op jit(solution)/shard_map/ppermute | solution.py:1336
  355.5 12.5 %collective-permute-start.57 = (bf16[128,1536]{1,0:T(8,128)(2,1)S(1)}, bf16[128,1536]{1,0:T(8,128)(2,1)S(1)}, u32[]{:S(2)}, u32[]{:S(2)}) collective-permute-start(bf16[128,1536]{1,0:T(8,128)(2,1)S(1)} %add_convert_fusion.15), channel_id=1, source_target_pairs={{0,2},{1,3},{2,4},{3,5},{4,6},{5,7},{6,0},{7,1},{8,10},{9,11},{10,... | collective-permute-start | bytes 1179656 | tf_op jit(solution)/shard_map/ppermute | solution.py:1336
  376.1 13.0 %collective-permute-start.59 = (bf16[128,1664]{1,0:T(8,128)(2,1)S(1)}, bf16[128,1664]{1,0:T(8,128)(2,1)S(1)}, u32[]{:S(2)}, u32[]{:S(2)}) collective-permute-start(bf16[128,1664]{1,0:T(8,128)(2,1)S(1)} %pad_maximum_fusion.grads_0), channel_id=1, source_target_pairs={{0,2},{1,3},{2,4},{3,5},{4,6},{5,7},{6,0},{7,1},{8,10},{9,11},{10,... | collective-permute-start | bytes 1277960 | tf_op jit(solution)/shard_map/ppermute | solution.py:1336
  376.1 17.3 %collective-permute-start.60 = (bf16[128,1664]{1,0:T(8,128)(2,1)S(1)}, bf16[128,1664]{1,0:T(8,128)(2,1)S(1)}, u32[]{:S(2)}, u32[]{:S(2)}) collective-permute-start(bf16[128,1664]{1,0:T(8,128)(2,1)S(1)} %pad_maximum_fusion.grads_0), channel_id=1, source_target_pairs={{0,1},{1,0},{2,3},{3,2},{4,5},{5,4},{6,7},{7,6},{8,9},{9,8},{10,11... | collective-permute-start | bytes 1277960 | tf_op jit(solution)/shard_map/ppermute | solution.py:1336
  389.1 13.6 %collective-permute-start.61 = (bf16[128,1664]{1,0:T(8,128)(2,1)S(1)}, bf16[128,1664]{1,0:T(8,128)(2,1)S(1)}, u32[]{:S(2)}, u32[]{:S(2)}) collective-permute-start(bf16[128,1664]{1,0:T(8,128)(2,1)S(1)} %collective-permute-done.59.grads_0), channel_id=1, source_target_pairs={{0,2},{1,3},{2,4},{3,5},{4,6},{5,7},{6,0},{7,1},{8,10},{9,11},{10,... | collective-permute-start | bytes 1277960 | tf_op jit(solution)/shard_map/ppermute | solution.py:1336
  389.2 17.2 %collective-permute-start.62 = (bf16[128,1664]{1,0:T(8,128)(2,1)S(1)}, bf16[128,1664]{1,0:T(8,128)(2,1)S(1)}, u32[]{:S(2)}, u32[]{:S(2)}) collective-permute-start(bf16[128,1664]{1,0:T(8,128)(2,1)S(1)} %collective-permute-done.59.grads_0), channel_id=1, source_target_pairs={{0,1},{1,0},{2,3},{3,2},{4,5},{5,4},{6,7},{7,6},{8,9},{9,8},{10,11... | collective-permute-start | bytes 1277960 | tf_op jit(solution)/shard_map/ppermute | solution.py:1336
  402.6 13.0 %collective-permute-start.63 = (bf16[128,1664]{1,0:T(8,128)(2,1)}, bf16[128,1664]{1,0:T(8,128)(2,1)S(1)}, u32[]{:S(2)}, u32[]{:S(2)}) collective-permute-start(bf16[128,1664]{1,0:T(8,128)(2,1)} %copy-done.51), channel_id=1, source_target_pairs={{0,6},{1,7},{2,0},{3,1},{4,2},{5,3},{6,4},{7,5},{8,14},{9,15},{10,... | collective-permute-start | bytes 1277960 | tf_op jit(solution)/shard_map/ppermute | solution.py:1336
  448.4 18.0 %collective-permute-start.71 = (bf16[128,1536]{1,0:T(8,128)(2,1)S(1)}, bf16[128,1536]{1,0:T(8,128)(2,1)S(1)}, u32[]{:S(2)}, u32[]{:S(2)}) collective-permute-start(bf16[128,1536]{1,0:T(8,128)(2,1)S(1)} %add_convert_fusion.11), channel_id=1, source_target_pairs={{0,2},{1,3},{2,4},{3,5},{4,6},{5,7},{6,0},{7,1},{8,10},{9,11},{10,... | collective-permute-start | bytes 1179656 | tf_op jit(solution)/shard_map/ppermute | solution.py:1336
  451.5 15.0 %collective-permute-start.72 = (bf16[768,1024]{1,0:T(8,128)(2,1)S(1)}, bf16[768,1024]{1,0:T(8,128)(2,1)S(1)}, u32[]{:S(2)}, u32[]{:S(2)}) collective-permute-start(bf16[768,1024]{1,0:T(8,128)(2,1)S(1)} %convolution_convert_fusion.9), channel_id=1, source_target_pairs={{0,8},{8,0},{16,24},{24,16},{1,9},{9,1},{17,25},{25,17},{2,10},{10... | collective-permute-start | bytes 4718600 | tf_op jit(solution)/shard_map/ppermute | solution.py:1336
  453.4 13.1 %collective-permute-start.73 = (bf16[768,1024]{1,0:T(8,128)(2,1)S(1)}, bf16[768,1024]{1,0:T(8,128)(2,1)S(1)}, u32[]{:S(2)}, u32[]{:S(2)}) collective-permute-start(bf16[768,1024]{1,0:T(8,128)(2,1)S(1)} %convolution_convert_fusion.8), channel_id=1, source_target_pairs={{0,8},{8,0},{16,24},{24,16},{1,9},{9,1},{17,25},{25,17},{2,10},{10... | collective-permute-start | bytes 4718600 | tf_op jit(solution)/shard_map/ppermute | solution.py:1336
  477.6 13.3 %collective-permute-start.75 = (bf16[128,1536]{1,0:T(8,128)(2,1)S(1)}, bf16[128,1536]{1,0:T(8,128)(2,1)}, u32[]{:S(2)}, u32[]{:S(2)}) collective-permute-start(bf16[128,1536]{1,0:T(8,128)(2,1)S(1)} %get-tuple-element.533.grad_0), channel_id=1, source_target_pairs={{0,8},{8,0},{16,24},{24,16},{1,9},{9,1},{17,25},{25,17},{2,10},{10... | collective-permute-start | bytes 1179656 | tf_op jit(solution)/shard_map/ppermute | solution.py:1336
  505.3 15.6 %collective-permute-start.78 = (bf16[128,1536]{1,0:T(8,128)(2,1)}, bf16[128,1536]{1,0:T(8,128)(2,1)}, u32[]{:S(2)}, u32[]{:S(2)}) collective-permute-start(bf16[128,1536]{1,0:T(8,128)(2,1)} %get-tuple-element.401), channel_id=1, source_target_pairs={{0,8},{8,0},{16,24},{24,16},{1,9},{9,1},{17,25},{25,17},{2,10},{10... | collective-permute-start | bytes 1179656 | tf_op jit(solution)/shard_map/ppermute | solution.py:1336
  525.1 14.1 %collective-permute-start.81 = (bf16[128,1664]{1,0:T(8,128)(2,1)S(1)}, bf16[128,1664]{1,0:T(8,128)(2,1)}, u32[]{:S(2)}, u32[]{:S(2)}) collective-permute-start(bf16[128,1664]{1,0:T(8,128)(2,1)S(1)} %pad_maximum_fusion.1.grads_0), channel_id=1, source_target_pairs={{0,2},{1,3},{2,4},{3,5},{4,6},{5,7},{6,0},{7,1},{8,10},{9,11},{10,... | collective-permute-start | bytes 1277960 | tf_op jit(solution)/shard_map/ppermute | solution.py:1336
  525.2 16.2 %collective-permute-start.82 = (bf16[128,1664]{1,0:T(8,128)(2,1)S(1)}, bf16[128,1664]{1,0:T(8,128)(2,1)S(1)}, u32[]{:S(2)}, u32[]{:S(2)}) collective-permute-start(bf16[128,1664]{1,0:T(8,128)(2,1)S(1)} %pad_maximum_fusion.1.grads_0), channel_id=1, source_target_pairs={{0,1},{1,0},{2,3},{3,2},{4,5},{5,4},{6,7},{7,6},{8,9},{9,8},{10,11... | collective-permute-start | bytes 1277960 | tf_op jit(solution)/shard_map/ppermute | solution.py:1336
  539.2 12.8 %collective-permute-start.83 = (bf16[128,1664]{1,0:T(8,128)(2,1)}, bf16[128,1664]{1,0:T(8,128)(2,1)S(1)}, u32[]{:S(2)}, u32[]{:S(2)}) collective-permute-start(bf16[128,1664]{1,0:T(8,128)(2,1)} %collective-permute-done.81.grads_0), channel_id=1, source_target_pairs={{0,2},{1,3},{2,4},{3,5},{4,6},{5,7},{6,0},{7,1},{8,10},{9,11},{10,... | collective-permute-start | bytes 1277960 | tf_op jit(solution)/shard_map/ppermute | solution.py:1336
  540.5 17.3 %collective-permute-start.84 = (bf16[128,1664]{1,0:T(8,128)(2,1)}, bf16[128,1664]{1,0:T(8,128)(2,1)S(1)}, u32[]{:S(2)}, u32[]{:S(2)}) collective-permute-start(bf16[128,1664]{1,0:T(8,128)(2,1)} %collective-permute-done.81.grads_0), channel_id=1, source_target_pairs={{0,1},{1,0},{2,3},{3,2},{4,5},{5,4},{6,7},{7,6},{8,9},{9,8},{10,11... | collective-permute-start | bytes 1277960 | tf_op jit(solution)/shard_map/ppermute | solution.py:1336
  552.1 15.1 %collective-permute-start.85 = (bf16[128,1664]{1,0:T(8,128)(2,1)S(1)}, bf16[128,1664]{1,0:T(8,128)(2,1)S(1)}, u32[]{:S(2)}, u32[]{:S(2)}) collective-permute-start(bf16[128,1664]{1,0:T(8,128)(2,1)S(1)} %copy-done.50), channel_id=1, source_target_pairs={{0,6},{1,7},{2,0},{3,1},{4,2},{5,3},{6,4},{7,5},{8,14},{9,15},{10,... | collective-permute-start | bytes 1277960 | tf_op jit(solution)/shard_map/ppermute | solution.py:1336
  554.9 23.8 %collective-permute-start.86 = (bf16[384,1024]{1,0:T(8,128)(2,1)S(1)}, bf16[384,1024]{1,0:T(8,128)(2,1)S(1)}, u32[]{:S(2)}, u32[]{:S(2)}) collective-permute-start(bf16[384,1024]{1,0:T(8,128)(2,1)S(1)} %get-tuple-element.551), channel_id=1, source_target_pairs={{0,16},{8,24},{16,0},{24,8},{1,17},{9,25},{17,1},{25,9},{2,18},{10... | collective-permute-start | bytes 2359304 | tf_op jit(solution)/shard_map/ppermute | solution.py:1336
  589.8 19.3 %collective-permute-start.98 = (bf16[384,1024]{1,0:T(8,128)(2,1)}, bf16[384,1024]{1,0:T(8,128)(2,1)S(1)}, u32[]{:S(2)}, u32[]{:S(2)}) collective-permute-start(bf16[384,1024]{1,0:T(8,128)(2,1)} %get-tuple-element.549), channel_id=1, source_target_pairs={{0,16},{8,24},{16,0},{24,8},{1,17},{9,25},{17,1},{25,9},{2,18},{10... | collective-permute-start | bytes 2359304 | tf_op jit(solution)/shard_map/ppermute | solution.py:1336
  603.7 18.7 %collective-permute-start.95 = (bf16[768,1024]{1,0:T(8,128)(2,1)S(1)}, bf16[768,1024]{1,0:T(8,128)(2,1)S(1)}, u32[]{:S(2)}, u32[]{:S(2)}) collective-permute-start(bf16[768,1024]{1,0:T(8,128)(2,1)S(1)} %convolution_convert_fusion.7), channel_id=1, source_target_pairs={{0,8},{8,0},{16,24},{24,16},{1,9},{9,1},{17,25},{25,17},{2,10},{10... | collective-permute-start | bytes 4718600 | tf_op jit(solution)/shard_map/ppermute | solution.py:1336
  606.2 16.2 %collective-permute-start.96 = (bf16[768,1024]{1,0:T(8,128)(2,1)S(1)}, bf16[768,1024]{1,0:T(8,128)(2,1)S(1)}, u32[]{:S(2)}, u32[]{:S(2)}) collective-permute-start(bf16[768,1024]{1,0:T(8,128)(2,1)S(1)} %convolution_convert_fusion.6), channel_id=1, source_target_pairs={{0,8},{8,0},{16,24},{24,16},{1,9},{9,1},{17,25},{25,17},{2,10},{10... | collective-permute-start | bytes 4718600 | tf_op jit(solution)/shard_map/ppermute | solution.py:1336
  608.8 13.6 %collective-permute-start.97 = (bf16[512,1536]{1,0:T(8,128)(2,1)S(1)}, bf16[512,1536]{1,0:T(8,128)(2,1)S(1)}, u32[]{:S(2)}, u32[]{:S(2)}) collective-permute-start(bf16[512,1536]{1,0:T(8,128)(2,1)S(1)} %convolution_convert_fusion.3), channel_id=1, source_target_pairs={{0,8},{8,0},{16,24},{24,16},{1,9},{9,1},{17,25},{25,17},{2,10},{10... | collective-permute-start | bytes 4718600 | tf_op jit(solution)/shard_map/ppermute | solution.py:1336
  608.9 13.3 %collective-permute-start.94 = (bf16[128,1536]{1,0:T(8,128)(2,1)S(1)}, bf16[128,1536]{1,0:T(8,128)(2,1)S(1)}, u32[]{:S(2)}, u32[]{:S(2)}) collective-permute-start(bf16[128,1536]{1,0:T(8,128)(2,1)S(1)} %add_convert_fusion.7), channel_id=1, source_target_pairs={{0,2},{1,3},{2,4},{3,5},{4,6},{5,7},{6,0},{7,1},{8,10},{9,11},{10,... | collective-permute-start | bytes 1179656 | tf_op jit(solution)/shard_map/ppermute | solution.py:1336
  609.1 13.1 %collective-permute-start.93 = (bf16[128,1536]{1,0:T(8,128)(2,1)S(1)}, bf16[128,1536]{1,0:T(8,128)(2,1)S(1)}, u32[]{:S(2)}, u32[]{:S(2)}) collective-permute-start(bf16[128,1536]{1,0:T(8,128)(2,1)S(1)} %copy-done.160), channel_id=1, source_target_pairs={{0,1},{1,0},{2,3},{3,2},{4,5},{5,4},{6,7},{7,6},{8,9},{9,8},{10,11... | collective-permute-start | bytes 1179656 | tf_op jit(solution)/shard_map/ppermute | solution.py:1336
  633.2 13.5 %collective-permute-start.107 = (bf16[192,1152]{1,0:T(8,128)(2,1)}, bf16[192,1152]{1,0:T(8,128)(2,1)}, u32[]{:S(2)}, u32[]{:S(2)}) collective-permute-start(bf16[192,1152]{1,0:T(8,128)(2,1)} %bitcast.46), channel_id=1, source_target_pairs={{0,1},{1,0},{2,3},{3,2},{4,5},{5,4},{6,7},{7,6},{8,9},{9,8},{10,11... | collective-permute-start | bytes 1327112 | tf_op jit(solution)/shard_map/ppermute | solution.py:1336
  636.3 12.5 %collective-permute-start.100 = (bf16[128,1536]{1,0:T(8,128)(2,1)S(1)}, bf16[128,1536]{1,0:T(8,128)(2,1)}, u32[]{:S(2)}, u32[]{:S(2)}) collective-permute-start(bf16[128,1536]{1,0:T(8,128)(2,1)S(1)} %get-tuple-element.526.grad_0), channel_id=1, source_target_pairs={{0,8},{8,0},{16,24},{24,16},{1,9},{9,1},{17,25},{25,17},{2,10},{10... | collective-permute-start | bytes 1179656 | tf_op jit(solution)/shard_map/ppermute | solution.py:1336
  636.4 34.9 %collective-permute-start.106 = (bf16[192,1152]{1,0:T(8,128)(2,1)}, bf16[192,1152]{1,0:T(8,128)(2,1)}, u32[]{:S(2)}, u32[]{:S(2)}) collective-permute-start(bf16[192,1152]{1,0:T(8,128)(2,1)} %bitcast.194), channel_id=1, source_target_pairs={{0,1},{1,0},{2,3},{3,2},{4,5},{5,4},{6,7},{7,6},{8,9},{9,8},{10,11... | collective-permute-start | bytes 1327112 | tf_op jit(solution)/shard_map/ppermute | solution.py:1336
  648.7 22.6 %collective-permute-start.108 = (bf16[192,1152]{1,0:T(8,128)(2,1)}, bf16[192,1152]{1,0:T(8,128)(2,1)}, u32[]{:S(2)}, u32[]{:S(2)}) collective-permute-start(bf16[192,1152]{1,0:T(8,128)(2,1)} %fusion.16), channel_id=1, source_target_pairs={{0,2},{1,3},{2,4},{3,5},{4,6},{5,7},{6,0},{7,1},{8,10},{9,11},{10,... | collective-permute-start | bytes 1327112 | tf_op jit(solution)/shard_map/ppermute | solution.py:1336
  663.2 17.7 %collective-permute-start.104 = (bf16[128,1536]{1,0:T(8,128)(2,1)}, bf16[128,1536]{1,0:T(8,128)(2,1)}, u32[]{:S(2)}, u32[]{:S(2)}) collective-permute-start(bf16[128,1536]{1,0:T(8,128)(2,1)} %get-tuple-element.472), channel_id=1, source_target_pairs={{0,8},{8,0},{16,24},{24,16},{1,9},{9,1},{17,25},{25,17},{2,10},{10... | collective-permute-start | bytes 1179656 | tf_op jit(solution)/shard_map/ppermute | solution.py:1336
  663.3 58.7 %collective-permute-start.103 = (bf16[128,1536]{1,0:T(8,128)(2,1)}, bf16[128,1536]{1,0:T(8,128)(2,1)}, u32[]{:S(2)}, u32[]{:S(2)}) collective-permute-start(bf16[128,1536]{1,0:T(8,128)(2,1)} %get-tuple-element.470), channel_id=1, source_target_pairs={{0,8},{8,0},{16,24},{24,16},{1,9},{9,1},{17,25},{25,17},{2,10},{10... | collective-permute-start | bytes 1179656 | tf_op jit(solution)/shard_map/ppermute | solution.py:1336
  672.6 29.0 %collective-permute-start.111 = (bf16[192,1152]{1,0:T(8,128)(2,1)S(1)}, bf16[192,1152]{1,0:T(8,128)(2,1)}, u32[]{:S(2)}, u32[]{:S(2)}) collective-permute-start(bf16[192,1152]{1,0:T(8,128)(2,1)S(1)} %fusion.18), channel_id=1, source_target_pairs={{0,2},{1,3},{2,4},{3,5},{4,6},{5,7},{6,0},{7,1},{8,10},{9,11},{10,... | collective-permute-start | bytes 1327112 | tf_op jit(solution)/shard_map/ppermute | solution.py:1336
  682.1 32.9 %collective-permute-start.105 = (bf16[128,1536]{1,0:T(8,128)(2,1)S(1)}, bf16[128,1536]{1,0:T(8,128)(2,1)S(1)}, u32[]{:S(2)}, u32[]{:S(2)}) collective-permute-start(bf16[128,1536]{1,0:T(8,128)(2,1)S(1)} %add_convert_fusion.5), channel_id=1, source_target_pairs={{0,16},{8,24},{16,0},{24,8},{1,17},{9,25},{17,1},{25,9},{2,18},{10... | collective-permute-start | bytes 1179656 | tf_op jit(solution)/shard_map/ppermute | solution.py:1336
  685.3 17.6 %collective-permute-start.112 = (bf16[192,1152]{1,0:T(8,128)(2,1)S(1)}, bf16[192,1152]{1,0:T(8,128)(2,1)S(1)}, u32[]{:S(2)}, u32[]{:S(2)}) collective-permute-start(bf16[192,1152]{1,0:T(8,128)(2,1)S(1)} %fusion.19), channel_id=1, source_target_pairs={{0,6},{1,7},{2,0},{3,1},{4,2},{5,3},{6,4},{7,5},{8,14},{9,15},{10,... | collective-permute-start | bytes 1327112 | tf_op jit(solution)/shard_map/ppermute | solution.py:1336
  700.6 13.1 %collective-permute-start.110 = (bf16[192,1152]{1,0:T(8,128)(2,1)S(1)}, bf16[192,1152]{1,0:T(8,128)(2,1)S(1)}, u32[]{:S(2)}, u32[]{:S(2)}) collective-permute-start(bf16[192,1152]{1,0:T(8,128)(2,1)S(1)} %bitcast.192), channel_id=1, source_target_pairs={{0,1},{1,0},{2,3},{3,2},{4,5},{5,4},{6,7},{7,6},{8,9},{9,8},{10,11... | collective-permute-start | bytes 1327112 | tf_op jit(solution)/shard_map/ppermute | solution.py:1336
  701.6 23.0 %collective-permute-start.113 = (bf16[192,1152]{1,0:T(8,128)(2,1)S(1)}, bf16[192,1152]{1,0:T(8,128)(2,1)S(1)}, u32[]{:S(2)}, u32[]{:S(2)}) collective-permute-start(bf16[192,1152]{1,0:T(8,128)(2,1)S(1)} %bitcast.196), channel_id=1, source_target_pairs={{0,1},{1,0},{2,3},{3,2},{4,5},{5,4},{6,7},{7,6},{8,9},{9,8},{10,11... | collective-permute-start | bytes 1327112 | tf_op jit(solution)/shard_map/ppermute | solution.py:1336
  702.8 48.2 %collective-permute-start.119 = (bf16[384,1024]{1,0:T(8,128)(2,1)}, bf16[384,1024]{1,0:T(8,128)(2,1)}, u32[]{:S(2)}, u32[]{:S(2)}) collective-permute-start(bf16[384,1024]{1,0:T(8,128)(2,1)} %get-tuple-element.548), channel_id=1, source_target_pairs={{0,16},{8,24},{16,0},{24,8},{1,17},{9,25},{17,1},{25,9},{2,18},{10... | collective-permute-start | bytes 2359304 | tf_op jit(solution)/shard_map/ppermute | solution.py:1336
  718.2 32.9 %collective-permute-start.120 = (bf16[384,1024]{1,0:T(8,128)(2,1)}, bf16[384,1024]{1,0:T(8,128)(2,1)}, u32[]{:S(2)}, u32[]{:S(2)}) collective-permute-start(bf16[384,1024]{1,0:T(8,128)(2,1)} %get-tuple-element.546), channel_id=1, source_target_pairs={{0,16},{8,24},{16,0},{24,8},{1,17},{9,25},{17,1},{25,9},{2,18},{10... | collective-permute-start | bytes 2359304 | tf_op jit(solution)/shard_map/ppermute | solution.py:1336
  721.9 37.3 %collective-permute-start.125 = (bf16[256,1536]{1,0:T(8,128)(2,1)S(1)}, bf16[256,1536]{1,0:T(8,128)(2,1)S(1)}, u32[]{:S(2)}, u32[]{:S(2)}) collective-permute-start(bf16[256,1536]{1,0:T(8,128)(2,1)S(1)} %get-tuple-element.543), channel_id=1, source_target_pairs={{0,16},{8,24},{16,0},{24,8},{1,17},{9,25},{17,1},{25,9},{2,18},{10... | collective-permute-start | bytes 2359304 | tf_op jit(solution)/shard_map/ppermute | solution.py:1336
  725.8 19.9 %collective-permute-start.118 = (bf16[192,1152]{1,0:T(8,128)(2,1)S(1)}, bf16[192,1152]{1,0:T(8,128)(2,1)S(1)}, u32[]{:S(2)}, u32[]{:S(2)}) collective-permute-start(bf16[192,1152]{1,0:T(8,128)(2,1)S(1)} %fusion.13), channel_id=1, source_target_pairs={{0,2},{1,3},{2,4},{3,5},{4,6},{5,7},{6,0},{7,1},{8,10},{9,11},{10,... | collective-permute-start | bytes 1327112 | tf_op jit(solution)/shard_map/ppermute | solution.py:1336
  737.1 12.8 %collective-permute-start.117 = (bf16[192,1152]{1,0:T(8,128)(2,1)}, bf16[192,1152]{1,0:T(8,128)(2,1)}, u32[]{:S(2)}, u32[]{:S(2)}) collective-permute-start(bf16[192,1152]{1,0:T(8,128)(2,1)} %bitcast.51), channel_id=1, source_target_pairs={{0,1},{1,0},{2,3},{3,2},{4,5},{5,4},{6,7},{7,6},{8,9},{9,8},{10,11... | collective-permute-start | bytes 1327112 | tf_op jit(solution)/shard_map/ppermute | solution.py:1336
  (247 other events, 2888.5 us)
Sparse Core Ops, SparseCore 0:
  148.9 63.9 all-gather.1
  636.4 37.6 reduce-scatter.1

commit v6 on v5

--- a/solution.py
+++ b/solution.py
@@ -519,35 +519,42 @@
 RING = (0, 2, 1, 3)
 
 
-def bring_expert_weights(bring, ctx_ref, weights, w_gate_up_here, w_down_here, e, p):
+def bring_expert_weights(bring, ctx_ref, weights, w_gate_up_here, w_down_here, e, p, down_first=False):
     hidden_width, width = w_down_here.shape[1:]
-    copies = []
-    for side in range(2):
-        span = slice(side * hidden_width + p * FE_STEP, side * hidden_width + (p + 1) * FE_STEP)
-        if len(weights) == 1:
-            copies.append(bring(weights[0].at[e, :, span], w_gate_up_here.at[e, :, span]))
-            continue
-        for r in range(4):
-            quarter = weights[4 * e + r]
-            rows = quarter.shape[0]
-            at = pl.ds(pl.multiple_of((ctx_ref[0] ^ r) * rows, rows), rows)
-            copies.append(bring(quarter.at[:, span], w_gate_up_here.at[e, at, span]))
-    if p == 0:
-        rows, part = hidden_width // 4, width // 3
-        for r in range(4):
-            if len(weights) > 1:
+    copies, downs = [], []
+
+    def bring_gate_up():
+        for side in range(2):
+            span = slice(side * hidden_width + p * FE_STEP, side * hidden_width + (p + 1) * FE_STEP)
+            if len(weights) == 1:
+                copies.append(bring(weights[0].at[e, :, span], w_gate_up_here.at[e, :, span]))
+                continue
+            for r in range(4):
+                quarter = weights[4 * e + r]
+                rows = quarter.shape[0]
                 at = pl.ds(pl.multiple_of((ctx_ref[0] ^ r) * rows, rows), rows)
-                copies.append(bring(weights[-4 + r].at[e], w_down_here.at[e, at, :]))
-                continue
-            for b in range(3):
-                source = slice((3 * r + b) * rows, (3 * r + b + 1) * rows)
-                copies.append(
-                    bring(
-                        weights[0].at[e, source, 2 * hidden_width :],
-                        w_down_here.at[e, r * rows : (r + 1) * rows, b * part : (b + 1) * part],
+                copies.append(bring(quarter.at[:, span], w_gate_up_here.at[e, at, span]))
+
+    def bring_down():
+        if p == 0:
+            rows, part = hidden_width // 4, width // 3
+            for r in range(4):
+                if len(weights) > 1:
+                    at = pl.ds(pl.multiple_of((ctx_ref[0] ^ r) * rows, rows), rows)
+                    downs.append(bring(weights[-4 + r].at[e], w_down_here.at[e, at, :]))
+                    continue
+                for b in range(3):
+                    source = slice((3 * r + b) * rows, (3 * r + b + 1) * rows)
+                    downs.append(
+                        bring(
+                            weights[0].at[e, source, 2 * hidden_width :],
+                            w_down_here.at[e, r * rows : (r + 1) * rows, b * part : (b + 1) * part],
+                        )
                     )
-                )
-    return copies
+
+    for part in (bring_down, bring_gate_up) if down_first else (bring_gate_up, bring_down):
+        part()
+    return copies, downs
 
 
 def join_experts(gate_up, down):
@@ -620,7 +627,7 @@
     for e in range(expert_count):
         chosen = jnp.sum(gates * own[e : e + 1, :], -1, keepdims=True)
         for p in range(steps):
-            for copy in weight_copies[e * steps + p]:
+            for copy in weight_copies[e * steps + p][0]:
                 copy.wait()
             lower = slice(p * FE_STEP, (p + 1) * FE_STEP)
             upper = slice(hidden_width + p * FE_STEP, hidden_width + (p + 1) * FE_STEP)
@@ -630,6 +637,8 @@
             gate_here[:, flat] = gate.astype(jnp.bfloat16)
             up_here[:, flat] = up.astype(jnp.bfloat16)
             hidden = (gate * jax.nn.sigmoid(gate) * up * chosen).astype(jnp.bfloat16)
+            for copy in weight_copies[e * steps + p][1]:
+                copy.wait()
             total = total + mm(hidden, w_down_here[e, lower, :])
     send(gate_here, all_gate.at[span])
     send(up_here, all_up.at[span])
@@ -739,13 +748,14 @@
     for e in range(expert_count):
         for p in range(steps):
             flat = slice(e * hidden_width + p * FE_STEP, e * hidden_width + (p + 1) * FE_STEP)
-            weight_copies.append(
-                [
-                    bring(gate_in.at[rows_here, flat], gates.at[:, flat]),
-                    bring(up_in.at[rows_here, flat], ups.at[:, flat]),
-                ]
-                + bring_expert_weights(bring, ctx_ref, refs[:weight_total], w_gate_up_here, w_down_here, e, p)
+            rows_copies = [
+                bring(gate_in.at[rows_here, flat], gates.at[:, flat]),
+                bring(up_in.at[rows_here, flat], ups.at[:, flat]),
+            ]
+            gate_up_copies, down_copies = bring_expert_weights(
+                bring, ctx_ref, refs[:weight_total], w_gate_up_here, w_down_here, e, p, True
             )
+            weight_copies.append((rows_copies + down_copies, gate_up_copies))
     outgoing = []
 
     def send(source, target):
@@ -768,7 +778,7 @@
         chosen = jnp.sum(probs[...] * mine, -1, keepdims=True)
         dots = jnp.zeros((count, 1), jnp.float32)
         for p in range(steps):
-            for copy in weight_copies[e * steps + p]:
+            for copy in weight_copies[e * steps + p][0]:
                 copy.wait()
             lower = slice(p * FE_STEP, (p + 1) * FE_STEP)
             upper = slice(hidden_width + p * FE_STEP, hidden_width + (p + 1) * FE_STEP)
@@ -797,6 +807,8 @@
             grad_up = (plain * silu_gate).astype(jnp.bfloat16)
             grad_gates[:, flat] = grad_gate
             grad_ups[:, flat] = grad_up
+            for copy in weight_copies[e * steps + p][1]:
+                copy.wait()
             total = (
                 total
                 + mm(grad_gate, w_gate_up_here[e, :, lower], NT)
@@ -899,9 +911,9 @@
 
 
 def attention_forward_body(
-    ctx_ref, rows_0, rows_1, rows_2, rows_3, w_qkv_in, w_out_in, cosine_in, sine_in,
+    gain_lane, ctx_ref, rows_0, rows_1, rows_2, rows_3, w_qkv_in, w_out_in, cosine_in, sine_in, small_in, root_in,
     out_0, out_1, out_2, out_3, all_rows, qkv_out, attended_out, logs_out,
-    rows, w_qkv, w_out, cosine, sine, ring_rows, qkv, attended, logs, result, in_sems, out_sems,
+    rows, w_qkv, w_out, cosine, sine, small, root, ring_rows, qkv, attended, logs, result, in_sems, out_sems,
 ):
     sources, outs = (rows_0, rows_1, rows_2, rows_3), (out_0, out_1, out_2, out_3)
     count, width = rows_0.shape
@@ -912,16 +924,24 @@
     incoming, outgoing = Copies(in_sems), Copies(out_sems)
     first = [incoming.start(w_qkv_in, w_qkv), incoming.start(rows_0, rows.at[spans[0]])]
     tables = [incoming.start(cosine_in, cosine), incoming.start(sine_in, sine)]
+    if gain_lane is not None:
+        tables.append(incoming.start(small_in, small))
+        tables.append(incoming.start(root_in, root))
     later = [incoming.start(sources[r], rows.at[spans[r]]) for r in range(1, 4)]
     last = incoming.start(w_out_in, w_out)
     for copy in first + tables:
         copy.wait()
     part = width // 4
     lane = lax.broadcasted_iota(jnp.int32, (count, 128), 1)
+    if gain_lane is not None:
+        gain = small[...].astype(jnp.float32).T[gain_lane : gain_lane + 1, :]
     for r in range(4):
         span = spans[r]
         if r:
             later[r - 1].wait()
+        if gain_lane is not None:
+            value = rows[span, :].astype(jnp.float32)
+            rows[span, :] = (value * root[span, :1] * gain).astype(jnp.bfloat16)
         raw = mm(rows[span, :], w_qkv[...])
         for j in range((q_width + kv_width) // 128):
             turned = turn(raw[:, 128 * j : 128 * j + 128], cosine[span, :], sine[span, :], lane)
@@ -956,14 +976,14 @@
     outgoing.wait()
 
 
-def attention_forward(ctx_ref, rows, w_qkv, w_out, total_width, tables):
+def attention_forward(ctx_ref, rows, w_qkv, w_out, total_width, tables, small, roots, gain_lane):
     count, width = rows[0].shape
     seq = 4 * count
     q_width = w_out.shape[0]
     low, f32 = jnp.bfloat16, jnp.float32
     outs = pl.pallas_call(
-        attention_forward_body,
-        in_specs=[smem()] + [anywhere()] * 8,
+        functools.partial(attention_forward_body, gain_lane),
+        in_specs=[smem()] + [anywhere()] * 10,
         out_specs=[anywhere()] * 8,
         out_shape=[shaped((count, width))] * 4
         + [
@@ -978,12 +998,14 @@
             pltpu.VMEM(w_out.shape, low),
             pltpu.VMEM((seq, 128), f32),
             pltpu.VMEM((seq, 128), f32),
+            pltpu.VMEM(small.shape, low),
+            pltpu.VMEM(roots.shape, f32),
             pltpu.VMEM((seq, width), low),
             pltpu.VMEM((seq, total_width), low),
             pltpu.VMEM((seq, q_width), low),
             pltpu.VMEM((seq, 128), f32),
             pltpu.VMEM((seq, width), low),
-            pltpu.SemaphoreType.DMA((8,)),
+            pltpu.SemaphoreType.DMA((10,)),
             pltpu.SemaphoreType.DMA((8,)),
         ],
         compiler_params=kernel_params(),
@@ -992,7 +1014,7 @@
             bytes_accessed=2 * (seq * width * 2 + width * (total_width + q_width)),
             transcendentals=seq * seq * (q_width // HEAD_DIM),
         ),
-    )(ctx_ref, *rows, w_qkv, w_out, *tables)
+    )(ctx_ref, *rows, w_qkv, w_out, *tables, small, roots)
     return outs[:4], outs[4], outs[5], outs[6], outs[7]
 
 
@@ -1123,29 +1145,40 @@
     return outs[:4], outs[4], outs[5], outs[6]
 
 
-def place_body(members, share, first, *refs):
-    shards, outs = refs[:8], refs[8:]
-    front = outs[0].shape[3]
-    for r in range(8):
-        for c in range(4):
-            outs[0][members[8 + c], members[r]] = shards[r][c, :, first : first + front]
-        for out in outs[1:]:
-            q_part = out.shape[1] // 4
+def place_body(members, share, total, parts, *refs):
+    shards, outs = refs[:total], list(refs[total:])
+
+    def rows_of(r, c, columns):
+        if r < 7 or total == 8:
+            return shards[r][c, :, columns]
+        return shards[7 + c // 2][c % 2, :, columns]
+
+    for first, front, rest in parts:
+        out = outs.pop(0)
+        for r in range(8):
+            for c in range(4):
+                out[members[8 + c], members[r]] = rows_of(r, c, slice(first, first + front))
+        if not rest:
+            continue
+        out = outs.pop(0)
+        for r in range(8):
             span = pl.ds(pl.multiple_of(members[r] * share, share), share)
             for j in range(4):
-                out[span, j * q_part : (j + 1) * q_part] = shards[r][
-                    j, :, first + front : first + front + q_part
-                ]
-
-
-def place(members, shards, first, front, rest):
+                out[span, j * rest : (j + 1) * rest] = rows_of(
+                    r, j, slice(first + front, first + front + rest)
+                )
+
+
+def place(members, shards, parts):
     four, share, width = shards[0].shape
-    outs = [shaped((four, 8, share, front))]
-    if rest:
-        outs.append(shaped((8 * share, four * rest)))
+    outs = []
+    for _, front, rest in parts:
+        outs.append(shaped((four, 8, share, front)))
+        if rest:
+            outs.append(shaped((8 * share, four * rest)))
     return pl.pallas_call(
-        lambda members_ref, *refs: place_body(members_ref, share, first, *refs),
-        in_specs=[smem()] + [vmem()] * 8,
+        lambda members_ref, *refs: place_body(members_ref, share, len(shards), parts, *refs),
+        in_specs=[smem()] + [vmem()] * len(shards),
         out_shape=outs,
         compiler_params=kernel_params(),
     )(members, *shards)
@@ -1384,8 +1417,9 @@
         above = move_z(after(block, far), -1)
         far_mirror = swap_y(far)
         above = after(above, far_mirror, beside[2])
-        above_mirror = swap_y(above)
-        return [block, own_mirror, below, below_mirror, far, far_mirror, above, above_mirror]
+        half = block.shape[0] // 2
+        above_mirrors = [swap_y(above[:half]), move_z(after(own_mirror, above)[half:], -1)]
+        return [block, own_mirror, below, below_mirror, far, far_mirror, above, *above_mirrors]
     far = move_z(below, 1)
     below_mirror = swap_y(below)
     done = work(0, (after(block, below), own_mirror))
@@ -1519,10 +1553,30 @@
     hidden_rows = gather_ctx(
         after(hidden_in.reshape(row_count, model_width), expert_weights[0][6])
     )
-    flat_shards = gather_fsdp(packed, None, [expert_weights[0][2], expert_weights[0][6], 0.0])
-    shards = [shard.reshape(ctx_total, share, -1) for shard in flat_shards]
+    hidden_roots = jnp.concatenate(
+        [
+            jnp.broadcast_to(rms_scaled(wide(block), 1.0)[1], (row_count, 128))
+            for block in hidden_rows
+        ],
+        0,
+    )
+    joined = join_experts(after(w_gate_up[1], hidden_rows[1]), w_down[1])
+    flat_shards = gather_fsdp(
+        packed,
+        None,
+        [expert_weights[0][2], expert_weights[0][6], after(hidden_roots, joined)],
+    )
+    shards = [shard.reshape(-1, share, shard.shape[1]) for shard in flat_shards]
+    flat_shards[7:] = [jnp.concatenate(flat_shards[7:], 0)]
     layer_part = qkv_part + q_part
-    small = place(members, shards, layer_total * layer_part, 128, 0)[0].reshape(model_width, 128)
+    ready = after(shards[0], *expert_weights[0])
+    small, qkv_weight, out_weight = place(
+        members,
+        [ready, *shards[1:]],
+        [(layer_total * layer_part, 128, 0), (0, qkv_part, q_part)],
+    )
+    small = small.reshape(model_width, 128)
+    attention_weights = [(qkv_weight.reshape(model_width, qkv_part), out_weight)]
     gains = [
         wide(small[:, gain_lane + 2 * i : gain_lane + 2 * i + 2]).T for i in range(layer_total)
     ]
@@ -1530,24 +1584,21 @@
 
     def place_layer(i, start):
         qkv_weight, out_weight = place(
-            members, [after(shards[0], start), *shards[1:]], i * layer_part, qkv_part, q_part
+            members,
+            [after(shards[0], start), *shards[1:]],
+            [(i * layer_part, qkv_part, q_part)],
         )
         return qkv_weight.reshape(model_width, qkv_part), out_weight
 
-    attention_weights = [place_layer(0, expert_weights[0][10])]
     residual = wide(hidden_in.reshape(row_count, model_width))
     saved = []
     for i in range(layer_total):
         qkv_weight, out_weight = attention_weights[i]
         normed, root_first = rms_scaled(residual, gains[i][0])
-        if i == 0:
-            rows = [
-                rms_scaled(wide(block), gains[i][0])[0].astype(low) for block in hidden_rows
-            ]
-        else:
-            rows = gather_ctx(normed.astype(low))
+        rows = hidden_rows if i == 0 else gather_ctx(normed.astype(low))
         branch, rows_first, qkv, attended, logs = attention_forward(
-            ctx_ref, rows, qkv_weight, out_weight, qkv_part, tables
+            ctx_ref, rows, qkv_weight, out_weight, qkv_part, tables, small,
+            hidden_roots, gain_lane if i == 0 else None,
         )
         middle = residual + scatter_ctx(branch)
         normed_second, root_second = rms_scaled(middle, gains[i][1])
@@ -1566,7 +1617,7 @@
         normed_second = normed_second.astype(low)
         beside = None
         if i == 0:
-            joined = join_experts(after(w_gate_up[1], middle), w_down[1])
+            joined = after(joined, middle)
             expert_weights.append([lax.all_gather(joined, "ctx", axis=1, tiled=True)])
             beside = (lambda start: [], lambda start: place_layer(1, start), lambda start: [])
         last = gather_fsdp(normed_second, forward_work)
@@ -1610,12 +1661,17 @@
         sent = jnp.concatenate([grad.astype(low), lanes.astype(low)], -1)
         parts, kept = [None] * groups, []
         if i == 0:
+            whole_down = dot_tn(after(upper_hidden, sent), upper_grads).astype(low)
             halves = add_core(sent, *pending)
+            upper_down = lax.psum_scatter(
+                whole_down.reshape(ctx_total, -1, model_width), "ctx", scatter_dimension=0, tiled=True
+            )
+            upper_down = (upper_down.reshape(-1, model_width), None)
             expert_grads.insert(0, [(half[0], swap_x(half[1])) for half in halves] + [upper_down])
 
         def backward_work(group, pair):
             if i == 0 and group == 0:
-                pair = (after(pair[0], *jax.tree.leaves(halves)), pair[1])
+                pair = (after(pair[0], whole_down, *jax.tree.leaves(halves)), pair[1])
             if i == 0 and group == 3:
                 pair = (after(pair[0], expert_grads[0][0][1]), pair[1])
             outs = experts_backward(
@@ -1630,7 +1686,7 @@
         grads_second, grad_gate, grad_up, hidden, grad_logits = kept
         half_width, half_hidden = model_width // 2, hidden.shape[1] // 2
 
-        came, whole_down = [], []
+        came = []
         pairs = [(rows_second, half_width, grad_gate), (rows_second, half_width, grad_up)]
         if i == 0:
             pairs.append((hidden, half_hidden, grads_second))
@@ -1638,27 +1694,32 @@
         def first_beside(start):
             for part, half, grads in pairs:
                 came.append(swap_core(dot_tn(after(part, start)[:, half:], grads).astype(low)))
-            if i > 0:
-                whole_down.append(dot_tn(after(hidden, start), grads_second).astype(low))
-            return came + whole_down
+            return came
 
         last_gate = [expert_grads[0][1][1]] if i == 0 else []
-        grad_second, _, _ = scatter_fsdp(
-            parts, (lambda start: last_gate, first_beside, lambda start: []), last
-        )
-        small_grads = dot_tn(rows_second, grad_logits)
+        grad_second, small_grads, _ = scatter_fsdp(
+            parts,
+            (
+                lambda start: [*first_beside(start), *last_gate],
+                lambda start: dot_tn(after(rows_second, start), grad_logits),
+                lambda start: [],
+            ),
+            last,
+        )
+        small_grads = small_grads[1]
         grad_middle, gain_second = rms_back(middle, root_second, gains[i][1], grad_second)
         grad_middle = grad_middle + grad
         branch_rows = grad_middle.astype(low)
         branch_grads = gather_ctx(branch_rows)
         if i > 0:
             pending = pairs, came
+            upper_hidden, upper_grads = hidden, grads_second
         back, rows_branch, grad_qkv, gain_first = attention_backward(
             ctx_ref, branch_grads, rows_first, qkv_weight, out_weight, qkv,
             logs, tables,
         )
         gain_first = gain_first[0] / ring_gains[i]
-        gain_second = ring(gain_second)
+        gain_second = ring(after(gain_second, back[0]))
         small_grads = jnp.where(
             expert_lane == gain_lane,
             gain_first[:, None],
@@ -1691,11 +1752,11 @@
             def second_beside(start):
                 halves.extend(add_core(start, pairs[1:], came[1:]))
                 crossed.extend(swap_x(half[1]) for half in halves[1:])
-                return jax.tree.leaves(halves)
+                return finish_layer(1, expert_grads[0], start, []), halves
 
             beside = [
                 second_beside,
-                lambda start: [crossed[0], finish_layer(1, expert_grads[0], start, [])],
+                lambda start: crossed[0],
                 lambda start: crossed[1],
             ]
             lower, finished, _ = scatter_fsdp(flat_packs, beside, below, None, upper)
@@ -1707,10 +1768,6 @@
         grad_first = scatter_ctx(back, layer_packs)
         grad_input, _ = rms_back(residual, root_first, gains[i][0], grad_first)
         grad = grad_input + grad_middle
-        if i > 0:
-            parts = after(whole_down[0], grad).reshape(ctx_total, -1, model_width)
-            upper_down = lax.psum_scatter(parts, "ctx", scatter_dimension=0, tiled=True)
-            upper_down = (upper_down.reshape(-1, model_width), None)
         packs = flat_packs
     attention_grads = [
         part.astype(low).reshape(ctx_total, share, -1) for part in attention_grads
@@ -1727,7 +1784,7 @@
         ],
         expert_total,
     )
-    outs = finish_layer(0, expert_grads[0], attention_grads[0], finished[1][1])
+    outs = finish_layer(0, expert_grads[0], attention_grads[0], finished[0][0])
     return (
         hidden_out,
         grad.reshape(1, row_count, model_width),

time: 788 us -> 760 us (0.964)
  waiting for transfers between devices: 288 us -> 268 us
  starting transfers between devices: 115 us -> 129 us
  Pallas kernels: 216 us -> 207 us
  local copies, waits for them, and re-layouts: 48.4 us -> 39.6 us
    ppermute x126 -> x127, waiting for transfers between devices: 288 us -> 268 us  [rotate_ranks(): lax.ppermute(values_in, axis_name, [(i, target_of(i)) for i in range(tota...]
    ppermute x126 -> x127, starting transfers between devices: 115 us -> 129 us  [rotate_ranks(): lax.ppermute(values_in, axis_name, [(i, target_of(i)) for i in range(tota...]
    unnamed x366 -> x353, local copies, waits for them, and re-layouts: 23.6 us -> 17.9 us
  transfers between devices with their start and end apart: 128 -> 129, of which waited for: 55 -> 55; matrix products, arithmetic and copies ran while one was open for 13% -> 14% of each run, Pallas kernels for 23% -> 22%
where the time goes in v6:
time: 760 us; the launch traced here: 755 us
  waiting for transfers between devices  268 us (35%)
  Pallas kernels  207 us (27%)
  starting transfers between devices  129 us (17%)
  other arithmetic  53.1 us (7%)
  matrix products  43 us (6%)
  local copies, waits for them, and re-layouts  39.6 us (5%)
  between operations  16.5 us (2%)
    ppermute x127, waiting for transfers between devices, rotate_ranks(): lax.ppermute(values_in, axis_name, [(i, target_of(i)) for i in range(tota...  268 us
    ppermute x127, starting transfers between devices, rotate_ranks(): lax.ppermute(values_in, axis_name, [(i, target_of(i)) for i in range(tota...  129 us
    pallas_call x8, Pallas kernels, experts_backward(): pl.pallas_call(functools.partial(experts_backward_body, len(weights), rin...  63.2 us
    pallas_call x8, Pallas kernels, experts_forward(): pl.pallas_call(functools.partial(experts_forward_body, len(weights), grou...  60.7 us
    dot_general x17, matrix products, mm(): return lax.dot_general(a, b, dims, preferred_element_type=jnp.float32)  43 us
    pallas_call x2, Pallas kernels, attention_backward(): pl.pallas_call(attention_backward_body, in_specs=[smem()] + [anywhere()]...  26.9 us
    pallas_call x2, Pallas kernels, attention_forward(): pl.pallas_call(functools.partial(attention_forward_body, gain_lane), in_s...  22.6 us
    unnamed x353, local copies, waits for them, and re-layouts  17.9 us
  transfers between devices with their start and end apart: 129, of which 55 were waited for; matrix products, arithmetic and copies ran while one was open for 14% of the time, Pallas kernels for 22%

profile of v6, /device:TPU:0, one launch (start us, length us, event | category | flops | bytes accessed | tf_op | source)
XLA Modules:
  0.0 755.3 jit_solution(4425583507944551659)
XLA Ops:
  13.0 4.5 collective-permute-done.1.block_2
  29.4 17.6 %collective-permute-done.3.refs_2_ = bf16[384,1024]{1,0:T(8,128)(2,1)S(1)} collective-permute-done((bf16[384,1024]{1,0:T(8,128)(2,1)S(1)}, bf16[384,1024]{1,0:T(8,128)(2,1)S(1)}, u32[]{:S(2)}, u32[]{:S(2)}) %collective-permute-start.3) | collective-permute-done | bytes 786464 | tf_op jit(solution)/shard_map/ppermute | solution.py:1369
  52.3 13.1 %collective-permute-done.4.refs_6_ = bf16[384,1024]{1,0:T(8,128)(2,1)} collective-permute-done((bf16[384,1024]{1,0:T(8,128)(2,1)S(1)}, bf16[384,1024]{1,0:T(8,128)(2,1)}, u32[]{:S(2)}, u32[]{:S(2)}) %collective-permute-start.4) | collective-permute-done | bytes 786464 | tf_op jit(solution)/shard_map/ppermute | solution.py:1369
  78.5 13.0 %collective-permute-done.13.refs_10_ = bf16[2,128,1536]{2,1,0:T(8,128)(2,1)S(1)} collective-permute-done((bf16[2,128,1536]{2,1,0:T(8,128)(2,1)S(1)}, bf16[2,128,1536]{2,1,0:T(8,128)(2,1)S(1)}, u32[]{:S(2)}, u32[]{:S(2)}) %collective-permute-start.13) | collective-permute-done | bytes 786464 | tf_op jit(solution)/shard_map/ppermute | solution.py:1369
  96.0 8.4 %collective-permute-done.21 = bf16[96,2176]{1,0:T(8,128)(2,1)S(1)} collective-permute-done((bf16[96,2176]{1,0:T(8,128)(2,1)S(1)}, bf16[96,2176]{1,0:T(8,128)(2,1)S(1)}, u32[]{:S(2)}, u32[]{:S(2)}) %collective-permute-start.21) | collective-permute-done | bytes 417824 | tf_op jit(solution)/shard_map/ppermute | solution.py:1369
  105.7 5.0 shard_map.171
  111.6 11.7 %shard_map.172 = (bf16[128,1536]{1,0:T(8,128)(2,1)}, bf16[128,1536]{1,0:T(8,128)(2,1)}, bf16[128,1536]{1,0:T(8,128)(2,1)}, bf16[128,1536]{1,0:T(8,128)(2,1)}, bf...) custom-call(s32[1]{0:T(128)} %bitcast.1.ctx_ref, ...), custom_call_target="tpu_custom_call" | custom-call | flops 2013265920 | bytes 6291456 | tf_op jit(solution)/shard_map/pallas_call | solution.py:984
  128.6 8.1 %collective-permute-done.25 = bf16[128,1536]{1,0:T(8,128)(2,1)S(1)} collective-permute-done((bf16[128,1536]{1,0:T(8,128)(2,1)S(1)}, bf16[128,1536]{1,0:T(8,128)(2,1)S(1)}, u32[]{:S(2)}, u32[]{:S(2)}) %collective-permute-start.25) | collective-permute-done | bytes 393248 | tf_op jit(solution)/shard_map/ppermute | solution.py:1369
  143.9 10.1 %collective-permute-done.26.rows_0 = bf16[128,1536]{1,0:T(8,128)(2,1)S(1)} collective-permute-done((bf16[128,1536]{1,0:T(8,128)(2,1)S(1)}, bf16[128,1536]{1,0:T(8,128)(2,1)S(1)}, u32[]{:S(2)}, u32[]{:S(2)}) %collective-permute-start.26) | collective-permute-done | bytes 393248 | tf_op jit(solution)/shard_map/ppermute | solution.py:1369
  157.2 7.5 shard_map.173
  170.0 7.6 %shard_map.174 = (bf16[128,1536]{1,0:T(8,128)(2,1)}, bf16[128,1536]{1,0:T(8,128)(2,1)}, bf16[1024,1536]{1,0:T(8,128)(2,1)}, bf16[1024,1024]{1,0:T(8,128)(2,1)}, ...) custom-call(s32[1]{0:T(128)} %bitcast.1.ctx_ref, ...), custom_call_target="tpu_custom_call", output_to_operand_aliasing={{2}: (19, {}), {3}: (20, {}), {4}: (21, {}), {5}: (22, {})} | custom-call | flops 2415919104 | bytes 9437184 | tf_op jit(solution)/shard_map/pallas_call | solution.py:688
  179.9 7.5 shard_map.175
  189.0 7.6 %shard_map.176 = (bf16[128,1536]{1,0:T(8,128)(2,1)}, bf16[128,1536]{1,0:T(8,128)(2,1)}, bf16[1024,1536]{1,0:T(8,128)(2,1)}, bf16[1024,1024]{1,0:T(8,128)(2,1)}, ...) custom-call(s32[1]{0:T(128)} %bitcast.1.ctx_ref, ...), custom_call_target="tpu_custom_call", output_to_operand_aliasing={{2}: (19, {}), {3}: (20, {}), {4}: (21, {}), {5}: (22, {})} | custom-call | flops 2415919104 | bytes 9437184 | tf_op jit(solution)/shard_map/pallas_call | solution.py:688
  198.4 6.4 collective-permute-done.33
  209.8 10.1 %collective-permute-done.36 = bf16[128,1536]{1,0:T(8,128)(2,1)S(1)} collective-permute-done((bf16[128,1536]{1,0:T(8,128)(2,1)S(1)}, bf16[128,1536]{1,0:T(8,128)(2,1)S(1)}, u32[]{:S(2)}, u32[]{:S(2)}) %collective-permute-start.36) | collective-permute-done | bytes 393248 | tf_op jit(solution)/shard_map/ppermute | solution.py:1369
  220.6 4.9 shard_map.177
  227.9 5.5 collective-permute-done.39
  235.8 6.5 collective-permute-done.41.rows_2
  244.8 10.9 %shard_map.178 = (bf16[128,1536]{1,0:T(8,128)(2,1)}, bf16[128,1536]{1,0:T(8,128)(2,1)}, bf16[128,1536]{1,0:T(8,128)(2,1)}, bf16[128,1536]{1,0:T(8,128)(2,1)}, bf...) custom-call(s32[1]{0:T(128)} %bitcast.1.ctx_ref, ...), custom_call_target="tpu_custom_call" | custom-call | flops 2013265920 | bytes 6291456 | tf_op jit(solution)/shard_map/pallas_call | solution.py:984
  260.1 9.9 %collective-permute-done.45 = bf16[128,1536]{1,0:T(8,128)(2,1)S(1)} collective-permute-done((bf16[128,1536]{1,0:T(8,128)(2,1)S(1)}, bf16[128,1536]{1,0:T(8,128)(2,1)S(1)}, u32[]{:S(2)}, u32[]{:S(2)}) %collective-permute-start.45) | collective-permute-done | bytes 393248 | tf_op jit(solution)/shard_map/ppermute | solution.py:1369
  273.9 10.7 %collective-permute-done.46.rows_0 = bf16[128,1536]{1,0:T(8,128)(2,1)S(1)} collective-permute-done((bf16[128,1536]{1,0:T(8,128)(2,1)S(1)}, bf16[128,1536]{1,0:T(8,128)(2,1)S(1)}, u32[]{:S(2)}, u32[]{:S(2)}) %collective-permute-start.46) | collective-permute-done | bytes 393248 | tf_op jit(solution)/shard_map/ppermute | solution.py:1369
  287.5 7.6 %shard_map.179 = (bf16[128,1536]{1,0:T(8,128)(2,1)}, bf16[128,1536]{1,0:T(8,128)(2,1)}, bf16[1024,1536]{1,0:T(8,128)(2,1)}, bf16[1024,1024]{1,0:T(8,128)(2,1)}, ...) custom-call(s32[1]{0:T(128)} %bitcast.1.ctx_ref, bf16[128,1536]{1,0:T(8,128)(2,1)} %copy-done.53, ...), custom_call_target="tpu_custom_call" | custom-call | flops 2415919104 | bytes 9437184 | tf_op jit(solution)/shard_map/pallas_call | solution.py:688
  295.9 3.5 collective-permute-start.50
  300.7 7.6 %shard_map.180 = (bf16[128,1536]{1,0:T(8,128)(2,1)}, bf16[128,1536]{1,0:T(8,128)(2,1)}, bf16[1024,1536]{1,0:T(8,128)(2,1)}, bf16[1024,1024]{1,0:T(8,128)(2,1)}, ...) custom-call(s32[1]{0:T(128)} %bitcast.1.ctx_ref, ...), custom_call_target="tpu_custom_call", output_to_operand_aliasing={{2}: (8, {}), {3}: (9, {}), {4}: (10, {}), {5}: (11, {})} | custom-call | flops 2415919104 | bytes 9437184 | tf_op jit(solution)/shard_map/pallas_call | solution.py:688
  310.6 7.6 %shard_map.181 = (bf16[128,1536]{1,0:T(8,128)(2,1)}, bf16[128,1536]{1,0:T(8,128)(2,1)}, bf16[1024,1536]{1,0:T(8,128)(2,1)}, bf16[1024,1024]{1,0:T(8,128)(2,1)}, ...) custom-call(s32[1]{0:T(128)} %bitcast.1.ctx_ref, ...), custom_call_target="tpu_custom_call", output_to_operand_aliasing={{2}: (8, {}), {3}: (9, {}), {4}: (10, {}), {5}: (11, {})} | custom-call | flops 2415919104 | bytes 9437184 | tf_op jit(solution)/shard_map/pallas_call | solution.py:688
  319.0 7.6 %shard_map.182 = (bf16[128,1536]{1,0:T(8,128)(2,1)}, bf16[128,1536]{1,0:T(8,128)(2,1)}, bf16[1024,1536]{1,0:T(8,128)(2,1)}, bf16[1024,1024]{1,0:T(8,128)(2,1)}, ...) custom-call(s32[1]{0:T(128)} %bitcast.1.ctx_ref, ...), custom_call_target="tpu_custom_call", output_to_operand_aliasing={{2}: (8, {}), {3}: (9, {}), {4}: (10, {}), {5}: (11, {})} | custom-call | flops 2415919104 | bytes 9437184 | tf_op jit(solution)/shard_map/pallas_call | solution.py:688
  328.3 6.7 collective-permute-done.53
  339.8 10.2 %collective-permute-done.56 = bf16[128,1536]{1,0:T(8,128)(2,1)S(1)} collective-permute-done((bf16[128,1536]{1,0:T(8,128)(2,1)S(1)}, bf16[128,1536]{1,0:T(8,128)(2,1)S(1)}, u32[]{:S(2)}, u32[]{:S(2)}) %collective-permute-start.56) | collective-permute-done | bytes 393248 | tf_op jit(solution)/shard_map/ppermute | solution.py:1369
  352.2 6.9 collective-permute-done.57
  360.5 5.3 collective-permute-start.61
  365.8 7.7 %collective-permute-done.60.grads_0 = bf16[128,1664]{1,0:T(8,128)(2,1)S(1)} collective-permute-done((bf16[128,1664]{1,0:T(8,128)(2,1)S(1)}, bf16[128,1664]{1,0:T(8,128)(2,1)S(1)}, u32[]{:S(2)}, u32[]{:S(2)}) %collective-permute-start.60) | collective-permute-done | bytes 426016 | tf_op jit(solution)/shard_map/ppermute | solution.py:1369
  373.7 4.1 collective-permute-start.63
  378.6 7.9 %shard_map.183 = (bf16[128,1536]{1,0:T(8,128)(2,1)}, bf16[128,1536]{1,0:T(8,128)(2,1)}, bf16[1024,1536]{1,0:T(8,128)(2,1)}, bf16[1024,1024]{1,0:T(8,128)(2,1)}, ...) custom-call(s32[1]{0:T(128)} %bitcast.1.ctx_ref, bf16[128,1664]{1,0:T(8,128)(2,1)} %copy-done.52, ...), custom_call_target="tpu_custom_call" | custom-call | flops 2415919104 | bytes 9437184 | tf_op jit(solution)/shard_map/pallas_call | solution.py:841
  386.6 3.7 collective-permute-start.64
  391.0 7.9 %shard_map.184 = (bf16[128,1536]{1,0:T(8,128)(2,1)}, bf16[128,1536]{1,0:T(8,128)(2,1)}, bf16[1024,1536]{1,0:T(8,128)(2,1)}, bf16[1024,1024]{1,0:T(8,128)(2,1)}, ...) custom-call(s32[1]{0:T(128)} %bitcast.1.ctx_ref, ...), custom_call_target="tpu_custom_call", output_to_operand_aliasing={{2}: (9, {}), {3}: (10, {}), {4}: (11, {}), {5}: (12, {}), ... | custom-call | flops 2415919104 | bytes 9437184 | tf_op jit(solution)/shard_map/pallas_call | solution.py:841
  401.9 7.9 %shard_map.185 = (bf16[128,1536]{1,0:T(8,128)(2,1)}, bf16[128,1536]{1,0:T(8,128)(2,1)}, bf16[1024,1536]{1,0:T(8,128)(2,1)}, bf16[1024,1024]{1,0:T(8,128)(2,1)}, ...) custom-call(s32[1]{0:T(128)} %bitcast.1.ctx_ref, ...), custom_call_target="tpu_custom_call", output_to_operand_aliasing={{2}: (9, {}), {3}: (10, {}), {4}: (11, {}), {5}: (12, {}), ... | custom-call | flops 2415919104 | bytes 9437184 | tf_op jit(solution)/shard_map/pallas_call | solution.py:841
  410.6 8.0 %shard_map.186 = (bf16[128,1536]{1,0:T(8,128)(2,1)}, bf16[128,1536]{1,0:T(8,128)(2,1)}, bf16[1024,1536]{1,0:T(8,128)(2,1)}, bf16[1024,1024]{1,0:T(8,128)(2,1)}, ...) custom-call(s32[1]{0:T(128)} %bitcast.1.ctx_ref, ...), custom_call_target="tpu_custom_call", output_to_operand_aliasing={{2}: (9, {}), {3}: (10, {}), {4}: (11, {}), {5}: (12, {}), ... | custom-call | flops 2415919104 | bytes 9437184 | tf_op jit(solution)/shard_map/pallas_call | solution.py:841
  420.6 3.6 convolution_convert_fusion.9
  431.1 8.8 %collective-permute-done.70 = bf16[128,1536]{1,0:T(8,128)(2,1)S(1)} collective-permute-done((bf16[128,1536]{1,0:T(8,128)(2,1)S(1)}, bf16[128,1536]{1,0:T(8,128)(2,1)S(1)}, u32[]{:S(2)}, u32[]{:S(2)}) %collective-permute-start.70) | collective-permute-done | bytes 393248 | tf_op jit(solution)/shard_map/ppermute | solution.py:1369
  443.8 4.0 collective-permute-done.71
  455.4 6.9 collective-permute-done.77.grad_2
  468.1 13.5 %shard_map.187 = (bf16[128,1536]{1,0:T(8,128)(2,1)}, bf16[128,1536]{1,0:T(8,128)(2,1)}, bf16[128,1536]{1,0:T(8,128)(2,1)}, bf16[128,1536]{1,0:T(8,128)(2,1)}, bf...) custom-call(s32[1]{0:T(128)} %bitcast.1.ctx_ref, ...), custom_call_target="tpu_custom_call" | custom-call | flops 2617245696 | bytes 7864320 | tf_op jit(solution)/shard_map/pallas_call | solution.py:1111
  490.3 3.5 convolution_convert_fusion.5.out
  496.7 4.2 shard_map.188
  506.7 5.0 convolution_convert_fusion
  523.1 7.9 %shard_map.189 = (bf16[128,1536]{1,0:T(8,128)(2,1)}, bf16[128,1536]{1,0:T(8,128)(2,1)}, bf16[1024,1536]{1,0:T(8,128)(2,1)}, bf16[1024,1024]{1,0:T(8,128)(2,1)}, ...) custom-call(s32[1]{0:T(128)} %bitcast.1.ctx_ref, bf16[128,1664]{1,0:T(8,128)(2,1)} %copy-done.50, ...), custom_call_target="tpu_custom_call" | custom-call | flops 2415919104 | bytes 9437184 | tf_op jit(solution)/shard_map/pallas_call | solution.py:841
  536.3 7.8 %shard_map.190 = (bf16[128,1536]{1,0:T(8,128)(2,1)}, bf16[128,1536]{1,0:T(8,128)(2,1)}, bf16[1024,1536]{1,0:T(8,128)(2,1)}, bf16[1024,1024]{1,0:T(8,128)(2,1)}, ...) custom-call(s32[1]{0:T(128)} %bitcast.1.ctx_ref, ...), custom_call_target="tpu_custom_call", output_to_operand_aliasing={{2}: (20, {}), {3}: (21, {}), {4}: (22, {}), {5}: (23, {}),... | custom-call | flops 2415919104 | bytes 9437184 | tf_op jit(solution)/shard_map/pallas_call | solution.py:841
  546.9 7.8 %shard_map.191 = (bf16[128,1536]{1,0:T(8,128)(2,1)}, bf16[128,1536]{1,0:T(8,128)(2,1)}, bf16[1024,1536]{1,0:T(8,128)(2,1)}, bf16[1024,1024]{1,0:T(8,128)(2,1)}, ...) custom-call(s32[1]{0:T(128)} %bitcast.1.ctx_ref, ...), custom_call_target="tpu_custom_call", output_to_operand_aliasing={{2}: (20, {}), {3}: (21, {}), {4}: (22, {}), {5}: (23, {}),... | custom-call | flops 2415919104 | bytes 9437184 | tf_op jit(solution)/shard_map/pallas_call | solution.py:841
  557.0 8.0 %shard_map.192 = (bf16[128,1536]{1,0:T(8,128)(2,1)}, bf16[128,1536]{1,0:T(8,128)(2,1)}, bf16[1024,1536]{1,0:T(8,128)(2,1)}, bf16[1024,1024]{1,0:T(8,128)(2,1)}, ...) custom-call(s32[1]{0:T(128)} %bitcast.1.ctx_ref, ...), custom_call_target="tpu_custom_call", output_to_operand_aliasing={{2}: (20, {}), {3}: (21, {}), {4}: (22, {}), {5}: (23, {}),... | custom-call | flops 2415919104 | bytes 9437184 | tf_op jit(solution)/shard_map/pallas_call | solution.py:841
  566.9 3.6 convolution_convert_fusion.7
  579.2 7.6 %collective-permute-done.93 = bf16[128,1536]{1,0:T(8,128)(2,1)S(1)} collective-permute-done((bf16[128,1536]{1,0:T(8,128)(2,1)S(1)}, bf16[128,1536]{1,0:T(8,128)(2,1)S(1)}, u32[]{:S(2)}, u32[]{:S(2)}) %collective-permute-start.93) | collective-permute-done | bytes 393248 | tf_op jit(solution)/shard_map/ppermute | solution.py:1369
  587.1 8.9 %collective-permute-done.99.refs_3_ = bf16[384,1024]{1,0:T(8,128)(2,1)S(1)} collective-permute-done((bf16[384,1024]{1,0:T(8,128)(2,1)S(1)}, bf16[384,1024]{1,0:T(8,128)(2,1)S(1)}, u32[]{:S(2)}, u32[]{:S(2)}) %collective-permute-start.99) | collective-permute-done | bytes 786464 | tf_op jit(solution)/shard_map/ppermute | solution.py:1369
  601.6 3.6 collective-permute-done.94
  605.3 3.6 collective-permute-done.100
  615.3 4.9 collective-permute-done.102.grad_2
  626.6 13.5 %shard_map.193 = (bf16[128,1536]{1,0:T(8,128)(2,1)}, bf16[128,1536]{1,0:T(8,128)(2,1)}, bf16[128,1536]{1,0:T(8,128)(2,1)}, bf16[128,1536]{1,0:T(8,128)(2,1)}, bf...) custom-call(s32[1]{0:T(128)} %bitcast.1.ctx_ref, ...), custom_call_target="tpu_custom_call" | custom-call | flops 2617245696 | bytes 7864320 | tf_op jit(solution)/shard_map/pallas_call | solution.py:1111
  644.0 3.6 convolution_convert_fusion.4.out
  656.0 4.2 shard_map.194
  672.6 5.3 collective-permute-done.115
  682.3 8.6 %collective-permute-done.111 = bf16[192,1152]{1,0:T(8,128)(2,1)S(1)} collective-permute-done((bf16[192,1152]{1,0:T(8,128)(2,1)S(1)}, bf16[192,1152]{1,0:T(8,128)(2,1)S(1)}, u32[]{:S(2)}, u32[]{:S(2)}) %collective-permute-start.111) | collective-permute-done | bytes 442400 | tf_op jit(solution)/shard_map/ppermute | solution.py:1369
  707.0 9.6 %collective-permute-done.117 = bf16[192,1152]{1,0:T(8,128)(2,1)S(1)} collective-permute-done((bf16[192,1152]{1,0:T(8,128)(2,1)S(1)}, bf16[192,1152]{1,0:T(8,128)(2,1)S(1)}, u32[]{:S(2)}, u32[]{:S(2)}) %collective-permute-start.117) | collective-permute-done | bytes 442400 | tf_op jit(solution)/shard_map/ppermute | solution.py:1369
  721.9 3.9 shard_map.195
  730.0 4.5 collective-permute-done.122
  738.9 3.9 shard_map.197
  (726 shorter events, 271.8 us)
Async XLA Ops:
  7.2 279.6 %all-gather.2.cloned.1.call-start = ((), (), s32[]{:S(2)}) async-start(), calls=%async_computation.1 | async-start | bytes 11796480 | tf_op jit(solution)/shard_map/all_gather | solution.py:1621
  23.2 25.3 %collective-permute-start.15 = (bf16[192,2176]{1,0:T(8,128)(2,1)}, bf16[192,2176]{1,0:T(8,128)(2,1)S(1)}, u32[]{:S(2)}, u32[]{:S(2)}) collective-permute-start(bf16[192,2176]{1,0:T(8,128)(2,1)} %shard_map.170.ids_0), channel_id=1, source_target_pairs={{0,1},{1,0},{2,3},{3,2},{4,5},{5,4},{6,7},{7,6},{8,9},{9,8},{10,11... | collective-permute-start | bytes 2506760 | tf_op jit(solution)/shard_map/ppermute | solution.py:1369
  24.8 23.8 %collective-permute-start.16 = (bf16[192,2176]{1,0:T(8,128)(2,1)}, bf16[192,2176]{1,0:T(8,128)(2,1)}, u32[]{:S(2)}, u32[]{:S(2)}) collective-permute-start(bf16[192,2176]{1,0:T(8,128)(2,1)} %shard_map.170.ids_0), channel_id=1, source_target_pairs={{0,2},{1,3},{2,4},{3,5},{4,6},{5,7},{6,0},{7,1},{8,10},{9,11},{10,... | collective-permute-start | bytes 2506760 | tf_op jit(solution)/shard_map/ppermute | solution.py:1369
  27.9 19.2 %collective-permute-start.3 = (bf16[384,1024]{1,0:T(8,128)(2,1)S(1)}, bf16[384,1024]{1,0:T(8,128)(2,1)S(1)}, u32[]{:S(2)}, u32[]{:S(2)}) collective-permute-start(bf16[384,1024]{1,0:T(8,128)(2,1)S(1)} %get-tuple-element.274.refs_0_), channel_id=1, source_target_pairs={{0,16},{8,24},{16,0},{24,8},{1,17},{9,25},{17,1},{25,9},{2,18},{10... | collective-permute-start | bytes 2359304 | tf_op jit(solution)/shard_map/ppermute | solution.py:1369
  47.0 18.4 %collective-permute-start.4 = (bf16[384,1024]{1,0:T(8,128)(2,1)S(1)}, bf16[384,1024]{1,0:T(8,128)(2,1)}, u32[]{:S(2)}, u32[]{:S(2)}) collective-permute-start(bf16[384,1024]{1,0:T(8,128)(2,1)S(1)} %get-tuple-element.275.refs_4_), channel_id=1, source_target_pairs={{0,16},{8,24},{16,0},{24,8},{1,17},{9,25},{17,1},{25,9},{2,18},{10... | collective-permute-start | bytes 2359304 | tf_op jit(solution)/shard_map/ppermute | solution.py:1369
  48.5 21.2 %collective-permute-start.18 = (bf16[192,2176]{1,0:T(8,128)(2,1)}, bf16[192,2176]{1,0:T(8,128)(2,1)}, u32[]{:S(2)}, u32[]{:S(2)}) collective-permute-start(bf16[192,2176]{1,0:T(8,128)(2,1)} %collective-permute-done.16.ids_0), channel_id=1, source_target_pairs={{0,2},{1,3},{2,4},{3,5},{4,6},{5,7},{6,0},{7,1},{8,10},{9,11},{10,... | collective-permute-start | bytes 2506760 | tf_op jit(solution)/shard_map/ppermute | solution.py:1369
  50.2 19.0 %collective-permute-start.17 = (bf16[192,2176]{1,0:T(8,128)(2,1)}, bf16[192,2176]{1,0:T(8,128)(2,1)}, u32[]{:S(2)}, u32[]{:S(2)}) collective-permute-start(bf16[192,2176]{1,0:T(8,128)(2,1)} %collective-permute-done.16.ids_0), channel_id=1, source_target_pairs={{0,1},{1,0},{2,3},{3,2},{4,5},{5,4},{6,7},{7,6},{8,9},{9,8},{10,11... | collective-permute-start | bytes 2506760 | tf_op jit(solution)/shard_map/ppermute | solution.py:1369
  51.7 18.6 %collective-permute-start.8 = (bf16[384,1024]{1,0:T(8,128)(2,1)S(1)}, bf16[384,1024]{1,0:T(8,128)(2,1)S(1)}, u32[]{:S(2)}, u32[]{:S(2)}) collective-permute-start(bf16[384,1024]{1,0:T(8,128)(2,1)S(1)} %get-tuple-element.274.refs_0_), channel_id=1, source_target_pairs={{0,8},{8,0},{16,24},{24,16},{1,9},{9,1},{17,25},{25,17},{2,10},{10... | collective-permute-start | bytes 2359304 | tf_op jit(solution)/shard_map/ppermute | solution.py:1369
  51.7 22.2 %collective-permute-start.9 = (bf16[384,1024]{1,0:T(8,128)(2,1)S(1)}, bf16[384,1024]{1,0:T(8,128)(2,1)S(1)}, u32[]{:S(2)}, u32[]{:S(2)}) collective-permute-start(bf16[384,1024]{1,0:T(8,128)(2,1)S(1)} %collective-permute-done.3.refs_2_), channel_id=1, source_target_pairs={{0,8},{8,0},{16,24},{24,16},{1,9},{9,1},{17,25},{25,17},{2,10},{10... | collective-permute-start | bytes 2359304 | tf_op jit(solution)/shard_map/ppermute | solution.py:1369
  65.4 12.3 %collective-permute-start.6 = (bf16[128,1536]{1,0:T(8,128)(2,1)}, bf16[128,1536]{1,0:T(8,128)(2,1)S(1)}, u32[]{:S(2)}, u32[]{:S(2)}) collective-permute-start(bf16[128,1536]{1,0:T(8,128)(2,1)} %bitcast.rows_0), channel_id=1, source_target_pairs={{0,16},{8,24},{16,0},{24,8},{1,17},{9,25},{17,1},{25,9},{2,18},{10... | collective-permute-start | bytes 1179656 | tf_op jit(solution)/shard_map/ppermute | solution.py:1369
  69.2 22.3 %collective-permute-start.13 = (bf16[2,128,1536]{2,1,0:T(8,128)(2,1)S(1)}, bf16[2,128,1536]{2,1,0:T(8,128)(2,1)S(1)}, u32[]{:S(2)}, u32[]{:S(2)}) collective-permute-start(bf16[2,128,1536]{2,1,0:T(8,128)(2,1)S(1)} %get-tuple-element.277.refs_8_), channel_id=1, source_target_pairs={{0,16},{8,24},{16,0},{24,8},{1,17},{9,25},{17,1},{25,9},{2,18},{10... | collective-permute-start | bytes 2359304 | tf_op jit(solution)/shard_map/ppermute | solution.py:1369
  69.8 21.7 %collective-permute-start.19 = (bf16[192,2176]{1,0:T(8,128)(2,1)}, bf16[192,2176]{1,0:T(8,128)(2,1)S(1)}, u32[]{:S(2)}, u32[]{:S(2)}) collective-permute-start(bf16[192,2176]{1,0:T(8,128)(2,1)} %collective-permute-done.18.ids_0), channel_id=1, source_target_pairs={{0,1},{1,0},{2,3},{3,2},{4,5},{5,4},{6,7},{7,6},{8,9},{9,8},{10,11... | collective-permute-start | bytes 2506760 | tf_op jit(solution)/shard_map/ppermute | solution.py:1369
  70.3 21.7 %collective-permute-start.20 = (bf16[192,2176]{1,0:T(8,128)(2,1)}, bf16[192,2176]{1,0:T(8,128)(2,1)S(1)}, u32[]{:S(2)}, u32[]{:S(2)}) collective-permute-start(bf16[192,2176]{1,0:T(8,128)(2,1)} %shard_map.170.ids_0), channel_id=1, source_target_pairs={{0,6},{1,7},{2,0},{3,1},{4,2},{5,3},{6,4},{7,5},{8,14},{9,15},{10,... | collective-permute-start | bytes 2506760 | tf_op jit(solution)/shard_map/ppermute | solution.py:1369
  77.7 14.6 %collective-permute-start.10 = (bf16[384,1024]{1,0:T(8,128)(2,1)S(1)}, bf16[384,1024]{1,0:T(8,128)(2,1)S(1)}, u32[]{:S(2)}, u32[]{:S(2)}) collective-permute-start(bf16[384,1024]{1,0:T(8,128)(2,1)S(1)} %get-tuple-element.275.refs_4_), channel_id=1, source_target_pairs={{0,8},{8,0},{16,24},{24,16},{1,9},{9,1},{17,25},{25,17},{2,10},{10... | collective-permute-start | bytes 2359304 | tf_op jit(solution)/shard_map/ppermute | solution.py:1369
  77.9 15.0 %collective-permute-start.7 = (bf16[128,1536]{1,0:T(8,128)(2,1)S(1)}, bf16[128,1536]{1,0:T(8,128)(2,1)S(1)}, u32[]{:S(2)}, u32[]{:S(2)}) collective-permute-start(bf16[128,1536]{1,0:T(8,128)(2,1)S(1)} %collective-permute-done.6.rows_2), channel_id=1, source_target_pairs={{0,8},{8,0},{16,24},{24,16},{1,9},{9,1},{17,25},{25,17},{2,10},{10... | collective-permute-start | bytes 1179656 | tf_op jit(solution)/shard_map/ppermute | solution.py:1369
  92.4 12.1 %collective-permute-start.21 = (bf16[96,2176]{1,0:T(8,128)(2,1)S(1)}, bf16[96,2176]{1,0:T(8,128)(2,1)S(1)}, u32[]{:S(2)}, u32[]{:S(2)}) collective-permute-start(bf16[96,2176]{1,0:T(8,128)(2,1)S(1)} %slice.158), channel_id=1, source_target_pairs={{0,1},{1,0},{2,3},{3,2},{4,5},{5,4},{6,7},{7,6},{8,9},{9,8},{10,11... | collective-permute-start | bytes 1253384 | tf_op jit(solution)/shard_map/ppermute | solution.py:1369
  124.3 12.4 %collective-permute-start.23 = (bf16[128,1536]{1,0:T(8,128)(2,1)S(1)}, bf16[128,1536]{1,0:T(8,128)(2,1)S(1)}, u32[]{:S(2)}, u32[]{:S(2)}) collective-permute-start(bf16[128,1536]{1,0:T(8,128)(2,1)S(1)} %copy-done.166), channel_id=1, source_target_pairs={{0,8},{8,0},{16,24},{24,16},{1,9},{9,1},{17,25},{25,17},{2,10},{10... | collective-permute-start | bytes 1179656 | tf_op jit(solution)/shard_map/ppermute | solution.py:1369
  138.1 583.8 %reduce-scatter.2.cloned.1.call-start = ((), (), s32[]{:S(2)}) async-start(), calls=%async_computation.2 | async-start | bytes 3932160 | tf_op jit(solution)/shard_map/reduce_scatter | solution.py:1666
  141.1 12.9 %collective-permute-start.26 = (bf16[128,1536]{1,0:T(8,128)(2,1)S(1)}, bf16[128,1536]{1,0:T(8,128)(2,1)S(1)}, u32[]{:S(2)}, u32[]{:S(2)}) collective-permute-start(bf16[128,1536]{1,0:T(8,128)(2,1)S(1)} %multiply_convert_fusion.2.rows_0), channel_id=1, source_target_pairs={{0,2},{1,3},{2,4},{3,5},{4,6},{5,7},{6,0},{7,1},{8,10},{9,11},{10,... | collective-permute-start | bytes 1179656 | tf_op jit(solution)/shard_map/ppermute | solution.py:1369
  142.4 14.1 %collective-permute-start.27 = (bf16[128,1536]{1,0:T(8,128)(2,1)S(1)}, bf16[128,1536]{1,0:T(8,128)(2,1)S(1)}, u32[]{:S(2)}, u32[]{:S(2)}) collective-permute-start(bf16[128,1536]{1,0:T(8,128)(2,1)S(1)} %multiply_convert_fusion.2.rows_0), channel_id=1, source_target_pairs={{0,1},{1,0},{2,3},{3,2},{4,5},{5,4},{6,7},{7,6},{8,9},{9,8},{10,11... | collective-permute-start | bytes 1179656 | tf_op jit(solution)/shard_map/ppermute | solution.py:1369
  155.0 14.2 %collective-permute-start.29 = (bf16[128,1536]{1,0:T(8,128)(2,1)S(1)}, bf16[128,1536]{1,0:T(8,128)(2,1)S(1)}, u32[]{:S(2)}, u32[]{:S(2)}) collective-permute-start(bf16[128,1536]{1,0:T(8,128)(2,1)S(1)} %collective-permute-done.26.rows_0), channel_id=1, source_target_pairs={{0,1},{1,0},{2,3},{3,2},{4,5},{5,4},{6,7},{7,6},{8,9},{9,8},{10,11... | collective-permute-start | bytes 1179656 | tf_op jit(solution)/shard_map/ppermute | solution.py:1369
  209.7 16.4 %collective-permute-start.38 = (bf16[128,1536]{1,0:T(8,128)(2,1)S(1)}, bf16[128,1536]{1,0:T(8,128)(2,1)S(1)}, u32[]{:S(2)}, u32[]{:S(2)}) collective-permute-start(bf16[128,1536]{1,0:T(8,128)(2,1)S(1)} %add_convert_fusion.19), channel_id=1, source_target_pairs={{0,2},{1,3},{2,4},{3,5},{4,6},{5,7},{6,0},{7,1},{8,10},{9,11},{10,... | collective-permute-start | bytes 1179656 | tf_op jit(solution)/shard_map/ppermute | solution.py:1369
  272.4 12.1 %collective-permute-start.46 = (bf16[128,1536]{1,0:T(8,128)(2,1)S(1)}, bf16[128,1536]{1,0:T(8,128)(2,1)S(1)}, u32[]{:S(2)}, u32[]{:S(2)}) collective-permute-start(bf16[128,1536]{1,0:T(8,128)(2,1)S(1)} %multiply_convert_fusion.rows_0), channel_id=1, source_target_pairs={{0,2},{1,3},{2,4},{3,5},{4,6},{5,7},{6,0},{7,1},{8,10},{9,11},{10,... | collective-permute-start | bytes 1179656 | tf_op jit(solution)/shard_map/ppermute | solution.py:1369
  272.4 14.3 %collective-permute-start.47 = (bf16[128,1536]{1,0:T(8,128)(2,1)S(1)}, bf16[128,1536]{1,0:T(8,128)(2,1)S(1)}, u32[]{:S(2)}, u32[]{:S(2)}) collective-permute-start(bf16[128,1536]{1,0:T(8,128)(2,1)S(1)} %multiply_convert_fusion.rows_0), channel_id=1, source_target_pairs={{0,1},{1,0},{2,3},{3,2},{4,5},{5,4},{6,7},{7,6},{8,9},{9,8},{10,11... | collective-permute-start | bytes 1179656 | tf_op jit(solution)/shard_map/ppermute | solution.py:1369
  285.3 14.6 %collective-permute-start.49 = (bf16[128,1536]{1,0:T(8,128)(2,1)S(1)}, bf16[128,1536]{1,0:T(8,128)(2,1)S(1)}, u32[]{:S(2)}, u32[]{:S(2)}) collective-permute-start(bf16[128,1536]{1,0:T(8,128)(2,1)S(1)} %collective-permute-done.46.rows_0), channel_id=1, source_target_pairs={{0,1},{1,0},{2,3},{3,2},{4,5},{5,4},{6,7},{7,6},{8,9},{9,8},{10,11... | collective-permute-start | bytes 1179656 | tf_op jit(solution)/shard_map/ppermute | solution.py:1369
  295.9 12.5 %collective-permute-start.50 = (bf16[128,1536]{1,0:T(8,128)(2,1)}, bf16[128,1536]{1,0:T(8,128)(2,1)S(1)}, u32[]{:S(2)}, u32[]{:S(2)}) collective-permute-start(bf16[128,1536]{1,0:T(8,128)(2,1)} %copy-done.53), channel_id=1, source_target_pairs={{0,6},{1,7},{2,0},{3,1},{4,2},{5,3},{6,4},{7,5},{8,14},{9,15},{10,... | collective-permute-start | bytes 1179656 | tf_op jit(solution)/shard_map/ppermute | solution.py:1369
  339.8 12.5 %collective-permute-start.58 = (bf16[128,1536]{1,0:T(8,128)(2,1)S(1)}, bf16[128,1536]{1,0:T(8,128)(2,1)S(1)}, u32[]{:S(2)}, u32[]{:S(2)}) collective-permute-start(bf16[128,1536]{1,0:T(8,128)(2,1)S(1)} %add_convert_fusion.15), channel_id=1, source_target_pairs={{0,2},{1,3},{2,4},{3,5},{4,6},{5,7},{6,0},{7,1},{8,10},{9,11},{10,... | collective-permute-start | bytes 1179656 | tf_op jit(solution)/shard_map/ppermute | solution.py:1369
  360.5 13.1 %collective-permute-start.60 = (bf16[128,1664]{1,0:T(8,128)(2,1)S(1)}, bf16[128,1664]{1,0:T(8,128)(2,1)S(1)}, u32[]{:S(2)}, u32[]{:S(2)}) collective-permute-start(bf16[128,1664]{1,0:T(8,128)(2,1)S(1)} %pad_maximum_fusion.grads_0), channel_id=1, source_target_pairs={{0,2},{1,3},{2,4},{3,5},{4,6},{5,7},{6,0},{7,1},{8,10},{9,11},{10,... | collective-permute-start | bytes 1277960 | tf_op jit(solution)/shard_map/ppermute | solution.py:1369
  360.5 17.3 %collective-permute-start.61 = (bf16[128,1664]{1,0:T(8,128)(2,1)S(1)}, bf16[128,1664]{1,0:T(8,128)(2,1)S(1)}, u32[]{:S(2)}, u32[]{:S(2)}) collective-permute-start(bf16[128,1664]{1,0:T(8,128)(2,1)S(1)} %pad_maximum_fusion.grads_0), channel_id=1, source_target_pairs={{0,1},{1,0},{2,3},{3,2},{4,5},{5,4},{6,7},{7,6},{8,9},{9,8},{10,11... | collective-permute-start | bytes 1277960 | tf_op jit(solution)/shard_map/ppermute | solution.py:1369
  373.6 13.0 %collective-permute-start.62 = (bf16[128,1664]{1,0:T(8,128)(2,1)S(1)}, bf16[128,1664]{1,0:T(8,128)(2,1)S(1)}, u32[]{:S(2)}, u32[]{:S(2)}) collective-permute-start(bf16[128,1664]{1,0:T(8,128)(2,1)S(1)} %collective-permute-done.60.grads_0), channel_id=1, source_target_pairs={{0,2},{1,3},{2,4},{3,5},{4,6},{5,7},{6,0},{7,1},{8,10},{9,11},{10,... | collective-permute-start | bytes 1277960 | tf_op jit(solution)/shard_map/ppermute | solution.py:1369
  373.7 16.5 %collective-permute-start.63 = (bf16[128,1664]{1,0:T(8,128)(2,1)S(1)}, bf16[128,1664]{1,0:T(8,128)(2,1)S(1)}, u32[]{:S(2)}, u32[]{:S(2)}) collective-permute-start(bf16[128,1664]{1,0:T(8,128)(2,1)S(1)} %collective-permute-done.60.grads_0), channel_id=1, source_target_pairs={{0,1},{1,0},{2,3},{3,2},{4,5},{5,4},{6,7},{7,6},{8,9},{9,8},{10,11... | collective-permute-start | bytes 1277960 | tf_op jit(solution)/shard_map/ppermute | solution.py:1369
  386.6 12.4 %collective-permute-start.64 = (bf16[128,1664]{1,0:T(8,128)(2,1)}, bf16[128,1664]{1,0:T(8,128)(2,1)S(1)}, u32[]{:S(2)}, u32[]{:S(2)}) collective-permute-start(bf16[128,1664]{1,0:T(8,128)(2,1)} %copy-done.52), channel_id=1, source_target_pairs={{0,6},{1,7},{2,0},{3,1},{4,2},{5,3},{6,4},{7,5},{8,14},{9,15},{10,... | collective-permute-start | bytes 1277960 | tf_op jit(solution)/shard_map/ppermute | solution.py:1369
  424.2 17.6 %collective-permute-start.73 = (bf16[768,1024]{1,0:T(8,128)(2,1)S(1)}, bf16[768,1024]{1,0:T(8,128)(2,1)S(1)}, u32[]{:S(2)}, u32[]{:S(2)}) collective-permute-start(bf16[768,1024]{1,0:T(8,128)(2,1)S(1)} %convolution_convert_fusion.9), channel_id=1, source_target_pairs={{0,8},{8,0},{16,24},{24,16},{1,9},{9,1},{17,25},{25,17},{2,10},{10... | collective-permute-start | bytes 4718600 | tf_op jit(solution)/shard_map/ppermute | solution.py:1369
  426.2 15.7 %collective-permute-start.74 = (bf16[768,1024]{1,0:T(8,128)(2,1)S(1)}, bf16[768,1024]{1,0:T(8,128)(2,1)S(1)}, u32[]{:S(2)}, u32[]{:S(2)}) collective-permute-start(bf16[768,1024]{1,0:T(8,128)(2,1)S(1)} %convolution_convert_fusion.8), channel_id=1, source_target_pairs={{0,8},{8,0},{16,24},{24,16},{1,9},{9,1},{17,25},{25,17},{2,10},{10... | collective-permute-start | bytes 4718600 | tf_op jit(solution)/shard_map/ppermute | solution.py:1369
  431.1 12.8 %collective-permute-start.72 = (bf16[128,1536]{1,0:T(8,128)(2,1)S(1)}, bf16[128,1536]{1,0:T(8,128)(2,1)S(1)}, u32[]{:S(2)}, u32[]{:S(2)}) collective-permute-start(bf16[128,1536]{1,0:T(8,128)(2,1)S(1)} %add_convert_fusion.11), channel_id=1, source_target_pairs={{0,2},{1,3},{2,4},{3,5},{4,6},{5,7},{6,0},{7,1},{8,10},{9,11},{10,... | collective-permute-start | bytes 1179656 | tf_op jit(solution)/shard_map/ppermute | solution.py:1369
  455.3 12.8 %collective-permute-start.76 = (bf16[128,1536]{1,0:T(8,128)(2,1)}, bf16[128,1536]{1,0:T(8,128)(2,1)}, u32[]{:S(2)}, u32[]{:S(2)}) collective-permute-start(bf16[128,1536]{1,0:T(8,128)(2,1)} %get-tuple-element.547.grad_0), channel_id=1, source_target_pairs={{0,8},{8,0},{16,24},{24,16},{1,9},{9,1},{17,25},{25,17},{2,10},{10... | collective-permute-start | bytes 1179656 | tf_op jit(solution)/shard_map/ppermute | solution.py:1369
  483.6 17.4 %collective-permute-start.79 = (bf16[128,1536]{1,0:T(8,128)(2,1)}, bf16[128,1536]{1,0:T(8,128)(2,1)}, u32[]{:S(2)}, u32[]{:S(2)}) collective-permute-start(bf16[128,1536]{1,0:T(8,128)(2,1)} %get-tuple-element.411), channel_id=1, source_target_pairs={{0,8},{8,0},{16,24},{24,16},{1,9},{9,1},{17,25},{25,17},{2,10},{10... | collective-permute-start | bytes 1179656 | tf_op jit(solution)/shard_map/ppermute | solution.py:1369
  488.7 12.2 %collective-permute-start.81 = (bf16[128,1536]{1,0:T(8,128)(2,1)S(1)}, bf16[128,1536]{1,0:T(8,128)(2,1)S(1)}, u32[]{:S(2)}, u32[]{:S(2)}) collective-permute-start(bf16[128,1536]{1,0:T(8,128)(2,1)S(1)} %add_convert_fusion.9), channel_id=1, source_target_pairs={{0,16},{8,24},{16,0},{24,8},{1,17},{9,25},{17,1},{25,9},{2,18},{10... | collective-permute-start | bytes 1179656 | tf_op jit(solution)/shard_map/ppermute | solution.py:1369
  504.4 14.6 %collective-permute-start.82 = (bf16[128,1664]{1,0:T(8,128)(2,1)S(1)}, bf16[128,1664]{1,0:T(8,128)(2,1)}, u32[]{:S(2)}, u32[]{:S(2)}) collective-permute-start(bf16[128,1664]{1,0:T(8,128)(2,1)S(1)} %pad_maximum_fusion.1.grads_0), channel_id=1, source_target_pairs={{0,2},{1,3},{2,4},{3,5},{4,6},{5,7},{6,0},{7,1},{8,10},{9,11},{10,... | collective-permute-start | bytes 1277960 | tf_op jit(solution)/shard_map/ppermute | solution.py:1369
  505.9 16.4 %collective-permute-start.83 = (bf16[128,1664]{1,0:T(8,128)(2,1)S(1)}, bf16[128,1664]{1,0:T(8,128)(2,1)S(1)}, u32[]{:S(2)}, u32[]{:S(2)}) collective-permute-start(bf16[128,1664]{1,0:T(8,128)(2,1)S(1)} %pad_maximum_fusion.1.grads_0), channel_id=1, source_target_pairs={{0,1},{1,0},{2,3},{3,2},{4,5},{5,4},{6,7},{7,6},{8,9},{9,8},{10,11... | collective-permute-start | bytes 1277960 | tf_op jit(solution)/shard_map/ppermute | solution.py:1369
  519.0 13.4 %collective-permute-start.84 = (bf16[128,1664]{1,0:T(8,128)(2,1)}, bf16[128,1664]{1,0:T(8,128)(2,1)S(1)}, u32[]{:S(2)}, u32[]{:S(2)}) collective-permute-start(bf16[128,1664]{1,0:T(8,128)(2,1)} %collective-permute-done.82.grads_0), channel_id=1, source_target_pairs={{0,2},{1,3},{2,4},{3,5},{4,6},{5,7},{6,0},{7,1},{8,10},{9,11},{10,... | collective-permute-start | bytes 1277960 | tf_op jit(solution)/shard_map/ppermute | solution.py:1369
  520.3 15.3 %collective-permute-start.85 = (bf16[128,1664]{1,0:T(8,128)(2,1)}, bf16[128,1664]{1,0:T(8,128)(2,1)S(1)}, u32[]{:S(2)}, u32[]{:S(2)}) collective-permute-start(bf16[128,1664]{1,0:T(8,128)(2,1)} %collective-permute-done.82.grads_0), channel_id=1, source_target_pairs={{0,1},{1,0},{2,3},{3,2},{4,5},{5,4},{6,7},{7,6},{8,9},{9,8},{10,11... | collective-permute-start | bytes 1277960 | tf_op jit(solution)/shard_map/ppermute | solution.py:1369
  535.1 21.0 %collective-permute-start.87 = (bf16[384,1024]{1,0:T(8,128)(2,1)S(1)}, bf16[384,1024]{1,0:T(8,128)(2,1)S(1)}, u32[]{:S(2)}, u32[]{:S(2)}) collective-permute-start(bf16[384,1024]{1,0:T(8,128)(2,1)S(1)} %get-tuple-element.565), channel_id=1, source_target_pairs={{0,16},{8,24},{16,0},{24,8},{1,17},{9,25},{17,1},{25,9},{2,18},{10... | collective-permute-start | bytes 2359304 | tf_op jit(solution)/shard_map/ppermute | solution.py:1369
  570.4 27.7 %collective-permute-start.96 = (bf16[768,1024]{1,0:T(8,128)(2,1)S(1)}, bf16[768,1024]{1,0:T(8,128)(2,1)S(1)}, u32[]{:S(2)}, u32[]{:S(2)}) collective-permute-start(bf16[768,1024]{1,0:T(8,128)(2,1)S(1)} %convolution_convert_fusion.7), channel_id=1, source_target_pairs={{0,8},{8,0},{16,24},{24,16},{1,9},{9,1},{17,25},{25,17},{2,10},{10... | collective-permute-start | bytes 4718600 | tf_op jit(solution)/shard_map/ppermute | solution.py:1369
  572.4 25.8 %collective-permute-start.97 = (bf16[768,1024]{1,0:T(8,128)(2,1)S(1)}, bf16[768,1024]{1,0:T(8,128)(2,1)S(1)}, u32[]{:S(2)}, u32[]{:S(2)}) collective-permute-start(bf16[768,1024]{1,0:T(8,128)(2,1)S(1)} %convolution_convert_fusion.6), channel_id=1, source_target_pairs={{0,8},{8,0},{16,24},{24,16},{1,9},{9,1},{17,25},{25,17},{2,10},{10... | collective-permute-start | bytes 4718600 | tf_op jit(solution)/shard_map/ppermute | solution.py:1369
  575.0 23.2 %collective-permute-start.98 = (bf16[512,1536]{1,0:T(8,128)(2,1)S(1)}, bf16[512,1536]{1,0:T(8,128)(2,1)S(1)}, u32[]{:S(2)}, u32[]{:S(2)}) collective-permute-start(bf16[512,1536]{1,0:T(8,128)(2,1)S(1)} %convolution_convert_fusion.3), channel_id=1, source_target_pairs={{0,8},{8,0},{16,24},{24,16},{1,9},{9,1},{17,25},{25,17},{2,10},{10... | collective-permute-start | bytes 4718600 | tf_op jit(solution)/shard_map/ppermute | solution.py:1369
  577.4 18.6 %collective-permute-start.99 = (bf16[384,1024]{1,0:T(8,128)(2,1)S(1)}, bf16[384,1024]{1,0:T(8,128)(2,1)S(1)}, u32[]{:S(2)}, u32[]{:S(2)}) collective-permute-start(bf16[384,1024]{1,0:T(8,128)(2,1)S(1)} %copy-done.64), channel_id=1, source_target_pairs={{0,16},{8,24},{16,0},{24,8},{1,17},{9,25},{17,1},{25,9},{2,18},{10... | collective-permute-start | bytes 2359304 | tf_op jit(solution)/shard_map/ppermute | solution.py:1369
  586.8 14.8 %collective-permute-start.95 = (bf16[128,1536]{1,0:T(8,128)(2,1)S(1)}, bf16[128,1536]{1,0:T(8,128)(2,1)S(1)}, u32[]{:S(2)}, u32[]{:S(2)}) collective-permute-start(bf16[128,1536]{1,0:T(8,128)(2,1)S(1)} %add_convert_fusion.7), channel_id=1, source_target_pairs={{0,2},{1,3},{2,4},{3,5},{4,6},{5,7},{6,0},{7,1},{8,10},{9,11},{10,... | collective-permute-start | bytes 1179656 | tf_op jit(solution)/shard_map/ppermute | solution.py:1369
  609.3 12.6 %collective-permute-start.108 = (bf16[192,1152]{1,0:T(8,128)(2,1)}, bf16[192,1152]{1,0:T(8,128)(2,1)}, u32[]{:S(2)}, u32[]{:S(2)}) collective-permute-start(bf16[192,1152]{1,0:T(8,128)(2,1)} %bitcast.47), channel_id=1, source_target_pairs={{0,1},{1,0},{2,3},{3,2},{4,5},{5,4},{6,7},{7,6},{8,9},{9,8},{10,11... | collective-permute-start | bytes 1327112 | tf_op jit(solution)/shard_map/ppermute | solution.py:1369
  614.1 34.8 %collective-permute-start.107 = (bf16[192,1152]{1,0:T(8,128)(2,1)}, bf16[192,1152]{1,0:T(8,128)(2,1)}, u32[]{:S(2)}, u32[]{:S(2)}) collective-permute-start(bf16[192,1152]{1,0:T(8,128)(2,1)} %bitcast.190), channel_id=1, source_target_pairs={{0,1},{1,0},{2,3},{3,2},{4,5},{5,4},{6,7},{7,6},{8,9},{9,8},{10,11... | collective-permute-start | bytes 1327112 | tf_op jit(solution)/shard_map/ppermute | solution.py:1369
  624.1 24.8 %collective-permute-start.109 = (bf16[192,1152]{1,0:T(8,128)(2,1)}, bf16[192,1152]{1,0:T(8,128)(2,1)}, u32[]{:S(2)}, u32[]{:S(2)}) collective-permute-start(bf16[192,1152]{1,0:T(8,128)(2,1)} %fusion.16), channel_id=1, source_target_pairs={{0,2},{1,3},{2,4},{3,5},{4,6},{5,7},{6,0},{7,1},{8,10},{9,11},{10,... | collective-permute-start | bytes 1327112 | tf_op jit(solution)/shard_map/ppermute | solution.py:1369
  640.0 20.2 %collective-permute-start.105 = (bf16[128,1536]{1,0:T(8,128)(2,1)}, bf16[128,1536]{1,0:T(8,128)(2,1)}, u32[]{:S(2)}, u32[]{:S(2)}) collective-permute-start(bf16[128,1536]{1,0:T(8,128)(2,1)} %get-tuple-element.487), channel_id=1, source_target_pairs={{0,8},{8,0},{16,24},{24,16},{1,9},{9,1},{17,25},{25,17},{2,10},{10... | collective-permute-start | bytes 1179656 | tf_op jit(solution)/shard_map/ppermute | solution.py:1369
  642.8 58.2 %collective-permute-start.104 = (bf16[128,1536]{1,0:T(8,128)(2,1)}, bf16[128,1536]{1,0:T(8,128)(2,1)S(1)}, u32[]{:S(2)}, u32[]{:S(2)}) collective-permute-start(bf16[128,1536]{1,0:T(8,128)(2,1)} %get-tuple-element.485), channel_id=1, source_target_pairs={{0,8},{8,0},{16,24},{24,16},{1,9},{9,1},{17,25},{25,17},{2,10},{10... | collective-permute-start | bytes 1179656 | tf_op jit(solution)/shard_map/ppermute | solution.py:1369
  650.9 28.2 %collective-permute-start.112 = (bf16[192,1152]{1,0:T(8,128)(2,1)}, bf16[192,1152]{1,0:T(8,128)(2,1)}, u32[]{:S(2)}, u32[]{:S(2)}) collective-permute-start(bf16[192,1152]{1,0:T(8,128)(2,1)} %fusion.18), channel_id=1, source_target_pairs={{0,2},{1,3},{2,4},{3,5},{4,6},{5,7},{6,0},{7,1},{8,10},{9,11},{10,... | collective-permute-start | bytes 1327112 | tf_op jit(solution)/shard_map/ppermute | solution.py:1369
  661.4 31.2 %collective-permute-start.106 = (bf16[128,1536]{1,0:T(8,128)(2,1)S(1)}, bf16[128,1536]{1,0:T(8,128)(2,1)S(1)}, u32[]{:S(2)}, u32[]{:S(2)}) collective-permute-start(bf16[128,1536]{1,0:T(8,128)(2,1)S(1)} %add_convert_fusion.5), channel_id=1, source_target_pairs={{0,16},{8,24},{16,0},{24,8},{1,17},{9,25},{17,1},{25,9},{2,18},{10... | collective-permute-start | bytes 1179656 | tf_op jit(solution)/shard_map/ppermute | solution.py:1369
  663.5 16.5 %collective-permute-start.113 = (bf16[192,1152]{1,0:T(8,128)(2,1)S(1)}, bf16[192,1152]{1,0:T(8,128)(2,1)S(1)}, u32[]{:S(2)}, u32[]{:S(2)}) collective-permute-start(bf16[192,1152]{1,0:T(8,128)(2,1)S(1)} %fusion.19), channel_id=1, source_target_pairs={{0,6},{1,7},{2,0},{3,1},{4,2},{5,3},{6,4},{7,5},{8,14},{9,15},{10,... | collective-permute-start | bytes 1327112 | tf_op jit(solution)/shard_map/ppermute | solution.py:1369
  677.8 13.1 %collective-permute-start.111 = (bf16[192,1152]{1,0:T(8,128)(2,1)S(1)}, bf16[192,1152]{1,0:T(8,128)(2,1)S(1)}, u32[]{:S(2)}, u32[]{:S(2)}) collective-permute-start(bf16[192,1152]{1,0:T(8,128)(2,1)S(1)} %bitcast.188), channel_id=1, source_target_pairs={{0,1},{1,0},{2,3},{3,2},{4,5},{5,4},{6,7},{7,6},{8,9},{9,8},{10,11... | collective-permute-start | bytes 1327112 | tf_op jit(solution)/shard_map/ppermute | solution.py:1369
  679.1 24.5 %collective-permute-start.114 = (bf16[192,1152]{1,0:T(8,128)(2,1)S(1)}, bf16[192,1152]{1,0:T(8,128)(2,1)S(1)}, u32[]{:S(2)}, u32[]{:S(2)}) collective-permute-start(bf16[192,1152]{1,0:T(8,128)(2,1)S(1)} %bitcast.192), channel_id=1, source_target_pairs={{0,1},{1,0},{2,3},{3,2},{4,5},{5,4},{6,7},{7,6},{8,9},{9,8},{10,11... | collective-permute-start | bytes 1327112 | tf_op jit(solution)/shard_map/ppermute | solution.py:1369
  680.1 49.9 %collective-permute-start.120 = (bf16[384,1024]{1,0:T(8,128)(2,1)}, bf16[384,1024]{1,0:T(8,128)(2,1)}, u32[]{:S(2)}, u32[]{:S(2)}) collective-permute-start(bf16[384,1024]{1,0:T(8,128)(2,1)} %get-tuple-element.562), channel_id=1, source_target_pairs={{0,16},{8,24},{16,0},{24,8},{1,17},{9,25},{17,1},{25,9},{2,18},{10... | collective-permute-start | bytes 2359304 | tf_op jit(solution)/shard_map/ppermute | solution.py:1369
  690.9 12.7 %collective-permute-start.116 = (bf16[192,1152]{1,0:T(8,128)(2,1)S(1)}, bf16[192,1152]{1,0:T(8,128)(2,1)S(1)}, u32[]{:S(2)}, u32[]{:S(2)}) collective-permute-start(bf16[192,1152]{1,0:T(8,128)(2,1)S(1)} %fusion.11), channel_id=1, source_target_pairs={{0,2},{1,3},{2,4},{3,5},{4,6},{5,7},{6,0},{7,1},{8,10},{9,11},{10,... | collective-permute-start | bytes 1327112 | tf_op jit(solution)/shard_map/ppermute | solution.py:1369
  695.5 34.4 %collective-permute-start.121 = (bf16[384,1024]{1,0:T(8,128)(2,1)S(1)}, bf16[384,1024]{1,0:T(8,128)(2,1)S(1)}, u32[]{:S(2)}, u32[]{:S(2)}) collective-permute-start(bf16[384,1024]{1,0:T(8,128)(2,1)S(1)} %get-tuple-element.560), channel_id=1, source_target_pairs={{0,16},{8,24},{16,0},{24,8},{1,17},{9,25},{17,1},{25,9},{2,18},{10... | collective-permute-start | bytes 2359304 | tf_op jit(solution)/shard_map/ppermute | solution.py:1369
  701.0 37.0 %collective-permute-start.126 = (bf16[256,1536]{1,0:T(8,128)(2,1)S(1)}, bf16[256,1536]{1,0:T(8,128)(2,1)S(1)}, u32[]{:S(2)}, u32[]{:S(2)}) collective-permute-start(bf16[256,1536]{1,0:T(8,128)(2,1)S(1)} %get-tuple-element.557), channel_id=1, source_target_pairs={{0,16},{8,24},{16,0},{24,8},{1,17},{9,25},{17,1},{25,9},{2,18},{10... | collective-permute-start | bytes 2359304 | tf_op jit(solution)/shard_map/ppermute | solution.py:1369
  704.6 12.0 %collective-permute-start.117 = (bf16[192,1152]{1,0:T(8,128)(2,1)S(1)}, bf16[192,1152]{1,0:T(8,128)(2,1)S(1)}, u32[]{:S(2)}, u32[]{:S(2)}) collective-permute-start(bf16[192,1152]{1,0:T(8,128)(2,1)S(1)} %bitcast.191), channel_id=1, source_target_pairs={{0,1},{1,0},{2,3},{3,2},{4,5},{5,4},{6,7},{7,6},{8,9},{9,8},{10,11... | collective-permute-start | bytes 1327112 | tf_op jit(solution)/shard_map/ppermute | solution.py:1369
  705.3 20.4 %collective-permute-start.119 = (bf16[192,1152]{1,0:T(8,128)(2,1)}, bf16[192,1152]{1,0:T(8,128)(2,1)}, u32[]{:S(2)}, u32[]{:S(2)}) collective-permute-start(bf16[192,1152]{1,0:T(8,128)(2,1)} %fusion.13), channel_id=1, source_target_pairs={{0,2},{1,3},{2,4},{3,5},{4,6},{5,7},{6,0},{7,1},{8,10},{9,11},{10,... | collective-permute-start | bytes 1327112 | tf_op jit(solution)/shard_map/ppermute | solution.py:1369
  (241 other events, 2712.8 us)
Sparse Core Ops, SparseCore 0:
  138.2 66.0 all-gather.1
  614.1 38.9 reduce-scatter.1

commit v7 on v6

--- a/solution.py
+++ b/solution.py
@@ -1672,8 +1672,8 @@
         def backward_work(group, pair):
             if i == 0 and group == 0:
                 pair = (after(pair[0], whole_down, *jax.tree.leaves(halves)), pair[1])
-            if i == 0 and group == 3:
-                pair = (after(pair[0], expert_grads[0][0][1]), pair[1])
+            if i == 0 and group > 1:
+                pair = (after(pair[0], expert_grads[0][group - 2][1]), pair[1])
             outs = experts_backward(
                 group, pair_total, ctx_ref, pair, probs, gate, up, small, own_experts[i],
                 expert_weights[i], kept, i == 0,
@@ -1696,11 +1696,10 @@
                 came.append(swap_core(dot_tn(after(part, start)[:, half:], grads).astype(low)))
             return came
 
-        last_gate = [expert_grads[0][1][1]] if i == 0 else []
         grad_second, small_grads, _ = scatter_fsdp(
             parts,
             (
-                lambda start: [*first_beside(start), *last_gate],
+                first_beside,
                 lambda start: dot_tn(after(rows_second, start), grad_logits),
                 lambda start: [],
             ),

time: 760 us -> 752 us (0.989)
    unnamed x353 -> x349, local copies, waits for them, and re-layouts: 17.9 us -> 18.2 us
  transfers between devices with their start and end apart: 129 -> 129, of which waited for: 55 -> 54; matrix products, arithmetic and copies ran while one was open for 14% -> 14% of each run, Pallas kernels for 22% -> 23%
where the time goes in v7:
time: 752 us; the launch traced here: 747 us
  waiting for transfers between devices  261 us (35%)
  Pallas kernels  207 us (28%)
  starting transfers between devices  126 us (17%)
  other arithmetic  52.9 us (7%)
  matrix products  43 us (6%)
  local copies, waits for them, and re-layouts  40 us (5%)
  between operations  16.5 us (2%)
    ppermute x127, waiting for transfers between devices, rotate_ranks(): lax.ppermute(values_in, axis_name, [(i, target_of(i)) for i in range(tota...  261 us
    ppermute x127, starting transfers between devices, rotate_ranks(): lax.ppermute(values_in, axis_name, [(i, target_of(i)) for i in range(tota...  126 us
    pallas_call x8, Pallas kernels, experts_backward(): pl.pallas_call(functools.partial(experts_backward_body, len(weights), rin...  63.2 us
    pallas_call x8, Pallas kernels, experts_forward(): pl.pallas_call(functools.partial(experts_forward_body, len(weights), grou...  60.7 us
    dot_general x17, matrix products, mm(): return lax.dot_general(a, b, dims, preferred_element_type=jnp.float32)  43 us
    pallas_call x2, Pallas kernels, attention_backward(): pl.pallas_call(attention_backward_body, in_specs=[smem()] + [anywhere()]...  27 us
    pallas_call x2, Pallas kernels, attention_forward(): pl.pallas_call(functools.partial(attention_forward_body, gain_lane), in_s...  22.7 us
    unnamed x349, local copies, waits for them, and re-layouts  18.2 us
  transfers between devices with their start and end apart: 129, of which 54 were waited for; matrix products, arithmetic and copies ran while one was open for 14% of the time, Pallas kernels for 23%

profile of v7, /device:TPU:0, one launch (start us, length us, event | category | flops | bytes accessed | tf_op | source)
XLA Modules:
  0.0 746.6 jit_solution(14985909957054527414)
XLA Ops:
  13.1 4.5 collective-permute-done.1.block_2
  29.5 17.6 %collective-permute-done.3.refs_2_ = bf16[384,1024]{1,0:T(8,128)(2,1)S(1)} collective-permute-done((bf16[384,1024]{1,0:T(8,128)(2,1)S(1)}, bf16[384,1024]{1,0:T(8,128)(2,1)S(1)}, u32[]{:S(2)}, u32[]{:S(2)}) %collective-permute-start.3) | collective-permute-done | bytes 786464 | tf_op jit(solution)/shard_map/ppermute | solution.py:1369
  52.4 13.1 %collective-permute-done.4.refs_6_ = bf16[384,1024]{1,0:T(8,128)(2,1)} collective-permute-done((bf16[384,1024]{1,0:T(8,128)(2,1)S(1)}, bf16[384,1024]{1,0:T(8,128)(2,1)}, u32[]{:S(2)}, u32[]{:S(2)}) %collective-permute-start.4) | collective-permute-done | bytes 786464 | tf_op jit(solution)/shard_map/ppermute | solution.py:1369
  78.5 13.0 %collective-permute-done.13.refs_10_ = bf16[2,128,1536]{2,1,0:T(8,128)(2,1)S(1)} collective-permute-done((bf16[2,128,1536]{2,1,0:T(8,128)(2,1)S(1)}, bf16[2,128,1536]{2,1,0:T(8,128)(2,1)S(1)}, u32[]{:S(2)}, u32[]{:S(2)}) %collective-permute-start.13) | collective-permute-done | bytes 786464 | tf_op jit(solution)/shard_map/ppermute | solution.py:1369
  96.1 8.4 %collective-permute-done.21 = bf16[96,2176]{1,0:T(8,128)(2,1)S(1)} collective-permute-done((bf16[96,2176]{1,0:T(8,128)(2,1)S(1)}, bf16[96,2176]{1,0:T(8,128)(2,1)S(1)}, u32[]{:S(2)}, u32[]{:S(2)}) %collective-permute-start.21) | collective-permute-done | bytes 417824 | tf_op jit(solution)/shard_map/ppermute | solution.py:1369
  105.8 5.0 shard_map.171
  111.6 11.7 %shard_map.172 = (bf16[128,1536]{1,0:T(8,128)(2,1)}, bf16[128,1536]{1,0:T(8,128)(2,1)}, bf16[128,1536]{1,0:T(8,128)(2,1)}, bf16[128,1536]{1,0:T(8,128)(2,1)}, bf...) custom-call(s32[1]{0:T(128)} %bitcast.1.ctx_ref, ...), custom_call_target="tpu_custom_call" | custom-call | flops 2013265920 | bytes 6291456 | tf_op jit(solution)/shard_map/pallas_call | solution.py:984
  128.6 8.1 %collective-permute-done.25 = bf16[128,1536]{1,0:T(8,128)(2,1)S(1)} collective-permute-done((bf16[128,1536]{1,0:T(8,128)(2,1)S(1)}, bf16[128,1536]{1,0:T(8,128)(2,1)S(1)}, u32[]{:S(2)}, u32[]{:S(2)}) %collective-permute-start.25) | collective-permute-done | bytes 393248 | tf_op jit(solution)/shard_map/ppermute | solution.py:1369
  144.0 10.1 %collective-permute-done.26.rows_0 = bf16[128,1536]{1,0:T(8,128)(2,1)S(1)} collective-permute-done((bf16[128,1536]{1,0:T(8,128)(2,1)S(1)}, bf16[128,1536]{1,0:T(8,128)(2,1)S(1)}, u32[]{:S(2)}, u32[]{:S(2)}) %collective-permute-start.26) | collective-permute-done | bytes 393248 | tf_op jit(solution)/shard_map/ppermute | solution.py:1369
  157.3 7.5 %shard_map.173 = (bf16[128,1536]{1,0:T(8,128)(2,1)}, bf16[128,1536]{1,0:T(8,128)(2,1)}, bf16[1024,1536]{1,0:T(8,128)(2,1)}, bf16[1024,1024]{1,0:T(8,128)(2,1)}, ...) custom-call(s32[1]{0:T(128)} %bitcast.1.ctx_ref, bf16[128,1536]{1,0:T(8,128)(2,1)} %copy-done.54, ...), custom_call_target="tpu_custom_call" | custom-call | flops 2415919104 | bytes 9437184 | tf_op jit(solution)/shard_map/pallas_call | solution.py:688
  170.0 7.6 %shard_map.174 = (bf16[128,1536]{1,0:T(8,128)(2,1)}, bf16[128,1536]{1,0:T(8,128)(2,1)}, bf16[1024,1536]{1,0:T(8,128)(2,1)}, bf16[1024,1024]{1,0:T(8,128)(2,1)}, ...) custom-call(s32[1]{0:T(128)} %bitcast.1.ctx_ref, ...), custom_call_target="tpu_custom_call", output_to_operand_aliasing={{2}: (19, {}), {3}: (20, {}), {4}: (21, {}), {5}: (22, {})} | custom-call | flops 2415919104 | bytes 9437184 | tf_op jit(solution)/shard_map/pallas_call | solution.py:688
  180.0 7.5 %shard_map.175 = (bf16[128,1536]{1,0:T(8,128)(2,1)}, bf16[128,1536]{1,0:T(8,128)(2,1)}, bf16[1024,1536]{1,0:T(8,128)(2,1)}, bf16[1024,1024]{1,0:T(8,128)(2,1)}, ...) custom-call(s32[1]{0:T(128)} %bitcast.1.ctx_ref, ...), custom_call_target="tpu_custom_call", output_to_operand_aliasing={{2}: (19, {}), {3}: (20, {}), {4}: (21, {}), {5}: (22, {})} | custom-call | flops 2415919104 | bytes 9437184 | tf_op jit(solution)/shard_map/pallas_call | solution.py:688
  189.1 7.6 %shard_map.176 = (bf16[128,1536]{1,0:T(8,128)(2,1)}, bf16[128,1536]{1,0:T(8,128)(2,1)}, bf16[1024,1536]{1,0:T(8,128)(2,1)}, bf16[1024,1024]{1,0:T(8,128)(2,1)}, ...) custom-call(s32[1]{0:T(128)} %bitcast.1.ctx_ref, ...), custom_call_target="tpu_custom_call", output_to_operand_aliasing={{2}: (19, {}), {3}: (20, {}), {4}: (21, {}), {5}: (22, {})} | custom-call | flops 2415919104 | bytes 9437184 | tf_op jit(solution)/shard_map/pallas_call | solution.py:688
  198.5 6.4 collective-permute-done.33
  209.8 10.1 %collective-permute-done.36 = bf16[128,1536]{1,0:T(8,128)(2,1)S(1)} collective-permute-done((bf16[128,1536]{1,0:T(8,128)(2,1)S(1)}, bf16[128,1536]{1,0:T(8,128)(2,1)S(1)}, u32[]{:S(2)}, u32[]{:S(2)}) %collective-permute-start.36) | collective-permute-done | bytes 393248 | tf_op jit(solution)/shard_map/ppermute | solution.py:1369
  220.6 4.9 shard_map.177
  228.0 5.5 collective-permute-done.39
  235.8 6.5 collective-permute-done.41.rows_2
  244.8 10.9 %shard_map.178 = (bf16[128,1536]{1,0:T(8,128)(2,1)}, bf16[128,1536]{1,0:T(8,128)(2,1)}, bf16[128,1536]{1,0:T(8,128)(2,1)}, bf16[128,1536]{1,0:T(8,128)(2,1)}, bf...) custom-call(s32[1]{0:T(128)} %bitcast.1.ctx_ref, ...), custom_call_target="tpu_custom_call" | custom-call | flops 2013265920 | bytes 6291456 | tf_op jit(solution)/shard_map/pallas_call | solution.py:984
  260.1 9.9 %collective-permute-done.45 = bf16[128,1536]{1,0:T(8,128)(2,1)S(1)} collective-permute-done((bf16[128,1536]{1,0:T(8,128)(2,1)S(1)}, bf16[128,1536]{1,0:T(8,128)(2,1)S(1)}, u32[]{:S(2)}, u32[]{:S(2)}) %collective-permute-start.45) | collective-permute-done | bytes 393248 | tf_op jit(solution)/shard_map/ppermute | solution.py:1369
  273.9 10.6 %collective-permute-done.46.rows_0 = bf16[128,1536]{1,0:T(8,128)(2,1)S(1)} collective-permute-done((bf16[128,1536]{1,0:T(8,128)(2,1)S(1)}, bf16[128,1536]{1,0:T(8,128)(2,1)S(1)}, u32[]{:S(2)}, u32[]{:S(2)}) %collective-permute-start.46) | collective-permute-done | bytes 393248 | tf_op jit(solution)/shard_map/ppermute | solution.py:1369
  287.5 7.6 %shard_map.179 = (bf16[128,1536]{1,0:T(8,128)(2,1)}, bf16[128,1536]{1,0:T(8,128)(2,1)}, bf16[1024,1536]{1,0:T(8,128)(2,1)}, bf16[1024,1024]{1,0:T(8,128)(2,1)}, ...) custom-call(s32[1]{0:T(128)} %bitcast.1.ctx_ref, bf16[128,1536]{1,0:T(8,128)(2,1)} %copy-done.53, ...), custom_call_target="tpu_custom_call" | custom-call | flops 2415919104 | bytes 9437184 | tf_op jit(solution)/shard_map/pallas_call | solution.py:688
  295.8 3.5 collective-permute-start.50
  300.7 7.6 %shard_map.180 = (bf16[128,1536]{1,0:T(8,128)(2,1)}, bf16[128,1536]{1,0:T(8,128)(2,1)}, bf16[1024,1536]{1,0:T(8,128)(2,1)}, bf16[1024,1024]{1,0:T(8,128)(2,1)}, ...) custom-call(s32[1]{0:T(128)} %bitcast.1.ctx_ref, ...), custom_call_target="tpu_custom_call", output_to_operand_aliasing={{2}: (8, {}), {3}: (9, {}), {4}: (10, {}), {5}: (11, {})} | custom-call | flops 2415919104 | bytes 9437184 | tf_op jit(solution)/shard_map/pallas_call | solution.py:688
  310.6 7.6 %shard_map.181 = (bf16[128,1536]{1,0:T(8,128)(2,1)}, bf16[128,1536]{1,0:T(8,128)(2,1)}, bf16[1024,1536]{1,0:T(8,128)(2,1)}, bf16[1024,1024]{1,0:T(8,128)(2,1)}, ...) custom-call(s32[1]{0:T(128)} %bitcast.1.ctx_ref, ...), custom_call_target="tpu_custom_call", output_to_operand_aliasing={{2}: (8, {}), {3}: (9, {}), {4}: (10, {}), {5}: (11, {})} | custom-call | flops 2415919104 | bytes 9437184 | tf_op jit(solution)/shard_map/pallas_call | solution.py:688
  319.0 7.6 %shard_map.182 = (bf16[128,1536]{1,0:T(8,128)(2,1)}, bf16[128,1536]{1,0:T(8,128)(2,1)}, bf16[1024,1536]{1,0:T(8,128)(2,1)}, bf16[1024,1024]{1,0:T(8,128)(2,1)}, ...) custom-call(s32[1]{0:T(128)} %bitcast.1.ctx_ref, ...), custom_call_target="tpu_custom_call", output_to_operand_aliasing={{2}: (8, {}), {3}: (9, {}), {4}: (10, {}), {5}: (11, {})} | custom-call | flops 2415919104 | bytes 9437184 | tf_op jit(solution)/shard_map/pallas_call | solution.py:688
  328.3 6.7 collective-permute-done.53
  339.8 10.2 %collective-permute-done.56 = bf16[128,1536]{1,0:T(8,128)(2,1)S(1)} collective-permute-done((bf16[128,1536]{1,0:T(8,128)(2,1)S(1)}, bf16[128,1536]{1,0:T(8,128)(2,1)S(1)}, u32[]{:S(2)}, u32[]{:S(2)}) %collective-permute-start.56) | collective-permute-done | bytes 393248 | tf_op jit(solution)/shard_map/ppermute | solution.py:1369
  352.2 6.9 collective-permute-done.57
  360.5 5.3 collective-permute-start.61
  365.8 7.7 %collective-permute-done.60.grads_0 = bf16[128,1664]{1,0:T(8,128)(2,1)S(1)} collective-permute-done((bf16[128,1664]{1,0:T(8,128)(2,1)S(1)}, bf16[128,1664]{1,0:T(8,128)(2,1)S(1)}, u32[]{:S(2)}, u32[]{:S(2)}) %collective-permute-start.60) | collective-permute-done | bytes 426016 | tf_op jit(solution)/shard_map/ppermute | solution.py:1369
  373.7 4.1 collective-permute-start.63
  378.6 7.9 %shard_map.183 = (bf16[128,1536]{1,0:T(8,128)(2,1)}, bf16[128,1536]{1,0:T(8,128)(2,1)}, bf16[1024,1536]{1,0:T(8,128)(2,1)}, bf16[1024,1024]{1,0:T(8,128)(2,1)}, ...) custom-call(s32[1]{0:T(128)} %bitcast.1.ctx_ref, bf16[128,1664]{1,0:T(8,128)(2,1)} %copy-done.52, ...), custom_call_target="tpu_custom_call" | custom-call | flops 2415919104 | bytes 9437184 | tf_op jit(solution)/shard_map/pallas_call | solution.py:841
  386.6 3.7 collective-permute-start.64
  391.0 7.9 %shard_map.184 = (bf16[128,1536]{1,0:T(8,128)(2,1)}, bf16[128,1536]{1,0:T(8,128)(2,1)}, bf16[1024,1536]{1,0:T(8,128)(2,1)}, bf16[1024,1024]{1,0:T(8,128)(2,1)}, ...) custom-call(s32[1]{0:T(128)} %bitcast.1.ctx_ref, ...), custom_call_target="tpu_custom_call", output_to_operand_aliasing={{2}: (9, {}), {3}: (10, {}), {4}: (11, {}), {5}: (12, {}), ... | custom-call | flops 2415919104 | bytes 9437184 | tf_op jit(solution)/shard_map/pallas_call | solution.py:841
  401.8 7.9 %shard_map.185 = (bf16[128,1536]{1,0:T(8,128)(2,1)}, bf16[128,1536]{1,0:T(8,128)(2,1)}, bf16[1024,1536]{1,0:T(8,128)(2,1)}, bf16[1024,1024]{1,0:T(8,128)(2,1)}, ...) custom-call(s32[1]{0:T(128)} %bitcast.1.ctx_ref, ...), custom_call_target="tpu_custom_call", output_to_operand_aliasing={{2}: (9, {}), {3}: (10, {}), {4}: (11, {}), {5}: (12, {}), ... | custom-call | flops 2415919104 | bytes 9437184 | tf_op jit(solution)/shard_map/pallas_call | solution.py:841
  410.5 8.0 %shard_map.186 = (bf16[128,1536]{1,0:T(8,128)(2,1)}, bf16[128,1536]{1,0:T(8,128)(2,1)}, bf16[1024,1536]{1,0:T(8,128)(2,1)}, bf16[1024,1024]{1,0:T(8,128)(2,1)}, ...) custom-call(s32[1]{0:T(128)} %bitcast.1.ctx_ref, ...), custom_call_target="tpu_custom_call", output_to_operand_aliasing={{2}: (9, {}), {3}: (10, {}), {4}: (11, {}), {5}: (12, {}), ... | custom-call | flops 2415919104 | bytes 9437184 | tf_op jit(solution)/shard_map/pallas_call | solution.py:841
  420.6 3.6 convolution_convert_fusion.9
  426.7 3.5 collective-permute-done.69
  431.0 8.8 %collective-permute-done.70 = bf16[128,1536]{1,0:T(8,128)(2,1)S(1)} collective-permute-done((bf16[128,1536]{1,0:T(8,128)(2,1)S(1)}, bf16[128,1536]{1,0:T(8,128)(2,1)S(1)}, u32[]{:S(2)}, u32[]{:S(2)}) %collective-permute-start.70) | collective-permute-done | bytes 393248 | tf_op jit(solution)/shard_map/ppermute | solution.py:1369
  443.8 4.0 collective-permute-done.71
  455.4 6.7 collective-permute-done.77.grad_2
  468.0 13.5 %shard_map.187 = (bf16[128,1536]{1,0:T(8,128)(2,1)}, bf16[128,1536]{1,0:T(8,128)(2,1)}, bf16[128,1536]{1,0:T(8,128)(2,1)}, bf16[128,1536]{1,0:T(8,128)(2,1)}, bf...) custom-call(s32[1]{0:T(128)} %bitcast.1.ctx_ref, ...), custom_call_target="tpu_custom_call" | custom-call | flops 2617245696 | bytes 7864320 | tf_op jit(solution)/shard_map/pallas_call | solution.py:1111
  490.4 3.5 convolution_convert_fusion.5.out
  496.8 4.2 shard_map.188
  511.0 5.0 convolution_convert_fusion
  522.8 7.9 %shard_map.189 = (bf16[128,1536]{1,0:T(8,128)(2,1)}, bf16[128,1536]{1,0:T(8,128)(2,1)}, bf16[1024,1536]{1,0:T(8,128)(2,1)}, bf16[1024,1024]{1,0:T(8,128)(2,1)}, ...) custom-call(s32[1]{0:T(128)} %bitcast.1.ctx_ref, bf16[128,1664]{1,0:T(8,128)(2,1)} %copy-done.50, ...), custom_call_target="tpu_custom_call" | custom-call | flops 2415919104 | bytes 9437184 | tf_op jit(solution)/shard_map/pallas_call | solution.py:841
  537.1 7.8 %shard_map.190 = (bf16[128,1536]{1,0:T(8,128)(2,1)}, bf16[128,1536]{1,0:T(8,128)(2,1)}, bf16[1024,1536]{1,0:T(8,128)(2,1)}, bf16[1024,1024]{1,0:T(8,128)(2,1)}, ...) custom-call(s32[1]{0:T(128)} %bitcast.1.ctx_ref, ...), custom_call_target="tpu_custom_call", output_to_operand_aliasing={{2}: (20, {}), {3}: (21, {}), {4}: (22, {}), {5}: (23, {}),... | custom-call | flops 2415919104 | bytes 9437184 | tf_op jit(solution)/shard_map/pallas_call | solution.py:841
  546.6 7.8 %shard_map.191 = (bf16[128,1536]{1,0:T(8,128)(2,1)}, bf16[128,1536]{1,0:T(8,128)(2,1)}, bf16[1024,1536]{1,0:T(8,128)(2,1)}, bf16[1024,1024]{1,0:T(8,128)(2,1)}, ...) custom-call(s32[1]{0:T(128)} %bitcast.1.ctx_ref, ...), custom_call_target="tpu_custom_call", output_to_operand_aliasing={{2}: (20, {}), {3}: (21, {}), {4}: (22, {}), {5}: (23, {}),... | custom-call | flops 2415919104 | bytes 9437184 | tf_op jit(solution)/shard_map/pallas_call | solution.py:841
  556.7 8.0 %shard_map.192 = (bf16[128,1536]{1,0:T(8,128)(2,1)}, bf16[128,1536]{1,0:T(8,128)(2,1)}, bf16[1024,1536]{1,0:T(8,128)(2,1)}, bf16[1024,1024]{1,0:T(8,128)(2,1)}, ...) custom-call(s32[1]{0:T(128)} %bitcast.1.ctx_ref, ...), custom_call_target="tpu_custom_call", output_to_operand_aliasing={{2}: (20, {}), {3}: (21, {}), {4}: (22, {}), {5}: (23, {}),... | custom-call | flops 2415919104 | bytes 9437184 | tf_op jit(solution)/shard_map/pallas_call | solution.py:841
  566.9 3.6 convolution_convert_fusion.7
  577.9 9.0 %collective-permute-done.94 = bf16[128,1536]{1,0:T(8,128)(2,1)S(1)} collective-permute-done((bf16[128,1536]{1,0:T(8,128)(2,1)S(1)}, bf16[128,1536]{1,0:T(8,128)(2,1)S(1)}, u32[]{:S(2)}, u32[]{:S(2)}) %collective-permute-start.94) | collective-permute-done | bytes 393248 | tf_op jit(solution)/shard_map/ppermute | solution.py:1369
  588.9 3.6 collective-permute-start.100
  592.5 3.8 collective-permute-done.95
  606.2 5.6 collective-permute-done.102.grad_2
  618.0 13.5 %shard_map.193 = (bf16[128,1536]{1,0:T(8,128)(2,1)}, bf16[128,1536]{1,0:T(8,128)(2,1)}, bf16[128,1536]{1,0:T(8,128)(2,1)}, bf16[128,1536]{1,0:T(8,128)(2,1)}, bf...) custom-call(s32[1]{0:T(128)} %bitcast.1.ctx_ref, ...), custom_call_target="tpu_custom_call" | custom-call | flops 2617245696 | bytes 7864320 | tf_op jit(solution)/shard_map/pallas_call | solution.py:1111
  635.6 3.5 convolution_convert_fusion.4.out
  647.0 4.2 shard_map.194
  663.5 5.9 collective-permute-done.115
  673.3 9.2 %collective-permute-done.111 = bf16[192,1152]{1,0:T(8,128)(2,1)S(1)} collective-permute-done((bf16[192,1152]{1,0:T(8,128)(2,1)S(1)}, bf16[192,1152]{1,0:T(8,128)(2,1)S(1)}, u32[]{:S(2)}, u32[]{:S(2)}) %collective-permute-start.111) | collective-permute-done | bytes 442400 | tf_op jit(solution)/shard_map/ppermute | solution.py:1369
  698.4 9.1 %collective-permute-done.117 = bf16[192,1152]{1,0:T(8,128)(2,1)S(1)} collective-permute-done((bf16[192,1152]{1,0:T(8,128)(2,1)S(1)}, bf16[192,1152]{1,0:T(8,128)(2,1)S(1)}, u32[]{:S(2)}, u32[]{:S(2)}) %collective-permute-start.117) | collective-permute-done | bytes 442400 | tf_op jit(solution)/shard_map/ppermute | solution.py:1369
  713.2 3.9 shard_map.195
  721.3 4.5 collective-permute-done.122
  730.2 3.9 shard_map.197
  (722 shorter events, 265.8 us)
Async XLA Ops:
  7.2 279.6 %all-gather.2.cloned.1.call-start = ((), (), s32[]{:S(2)}) async-start(), calls=%async_computation.1 | async-start | bytes 11796480 | tf_op jit(solution)/shard_map/all_gather | solution.py:1621
  23.3 25.3 %collective-permute-start.15 = (bf16[192,2176]{1,0:T(8,128)(2,1)}, bf16[192,2176]{1,0:T(8,128)(2,1)S(1)}, u32[]{:S(2)}, u32[]{:S(2)}) collective-permute-start(bf16[192,2176]{1,0:T(8,128)(2,1)} %shard_map.170.ids_0), channel_id=1, source_target_pairs={{0,1},{1,0},{2,3},{3,2},{4,5},{5,4},{6,7},{7,6},{8,9},{9,8},{10,11... | collective-permute-start | bytes 2506760 | tf_op jit(solution)/shard_map/ppermute | solution.py:1369
  24.8 23.8 %collective-permute-start.16 = (bf16[192,2176]{1,0:T(8,128)(2,1)}, bf16[192,2176]{1,0:T(8,128)(2,1)}, u32[]{:S(2)}, u32[]{:S(2)}) collective-permute-start(bf16[192,2176]{1,0:T(8,128)(2,1)} %shard_map.170.ids_0), channel_id=1, source_target_pairs={{0,2},{1,3},{2,4},{3,5},{4,6},{5,7},{6,0},{7,1},{8,10},{9,11},{10,... | collective-permute-start | bytes 2506760 | tf_op jit(solution)/shard_map/ppermute | solution.py:1369
  27.9 19.2 %collective-permute-start.3 = (bf16[384,1024]{1,0:T(8,128)(2,1)S(1)}, bf16[384,1024]{1,0:T(8,128)(2,1)S(1)}, u32[]{:S(2)}, u32[]{:S(2)}) collective-permute-start(bf16[384,1024]{1,0:T(8,128)(2,1)S(1)} %get-tuple-element.275.refs_0_), channel_id=1, source_target_pairs={{0,16},{8,24},{16,0},{24,8},{1,17},{9,25},{17,1},{25,9},{2,18},{10... | collective-permute-start | bytes 2359304 | tf_op jit(solution)/shard_map/ppermute | solution.py:1369
  47.1 18.4 %collective-permute-start.4 = (bf16[384,1024]{1,0:T(8,128)(2,1)S(1)}, bf16[384,1024]{1,0:T(8,128)(2,1)}, u32[]{:S(2)}, u32[]{:S(2)}) collective-permute-start(bf16[384,1024]{1,0:T(8,128)(2,1)S(1)} %get-tuple-element.276.refs_4_), channel_id=1, source_target_pairs={{0,16},{8,24},{16,0},{24,8},{1,17},{9,25},{17,1},{25,9},{2,18},{10... | collective-permute-start | bytes 2359304 | tf_op jit(solution)/shard_map/ppermute | solution.py:1369
  48.6 21.2 %collective-permute-start.18 = (bf16[192,2176]{1,0:T(8,128)(2,1)}, bf16[192,2176]{1,0:T(8,128)(2,1)}, u32[]{:S(2)}, u32[]{:S(2)}) collective-permute-start(bf16[192,2176]{1,0:T(8,128)(2,1)} %collective-permute-done.16.ids_0), channel_id=1, source_target_pairs={{0,2},{1,3},{2,4},{3,5},{4,6},{5,7},{6,0},{7,1},{8,10},{9,11},{10,... | collective-permute-start | bytes 2506760 | tf_op jit(solution)/shard_map/ppermute | solution.py:1369
  50.2 19.0 %collective-permute-start.17 = (bf16[192,2176]{1,0:T(8,128)(2,1)}, bf16[192,2176]{1,0:T(8,128)(2,1)}, u32[]{:S(2)}, u32[]{:S(2)}) collective-permute-start(bf16[192,2176]{1,0:T(8,128)(2,1)} %collective-permute-done.16.ids_0), channel_id=1, source_target_pairs={{0,1},{1,0},{2,3},{3,2},{4,5},{5,4},{6,7},{7,6},{8,9},{9,8},{10,11... | collective-permute-start | bytes 2506760 | tf_op jit(solution)/shard_map/ppermute | solution.py:1369
  51.8 18.6 %collective-permute-start.8 = (bf16[384,1024]{1,0:T(8,128)(2,1)S(1)}, bf16[384,1024]{1,0:T(8,128)(2,1)S(1)}, u32[]{:S(2)}, u32[]{:S(2)}) collective-permute-start(bf16[384,1024]{1,0:T(8,128)(2,1)S(1)} %get-tuple-element.275.refs_0_), channel_id=1, source_target_pairs={{0,8},{8,0},{16,24},{24,16},{1,9},{9,1},{17,25},{25,17},{2,10},{10... | collective-permute-start | bytes 2359304 | tf_op jit(solution)/shard_map/ppermute | solution.py:1369
  51.8 22.2 %collective-permute-start.9 = (bf16[384,1024]{1,0:T(8,128)(2,1)S(1)}, bf16[384,1024]{1,0:T(8,128)(2,1)S(1)}, u32[]{:S(2)}, u32[]{:S(2)}) collective-permute-start(bf16[384,1024]{1,0:T(8,128)(2,1)S(1)} %collective-permute-done.3.refs_2_), channel_id=1, source_target_pairs={{0,8},{8,0},{16,24},{24,16},{1,9},{9,1},{17,25},{25,17},{2,10},{10... | collective-permute-start | bytes 2359304 | tf_op jit(solution)/shard_map/ppermute | solution.py:1369
  65.5 12.3 %collective-permute-start.6 = (bf16[128,1536]{1,0:T(8,128)(2,1)}, bf16[128,1536]{1,0:T(8,128)(2,1)S(1)}, u32[]{:S(2)}, u32[]{:S(2)}) collective-permute-start(bf16[128,1536]{1,0:T(8,128)(2,1)} %bitcast.rows_0), channel_id=1, source_target_pairs={{0,16},{8,24},{16,0},{24,8},{1,17},{9,25},{17,1},{25,9},{2,18},{10... | collective-permute-start | bytes 1179656 | tf_op jit(solution)/shard_map/ppermute | solution.py:1369
  69.2 22.3 %collective-permute-start.13 = (bf16[2,128,1536]{2,1,0:T(8,128)(2,1)S(1)}, bf16[2,128,1536]{2,1,0:T(8,128)(2,1)S(1)}, u32[]{:S(2)}, u32[]{:S(2)}) collective-permute-start(bf16[2,128,1536]{2,1,0:T(8,128)(2,1)S(1)} %get-tuple-element.278.refs_8_), channel_id=1, source_target_pairs={{0,16},{8,24},{16,0},{24,8},{1,17},{9,25},{17,1},{25,9},{2,18},{10... | collective-permute-start | bytes 2359304 | tf_op jit(solution)/shard_map/ppermute | solution.py:1369
  69.9 21.7 %collective-permute-start.19 = (bf16[192,2176]{1,0:T(8,128)(2,1)}, bf16[192,2176]{1,0:T(8,128)(2,1)S(1)}, u32[]{:S(2)}, u32[]{:S(2)}) collective-permute-start(bf16[192,2176]{1,0:T(8,128)(2,1)} %collective-permute-done.18.ids_0), channel_id=1, source_target_pairs={{0,1},{1,0},{2,3},{3,2},{4,5},{5,4},{6,7},{7,6},{8,9},{9,8},{10,11... | collective-permute-start | bytes 2506760 | tf_op jit(solution)/shard_map/ppermute | solution.py:1369
  70.4 21.7 %collective-permute-start.20 = (bf16[192,2176]{1,0:T(8,128)(2,1)}, bf16[192,2176]{1,0:T(8,128)(2,1)S(1)}, u32[]{:S(2)}, u32[]{:S(2)}) collective-permute-start(bf16[192,2176]{1,0:T(8,128)(2,1)} %shard_map.170.ids_0), channel_id=1, source_target_pairs={{0,6},{1,7},{2,0},{3,1},{4,2},{5,3},{6,4},{7,5},{8,14},{9,15},{10,... | collective-permute-start | bytes 2506760 | tf_op jit(solution)/shard_map/ppermute | solution.py:1369
  77.8 14.6 %collective-permute-start.10 = (bf16[384,1024]{1,0:T(8,128)(2,1)S(1)}, bf16[384,1024]{1,0:T(8,128)(2,1)S(1)}, u32[]{:S(2)}, u32[]{:S(2)}) collective-permute-start(bf16[384,1024]{1,0:T(8,128)(2,1)S(1)} %get-tuple-element.276.refs_4_), channel_id=1, source_target_pairs={{0,8},{8,0},{16,24},{24,16},{1,9},{9,1},{17,25},{25,17},{2,10},{10... | collective-permute-start | bytes 2359304 | tf_op jit(solution)/shard_map/ppermute | solution.py:1369
  78.0 15.0 %collective-permute-start.7 = (bf16[128,1536]{1,0:T(8,128)(2,1)S(1)}, bf16[128,1536]{1,0:T(8,128)(2,1)S(1)}, u32[]{:S(2)}, u32[]{:S(2)}) collective-permute-start(bf16[128,1536]{1,0:T(8,128)(2,1)S(1)} %collective-permute-done.6.rows_2), channel_id=1, source_target_pairs={{0,8},{8,0},{16,24},{24,16},{1,9},{9,1},{17,25},{25,17},{2,10},{10... | collective-permute-start | bytes 1179656 | tf_op jit(solution)/shard_map/ppermute | solution.py:1369
  92.4 12.1 %collective-permute-start.21 = (bf16[96,2176]{1,0:T(8,128)(2,1)S(1)}, bf16[96,2176]{1,0:T(8,128)(2,1)S(1)}, u32[]{:S(2)}, u32[]{:S(2)}) collective-permute-start(bf16[96,2176]{1,0:T(8,128)(2,1)S(1)} %slice.158), channel_id=1, source_target_pairs={{0,1},{1,0},{2,3},{3,2},{4,5},{5,4},{6,7},{7,6},{8,9},{9,8},{10,11... | collective-permute-start | bytes 1253384 | tf_op jit(solution)/shard_map/ppermute | solution.py:1369
  124.4 12.4 %collective-permute-start.23 = (bf16[128,1536]{1,0:T(8,128)(2,1)S(1)}, bf16[128,1536]{1,0:T(8,128)(2,1)S(1)}, u32[]{:S(2)}, u32[]{:S(2)}) collective-permute-start(bf16[128,1536]{1,0:T(8,128)(2,1)S(1)} %copy-done.164), channel_id=1, source_target_pairs={{0,8},{8,0},{16,24},{24,16},{1,9},{9,1},{17,25},{25,17},{2,10},{10... | collective-permute-start | bytes 1179656 | tf_op jit(solution)/shard_map/ppermute | solution.py:1369
  138.1 575.1 %reduce-scatter.2.cloned.1.call-start = ((), (), s32[]{:S(2)}) async-start(), calls=%async_computation.2 | async-start | bytes 3932160 | tf_op jit(solution)/shard_map/reduce_scatter | solution.py:1666
  141.2 12.9 %collective-permute-start.26 = (bf16[128,1536]{1,0:T(8,128)(2,1)S(1)}, bf16[128,1536]{1,0:T(8,128)(2,1)S(1)}, u32[]{:S(2)}, u32[]{:S(2)}) collective-permute-start(bf16[128,1536]{1,0:T(8,128)(2,1)S(1)} %multiply_convert_fusion.2.rows_0), channel_id=1, source_target_pairs={{0,2},{1,3},{2,4},{3,5},{4,6},{5,7},{6,0},{7,1},{8,10},{9,11},{10,... | collective-permute-start | bytes 1179656 | tf_op jit(solution)/shard_map/ppermute | solution.py:1369
  142.5 14.0 %collective-permute-start.27 = (bf16[128,1536]{1,0:T(8,128)(2,1)S(1)}, bf16[128,1536]{1,0:T(8,128)(2,1)S(1)}, u32[]{:S(2)}, u32[]{:S(2)}) collective-permute-start(bf16[128,1536]{1,0:T(8,128)(2,1)S(1)} %multiply_convert_fusion.2.rows_0), channel_id=1, source_target_pairs={{0,1},{1,0},{2,3},{3,2},{4,5},{5,4},{6,7},{7,6},{8,9},{9,8},{10,11... | collective-permute-start | bytes 1179656 | tf_op jit(solution)/shard_map/ppermute | solution.py:1369
  155.1 14.2 %collective-permute-start.29 = (bf16[128,1536]{1,0:T(8,128)(2,1)S(1)}, bf16[128,1536]{1,0:T(8,128)(2,1)S(1)}, u32[]{:S(2)}, u32[]{:S(2)}) collective-permute-start(bf16[128,1536]{1,0:T(8,128)(2,1)S(1)} %collective-permute-done.26.rows_0), channel_id=1, source_target_pairs={{0,1},{1,0},{2,3},{3,2},{4,5},{5,4},{6,7},{7,6},{8,9},{9,8},{10,11... | collective-permute-start | bytes 1179656 | tf_op jit(solution)/shard_map/ppermute | solution.py:1369
  209.8 16.3 %collective-permute-start.38 = (bf16[128,1536]{1,0:T(8,128)(2,1)S(1)}, bf16[128,1536]{1,0:T(8,128)(2,1)S(1)}, u32[]{:S(2)}, u32[]{:S(2)}) collective-permute-start(bf16[128,1536]{1,0:T(8,128)(2,1)S(1)} %add_convert_fusion.19), channel_id=1, source_target_pairs={{0,2},{1,3},{2,4},{3,5},{4,6},{5,7},{6,0},{7,1},{8,10},{9,11},{10,... | collective-permute-start | bytes 1179656 | tf_op jit(solution)/shard_map/ppermute | solution.py:1369
  272.4 12.1 %collective-permute-start.46 = (bf16[128,1536]{1,0:T(8,128)(2,1)S(1)}, bf16[128,1536]{1,0:T(8,128)(2,1)S(1)}, u32[]{:S(2)}, u32[]{:S(2)}) collective-permute-start(bf16[128,1536]{1,0:T(8,128)(2,1)S(1)} %multiply_convert_fusion.rows_0), channel_id=1, source_target_pairs={{0,2},{1,3},{2,4},{3,5},{4,6},{5,7},{6,0},{7,1},{8,10},{9,11},{10,... | collective-permute-start | bytes 1179656 | tf_op jit(solution)/shard_map/ppermute | solution.py:1369
  272.4 14.3 %collective-permute-start.47 = (bf16[128,1536]{1,0:T(8,128)(2,1)S(1)}, bf16[128,1536]{1,0:T(8,128)(2,1)S(1)}, u32[]{:S(2)}, u32[]{:S(2)}) collective-permute-start(bf16[128,1536]{1,0:T(8,128)(2,1)S(1)} %multiply_convert_fusion.rows_0), channel_id=1, source_target_pairs={{0,1},{1,0},{2,3},{3,2},{4,5},{5,4},{6,7},{7,6},{8,9},{9,8},{10,11... | collective-permute-start | bytes 1179656 | tf_op jit(solution)/shard_map/ppermute | solution.py:1369
  285.3 14.6 %collective-permute-start.49 = (bf16[128,1536]{1,0:T(8,128)(2,1)S(1)}, bf16[128,1536]{1,0:T(8,128)(2,1)S(1)}, u32[]{:S(2)}, u32[]{:S(2)}) collective-permute-start(bf16[128,1536]{1,0:T(8,128)(2,1)S(1)} %collective-permute-done.46.rows_0), channel_id=1, source_target_pairs={{0,1},{1,0},{2,3},{3,2},{4,5},{5,4},{6,7},{7,6},{8,9},{9,8},{10,11... | collective-permute-start | bytes 1179656 | tf_op jit(solution)/shard_map/ppermute | solution.py:1369
  295.8 12.5 %collective-permute-start.50 = (bf16[128,1536]{1,0:T(8,128)(2,1)}, bf16[128,1536]{1,0:T(8,128)(2,1)S(1)}, u32[]{:S(2)}, u32[]{:S(2)}) collective-permute-start(bf16[128,1536]{1,0:T(8,128)(2,1)} %copy-done.53), channel_id=1, source_target_pairs={{0,6},{1,7},{2,0},{3,1},{4,2},{5,3},{6,4},{7,5},{8,14},{9,15},{10,... | collective-permute-start | bytes 1179656 | tf_op jit(solution)/shard_map/ppermute | solution.py:1369
  339.8 12.5 %collective-permute-start.58 = (bf16[128,1536]{1,0:T(8,128)(2,1)S(1)}, bf16[128,1536]{1,0:T(8,128)(2,1)S(1)}, u32[]{:S(2)}, u32[]{:S(2)}) collective-permute-start(bf16[128,1536]{1,0:T(8,128)(2,1)S(1)} %add_convert_fusion.15), channel_id=1, source_target_pairs={{0,2},{1,3},{2,4},{3,5},{4,6},{5,7},{6,0},{7,1},{8,10},{9,11},{10,... | collective-permute-start | bytes 1179656 | tf_op jit(solution)/shard_map/ppermute | solution.py:1369
  360.5 13.1 %collective-permute-start.60 = (bf16[128,1664]{1,0:T(8,128)(2,1)S(1)}, bf16[128,1664]{1,0:T(8,128)(2,1)S(1)}, u32[]{:S(2)}, u32[]{:S(2)}) collective-permute-start(bf16[128,1664]{1,0:T(8,128)(2,1)S(1)} %pad_maximum_fusion.grads_0), channel_id=1, source_target_pairs={{0,2},{1,3},{2,4},{3,5},{4,6},{5,7},{6,0},{7,1},{8,10},{9,11},{10,... | collective-permute-start | bytes 1277960 | tf_op jit(solution)/shard_map/ppermute | solution.py:1369
  360.5 17.3 %collective-permute-start.61 = (bf16[128,1664]{1,0:T(8,128)(2,1)S(1)}, bf16[128,1664]{1,0:T(8,128)(2,1)S(1)}, u32[]{:S(2)}, u32[]{:S(2)}) collective-permute-start(bf16[128,1664]{1,0:T(8,128)(2,1)S(1)} %pad_maximum_fusion.grads_0), channel_id=1, source_target_pairs={{0,1},{1,0},{2,3},{3,2},{4,5},{5,4},{6,7},{7,6},{8,9},{9,8},{10,11... | collective-permute-start | bytes 1277960 | tf_op jit(solution)/shard_map/ppermute | solution.py:1369
  373.5 13.1 %collective-permute-start.62 = (bf16[128,1664]{1,0:T(8,128)(2,1)S(1)}, bf16[128,1664]{1,0:T(8,128)(2,1)S(1)}, u32[]{:S(2)}, u32[]{:S(2)}) collective-permute-start(bf16[128,1664]{1,0:T(8,128)(2,1)S(1)} %collective-permute-done.60.grads_0), channel_id=1, source_target_pairs={{0,2},{1,3},{2,4},{3,5},{4,6},{5,7},{6,0},{7,1},{8,10},{9,11},{10,... | collective-permute-start | bytes 1277960 | tf_op jit(solution)/shard_map/ppermute | solution.py:1369
  373.7 16.6 %collective-permute-start.63 = (bf16[128,1664]{1,0:T(8,128)(2,1)S(1)}, bf16[128,1664]{1,0:T(8,128)(2,1)S(1)}, u32[]{:S(2)}, u32[]{:S(2)}) collective-permute-start(bf16[128,1664]{1,0:T(8,128)(2,1)S(1)} %collective-permute-done.60.grads_0), channel_id=1, source_target_pairs={{0,1},{1,0},{2,3},{3,2},{4,5},{5,4},{6,7},{7,6},{8,9},{9,8},{10,11... | collective-permute-start | bytes 1277960 | tf_op jit(solution)/shard_map/ppermute | solution.py:1369
  386.6 12.4 %collective-permute-start.64 = (bf16[128,1664]{1,0:T(8,128)(2,1)}, bf16[128,1664]{1,0:T(8,128)(2,1)S(1)}, u32[]{:S(2)}, u32[]{:S(2)}) collective-permute-start(bf16[128,1664]{1,0:T(8,128)(2,1)} %copy-done.52), channel_id=1, source_target_pairs={{0,6},{1,7},{2,0},{3,1},{4,2},{5,3},{6,4},{7,5},{8,14},{9,15},{10,... | collective-permute-start | bytes 1277960 | tf_op jit(solution)/shard_map/ppermute | solution.py:1369
  424.1 17.6 %collective-permute-start.73 = (bf16[768,1024]{1,0:T(8,128)(2,1)S(1)}, bf16[768,1024]{1,0:T(8,128)(2,1)S(1)}, u32[]{:S(2)}, u32[]{:S(2)}) collective-permute-start(bf16[768,1024]{1,0:T(8,128)(2,1)S(1)} %convolution_convert_fusion.9), channel_id=1, source_target_pairs={{0,8},{8,0},{16,24},{24,16},{1,9},{9,1},{17,25},{25,17},{2,10},{10... | collective-permute-start | bytes 4718600 | tf_op jit(solution)/shard_map/ppermute | solution.py:1369
  426.1 15.7 %collective-permute-start.74 = (bf16[768,1024]{1,0:T(8,128)(2,1)S(1)}, bf16[768,1024]{1,0:T(8,128)(2,1)S(1)}, u32[]{:S(2)}, u32[]{:S(2)}) collective-permute-start(bf16[768,1024]{1,0:T(8,128)(2,1)S(1)} %convolution_convert_fusion.8), channel_id=1, source_target_pairs={{0,8},{8,0},{16,24},{24,16},{1,9},{9,1},{17,25},{25,17},{2,10},{10... | collective-permute-start | bytes 4718600 | tf_op jit(solution)/shard_map/ppermute | solution.py:1369
  431.0 12.8 %collective-permute-start.72 = (bf16[128,1536]{1,0:T(8,128)(2,1)S(1)}, bf16[128,1536]{1,0:T(8,128)(2,1)S(1)}, u32[]{:S(2)}, u32[]{:S(2)}) collective-permute-start(bf16[128,1536]{1,0:T(8,128)(2,1)S(1)} %add_convert_fusion.11), channel_id=1, source_target_pairs={{0,2},{1,3},{2,4},{3,5},{4,6},{5,7},{6,0},{7,1},{8,10},{9,11},{10,... | collective-permute-start | bytes 1179656 | tf_op jit(solution)/shard_map/ppermute | solution.py:1369
  455.4 12.6 %collective-permute-start.76 = (bf16[128,1536]{1,0:T(8,128)(2,1)}, bf16[128,1536]{1,0:T(8,128)(2,1)}, u32[]{:S(2)}, u32[]{:S(2)}) collective-permute-start(bf16[128,1536]{1,0:T(8,128)(2,1)} %get-tuple-element.549.grad_0), channel_id=1, source_target_pairs={{0,8},{8,0},{16,24},{24,16},{1,9},{9,1},{17,25},{25,17},{2,10},{10... | collective-permute-start | bytes 1179656 | tf_op jit(solution)/shard_map/ppermute | solution.py:1369
  483.5 17.6 %collective-permute-start.79 = (bf16[128,1536]{1,0:T(8,128)(2,1)}, bf16[128,1536]{1,0:T(8,128)(2,1)}, u32[]{:S(2)}, u32[]{:S(2)}) collective-permute-start(bf16[128,1536]{1,0:T(8,128)(2,1)} %get-tuple-element.412), channel_id=1, source_target_pairs={{0,8},{8,0},{16,24},{24,16},{1,9},{9,1},{17,25},{25,17},{2,10},{10... | collective-permute-start | bytes 1179656 | tf_op jit(solution)/shard_map/ppermute | solution.py:1369
  488.6 12.4 %collective-permute-start.81 = (bf16[128,1536]{1,0:T(8,128)(2,1)S(1)}, bf16[128,1536]{1,0:T(8,128)(2,1)S(1)}, u32[]{:S(2)}, u32[]{:S(2)}) collective-permute-start(bf16[128,1536]{1,0:T(8,128)(2,1)S(1)} %add_convert_fusion.9), channel_id=1, source_target_pairs={{0,16},{8,24},{16,0},{24,8},{1,17},{9,25},{17,1},{25,9},{2,18},{10... | collective-permute-start | bytes 1179656 | tf_op jit(solution)/shard_map/ppermute | solution.py:1369
  504.5 14.6 %collective-permute-start.82 = (bf16[128,1664]{1,0:T(8,128)(2,1)S(1)}, bf16[128,1664]{1,0:T(8,128)(2,1)}, u32[]{:S(2)}, u32[]{:S(2)}) collective-permute-start(bf16[128,1664]{1,0:T(8,128)(2,1)S(1)} %pad_maximum_fusion.1.grads_0), channel_id=1, source_target_pairs={{0,2},{1,3},{2,4},{3,5},{4,6},{5,7},{6,0},{7,1},{8,10},{9,11},{10,... | collective-permute-start | bytes 1277960 | tf_op jit(solution)/shard_map/ppermute | solution.py:1369
  505.9 16.2 %collective-permute-start.83 = (bf16[128,1664]{1,0:T(8,128)(2,1)S(1)}, bf16[128,1664]{1,0:T(8,128)(2,1)S(1)}, u32[]{:S(2)}, u32[]{:S(2)}) collective-permute-start(bf16[128,1664]{1,0:T(8,128)(2,1)S(1)} %pad_maximum_fusion.1.grads_0), channel_id=1, source_target_pairs={{0,1},{1,0},{2,3},{3,2},{4,5},{5,4},{6,7},{7,6},{8,9},{9,8},{10,11... | collective-permute-start | bytes 1277960 | tf_op jit(solution)/shard_map/ppermute | solution.py:1369
  509.9 35.9 %collective-permute-start.89 = (bf16[384,1024]{1,0:T(8,128)(2,1)}, bf16[384,1024]{1,0:T(8,128)(2,1)}, u32[]{:S(2)}, u32[]{:S(2)}) collective-permute-start(bf16[384,1024]{1,0:T(8,128)(2,1)} %get-tuple-element.567), channel_id=1, source_target_pairs={{0,16},{8,24},{16,0},{24,8},{1,17},{9,25},{17,1},{25,9},{2,18},{10... | collective-permute-start | bytes 2359304 | tf_op jit(solution)/shard_map/ppermute | solution.py:1369
  519.1 13.4 %collective-permute-start.84 = (bf16[128,1664]{1,0:T(8,128)(2,1)}, bf16[128,1664]{1,0:T(8,128)(2,1)S(1)}, u32[]{:S(2)}, u32[]{:S(2)}) collective-permute-start(bf16[128,1664]{1,0:T(8,128)(2,1)} %collective-permute-done.82.grads_0), channel_id=1, source_target_pairs={{0,2},{1,3},{2,4},{3,5},{4,6},{5,7},{6,0},{7,1},{8,10},{9,11},{10,... | collective-permute-start | bytes 1277960 | tf_op jit(solution)/shard_map/ppermute | solution.py:1369
  520.8 15.5 %collective-permute-start.85 = (bf16[128,1664]{1,0:T(8,128)(2,1)}, bf16[128,1664]{1,0:T(8,128)(2,1)S(1)}, u32[]{:S(2)}, u32[]{:S(2)}) collective-permute-start(bf16[128,1664]{1,0:T(8,128)(2,1)} %collective-permute-done.82.grads_0), channel_id=1, source_target_pairs={{0,1},{1,0},{2,3},{3,2},{4,5},{5,4},{6,7},{7,6},{8,9},{9,8},{10,11... | collective-permute-start | bytes 1277960 | tf_op jit(solution)/shard_map/ppermute | solution.py:1369
  532.5 12.4 %collective-permute-start.86 = (bf16[128,1664]{1,0:T(8,128)(2,1)S(1)}, bf16[128,1664]{1,0:T(8,128)(2,1)S(1)}, u32[]{:S(2)}, u32[]{:S(2)}) collective-permute-start(bf16[128,1664]{1,0:T(8,128)(2,1)S(1)} %copy-done.51), channel_id=1, source_target_pairs={{0,6},{1,7},{2,0},{3,1},{4,2},{5,3},{6,4},{7,5},{8,14},{9,15},{10,... | collective-permute-start | bytes 1277960 | tf_op jit(solution)/shard_map/ppermute | solution.py:1369
  534.8 21.0 %collective-permute-start.87 = (bf16[384,1024]{1,0:T(8,128)(2,1)S(1)}, bf16[384,1024]{1,0:T(8,128)(2,1)S(1)}, u32[]{:S(2)}, u32[]{:S(2)}) collective-permute-start(bf16[384,1024]{1,0:T(8,128)(2,1)S(1)} %get-tuple-element.565), channel_id=1, source_target_pairs={{0,16},{8,24},{16,0},{24,8},{1,17},{9,25},{17,1},{25,9},{2,18},{10... | collective-permute-start | bytes 2359304 | tf_op jit(solution)/shard_map/ppermute | solution.py:1369
  570.5 18.4 %collective-permute-start.97 = (bf16[768,1024]{1,0:T(8,128)(2,1)S(1)}, bf16[768,1024]{1,0:T(8,128)(2,1)S(1)}, u32[]{:S(2)}, u32[]{:S(2)}) collective-permute-start(bf16[768,1024]{1,0:T(8,128)(2,1)S(1)} %convolution_convert_fusion.7), channel_id=1, source_target_pairs={{0,8},{8,0},{16,24},{24,16},{1,9},{9,1},{17,25},{25,17},{2,10},{10... | collective-permute-start | bytes 4718600 | tf_op jit(solution)/shard_map/ppermute | solution.py:1369
  572.4 16.4 %collective-permute-start.98 = (bf16[768,1024]{1,0:T(8,128)(2,1)S(1)}, bf16[768,1024]{1,0:T(8,128)(2,1)S(1)}, u32[]{:S(2)}, u32[]{:S(2)}) collective-permute-start(bf16[768,1024]{1,0:T(8,128)(2,1)S(1)} %convolution_convert_fusion.6), channel_id=1, source_target_pairs={{0,8},{8,0},{16,24},{24,16},{1,9},{9,1},{17,25},{25,17},{2,10},{10... | collective-permute-start | bytes 4718600 | tf_op jit(solution)/shard_map/ppermute | solution.py:1369
  575.0 13.9 %collective-permute-start.99 = (bf16[512,1536]{1,0:T(8,128)(2,1)S(1)}, bf16[512,1536]{1,0:T(8,128)(2,1)S(1)}, u32[]{:S(2)}, u32[]{:S(2)}) collective-permute-start(bf16[512,1536]{1,0:T(8,128)(2,1)S(1)} %convolution_convert_fusion.3), channel_id=1, source_target_pairs={{0,8},{8,0},{16,24},{24,16},{1,9},{9,1},{17,25},{25,17},{2,10},{10... | collective-permute-start | bytes 4718600 | tf_op jit(solution)/shard_map/ppermute | solution.py:1369
  577.8 14.7 %collective-permute-start.96 = (bf16[128,1536]{1,0:T(8,128)(2,1)S(1)}, bf16[128,1536]{1,0:T(8,128)(2,1)S(1)}, u32[]{:S(2)}, u32[]{:S(2)}) collective-permute-start(bf16[128,1536]{1,0:T(8,128)(2,1)S(1)} %add_convert_fusion.7), channel_id=1, source_target_pairs={{0,2},{1,3},{2,4},{3,5},{4,6},{5,7},{6,0},{7,1},{8,10},{9,11},{10,... | collective-permute-start | bytes 1179656 | tf_op jit(solution)/shard_map/ppermute | solution.py:1369
  600.2 12.4 %collective-permute-start.108 = (bf16[192,1152]{1,0:T(8,128)(2,1)}, bf16[192,1152]{1,0:T(8,128)(2,1)}, u32[]{:S(2)}, u32[]{:S(2)}) collective-permute-start(bf16[192,1152]{1,0:T(8,128)(2,1)} %bitcast.47), channel_id=1, source_target_pairs={{0,1},{1,0},{2,3},{3,2},{4,5},{5,4},{6,7},{7,6},{8,9},{9,8},{10,11... | collective-permute-start | bytes 1327112 | tf_op jit(solution)/shard_map/ppermute | solution.py:1369
  605.2 35.0 %collective-permute-start.107 = (bf16[192,1152]{1,0:T(8,128)(2,1)}, bf16[192,1152]{1,0:T(8,128)(2,1)}, u32[]{:S(2)}, u32[]{:S(2)}) collective-permute-start(bf16[192,1152]{1,0:T(8,128)(2,1)} %bitcast.190), channel_id=1, source_target_pairs={{0,1},{1,0},{2,3},{3,2},{4,5},{5,4},{6,7},{7,6},{8,9},{9,8},{10,11... | collective-permute-start | bytes 1327112 | tf_op jit(solution)/shard_map/ppermute | solution.py:1369
  614.8 25.5 %collective-permute-start.109 = (bf16[192,1152]{1,0:T(8,128)(2,1)}, bf16[192,1152]{1,0:T(8,128)(2,1)}, u32[]{:S(2)}, u32[]{:S(2)}) collective-permute-start(bf16[192,1152]{1,0:T(8,128)(2,1)} %fusion.16), channel_id=1, source_target_pairs={{0,2},{1,3},{2,4},{3,5},{4,6},{5,7},{6,0},{7,1},{8,10},{9,11},{10,... | collective-permute-start | bytes 1327112 | tf_op jit(solution)/shard_map/ppermute | solution.py:1369
  631.6 19.7 %collective-permute-start.105 = (bf16[128,1536]{1,0:T(8,128)(2,1)}, bf16[128,1536]{1,0:T(8,128)(2,1)}, u32[]{:S(2)}, u32[]{:S(2)}) collective-permute-start(bf16[128,1536]{1,0:T(8,128)(2,1)} %get-tuple-element.489), channel_id=1, source_target_pairs={{0,8},{8,0},{16,24},{24,16},{1,9},{9,1},{17,25},{25,17},{2,10},{10... | collective-permute-start | bytes 1179656 | tf_op jit(solution)/shard_map/ppermute | solution.py:1369
  634.3 57.6 %collective-permute-start.104 = (bf16[128,1536]{1,0:T(8,128)(2,1)}, bf16[128,1536]{1,0:T(8,128)(2,1)S(1)}, u32[]{:S(2)}, u32[]{:S(2)}) collective-permute-start(bf16[128,1536]{1,0:T(8,128)(2,1)} %get-tuple-element.487), channel_id=1, source_target_pairs={{0,8},{8,0},{16,24},{24,16},{1,9},{9,1},{17,25},{25,17},{2,10},{10... | collective-permute-start | bytes 1179656 | tf_op jit(solution)/shard_map/ppermute | solution.py:1369
  642.4 27.7 %collective-permute-start.112 = (bf16[192,1152]{1,0:T(8,128)(2,1)}, bf16[192,1152]{1,0:T(8,128)(2,1)}, u32[]{:S(2)}, u32[]{:S(2)}) collective-permute-start(bf16[192,1152]{1,0:T(8,128)(2,1)} %fusion.18), channel_id=1, source_target_pairs={{0,2},{1,3},{2,4},{3,5},{4,6},{5,7},{6,0},{7,1},{8,10},{9,11},{10,... | collective-permute-start | bytes 1327112 | tf_op jit(solution)/shard_map/ppermute | solution.py:1369
  652.5 31.5 %collective-permute-start.106 = (bf16[128,1536]{1,0:T(8,128)(2,1)S(1)}, bf16[128,1536]{1,0:T(8,128)(2,1)S(1)}, u32[]{:S(2)}, u32[]{:S(2)}) collective-permute-start(bf16[128,1536]{1,0:T(8,128)(2,1)S(1)} %add_convert_fusion.5), channel_id=1, source_target_pairs={{0,16},{8,24},{16,0},{24,8},{1,17},{9,25},{17,1},{25,9},{2,18},{10... | collective-permute-start | bytes 1179656 | tf_op jit(solution)/shard_map/ppermute | solution.py:1369
  656.1 15.5 %collective-permute-start.113 = (bf16[192,1152]{1,0:T(8,128)(2,1)S(1)}, bf16[192,1152]{1,0:T(8,128)(2,1)S(1)}, u32[]{:S(2)}, u32[]{:S(2)}) collective-permute-start(bf16[192,1152]{1,0:T(8,128)(2,1)S(1)} %fusion.19), channel_id=1, source_target_pairs={{0,6},{1,7},{2,0},{3,1},{4,2},{5,3},{6,4},{7,5},{8,14},{9,15},{10,... | collective-permute-start | bytes 1327112 | tf_op jit(solution)/shard_map/ppermute | solution.py:1369
  669.4 13.1 %collective-permute-start.111 = (bf16[192,1152]{1,0:T(8,128)(2,1)S(1)}, bf16[192,1152]{1,0:T(8,128)(2,1)S(1)}, u32[]{:S(2)}, u32[]{:S(2)}) collective-permute-start(bf16[192,1152]{1,0:T(8,128)(2,1)S(1)} %bitcast.188), channel_id=1, source_target_pairs={{0,1},{1,0},{2,3},{3,2},{4,5},{5,4},{6,7},{7,6},{8,9},{9,8},{10,11... | collective-permute-start | bytes 1327112 | tf_op jit(solution)/shard_map/ppermute | solution.py:1369
  670.1 24.4 %collective-permute-start.114 = (bf16[192,1152]{1,0:T(8,128)(2,1)S(1)}, bf16[192,1152]{1,0:T(8,128)(2,1)S(1)}, u32[]{:S(2)}, u32[]{:S(2)}) collective-permute-start(bf16[192,1152]{1,0:T(8,128)(2,1)S(1)} %bitcast.192), channel_id=1, source_target_pairs={{0,1},{1,0},{2,3},{3,2},{4,5},{5,4},{6,7},{7,6},{8,9},{9,8},{10,11... | collective-permute-start | bytes 1327112 | tf_op jit(solution)/shard_map/ppermute | solution.py:1369
  671.6 49.7 %collective-permute-start.120 = (bf16[384,1024]{1,0:T(8,128)(2,1)}, bf16[384,1024]{1,0:T(8,128)(2,1)}, u32[]{:S(2)}, u32[]{:S(2)}) collective-permute-start(bf16[384,1024]{1,0:T(8,128)(2,1)} %get-tuple-element.564), channel_id=1, source_target_pairs={{0,16},{8,24},{16,0},{24,8},{1,17},{9,25},{17,1},{25,9},{2,18},{10... | collective-permute-start | bytes 2359304 | tf_op jit(solution)/shard_map/ppermute | solution.py:1369
  682.5 12.1 %collective-permute-start.116 = (bf16[192,1152]{1,0:T(8,128)(2,1)S(1)}, bf16[192,1152]{1,0:T(8,128)(2,1)S(1)}, u32[]{:S(2)}, u32[]{:S(2)}) collective-permute-start(bf16[192,1152]{1,0:T(8,128)(2,1)S(1)} %fusion.11), channel_id=1, source_target_pairs={{0,2},{1,3},{2,4},{3,5},{4,6},{5,7},{6,0},{7,1},{8,10},{9,11},{10,... | collective-permute-start | bytes 1327112 | tf_op jit(solution)/shard_map/ppermute | solution.py:1369
  686.9 34.4 %collective-permute-start.121 = (bf16[384,1024]{1,0:T(8,128)(2,1)S(1)}, bf16[384,1024]{1,0:T(8,128)(2,1)S(1)}, u32[]{:S(2)}, u32[]{:S(2)}) collective-permute-start(bf16[384,1024]{1,0:T(8,128)(2,1)S(1)} %get-tuple-element.562), channel_id=1, source_target_pairs={{0,16},{8,24},{16,0},{24,8},{1,17},{9,25},{17,1},{25,9},{2,18},{10... | collective-permute-start | bytes 2359304 | tf_op jit(solution)/shard_map/ppermute | solution.py:1369
  691.9 37.4 %collective-permute-start.126 = (bf16[256,1536]{1,0:T(8,128)(2,1)S(1)}, bf16[256,1536]{1,0:T(8,128)(2,1)S(1)}, u32[]{:S(2)}, u32[]{:S(2)}) collective-permute-start(bf16[256,1536]{1,0:T(8,128)(2,1)S(1)} %get-tuple-element.559), channel_id=1, source_target_pairs={{0,16},{8,24},{16,0},{24,8},{1,17},{9,25},{17,1},{25,9},{2,18},{10... | collective-permute-start | bytes 2359304 | tf_op jit(solution)/shard_map/ppermute | solution.py:1369
  696.7 20.4 %collective-permute-start.119 = (bf16[192,1152]{1,0:T(8,128)(2,1)}, bf16[192,1152]{1,0:T(8,128)(2,1)}, u32[]{:S(2)}, u32[]{:S(2)}) collective-permute-start(bf16[192,1152]{1,0:T(8,128)(2,1)} %fusion.13), channel_id=1, source_target_pairs={{0,2},{1,3},{2,4},{3,5},{4,6},{5,7},{6,0},{7,1},{8,10},{9,11},{10,... | collective-permute-start | bytes 1327112 | tf_op jit(solution)/shard_map/ppermute | solution.py:1369
  (239 other events, 2693.1 us)
Sparse Core Ops, SparseCore 0:
  138.2 66.0 all-gather.1
  605.3 38.7 reduce-scatter.1
